TPU v7x, 32 devices: a whole 2x2x4 slice. The times are simulated.
32 devices in a mesh: cell: 16 (over z, x, core), blk: 2 (over y).
Axes of the slice: x: 2, y: 2, z: 4, core: 2. Of those that a mesh axis runs over, the one named last changes fastest.
Arguments:
- hidden_in: bfloat16 [32, 1024, 1280], P('cell', 'blk'), may hold values from -6 to 6
- lengths: int32 [32], P('cell'), may hold values from 256 to 1024, as said below
- ln1_gain: float32 [1280], replicated, may hold values from 0.1 to 1.9
- ln1_bias: float32 [1280], replicated, may hold values from -1.75 to 1.75
- w_qkv: bfloat16 [1280, 3840], P('cell'), may hold values from -0.15625 to 0.15625
- q_bias: float32 [1280], replicated, may hold values from -3 to 3
- v_bias: float32 [1280], replicated, may hold values from -0.3125 to 0.3125
- w_out: bfloat16 [1280, 1280], P('cell'), may hold values from -2.5 to 2.5
- out_bias: float32 [1280], replicated, may hold values from -1.75 to 1.75
- ln2_gain: float32 [1280], replicated, may hold values from 0.1 to 1.9
- ln2_bias: float32 [1280], replicated, may hold values from -1.75 to 1.75
- w_up: bfloat16 [5120, 1280], P('cell'), may hold values from -0.15625 to 0.15625
- up_bias: float32 [5120], replicated, may hold values from -3 to 3
- w_down: bfloat16 [5120, 1280], P('cell'), may hold values from -0.078125 to 0.078125
- down_bias: float32 [1280], replicated, may hold values from -1.75 to 1.75
- cotangent: bfloat16 [32, 1024, 1280], P('cell', 'blk'), may hold values from -6 to 6
Outputs:
- out_hidden: bfloat16 [32, 1024, 1280], P('cell', 'blk')
- in_grad: float32 [32, 1024, 1280], P('cell', 'blk')
- ln1_gain_grad: float32 [1280], replicated
- ln1_bias_grad: float32 [1280], replicated
- w_qkv_grad: float32 [1280, 3840], P('cell')
- q_bias_grad: float32 [1280], replicated
- v_bias_grad: float32 [1280], replicated
- w_out_grad: float32 [1280, 1280], P('cell')
- out_bias_grad: float32 [1280], replicated
- ln2_gain_grad: float32 [1280], replicated
- ln2_bias_grad: float32 [1280], replicated
- w_up_grad: float32 [5120, 1280], P('cell')
- up_bias_grad: float32 [5120], replicated
- w_down_grad: float32 [5120, 1280], P('cell')
- down_bias_grad: float32 [1280], replicated
Inputs may be any that keep to these rules, and one draw needn't show every extreme that they name: `lengths`: in each aligned block of 2 cells, one cell drawn from the seed has exactly 1024 valid genes; the others have 1024 // 4 to 1024.
All inputs are finite; a program needn't handle non-finite values.
Results may differ from a plain program's by a relative error of at most 0.015.
Values may be sent and summed in bfloat16 or wider, within the bound.
No kernel may reach another device: no remote copies, remote signals or barrier semaphores. Data moves between devices by JAX's collectives and lax.ppermute only.
A program may use at most 576 MiB of HBM per device.

v0:
```python
from functools import partial
import math

import jax
import jax.numpy as jnp
from jax import lax
from jax.sharding import PartitionSpec as P

HEAD_DIM = 64


epsilon = 1e-05
far_below = -1e30
row_contract = (((0,), (0,)), ((), ()))
col_contract = (((1,), (1,)), ((), ()))


def passed_along(x, axis, by):
    count = lax.axis_size(axis)
    return lax.ppermute(x, axis, [(i, (i + by) % count) for i in range(count)])


def layer_norm(source, gain_vec, shift_vec):
    row_mean = jnp.mean(source, axis=-1, keepdims=True)
    centered = source - row_mean
    row_var = jnp.mean(centered * centered, axis=-1, keepdims=True)
    return centered * lax.rsqrt(row_var + epsilon) * gain_vec + shift_vec


def local(
    hidden_in,
    lengths,
    ln1_gain,
    ln1_bias,
    w_qkv,
    q_bias,
    v_bias,
    w_out,
    out_bias,
    ln2_gain,
    ln2_bias,
    w_up,
    up_bias,
    w_down,
    down_bias,
    cotangent,
):
    cell_count, local_genes, model_width = hidden_in.shape
    row_count = cell_count * local_genes
    head_count = model_width // HEAD_DIM
    score_scale = 1.0 / math.sqrt(HEAD_DIM)
    cycle_size = lax.axis_size("blk")
    cycle_place = lax.axis_index("blk")
    ratio_ff = up_bias.shape[0] // model_width
    head_shape = (cell_count, local_genes, head_count, HEAD_DIM)
    stat_shape = (cell_count, head_count, local_genes)
    inputs = hidden_in.astype(jnp.float32).reshape(row_count, model_width)
    cot_rows = cotangent.reshape(row_count, model_width)
    gene_index = jnp.arange(local_genes, dtype=jnp.int32)
    query_valid = (cycle_place * local_genes + gene_index)[None, :] < lengths[:, None]
    normed, ln1_pull = jax.vjp(layer_norm, inputs, ln1_gain, ln1_bias)
    normed_low = normed.astype(jnp.bfloat16)
    part_cols = normed_low
    joined = jnp.dot(
        part_cols,
        lax.all_gather(w_qkv, "cell", axis=0, tiled=True),
        preferred_element_type=jnp.float32,
    )
    queries = (joined[:, :model_width] + q_bias).astype(jnp.bfloat16).reshape(head_shape)
    keys_own = joined[:, model_width : 2 * model_width].astype(jnp.bfloat16).reshape(head_shape)
    values_own = (joined[:, 2 * model_width :] + v_bias).astype(jnp.bfloat16).reshape(head_shape)

    def block_scores(key_block, owner_index):
        scores = (
            jnp.einsum("cqhd,ckhd->chqk", queries, key_block, preferred_element_type=jnp.float32)
            * score_scale
        )
        key_valid = (owner_index * local_genes + gene_index)[None, :] < lengths[:, None]
        return (scores, key_valid[:, None, None, :])

    def stats_turn(owner_index, carried, key_block):
        row_top, row_total = carried
        scores, is_valid = block_scores(key_block, owner_index)
        new_top = jnp.maximum(row_top, jnp.max(jnp.where(is_valid, scores, far_below), axis=-1))
        raised = jnp.where(is_valid, jnp.exp(scores - new_top[..., None]), 0.0)
        return (new_top, row_total * jnp.exp(row_top - new_top) + jnp.sum(raised, axis=-1))

    first_stats = stats_turn(
        cycle_place,
        (jnp.full(stat_shape, far_below, jnp.float32), jnp.zeros(stat_shape, jnp.float32)),
        keys_own,
    )

    def stats_step(step_index, carried):
        stats_now, key_block = carried
        key_block = passed_along(key_block, "blk", 1)
        return (
            stats_turn((cycle_place - step_index) % cycle_size, stats_now, key_block),
            key_block,
        )

    final_stats = lax.fori_loop(1, cycle_size, stats_step, (first_stats, keys_own))[0]
    log_total = final_stats[0] + jnp.log(final_stats[1])

    def block_weights(key_block, owner_index):
        scores, is_valid = block_scores(key_block, owner_index)
        return jnp.where(is_valid, jnp.exp(scores - log_total[..., None]), 0.0)

    def mix_turn(owner_index, mixed_sum, key_block, value_block):
        weights = block_weights(key_block, owner_index).astype(jnp.bfloat16)
        return mixed_sum + jnp.einsum(
            "chqk,ckhd->cqhd", weights, value_block, preferred_element_type=jnp.float32
        )

    mixed_start = mix_turn(cycle_place, jnp.zeros(head_shape, jnp.float32), keys_own, values_own)

    def pair_step(step_index, carried):
        inner, key_block, value_block = carried
        key_block, value_block = passed_along((key_block, value_block), "blk", 1)
        return (
            mix_turn((cycle_place - step_index) % cycle_size, inner, key_block, value_block),
            key_block,
            value_block,
        )

    mixed_sum = lax.fori_loop(1, cycle_size, pair_step, (mixed_start, keys_own, values_own))[0]
    mixed_low = (
        jnp.where(query_valid[:, :, None, None], mixed_sum, 0.0)
        .astype(jnp.bfloat16)
        .reshape(row_count, model_width)
    )
    part_cols = mixed_low
    branch = jnp.dot(
        part_cols,
        lax.all_gather(w_out, "cell", axis=0, tiled=True),
        preferred_element_type=jnp.float32,
    )
    middle = inputs + branch + out_bias
    normed2, ln2_pull = jax.vjp(layer_norm, middle, ln2_gain, ln2_bias)
    normed2_low = normed2.astype(jnp.bfloat16)
    gelu_exact = partial(jax.nn.gelu, approximate=False)
    ff_total = up_bias.shape[0]
    out_sum = jnp.zeros((row_count, model_width), jnp.float32)
    ffn_hidden = jnp.zeros((row_count, ff_total), jnp.bfloat16)
    up_piece = lax.all_gather(w_up, "cell", axis=0, tiled=True)
    down_piece = lax.all_gather(w_down, "cell", axis=0, tiled=True)
    pre_gelu = lax.dot_general(
        normed2_low, up_piece, col_contract, preferred_element_type=jnp.float32
    )
    pre_gelu = pre_gelu + up_bias
    activation, gelu_pull = jax.vjp(gelu_exact, pre_gelu)
    active_low = activation.astype(jnp.bfloat16)
    out_sum = out_sum + jnp.dot(active_low, down_piece, preferred_element_type=jnp.float32)
    grad_active = lax.dot_general(
        cot_rows, down_piece, col_contract, preferred_element_type=jnp.float32
    )
    pre_low = gelu_pull(grad_active)[0].astype(jnp.bfloat16)
    back_sum = jnp.dot(pre_low, up_piece, preferred_element_type=jnp.float32)
    ffn_hidden = lax.dynamic_update_slice_in_dim(ffn_hidden, active_low, jnp.int32(0), 1)
    out_sum, back_sum, pre_grads, hidden = (out_sum, back_sum, pre_low, ffn_hidden)
    out_hidden = (middle + out_sum + down_bias).astype(jnp.bfloat16).reshape(hidden_in.shape)
    grad_ln2, ln2_gain_part, ln2_bias_part = ln2_pull(back_sum)
    grad_middle = cot_rows.astype(jnp.float32) + grad_ln2
    branch_grad = grad_middle.astype(jnp.bfloat16)
    grad_mixed = lax.dot_general(
        branch_grad,
        lax.all_gather(w_out, "cell", axis=0, tiled=True),
        col_contract,
        preferred_element_type=jnp.float32,
    )
    grad_out = jnp.where(
        query_valid[:, :, None, None], grad_mixed.astype(jnp.bfloat16).reshape(head_shape), 0.0
    )
    delta = jnp.einsum("cqhd,cqhd->chq", grad_out.astype(jnp.float32), mixed_sum)

    def grad_step(step_index, carried):
        query_grad, key_block, value_block, key_grad, value_grad = carried
        owner_index = (cycle_place - step_index) % cycle_size
        weights = block_weights(key_block, owner_index)
        grad_weights = jnp.einsum(
            "cqhd,ckhd->chqk", grad_out, value_block, preferred_element_type=jnp.float32
        )
        score_grad = (weights * (grad_weights - delta[..., None])).astype(jnp.bfloat16)
        query_grad = (
            query_grad
            + jnp.einsum(
                "chqk,ckhd->cqhd", score_grad, key_block, preferred_element_type=jnp.float32
            )
            * score_scale
        )
        key_grad = (
            key_grad
            + jnp.einsum("chqk,cqhd->ckhd", score_grad, queries, preferred_element_type=jnp.float32)
            * score_scale
        )
        value_grad = value_grad + jnp.einsum(
            "chqk,cqhd->ckhd",
            weights.astype(jnp.bfloat16),
            grad_out,
            preferred_element_type=jnp.float32,
        )
        key_block, value_block, key_grad, value_grad = (
            passed_along(key_block, "blk", 1),
            passed_along(value_block, "blk", 1),
            passed_along(key_grad.astype(jnp.bfloat16), "blk", 1).astype(key_grad.dtype),
            passed_along(value_grad.astype(jnp.bfloat16), "blk", 1).astype(value_grad.dtype),
        )
        return (query_grad, key_block, value_block, key_grad, value_grad)

    zero_heads = jnp.zeros(head_shape, jnp.float32)
    cycle_done = lax.fori_loop(
        0, cycle_size, grad_step, (zero_heads, keys_own, values_own, zero_heads, zero_heads)
    )
    query_low = cycle_done[0].astype(jnp.bfloat16).reshape(row_count, model_width)
    key_low = cycle_done[3].astype(jnp.bfloat16).reshape(row_count, model_width)
    value_low = cycle_done[4].astype(jnp.bfloat16).reshape(row_count, model_width)
    grad_joined = jnp.concatenate([query_low, key_low, value_low], axis=1)
    grad_normed = lax.dot_general(
        grad_joined,
        lax.all_gather(w_qkv, "cell", axis=0, tiled=True),
        col_contract,
        preferred_element_type=jnp.float32,
    )
    grad_ln1, ln1_gain_part, ln1_bias_part = ln1_pull(grad_normed)
    in_grad = (grad_middle + grad_ln1).reshape(hidden_in.shape)
    qkv_term = lax.dot_general(
        normed_low, grad_joined, row_contract, preferred_element_type=jnp.float32
    )
    out_term = lax.dot_general(
        mixed_low, branch_grad, row_contract, preferred_element_type=jnp.float32
    )
    up_term = lax.dot_general(
        pre_grads, normed2_low, row_contract, preferred_element_type=jnp.float32
    )
    down_term = lax.dot_general(hidden, cot_rows, row_contract, preferred_element_type=jnp.float32)
    ffn_term = jnp.concatenate([up_term, down_term], axis=1).reshape(
        lax.axis_size("cell") * (model_width // lax.axis_size("cell")), ratio_ff * 2 * model_width
    )
    summed = lax.psum_scatter(
        jnp.concatenate([qkv_term, out_term, ffn_term], axis=1).astype(jnp.bfloat16),
        "cell",
        scatter_dimension=0,
        tiled=True,
    ).astype(jnp.float32)
    summed = lax.psum(summed.astype(jnp.bfloat16), "blk").astype(jnp.float32)
    own_rows = summed.shape[0]
    w_qkv_grad = summed[:, : 3 * model_width]
    w_out_grad = summed[:, 3 * model_width : 4 * model_width]
    ffn_grads = summed[:, 4 * model_width :].reshape(own_rows * ratio_ff, 2 * model_width)
    w_up_grad = ffn_grads[:, :model_width]
    w_down_grad = ffn_grads[:, model_width:]
    vectors = lax.psum(
        (
            ln1_gain_part,
            ln1_bias_part,
            jnp.sum(query_low, axis=0, dtype=jnp.float32),
            jnp.sum(value_low, axis=0, dtype=jnp.float32),
            jnp.sum(branch_grad, axis=0, dtype=jnp.float32),
            ln2_gain_part,
            ln2_bias_part,
            jnp.sum(pre_grads, axis=0, dtype=jnp.float32),
            jnp.sum(cot_rows, axis=0, dtype=jnp.float32),
        ),
        ("cell", "blk"),
    )
    return (
        out_hidden,
        in_grad,
        vectors[0],
        vectors[1],
        w_qkv_grad,
        vectors[2],
        vectors[3],
        w_out_grad,
        vectors[4],
        vectors[5],
        vectors[6],
        w_up_grad,
        vectors[7],
        w_down_grad,
        vectors[8],
    )


def solution(mesh):
    placed = (
        P("cell", "blk", None),
        P("cell"),
        P(),
        P(),
        P("cell", None),
        P(),
        P(),
        P("cell", None),
        P(),
        P(),
        P(),
        P("cell", None),
        P(),
        P("cell", None),
        P(),
        P("cell", "blk", None),
    )
    return jax.shard_map(
        local,
        mesh=mesh,
        in_specs=placed,
        out_specs=(
            P("cell", "blk", None),
            P("cell", "blk", None),
            P(),
            P(),
            P("cell", None),
            P(),
            P(),
            P("cell", None),
            P(),
            P(),
            P(),
            P("cell", None),
            P(),
            P("cell", None),
            P(),
        ),
        check_vma=False,
    )
```

profile of v0, /device:TPU:0, one launch (start us, length us, event | category | flops | bytes accessed | tf_op | source)
XLA Modules:
  0.0 1748.9 jit_solution(2791342807904392032)
XLA Ops:
  15.9 81.1 %all-gather.5.cloned.1.call-done = bf16[1280,3840]{1,0:T(8,128)(2,1)} async-done(((bf16[80,3840]{1,0:T(8,128)(2,1)}), bf16[1280,3840]{1,0:T(8,128)(2,1)}) %all-gather.5.cloned.1.call-update) | async-done | bytes 9830416 | tf_op jit(solution)/shard_map/all_gather | solution.py:66
  148.1 20.6 %select_reduce_fusion.3 = (f32[2,20,512]{2,1,0:T(8,128)S(1)}, f32[2,20,512,512]{2,3,1,0:T(8,128)}) fusion(pred[2,512]{1,0:T(4,128)(4,1)S(1)} %get-tuple-element.513, bf16[2,512,20,64]{1,0,3,2:T(2,128)(2,1)} %copy-done.5, bf16[2,512,20,64]{1,0,3,2:T(2,128)(2,1)S(1)} %reshape.303), kind=kOutput, calls=%fused_computation.20 | convolution fusion | flops 1373614080 | bytes 47268864 | tf_op jit(solution)/shard_map/cqhd,ckhd->chqk/dot_general | solution.py:75
  168.6 70.9 %collective-permute-done.4 = bf16[2,512,20,64]{1,3,2,0:T(8,128)(2,1)} collective-permute-done((bf16[2,512,20,64]{1,3,2,0:T(8,128)(2,1)}, bf16[2,512,20,64]{1,3,2,0:T(8,128)(2,1)}, u32[]{:S(2)}, u32[]{:S(2)}) %collective-permute-start.4) | collective-permute-done | bytes 2621472 | tf_op jit(solution)/shard_map/while/body/eval_jaxpr/ppermute | solution.py:20
  239.6 20.8 %select_reduce_fusion.2 = (f32[2,20,512]{2,1,0:T(8,128)S(1)}, f32[2,20,512,512]{2,3,1,0:T(8,128)}) fusion(pred[2,512]{1,0:T(4,128)(4,1)S(1)} %get-tuple-element.512, bf16[2,512,20,64]{1,3,2,0:T(8,128)(2,1)} %collective-permute-done.4, bf16[2,512,20,64]{1,0,3,2:T(2,128)(2,1)S(1)} %reshape.303), kind=kOutput, calls=%fused_computation.19 | convolution fusion | flops 1373614080 | bytes 47268864 | tf_op jit(solution)/shard_map/while/body/eval_jaxpr/cqhd,ckhd->chqk/dot_general | solution.py:75
  260.4 27.2 %select_reduce_fusion = (f32[2,20,512]{2,1,0:T(8,128)S(1)}, f32[2,20,512]{2,1,0:T(8,128)S(1)}) fusion(f32[2,20,512,512]{2,3,1,0:T(8,128)} %get-tuple-element.517, f32[2,20,512]{2,1,0:T(8,128)S(1)} %get-tuple-element.509, pred[2,512]{1,0:T(4,128)(4,1)S(1)} %get-tuple-element.512, f32[2,20,512]{2,1,0:T(8,128)S(1)} %get-tuple-element.508, ...), kind=kLoop, calls=%fused_computation.17 | loop fusion | flops 83845120 | bytes 84215808 | tf_op jit(solution)/shard_map/while/body/eval_jaxpr/reduce_sum | solution.py:86
  287.7 21.9 %fusion.19 = f32[2,20,64,512]{3,2,1,0:T(8,128)} fusion(bf16[2,512,20,64]{1,3,2,0:T(8,128)(2,1)} %collective-permute-done.5, f32[2,20,512,512]{2,3,1,0:T(8,128)} %get-tuple-element.517, f32[2,20,512]{2,1,0:T(8,128)S(1)} %log_add_fusion, pred[2,512]{1,0:T(4,128)(4,1)S(1)} %get-tuple-element.512), kind=kOutput, calls=%fused_computation.41 | convolution fusion | flops 1384120320 | bytes 49890304 | tf_op jit(solution)/shard_map/while/body/eval_jaxpr/chqk,ckhd->cqhd/dot_general | solution.py:111
  309.7 19.9 %fusion.25 = (bf16[2,512,20,64]{1,3,2,0:T(8,128)(2,1)S(1)}, f32[2,20,64,512]{3,2,1,0:T(8,128)}) fusion(pred[2,512]{1,0:T(4,128)(4,1)S(1)} %get-tuple-element.513, f32[2,20,64,512]{3,2,1,0:T(8,128)} %fusion.19, f32[2,20,512,512]{2,3,1,0:T(8,128)} %get-tuple-element.515, f32[2,20,512]{2,1,0:T(8,128)S(1)} %log_add_fusion, ...), kind=kOutput, calls=%fused_computation.59 | convolution fusion | flops 1388052480 | bytes 57754624 | tf_op jit(solution)/shard_map/chqk,ckhd->cqhd/dot_general | solution.py:111
  344.2 23.4 %fusion.53 = f32[1024,5120]{1,0:T(8,128)} fusion(bf16[5120,1280]{1,0:T(8,128)(2,1)} %all-gather.9.cloned.1.call-done, f32[1024,1280]{1,0:T(8,128)} %copy-done.8, f32[1280]{0:T(1024)S(1)} %copy-done.50, f32[1280]{0:T(1024)S(1)} %copy-done.44, f32[1024]{0:T(1024)S(1)} %fusion.39, f32[1024]{0:T(1024)S(1)} %broadcast_multiply_fusion), kind=kOutput, calls=%fused_computation.121 | convolution fusion | flops 13428326400 | bytes 39340032 | tf_op jit(solution)/shard_map/dot_general | solution.py:147
  367.5 65.6 %convert_reduce_fusion = (f32[5120]{0:T(1024)}, bf16[1024,5120]{1,0:T(8,128)(2,1)}, f32[1024,5120]{1,0:T(8,128)S(1)}) fusion(f32[1024,5120]{1,0:T(8,128)} %fusion.53, f32[5120]{0:T(1024)S(1)} %copy-done.35, bf16[1024,1280]{1,0:T(8,128)(2,1)S(1)} %bitcast.149, bf16[5120,1280]{1,0:T(8,128)(2,1)} %all-gather.11.cloned.1.call-done), kind=kOutput, calls=%fused_computation.25 | convolution fusion | flops 13814983680 | bytes 68198400 | tf_op jit(solution)/shard_map/dot_general | solution.py:154
  447.6 21.6 %convolution_convert_fusion.1 = bf16[5120,1280]{0,1:T(8,128)(2,1)} fusion(bf16[1024,5120]{1,0:T(8,128)(2,1)} %get-tuple-element.492, f32[1024,1280]{1,0:T(8,128)} %copy-done.8, f32[1280]{0:T(1024)S(1)} %copy-done.51, f32[1280]{0:T(1024)S(1)} %copy-done.45, f32[1024]{0:T(1024)S(1)} %copy-done.40, f32[1024]{0:T(1024)S(1)} %copy-done.33), kind=kOutput, calls=%fused_computation.46 | convolution fusion | flops 13434880000 | bytes 28854272 | tf_op jit(solution)/shard_map/dot_general | solution.py:232
  469.3 21.8 %multiply_reduce_fusion = (f32[1280]{0:T(1024)}, f32[1024]{0:T(1024)S(1)}, f32[1280]{0:T(1024)}, f32[1024,1280]{1,0:T(8,128)S(1)}) fusion(f32[1024,1280]{1,0:T(8,128)} %copy-done.8, f32[1024]{0:T(1024)S(1)} %copy-done.40, f32[1024]{0:T(1024)S(1)} %copy-done.33, f32[1280]{0:T(1024)S(1)} %copy-done.45, bf16[1024,5120]{1,0:T(8,128)(2,1)} %get-tuple-element.492, ...), kind=kOutput, calls=%fused_computation.77 | convolution fusion | flops 13432255488 | bytes 34106368 | tf_op jit(solution)/shard_map/dot_general | solution.py:158
  521.7 576.6 %while.7 = (s32[]{:T(128)}, f32[2,512,20,64]{1,3,2,0:T(8,128)}, bf16[2,512,20,64]{1,3,2,0:T(8,128)(2,1)}, bf16[2,512,20,64]{1,3,2,0:T(8,128)(2,1)}, f32[2,512,20...) while((s32[]{:T(128)}, f32[2,512,20,64]{1,3,2,0:T(8,128)}, ...), condition=%wide.region_11.12_spmd.clone, body=%wide.region_10.11_spmd.clone.sunk | while | flops 6831474176 | bytes 322690528 | solution.py:211
  543.8 26.1 %multiply_convert_fusion.3 = bf16[2,20,512,512]{3,2,1,0:T(8,128)(2,1)} fusion(f32[2,20,512,512]{3,2,1,0:T(8,128)} %fusion.118, f32[2,20,512]{2,1,0:T(8,128)S(1)} %get-tuple-element.642, f32[2,20,512]{2,1,0:T(8,128)S(1)} %get-tuple-element.640, pred[2,512]{1,0:T(4,128)(4,1)S(1)} %broadcast_compare_fusion.4, ...), kind=kOutput, calls=%fused_computation.1.clone.1 | convolution fusion | flops 1405091840 | bytes 68322304 | tf_op jit(solution)/shard_map/while/body/eval_jaxpr/cqhd,ckhd->chqk/dot_general | solution.py:180
  615.4 27.4 %collective-permute-done.2 = bf16[2,512,20,64]{1,3,2,0:T(8,128)(2,1)} collective-permute-done((bf16[2,512,20,64]{1,3,2,0:T(8,128)(2,1)}, bf16[2,512,20,64]{1,3,2,0:T(8,128)(2,1)}, u32[]{:S(2)}, u32[]{:S(2)}) %collective-permute-start.2) | collective-permute-done | bytes 2621472 | tf_op jit(solution)/shard_map/while/body/eval_jaxpr/ppermute | solution.py:20
  647.7 51.3 %collective-permute-done.3 = bf16[2,512,20,64]{1,3,2,0:T(8,128)(2,1)} collective-permute-done((bf16[2,512,20,64]{1,3,2,0:T(8,128)(2,1)}, bf16[2,512,20,64]{1,3,2,0:T(8,128)(2,1)}, u32[]{:S(2)}, u32[]{:S(2)}) %collective-permute-start.3) | collective-permute-done | bytes 2621472 | tf_op jit(solution)/shard_map/while/body/eval_jaxpr/ppermute | solution.py:20
  703.8 51.5 %collective-permute-done = bf16[2,512,20,64]{1,3,2,0:T(8,128)(2,1)} collective-permute-done((bf16[2,512,20,64]{1,3,2,0:T(8,128)(2,1)S(1)}, bf16[2,512,20,64]{1,3,2,0:T(8,128)(2,1)}, u32[]{:S(2)}, u32[]{:S(2)}) %collective-permute-start) | collective-permute-done | bytes 2621472 | tf_op jit(solution)/shard_map/while/body/eval_jaxpr/ppermute | solution.py:20
  755.2 54.7 %collective-permute-done.1 = bf16[2,512,20,64]{1,3,2,0:T(8,128)(2,1)} collective-permute-done((bf16[2,512,20,64]{1,3,2,0:T(8,128)(2,1)}, bf16[2,512,20,64]{1,3,2,0:T(8,128)(2,1)}, u32[]{:S(2)}, u32[]{:S(2)}) %collective-permute-start.1) | collective-permute-done | bytes 2621472 | tf_op jit(solution)/shard_map/while/body/eval_jaxpr/ppermute | solution.py:20
  831.6 26.1 %multiply_convert_fusion.3 = bf16[2,20,512,512]{3,2,1,0:T(8,128)(2,1)} fusion(f32[2,20,512,512]{3,2,1,0:T(8,128)} %fusion.118, f32[2,20,512]{2,1,0:T(8,128)S(1)} %get-tuple-element.642, f32[2,20,512]{2,1,0:T(8,128)S(1)} %get-tuple-element.640, pred[2,512]{1,0:T(4,128)(4,1)S(1)} %broadcast_compare_fusion.4, ...), kind=kOutput, calls=%fused_computation.1.clone.1 | convolution fusion | flops 1405091840 | bytes 68322304 | tf_op jit(solution)/shard_map/while/body/eval_jaxpr/cqhd,ckhd->chqk/dot_general | solution.py:180
  907.4 24.7 %collective-permute-done.2 = bf16[2,512,20,64]{1,3,2,0:T(8,128)(2,1)} collective-permute-done((bf16[2,512,20,64]{1,3,2,0:T(8,128)(2,1)}, bf16[2,512,20,64]{1,3,2,0:T(8,128)(2,1)}, u32[]{:S(2)}, u32[]{:S(2)}) %collective-permute-start.2) | collective-permute-done | bytes 2621472 | tf_op jit(solution)/shard_map/while/body/eval_jaxpr/ppermute | solution.py:20
  936.9 51.3 %collective-permute-done.3 = bf16[2,512,20,64]{1,3,2,0:T(8,128)(2,1)} collective-permute-done((bf16[2,512,20,64]{1,3,2,0:T(8,128)(2,1)}, bf16[2,512,20,64]{1,3,2,0:T(8,128)(2,1)}, u32[]{:S(2)}, u32[]{:S(2)}) %collective-permute-start.3) | collective-permute-done | bytes 2621472 | tf_op jit(solution)/shard_map/while/body/eval_jaxpr/ppermute | solution.py:20
  993.0 51.5 %collective-permute-done = bf16[2,512,20,64]{1,3,2,0:T(8,128)(2,1)} collective-permute-done((bf16[2,512,20,64]{1,3,2,0:T(8,128)(2,1)S(1)}, bf16[2,512,20,64]{1,3,2,0:T(8,128)(2,1)}, u32[]{:S(2)}, u32[]{:S(2)}) %collective-permute-start) | collective-permute-done | bytes 2621472 | tf_op jit(solution)/shard_map/while/body/eval_jaxpr/ppermute | solution.py:20
  1044.4 53.7 %collective-permute-done.1 = bf16[2,512,20,64]{1,3,2,0:T(8,128)(2,1)} collective-permute-done((bf16[2,512,20,64]{1,3,2,0:T(8,128)(2,1)}, bf16[2,512,20,64]{1,3,2,0:T(8,128)(2,1)}, u32[]{:S(2)}, u32[]{:S(2)}) %collective-permute-start.1) | collective-permute-done | bytes 2621472 | tf_op jit(solution)/shard_map/while/body/eval_jaxpr/ppermute | solution.py:20
  1117.6 20.5 %convolution_convert_fusion = bf16[5120,1280]{0,1:T(8,128)(2,1)} fusion(bf16[1024,5120]{1,0:T(8,128)(2,1)} %multiply_convert_fusion.1, bf16[1024,1280]{1,0:T(8,128)(2,1)S(1)} %bitcast.150), kind=kOutput, calls=%fused_computation.45 | convolution fusion | flops 13428326400 | bytes 26214400 | tf_op jit(solution)/shard_map/dot_general | solution.py:235
  1138.1 18.4 %pad_maximum_fusion.1 = bf16[5120,2560]{0,1:T(8,128)(2,1)} fusion(bf16[5120,1280]{0,1:T(8,128)(2,1)} %convolution_convert_fusion, bf16[5120,1280]{0,1:T(8,128)(2,1)} %convolution_convert_fusion.1), kind=kLoop, calls=%fused_computation.23 | loop fusion | flops 52428800 | bytes 52428800 | tf_op jit(solution)/shard_map/concatenate | solution.py:236
  1156.5 32.3 %copy.63 = bf16[5120,2560]{1,0:T(8,128)(2,1)} copy(bf16[5120,2560]{0,1:T(8,128)(2,1)} %pad_maximum_fusion.1) | data formatting | bytes 52428800 | tf_op jit(solution)/shard_map/concatenate | solution.py:236
  1188.8 39.2 %reshape.313 = bf16[1280,10240]{1,0:T(8,128)(2,1)} reshape(bf16[5120,2560]{1,0:T(8,128)(2,1)} %copy.63) | data formatting | bytes 52428800 | tf_op jit(solution)/shard_map/reshape | solution.py:236
  1253.7 25.5 %pad_maximum_fusion = bf16[1280,15360]{1,0:T(8,128)(2,1)} fusion(bf16[1280,10240]{1,0:T(8,128)(2,1)} %reshape.313, bf16[1280,1280]{1,0:T(8,128)(2,1)S(1)} %copy.64, bf16[1280,3840]{1,0:T(8,128)(2,1)} %convolution_convert_fusion.2), kind=kLoop, calls=%fused_computation.21 | loop fusion | flops 117964800 | bytes 78643200 | tf_op jit(solution)/shard_map/concatenate | solution.py:240
  1281.9 20.8 %fusion.54 = (f32[1280]{0:T(1024)S(1)}, f32[1024]{0:T(1024)S(1)}, f32[1024,1280]{1,0:T(8,128)}) fusion(f32[1280]{0:T(1024)S(1)} %copy-done.21, f32[1024]{0:T(1024)S(1)} %bitcast.166, bf16[2,512,1280]{2,1,0:T(8,128)(2,1)S(1)} %copy-done.3, bf16[1024,3840]{0,1:T(8,128)(2,1)} %constant_dynamic-update-slice_fusion, ...), kind=kOutput, calls=%fused_computation.122 | convolution fusion | flops 10074191872 | bytes 25577472 | tf_op jit(solution)/shard_map/dot_general | solution.py:218
  1302.7 25.3 %add_convert_fusion.1 = bf16[1024,1280]{1,0:T(8,128)(2,1)} fusion(f32[1024,1280]{1,0:T(8,128)} %copy-done.8, bf16[1024,5120]{1,0:T(8,128)(2,1)} %multiply_convert_fusion.1, bf16[5120,1280]{1,0:T(8,128)(2,1)} %all-gather.11.cloned.1.call-done, f32[1280]{0:T(1024)S(1)} %copy-done.52), kind=kOutput, calls=%fused_computation.84 | convolution fusion | flops 13425704960 | bytes 31462400 | tf_op jit(solution)/shard_map/dot_general | solution.py:153
  1328.0 329.8 %reduce-scatter.2.cloned.1.call-done = bf16[80,15360]{1,0:T(8,128)(2,1)} async-done(((bf16[1280,15360]{1,0:T(8,128)(2,1)}), bf16[80,15360]{1,0:T(8,128)(2,1)}) %reduce-scatter.2.cloned.1.call-update) | async-done | bytes 2457616 | tf_op jit(solution)/shard_map/reduce_scatter | solution.py:239
  1662.3 42.4 %all-reduce = (f32[1280]{0:T(1024)}, f32[1280]{0:T(1024)}, f32[1280]{0:T(1024)}, f32[1280]{0:T(1024)}, f32[1280]{0:T(1024)}, /*index=5*/f32[1280]{0:T(1024)}, f32[1280]{0:T(1024)}, f32[5120]{0:T(1024)}, f32[1280]{0:T(1024)}) all-reduce(f32[1280]{0:T(1024)S(1)} %get-tuple-element.453, ...), channel_id=1, replica_groups=mesh['cell'=16,'blk'=2] {'cell','blk'}, use_global_device_ids=true, to_apply=%region_15.16 | all-reduce | flops 15360 | bytes 122880 | tf_op jit(solution)/shard_map/psum | solution.py:252
  1712.2 18.5 %all-reduce.3.cloned.1.call-done = bf16[80,15360]{1,0:T(8,128)(2,1)} async-done(((bf16[80,15360]{1,0:T(8,128)(2,1)}), bf16[80,15360]{1,0:T(8,128)(2,1)}) %all-reduce.3.cloned.1.call-update) | async-done | bytes 2457616 | tf_op jit(solution)/shard_map/psum | solution.py:245
  (241 shorter events, 347.3 us)
Async XLA Ops:
  7.2 89.7 %all-gather.5.cloned.1.call-start = ((), (), s32[]{:S(2)}) async-start(), calls=%async_computation.1 | async-start | bytes 10444800 | tf_op jit(solution)/shard_map/all_gather | solution.py:66
  8.0 326.6 %all-gather.7.cloned.1.call-start = ((), (), s32[]{:S(2)}) async-start(), calls=%async_computation.2 | async-start | bytes 3481600 | tf_op jit(solution)/shard_map/all_gather | solution.py:135
  8.7 335.4 %all-gather.9.cloned.1.call-start = ((), (), s32[]{:S(2)}) async-start(), calls=%async_computation.3 | async-start | bytes 13926400 | tf_op jit(solution)/shard_map/all_gather | solution.py:145
  9.4 358.1 %all-gather.11.cloned.1.call-start = ((), (), s32[]{:S(2)}) async-start(), calls=%async_computation.4 | async-start | bytes 13926400 | tf_op jit(solution)/shard_map/all_gather | solution.py:146
  10.0 1647.8 %reduce-scatter.2.cloned.1.call-start = ((), (), s32[]{:S(2)}) async-start(), calls=%async_computation.5 | async-start | bytes 41779200 | tf_op jit(solution)/shard_map/reduce_scatter | solution.py:239
  13.2 97.2 %copy-start.30 = (f32[1,4,2,128]{3,1,2,0:T(4,128)}, f32[1,4,2,128]{3,1,2,0:T(4,128)S(1)}, u32[]{:S(2)}) copy-start(f32[1,4,2,128]{3,1,2,0:T(4,128)S(1)} %copy.75) | copy-start | bytes 12292
  13.2 97.2 %copy-start.22 = (f32[1024]{0:T(1024)}, f32[1024]{0:T(1024)S(1)}, u32[]{:S(2)}) copy-start(f32[1024]{0:T(1024)S(1)} %rsqrt.20) | copy-start | bytes 12292
  13.2 97.2 %copy-start.24 = (f32[1,4,2,128]{3,1,2,0:T(4,128)}, f32[1,4,2,128]{3,1,2,0:T(4,128)S(1)}, u32[]{:S(2)}) copy-start(f32[1,4,2,128]{3,1,2,0:T(4,128)S(1)} %copy.74) | copy-start | bytes 12292
  13.3 296.3 %copy-start.16 = (pred[2,512]{1,0:T(4,128)(4,1)}, pred[2,512]{1,0:T(4,128)(4,1)S(1)}, u32[]{:S(2)}) copy-start(pred[2,512]{1,0:T(4,128)(4,1)S(1)} %get-tuple-element.513) | copy-start | bytes 3076
  124.0 163.7 %collective-permute-start.5 = (bf16[2,512,20,64]{1,3,2,0:T(8,128)(2,1)}, bf16[2,512,20,64]{1,3,2,0:T(8,128)(2,1)}, u32[]{:S(2)}, u32[]{:S(2)}) collective-permute-start(bf16[2,512,20,64]{1,3,2,0:T(8,128)(2,1)} %copy.50), channel_id=1, source_target_pairs={{0,1},{1,0},{2,3},{3,2},{4,5},{5,4},{6,7},{7,6},{8,9},{9,8},{10,11... | collective-permute-start | bytes 7864328 | tf_op jit(solution)/shard_map/while/body/eval_jaxpr/ppermute | solution.py:20
  136.7 102.9 %collective-permute-start.4 = (bf16[2,512,20,64]{1,3,2,0:T(8,128)(2,1)}, bf16[2,512,20,64]{1,3,2,0:T(8,128)(2,1)}, u32[]{:S(2)}, u32[]{:S(2)}) collective-permute-start(bf16[2,512,20,64]{1,3,2,0:T(8,128)(2,1)} %copy.47), channel_id=1, source_target_pairs={{0,1},{1,0},{2,3},{3,2},{4,5},{5,4},{6,7},{7,6},{8,9},{9,8},{10,11... | collective-permute-start | bytes 7864328 | tf_op jit(solution)/shard_map/while/body/eval_jaxpr/ppermute | solution.py:20
  341.3 26.3 %copy-start.32 = (f32[1024]{0:T(1024)}, f32[1024]{0:T(1024)S(1)}, u32[]{:S(2)}) copy-start(f32[1024]{0:T(1024)S(1)} %broadcast_multiply_fusion) | copy-start | bytes 12292
  344.1 23.4 %copy-start.39 = (f32[1024]{0:T(1024)}, f32[1024]{0:T(1024)S(1)}, u32[]{:S(2)}) copy-start(f32[1024]{0:T(1024)S(1)} %fusion.39) | copy-start | bytes 12292
  344.1 23.4 %copy-start.6 = (bf16[2,512,1280]{2,1,0:T(8,128)(2,1)S(1)}, bf16[2,512,1280]{2,1,0:T(8,128)(2,1)}, u32[]{:S(2)}) copy-start(bf16[2,512,1280]{2,1,0:T(8,128)(2,1)} %param.33) | copy-start | bytes 7864324
  344.1 23.5 %copy-start.35 = (f32[5120]{0:T(1024)S(1)}, f32[5120]{0:T(1024)}, u32[]{:S(2)}) copy-start(f32[5120]{0:T(1024)} %param.30) | copy-start | bytes 61444
  447.6 43.5 %slice-start.2 = ((s8[5242880]{0:T(1024)(128)(4,1)}), s8[1048576]{0:T(1024)(128)(4,1)S(1)}, s32[]{:S(2)}) async-start(s8[5242880]{0:T(1024)(128)(4,1)} %bitcast.151), calls=%async_computation.9 | async-start | bytes 2097152
  582.7 60.1 %collective-permute-start.2 = (bf16[2,512,20,64]{1,3,2,0:T(8,128)(2,1)}, bf16[2,512,20,64]{1,3,2,0:T(8,128)(2,1)}, u32[]{:S(2)}, u32[]{:S(2)}) collective-permute-start(bf16[2,512,20,64]{1,3,2,0:T(8,128)(2,1)} %fusion.119), channel_id=1, source_target_pairs={{0,1},{1,0},{2,3},{3,2},{4,5},{5,4},{6,7},{7,6},{8,9},{9,8},{10,11... | collective-permute-start | bytes 7864328 | tf_op jit(solution)/shard_map/while/body/eval_jaxpr/ppermute | solution.py:20
  600.9 98.1 %collective-permute-start.3 = (bf16[2,512,20,64]{1,3,2,0:T(8,128)(2,1)}, bf16[2,512,20,64]{1,3,2,0:T(8,128)(2,1)}, u32[]{:S(2)}, u32[]{:S(2)}) collective-permute-start(bf16[2,512,20,64]{1,3,2,0:T(8,128)(2,1)} %fusion.120), channel_id=1, source_target_pairs={{0,1},{1,0},{2,3},{3,2},{4,5},{5,4},{6,7},{7,6},{8,9},{9,8},{10,11... | collective-permute-start | bytes 7864328 | tf_op jit(solution)/shard_map/while/body/eval_jaxpr/ppermute | solution.py:20
  601.4 153.8 %collective-permute-start = (bf16[2,512,20,64]{1,3,2,0:T(8,128)(2,1)S(1)}, bf16[2,512,20,64]{1,3,2,0:T(8,128)(2,1)}, u32[]{:S(2)}, u32[]{:S(2)}) collective-permute-start(bf16[2,512,20,64]{1,3,2,0:T(8,128)(2,1)S(1)} %copy.106), channel_id=1, source_target_pairs={{0,1},{1,0},{2,3},{3,2},{4,5},{5,4},{6,7},{7,6},{8,9},{9,8},{10,11... | collective-permute-start | bytes 7864328 | tf_op jit(solution)/shard_map/while/body/eval_jaxpr/ppermute | solution.py:20
  602.9 207.0 %collective-permute-start.1 = (bf16[2,512,20,64]{1,3,2,0:T(8,128)(2,1)}, bf16[2,512,20,64]{1,3,2,0:T(8,128)(2,1)}, u32[]{:S(2)}, u32[]{:S(2)}) collective-permute-start(bf16[2,512,20,64]{1,3,2,0:T(8,128)(2,1)} %copy.107), channel_id=1, source_target_pairs={{0,1},{1,0},{2,3},{3,2},{4,5},{5,4},{6,7},{7,6},{8,9},{9,8},{10,11... | collective-permute-start | bytes 7864328 | tf_op jit(solution)/shard_map/while/body/eval_jaxpr/ppermute | solution.py:20
  871.9 60.1 %collective-permute-start.2 = (bf16[2,512,20,64]{1,3,2,0:T(8,128)(2,1)}, bf16[2,512,20,64]{1,3,2,0:T(8,128)(2,1)}, u32[]{:S(2)}, u32[]{:S(2)}) collective-permute-start(bf16[2,512,20,64]{1,3,2,0:T(8,128)(2,1)} %fusion.119), channel_id=1, source_target_pairs={{0,1},{1,0},{2,3},{3,2},{4,5},{5,4},{6,7},{7,6},{8,9},{9,8},{10,11... | collective-permute-start | bytes 7864328 | tf_op jit(solution)/shard_map/while/body/eval_jaxpr/ppermute | solution.py:20
  891.7 96.6 %collective-permute-start.3 = (bf16[2,512,20,64]{1,3,2,0:T(8,128)(2,1)}, bf16[2,512,20,64]{1,3,2,0:T(8,128)(2,1)}, u32[]{:S(2)}, u32[]{:S(2)}) collective-permute-start(bf16[2,512,20,64]{1,3,2,0:T(8,128)(2,1)} %fusion.120), channel_id=1, source_target_pairs={{0,1},{1,0},{2,3},{3,2},{4,5},{5,4},{6,7},{7,6},{8,9},{9,8},{10,11... | collective-permute-start | bytes 7864328 | tf_op jit(solution)/shard_map/while/body/eval_jaxpr/ppermute | solution.py:20
  892.2 152.2 %collective-permute-start = (bf16[2,512,20,64]{1,3,2,0:T(8,128)(2,1)S(1)}, bf16[2,512,20,64]{1,3,2,0:T(8,128)(2,1)}, u32[]{:S(2)}, u32[]{:S(2)}) collective-permute-start(bf16[2,512,20,64]{1,3,2,0:T(8,128)(2,1)S(1)} %copy.106), channel_id=1, source_target_pairs={{0,1},{1,0},{2,3},{3,2},{4,5},{5,4},{6,7},{7,6},{8,9},{9,8},{10,11... | collective-permute-start | bytes 7864328 | tf_op jit(solution)/shard_map/while/body/eval_jaxpr/ppermute | solution.py:20
  893.7 204.5 %collective-permute-start.1 = (bf16[2,512,20,64]{1,3,2,0:T(8,128)(2,1)}, bf16[2,512,20,64]{1,3,2,0:T(8,128)(2,1)}, u32[]{:S(2)}, u32[]{:S(2)}) collective-permute-start(bf16[2,512,20,64]{1,3,2,0:T(8,128)(2,1)} %copy.107), channel_id=1, source_target_pairs={{0,1},{1,0},{2,3},{3,2},{4,5},{5,4},{6,7},{7,6},{8,9},{9,8},{10,11... | collective-permute-start | bytes 7864328 | tf_op jit(solution)/shard_map/while/body/eval_jaxpr/ppermute | solution.py:20
  1279.3 451.4 %all-reduce.3.cloned.1.call-start = ((), (), s32[]{:S(2)}) async-start(), calls=%async_computation.6 | async-start | bytes 4915200 | tf_op jit(solution)/shard_map/psum | solution.py:245
  1302.7 355.2 %copy-start.31 = (f32[1,4,2,128]{3,1,2,0:T(4,128)S(1)}, f32[1,4,2,128]{3,1,2,0:T(4,128)}, u32[]{:S(2)}) copy-start(f32[1,4,2,128]{3,1,2,0:T(4,128)} %copy-done.30) | copy-start | bytes 12292
  1302.7 355.2 %copy-start.23 = (f32[1024]{0:T(1024)S(1)}, f32[1024]{0:T(1024)}, u32[]{:S(2)}) copy-start(f32[1024]{0:T(1024)} %copy-done.22) | copy-start | bytes 12292
  1328.0 334.3 %copy-start.34 = (f32[1280]{0:T(1024)S(1)}, f32[1280]{0:T(1024)}, u32[]{:S(2)}) copy-start(f32[1280]{0:T(1024)} %get-tuple-element.494) | copy-start | bytes 15364
  1328.0 334.3 %copy-start.36 = (f32[5120]{0:T(1024)S(1)}, f32[5120]{0:T(1024)}, u32[]{:S(2)}) copy-start(f32[5120]{0:T(1024)} %get-tuple-element.491) | copy-start | bytes 61444
  1328.0 334.3 %copy-start.46 = (f32[1280]{0:T(1024)S(1)}, f32[1280]{0:T(1024)}, u32[]{:S(2)}) copy-start(f32[1280]{0:T(1024)} %get-tuple-element.451) | copy-start | bytes 15364
  1328.0 334.3 %copy-start.47 = (f32[1280]{0:T(1024)S(1)}, f32[1280]{0:T(1024)}, u32[]{:S(2)}) copy-start(f32[1280]{0:T(1024)} %get-tuple-element.455) | copy-start | bytes 15364
  1328.0 376.7 %copy-start.27 = (f32[1024]{0:T(1024)S(1)}, f32[1024]{0:T(1024)}, u32[]{:S(2)}) copy-start(f32[1024]{0:T(1024)} %copy-done.26) | copy-start | bytes 12292
  (45 other events, 336.0 us)
Sparse Core Ops, SparseCore 0:
  10.3 86.5 all-gather.4
  99.2 43.9 all-gather.6
  145.5 102.8 all-gather.8
  250.5 102.1 all-gather.10
  1279.5 378.3 reduce-scatter.1
  1660.0 70.7 all-reduce.2
where the time goes:
time: 1760 us; the launch traced here: 1750 us
  waiting for transfers between devices  869 us (49%)
  matrix products  500 us (28%)
  local copies, waits for them, and re-layouts  168 us (10%)
  other arithmetic  143 us (8%)
  blocking collectives  42.4 us (2%)
    ppermute x10, waiting for transfers between devices, passed_along(): return lax.ppermute(x, axis, [(i, (i + by) % count) for i in range(count)])  437 us
    reduce_scatter x1, waiting for transfers between devices, local(): lax.psum_scatter(jnp.concatenate([qkv_term, out_term, ffn_term], axis=1)....  330 us
    all_gather x1, waiting for transfers between devices, local(): lax.all_gather(w_qkv, 'cell', axis=0, tiled=True)  81.1 us
    dot_general x4, matrix products, block_scores(): jnp.einsum('cqhd,ckhd->chqk', queries, key_block, preferred_element_type=...  73.7 us
    dot_general x1, matrix products, local(): lax.dot_general(cot_rows, down_piece, col_contract, preferred_element_typ...  65.6 us
    dot_general x2, matrix products, grad_step(): jnp.einsum('cqhd,ckhd->chqk', grad_out, value_block, preferred_element_ty...  52.2 us
    psum x1, blocking collectives, local(): lax.psum((ln1_gain_part, ln1_bias_part, jnp.sum(query_low, axis=0, dtype=...  42.4 us
    dot_general x2, matrix products, mix_turn(): jnp.einsum('chqk,ckhd->cqhd', weights, value_block, preferred_element_typ...  41.9 us
  transfers between devices with their start and end apart: 16, of which 12 were waited for; matrix products, arithmetic and copies ran while one was open for 19% of the time, Pallas kernels for 0%

commit v1 on v0

--- a/solution.py
+++ b/solution.py
@@ -4,6 +4,8 @@
 import jax
 import jax.numpy as jnp
 from jax import lax
+from jax.experimental import pallas as pl
+from jax.experimental.pallas import tpu as pltpu
 from jax.sharding import PartitionSpec as P
 
 HEAD_DIM = 64
@@ -282,6 +284,877 @@
     )
 
 
+bf16 = jnp.bfloat16
+f32 = jnp.float32
+NN = (((1,), (0,)), ((), ()))
+NT = (((1,), (1,)), ((), ()))
+TN = (((0,), (0,)), ((), ()))
+AXES = ("cell", "blk")
+VMEM_LIMIT = 60 * 2**20
+ROWS = 256
+OFFSETS = (0, -1, -2, -3, -4, 1, 2, 3)
+
+
+def swappable(mesh):
+    return dict(mesh.shape) == {"cell": 16, "blk": 2}
+
+
+def dot(a, b, dims):
+    return lax.dot_general(a, b, dims, preferred_element_type=f32)
+
+
+def params():
+    return pltpu.CompilerParams(vmem_limit_bytes=VMEM_LIMIT)
+
+
+def cost(flops, nbytes, trans=0):
+    return pl.CostEstimate(
+        flops=int(flops), bytes_accessed=int(nbytes), transcendentals=int(trans)
+    )
+
+
+def shape(dims, dtype):
+    return jax.ShapeDtypeStruct(dims, dtype)
+
+
+ANY = pl.BlockSpec(memory_space=pl.ANY)
+
+
+def fixed(dims):
+    return pl.BlockSpec(dims, lambda *_: (0,) * len(dims))
+
+
+def rowed(rows, width):
+    return pl.BlockSpec((rows, width), lambda i, *_: (i, 0))
+
+
+class Ring:
+    def __init__(self, sizes):
+        self.cells, self.blks = sizes["cell"], sizes["blk"]
+        self.chips = self.cells // 2
+        depth = self.chips // 2
+        self.order = [2 * z for z in range(depth)] + [2 * z + 1 for z in reversed(range(depth))]
+        self.place = [self.order.index(c) for c in range(self.chips)]
+
+    def permute(self, x, target):
+        pairs = []
+        for cell in range(self.cells):
+            for blk in range(self.blks):
+                to_cell, to_blk = target(cell, blk)
+                pairs.append((cell * self.blks + blk, to_cell * self.blks + to_blk))
+        return lax.ppermute(x, AXES, pairs)
+
+    def shift(self, x, by):
+        def target(cell, blk):
+            chip, core = cell // 2, cell % 2
+            way = 1 - 2 * ((core + blk) % 2)
+            return self.order[(self.place[chip] + way * by) % self.chips] * 2 + core, blk
+
+        return self.permute(x, target)
+
+    def swap_core(self, x):
+        return self.permute(x, lambda cell, blk: (cell ^ 1, blk))
+
+    def swap_blk(self, x):
+        return self.permute(x, lambda cell, blk: (cell, 1 - blk))
+
+    def chips_of_slots(self, core):
+        chip = lax.axis_index("cell") // 2
+        way = 1 - 2 * ((core + lax.axis_index("blk")) % 2)
+        place = jnp.array(self.place, jnp.int32)[chip]
+        return jnp.array(self.order, jnp.int32)[
+            (place + way * jnp.array(OFFSETS, jnp.int32)) % self.chips
+        ]
+
+    def gather(self, x, back):
+        ahead = [x]
+        for _ in range(4):
+            ahead.append(self.shift(ahead[-1], 1))
+        behind = []
+        for k in range(1, 4):
+            if k <= back:
+                behind.append(self.shift(behind[-1] if behind else x, -1))
+            else:
+                behind.append(self.swap_blk(ahead[k]))
+        return ahead + behind
+
+    def reduce(self, parts, back):
+        def added(terms):
+            total = terms[0].astype(f32)
+            for t in terms[1:]:
+                total = total + t.astype(f32)
+            return total
+
+        across = {}
+        for k in range(back + 1, 4):
+            across[k] = self.swap_blk(added(parts(4 + k)).astype(bf16))
+        run = added(parts(4)).astype(bf16)
+        for k in (3, 2, 1):
+            extra = [across[k]] if k in across else []
+            run = added([self.shift(run, -1)] + parts(k) + extra).astype(bf16)
+        last = [self.shift(run, -1)]
+        run = None
+        for k in range(back, 0, -1):
+            moved = [] if run is None else [self.shift(run, 1)]
+            run = added(moved + parts(4 + k)).astype(bf16)
+        if run is not None:
+            last.append(self.shift(run, 1))
+        total = added(last + parts(0)).astype(bf16)
+        return total.astype(f32) + self.swap_blk(total).astype(f32)
+
+    def total(self, x):
+        bit = 1
+        while bit < self.cells * self.blks:
+            other = bit
+            x = x + self.permute(
+                x,
+                lambda cell, blk: divmod((cell * self.blks + blk) ^ other, self.blks),
+            )
+            bit *= 2
+        return x
+
+
+def norm_parts(x):
+    mean = jnp.mean(x, axis=-1, keepdims=True)
+    centered = x - mean
+    var = jnp.mean(centered * centered, axis=-1, keepdims=True)
+    scale = lax.rsqrt(var + epsilon)
+    return centered * scale, scale
+
+
+def norm_back(xh, scale, gain, grad):
+    e = grad * gain
+    return scale * (
+        e - jnp.mean(e, axis=-1, keepdims=True) - xh * jnp.mean(e * xh, axis=-1, keepdims=True)
+    )
+
+
+def colsum(x):
+    return jnp.sum(x, axis=0, keepdims=True)
+
+
+def place_rows(slots, target, place_ref, sem, height, first=0):
+    return [
+        pltpu.make_async_copy(
+            slot,
+            target.at[pl.ds(pl.multiple_of(place_ref[first + i] * height, 16), height), :],
+            sem.at[first + i],
+        )
+        for i, slot in enumerate(slots)
+    ]
+
+
+def qkv_kernel(n, place_ref, x_ref, gain_ref, bias_ref, qb_ref, vb_ref, *refs):
+    slots, (a_ref, q_ref, k_ref, v_ref, w, sem) = refs[:n], refs[n:]
+    height = slots[0].shape[0]
+    width = x_ref.shape[1]
+    copies = place_rows(slots, w, place_ref, sem, height)
+
+    @pl.when(pl.program_id(0) == 0)
+    def _():
+        for c in copies:
+            c.start()
+        for c in copies:
+            c.wait()
+
+    xh, _ = norm_parts(x_ref[...].astype(f32))
+    a = (xh * gain_ref[...] + bias_ref[...]).astype(bf16)
+    a_ref[...] = a
+    q_ref[...] = (dot(a, w[:, :width], NN) + qb_ref[...]).astype(bf16)
+    k_ref[...] = dot(a, w[:, width : 2 * width], NN).astype(bf16)
+    v_ref[...] = (dot(a, w[:, 2 * width :], NN) + vb_ref[...]).astype(bf16)
+
+
+def qkv_call(place, x, gain, bias, qb, vb, slots):
+    rows, width = x.shape
+    n = len(slots)
+    block = rowed(ROWS, width)
+    vec = fixed((1, width))
+    return pl.pallas_call(
+        partial(qkv_kernel, n),
+        grid_spec=pltpu.PrefetchScalarGridSpec(
+            num_scalar_prefetch=1,
+            grid=(rows // ROWS,),
+            in_specs=[block, vec, vec, vec, vec] + [ANY] * n,
+            out_specs=[block] * 4,
+            scratch_shapes=[
+                pltpu.VMEM((width, 3 * width), bf16),
+                pltpu.SemaphoreType.DMA((n,)),
+            ],
+        ),
+        out_shape=[shape((rows, width), bf16)] * 4,
+        compiler_params=params(),
+        cost_estimate=cost(6 * rows * width * width, 2 * width * (5 * rows + 3 * width)),
+        name="qkv",
+    )(place, x, gain, bias, qb, vb, *slots)
+
+
+def attend_kernel(qrows, mask_ref, keep_ref, q_ref, k_ref, v_ref, o_ref, lse_ref):
+    n = q_ref.shape[0]
+    lane = lax.broadcasted_iota(jnp.int32, (n, 128), 1)
+    k, v, mask = k_ref[...], v_ref[...], mask_ref[...]
+    for half in range(2):
+        mine = (lane < HEAD_DIM) if half == 0 else (lane >= HEAD_DIM)
+        here = mine[:qrows]
+        one = ((lane == HEAD_DIM) if half == 0 else (lane == 0))[:qrows]
+        keys = jnp.where(mine, k.astype(f32), mask).astype(bf16)
+        vals = jnp.where(mine, v.astype(f32), 1.0).astype(bf16)
+        for i in range(n // qrows):
+            rows = pl.ds(i * qrows, qrows)
+            q = q_ref[rows, :].astype(f32) * (1.0 / math.sqrt(HEAD_DIM))
+            q = jnp.where(here, q, jnp.where(one, 1.0, 0.0)).astype(bf16)
+            s = dot(q, keys, NT)
+            top = jnp.max(s, axis=1, keepdims=True)
+            mixed = dot(jnp.exp(s - top).astype(bf16), vals, NN)
+            total = pltpu.roll(mixed, HEAD_DIM, 1)
+            o = (mixed / total * keep_ref[rows, :]).astype(bf16)
+            if half == 0:
+                o_ref[rows, :] = o
+            else:
+                o_ref[rows, :] = jnp.where(here, o, o_ref[rows, :])
+            lse = jnp.transpose(top + jnp.log(total))
+            first = half * HEAD_DIM
+            lse_ref[half, :, rows] = lse[first : first + 1, :]
+
+
+def attend_call(mask, keep, q, k, v, first, count, qrows=512):
+    n = q.shape[0]
+    block = pl.BlockSpec((n, 128), lambda h: (0, h + first))
+    return pl.pallas_call(
+        partial(attend_kernel, qrows),
+        grid=(count,),
+        in_specs=[fixed((n, 1)), fixed((n, 1)), block, block, block],
+        out_specs=[
+            pl.BlockSpec((n, 128), lambda h: (0, h)),
+            pl.BlockSpec((2, 1, n), lambda h: (h, 0, 0)),
+        ],
+        out_shape=[shape((n, 128 * count), bf16), shape((2 * count, 1, n), f32)],
+        compiler_params=params(),
+        cost_estimate=cost(20 * count * n * n * 128, 8 * n * 128 * count, 2 * count * n * n),
+        name="attend",
+    )(mask, keep, q, k, v)
+
+
+def attend_back_kernel(
+    qrows, mask_ref, q_ref, k_ref, v_ref, o_ref, go_ref, lse_ref,
+    gq_ref, gk_ref, gv_ref, sq_ref, sv_ref, gk_sum, gv_sum,
+):
+    n = q_ref.shape[0]
+    lane = lax.broadcasted_iota(jnp.int32, (n, 128), 1)
+    k, v, mask = k_ref[...], v_ref[...], mask_ref[...]
+    scale = 1.0 / math.sqrt(HEAD_DIM)
+    prod = jnp.transpose(o_ref[...].astype(f32) * go_ref[...].astype(f32))
+    for half in range(2):
+        mine = (lane < HEAD_DIM) if half == 0 else (lane >= HEAD_DIM)
+        here = mine[:qrows]
+        one = ((lane == HEAD_DIM) if half == 0 else (lane == 0))[:qrows]
+        keys = jnp.where(mine, k.astype(f32), mask).astype(bf16)
+        vals = jnp.where(mine, v, jnp.zeros_like(v))
+        delta = colsum(prod[half * HEAD_DIM : (half + 1) * HEAD_DIM, :])
+        for i in range(n // qrows):
+            rows = pl.ds(i * qrows, qrows)
+            q_raw, go = q_ref[rows, :], go_ref[rows, :]
+            q = jnp.where(here, q_raw.astype(f32) * scale, jnp.where(one, 1.0, 0.0)).astype(bf16)
+            p = jnp.exp(dot(keys, q, NT) - lse_ref[half, :, rows])
+            gp = dot(vals, go, NT)
+            gs = (p * (gp - delta[:, i * qrows : (i + 1) * qrows])).astype(bf16)
+            gv = dot(p.astype(bf16), go, NN)
+            gk = dot(gs, q_raw, NN)
+            if i == 0:
+                gv_sum[half], gk_sum[half] = gv, gk
+            else:
+                gv_sum[half] += gv
+                gk_sum[half] += gk
+            gq = (dot(gs, k, TN) * scale).astype(bf16)
+            if half == 0:
+                gq_ref[rows, :] = gq
+            else:
+                gq_ref[rows, :] = jnp.where(here, gq, gq_ref[rows, :])
+    low = lane < HEAD_DIM
+    gk_ref[...] = (jnp.where(low, gk_sum[0], gk_sum[1]) * scale).astype(bf16)
+    gv = jnp.where(low, gv_sum[0], gv_sum[1]).astype(bf16)
+    gv_ref[...] = gv
+    sq_ref[...] = colsum(gq_ref[...].astype(f32))
+    sv_ref[...] = colsum(gv.astype(f32))
+
+
+def attend_back_call(mask, q, k, v, o, go, lse, first, count, qrows=512):
+    n = q.shape[0]
+    block = pl.BlockSpec((n, 128), lambda h: (0, h + first))
+    own = pl.BlockSpec((n, 128), lambda h: (0, h))
+    vec = pl.BlockSpec((1, 128), lambda h: (0, h))
+    return pl.pallas_call(
+        partial(attend_back_kernel, qrows),
+        grid=(count,),
+        in_specs=[
+            fixed((n, 1)), block, block, block, own, block,
+            pl.BlockSpec((2, 1, n), lambda h: (h, 0, 0)),
+        ],
+        out_specs=[own, own, own, vec, vec],
+        out_shape=[shape((n, 128 * count), bf16)] * 3 + [shape((1, 128 * count), f32)] * 2,
+        scratch_shapes=[pltpu.VMEM((2, n, 128), f32)] * 2,
+        compiler_params=params(),
+        cost_estimate=cost(32 * count * n * n * 128, 16 * n * 128 * count, 2 * count * n * n),
+        name="attend_back",
+    )(mask, q, k, v, o, go, lse)
+
+
+def out_kernel(parts, place_ref, x_ref, bias_ref, gain_ref, shift_ref, own_ref, sib_ref, *refs):
+    o_refs, (m_ref, b_ref, w, sem) = refs[:parts], refs[parts:]
+    copies = wout_copies(own_ref, sib_ref, w, place_ref, sem)
+
+    @pl.when(pl.program_id(0) == 0)
+    def _():
+        for c in copies:
+            c.start()
+        for c in copies:
+            c.wait()
+
+    m = x_ref[...].astype(f32) + bias_ref[...]
+    first = 0
+    for o_ref in o_refs:
+        m = m + dot(o_ref[...], w[first : first + o_ref.shape[1], :], NN)
+        first += o_ref.shape[1]
+    m_ref[...] = m
+    xh, _ = norm_parts(m)
+    b_ref[...] = (xh * gain_ref[...] + shift_ref[...]).astype(bf16)
+
+
+def wout_copies(own_ref, sib_ref, w, place_ref, sem):
+    n = len(OFFSETS)
+    height = own_ref.shape[0] // n
+    return place_rows(
+        [ref.at[pl.ds(height * i, height), :] for ref in (own_ref, sib_ref) for i in range(n)],
+        w,
+        place_ref,
+        sem,
+        height,
+    )
+
+
+def out_call(place, x, o_parts, own, sib, bias, gain, shift):
+    rows, width = x.shape
+    vec = fixed((1, width))
+    block = rowed(ROWS, width)
+    return pl.pallas_call(
+        partial(out_kernel, len(o_parts)),
+        grid_spec=pltpu.PrefetchScalarGridSpec(
+            num_scalar_prefetch=1,
+            grid=(rows // ROWS,),
+            in_specs=[block, vec, vec, vec, ANY, ANY] + [rowed(ROWS, o.shape[1]) for o in o_parts],
+            out_specs=[block, block],
+            scratch_shapes=[
+                pltpu.VMEM((width, width), bf16),
+                pltpu.SemaphoreType.DMA((2 * len(OFFSETS),)),
+            ],
+        ),
+        out_shape=[shape((rows, width), f32), shape((rows, width), bf16)],
+        compiler_params=params(),
+        cost_estimate=cost(4 * rows * width * width, width * (10 * rows + 2 * width)),
+        name="out",
+    )(place, x, bias, gain, shift, own, sib, *o_parts)
+
+
+def gelu_both(z, gh):
+    t = 1.0 / (1.0 + jnp.abs(z) * (0.3275911 / math.sqrt(2.0)))
+    e = jnp.exp(z * z * -0.5)
+    half = (0.254829592, -0.284496736, 1.421413741, -1.453152027, 1.061405429)
+    tail = half[4] * 0.5
+    for c in half[3::-1]:
+        tail = tail * t + 0.5 * c
+    tail = tail * t * e
+    phi = jnp.where(z > 0, 1.0 - tail, tail)
+    return z * phi, gh * (phi + z * e * (1.0 / math.sqrt(2.0 * math.pi)))
+
+
+def ffn_kernel(n, later, *refs):
+    b_own, b_sib, g_own, g_sib, ub_ref = refs[:5]
+    slots = refs[5 : 5 + n]
+    refs = refs[5 + n :]
+    if later:
+        acc_o, acc_g = refs[:2]
+        refs = refs[2:]
+        h_ref, gz_ref, sum_ref, oo_ref, go_ref, os_ref, gs_ref, us, ds, sem = refs
+    else:
+        h_ref, gz_ref, sum_ref, oo_ref, go_ref, us, ds, sem = refs
+    units = us.shape[0] // n
+    i = pl.program_id(0)
+    near = i < pl.num_programs(0) // 2
+    copies = []
+    for s, slot in enumerate(slots):
+        rows = pl.ds(s * units, units)
+        copies.append(
+            pltpu.make_async_copy(slot.at[pl.ds(0, units), :], us.at[rows, :], sem.at[0, s])
+        )
+        copies.append(
+            pltpu.make_async_copy(slot.at[pl.ds(units, units), :], ds.at[rows, :], sem.at[1, s])
+        )
+
+    @pl.when(i == 0)
+    def _():
+        for c in copies:
+            c.start()
+        for c in copies:
+            c.wait()
+        sum_ref[...] = jnp.zeros_like(sum_ref)
+
+    b = jnp.where(near, b_own[...], b_sib[...])
+    g = jnp.where(near, g_own[...], g_sib[...])
+    h, gz = gelu_both(dot(b, us[...], NT) + ub_ref[...], dot(g, ds[...], NT))
+    h, gz = h.astype(bf16), gz.astype(bf16)
+    h_ref[...] = h
+    gz_ref[...] = gz
+    sum_ref[...] += colsum(gz.astype(f32))
+    out = dot(h, ds[...], NN)
+    back = dot(gz, us[...], NN)
+    if not later:
+        oo_ref[...] = out
+        go_ref[...] = back
+        return
+    out = out + acc_o[...]
+    back = back + acc_g[...]
+
+    @pl.when(near)
+    def _():
+        oo_ref[...] = out
+        go_ref[...] = back
+
+    @pl.when(jnp.logical_not(near))
+    def _():
+        os_ref[...] = out.astype(bf16)
+        gs_ref[...] = back.astype(bf16)
+
+
+def ffn_call(b_own, b_sib, g_own, g_sib, ub, slots, acc=None):
+    rows, width = b_own.shape
+    half = rows // ROWS
+    n = len(slots)
+    units = ub.shape[1]
+    later = acc is not None
+    near = pl.BlockSpec((ROWS, width), lambda i: (jnp.minimum(i, half - 1), 0))
+    far = pl.BlockSpec((ROWS, width), lambda i: (jnp.maximum(i - half, 0), 0))
+    both = rowed(ROWS, width)
+    acc = list(acc or ())
+    out_specs = [rowed(ROWS, units), rowed(ROWS, units), fixed((1, units))]
+    out_shape = [shape((2 * rows, units), bf16)] * 2 + [shape((1, units), f32)]
+    if later:
+        out_specs += [near, near, far, far]
+        out_shape += [shape((rows, width), f32)] * 2 + [shape((rows, width), bf16)] * 2
+    else:
+        out_specs += [both, both]
+        out_shape += [shape((2 * rows, width), f32)] * 2
+    return pl.pallas_call(
+        partial(ffn_kernel, n, later),
+        grid=(2 * half,),
+        in_specs=[near, far, near, far, fixed((1, units))] + [ANY] * n + [both] * len(acc),
+        out_specs=out_specs,
+        out_shape=out_shape,
+        scratch_shapes=[
+            pltpu.VMEM((units, width), bf16),
+            pltpu.VMEM((units, width), bf16),
+            pltpu.SemaphoreType.DMA((2, n)),
+        ],
+        compiler_params=params(),
+        cost_estimate=cost(
+            24 * rows * width * units, rows * width * (24 + 16 * later), 4 * rows * units
+        ),
+        name="ffn",
+    )(b_own, b_sib, g_own, g_sib, ub, *slots, *acc)
+
+
+def ffn_weights_kernel(n, gz, h, b_own, b_sib, g_own, g_sib, *refs):
+    outs = refs[:n]
+    lv, rv, ov, lsem, rsem, osem = refs[n:]
+    rows = b_own.shape[0]
+    units = outs[0].shape[0] // 2
+    loads = []
+    for which, (left, parts) in enumerate(((gz, (b_own, b_sib)), (h, (g_own, g_sib)))):
+        loads.append(pltpu.make_async_copy(left, lv.at[which], lsem.at[which]))
+        for j, part in enumerate(parts):
+            loads.append(
+                pltpu.make_async_copy(
+                    part, rv.at[which, pl.ds(j * rows, rows), :], rsem.at[which, j]
+                )
+            )
+    for c in loads:
+        c.start()
+    stores = []
+    step = 0
+    for which in range(2):
+        for c in loads[3 * which : 3 * which + 3]:
+            c.wait()
+        for pair in range(n // 2):
+            slot = step % 2
+            if step >= 2:
+                for c in stores[2 * (step - 2) : 2 * (step - 2) + 2]:
+                    c.wait()
+            cols = pl.ds(pair * 2 * units, 2 * units)
+            ov[slot] = dot(lv[which, :, cols], rv[which], TN).astype(bf16)
+            for j in range(2):
+                c = pltpu.make_async_copy(
+                    ov.at[slot, pl.ds(j * units, units), :],
+                    outs[2 * pair + j].at[pl.ds(which * units, units), :],
+                    osem.at[slot, j],
+                )
+                c.start()
+                stores.append(c)
+            step += 1
+    for c in stores[2 * (step - 2) :]:
+        c.wait()
+
+
+def ffn_weights_call(gz, h, b_own, b_sib, g_own, g_sib, n):
+    rows, units = gz.shape
+    width = b_own.shape[1]
+    return pl.pallas_call(
+        partial(ffn_weights_kernel, n),
+        in_specs=[ANY] * 6,
+        out_specs=[ANY] * n,
+        out_shape=[shape((2 * units // n, width), bf16)] * n,
+        scratch_shapes=[
+            pltpu.VMEM((2, rows, units), bf16),
+            pltpu.VMEM((2, rows, width), bf16),
+            pltpu.VMEM((2, 2 * units // n, width), bf16),
+            pltpu.SemaphoreType.DMA((2,)),
+            pltpu.SemaphoreType.DMA((2, 2)),
+            pltpu.SemaphoreType.DMA((2, 2)),
+        ],
+        compiler_params=params(),
+        cost_estimate=cost(6 * rows * units * width, 4 * rows * (units + width)),
+        name="ffn_weights",
+    )(gz, h, b_own, b_sib, g_own, g_sib)
+
+
+def mid_kernel(
+    place_ref, oo_ref, os_ref, go_ref, gs_ref, m_ref, g_ref, keep_ref, db_ref, gain_ref, own_ref, sib_ref,
+    hid_ref, gm_ref, gr_ref, gatt_ref, sums_ref, w, sem,
+):
+    copies = wout_copies(own_ref, sib_ref, w, place_ref, sem)
+
+    @pl.when(pl.program_id(0) == 0)
+    def _():
+        for c in copies:
+            c.start()
+        for c in copies:
+            c.wait()
+        sums_ref[...] = jnp.zeros_like(sums_ref)
+
+    m = m_ref[...]
+    g = g_ref[...].astype(f32)
+    hid_ref[...] = (m + oo_ref[...] + os_ref[...].astype(f32) + db_ref[...]).astype(bf16)
+    gb = go_ref[...] + gs_ref[...].astype(f32)
+    xh, scale = norm_parts(m)
+    gm = g + norm_back(xh, scale, gain_ref[...], gb)
+    gr = gm.astype(bf16)
+    gm_ref[...] = gm
+    gr_ref[...] = gr
+    gatt_ref[...] = (dot(gr, w[...], NT) * keep_ref[...]).astype(bf16)
+    sums_ref[0:1, :] += colsum(gb * xh)
+    sums_ref[1:2, :] += colsum(gb)
+    sums_ref[2:3, :] += colsum(gr.astype(f32))
+    sums_ref[3:4, :] += colsum(g)
+
+
+def mid_call(place, oo, os, go, gs, m, g, keep, db, gain, own, sib):
+    rows, width = m.shape
+    block = rowed(ROWS, width)
+    vec = fixed((1, width))
+    return pl.pallas_call(
+        mid_kernel,
+        grid_spec=pltpu.PrefetchScalarGridSpec(
+            num_scalar_prefetch=1,
+            grid=(rows // ROWS,),
+            in_specs=[block] * 6 + [rowed(ROWS, 1), vec, vec, ANY, ANY],
+            out_specs=[block] * 4 + [fixed((8, width))],
+            scratch_shapes=[
+                pltpu.VMEM((width, width), bf16),
+                pltpu.SemaphoreType.DMA((2 * len(OFFSETS),)),
+            ],
+        ),
+        out_shape=[
+            shape((rows, width), bf16),
+            shape((rows, width), f32),
+            shape((rows, width), bf16),
+            shape((rows, width), bf16),
+            shape((8, width), f32),
+        ],
+        compiler_params=params(),
+        cost_estimate=cost(4 * rows * width * width, width * (30 * rows + 2 * width)),
+        name="mid",
+    )(place, oo, os, go, gs, m, g, keep, db, gain, own, sib)
+
+
+def att_weights_kernel(n, jobs, place_ref, *refs):
+    lefts, rights = refs[: jobs[0]], refs[jobs[0] : jobs[0] + jobs[1]]
+    refs = refs[jobs[0] + jobs[1] :]
+    outs, refs = refs[: n + 1], refs[n + 1 :]
+    lv, rv, ov, lsem, rsem, osem = refs
+    table = jobs[2]
+    height = outs[0].shape[0]
+    loads = [pltpu.make_async_copy(r, lv.at[i], lsem.at[i]) for i, r in enumerate(lefts)]
+    col = 0
+    right_loads = []
+    for i, r in enumerate(rights):
+        right_loads.append(
+            pltpu.make_async_copy(r, rv.at[:, pl.ds(col, r.shape[1])], rsem.at[i])
+        )
+        col += r.shape[1]
+    loads[0].start()
+    for c in right_loads:
+        c.start()
+    for c in loads[1:]:
+        c.start()
+    have = set()
+    stores = []
+    col = 0
+    for step, (left, r) in enumerate(zip(table, rights, strict=True)):
+        if left not in have:
+            loads[left].wait()
+            have.add(left)
+        right_loads[step].wait()
+        slot = step % 2
+        if step >= 2:
+            for c in stores[step - 2]:
+                c.wait()
+        wide = r.shape[1]
+        cols = pl.ds(col, wide)
+        ov[slot, :, pl.ds(0, wide)] = dot(lv[left], rv[:, cols], TN).astype(bf16)
+        stores.append([])
+        for i in range(2 * n):
+            rows = pl.ds(pl.multiple_of(place_ref[i] * height, 16), height)
+            goal = outs[i].at[:, cols] if i < n else outs[n].at[i - n, :, cols]
+            c = pltpu.make_async_copy(ov.at[slot, rows, pl.ds(0, wide)], goal, osem.at[slot, i])
+            c.start()
+            stores[-1].append(c)
+        col += wide
+    for group in stores[-2:]:
+        for c in group:
+            c.wait()
+
+
+def att_weights_call(place, lefts, rights, table):
+    rows, width = lefts[0].shape
+    n = len(OFFSETS)
+    total = sum(r.shape[1] for r in rights)
+    wide = max(r.shape[1] for r in rights)
+    height = width // (2 * n)
+    return pl.pallas_call(
+        partial(att_weights_kernel, n, (len(lefts), len(rights), table)),
+        grid_spec=pltpu.PrefetchScalarGridSpec(
+            num_scalar_prefetch=1,
+            grid=(1,),
+            in_specs=[ANY] * (len(lefts) + len(rights)),
+            out_specs=[ANY] * (n + 1),
+            scratch_shapes=[
+                pltpu.VMEM((len(lefts), rows, width), bf16),
+                pltpu.VMEM((rows, total), bf16),
+                pltpu.VMEM((2, width, wide), bf16),
+                pltpu.SemaphoreType.DMA((len(lefts),)),
+                pltpu.SemaphoreType.DMA((len(rights),)),
+                pltpu.SemaphoreType.DMA((2, 2 * n)),
+            ],
+        ),
+        out_shape=[shape((height, total), bf16)] * n + [shape((n, height, total), bf16)],
+        compiler_params=params(),
+        cost_estimate=cost(3 * rows * width * total, 2 * (rows + width) * total),
+        name="att_weights",
+    )(place, *lefts, *rights)
+
+
+def in_kernel(n, pieces, place_ref, x_ref, gm_ref, gain_ref, *refs):
+    grads, slots = refs[:pieces], refs[pieces : pieces + n]
+    own_ref, send_ref, sums_ref, w, sem = refs[pieces + n :]
+    height = slots[0].shape[0]
+    copies = place_rows(slots, w, place_ref, sem, height)
+    i = pl.program_id(0)
+
+    @pl.when(i == 0)
+    def _():
+        for c in copies:
+            c.start()
+        for c in copies:
+            c.wait()
+        sums_ref[...] = jnp.zeros_like(sums_ref)
+
+    ga = None
+    col = 0
+    for r in grads:
+        part = dot(r[...], w[:, col : col + r.shape[1]], NT)
+        ga = part if ga is None else ga + part
+        col += r.shape[1]
+    xh, scale = norm_parts(x_ref[...].astype(f32))
+    res = gm_ref[...] + norm_back(xh, scale, gain_ref[...], ga)
+    sums_ref[0:1, :] += colsum(ga * xh)
+    sums_ref[1:2, :] += colsum(ga)
+    half = pl.num_programs(0) // 2
+
+    @pl.when(i < half)
+    def _():
+        send_ref[...] = res.astype(bf16)
+
+    @pl.when(i >= half)
+    def _():
+        own_ref[...] = res
+
+
+def in_call(place, x, gm, gain, grads, slots):
+    rows, width = x.shape
+    n = len(slots)
+    half = rows // ROWS // 2
+
+    def turned(w):
+        return pl.BlockSpec((ROWS, w), lambda i, *_: ((i + half) % (2 * half), 0))
+
+    return pl.pallas_call(
+        partial(in_kernel, n, len(grads)),
+        grid_spec=pltpu.PrefetchScalarGridSpec(
+            num_scalar_prefetch=1,
+            grid=(2 * half,),
+            in_specs=[turned(width), turned(width), fixed((1, width))]
+            + [turned(g.shape[1]) for g in grads]
+            + [ANY] * n,
+            out_specs=[
+                pl.BlockSpec((ROWS, width), lambda i, *_: (jnp.maximum(i - half, 0), 0)),
+                pl.BlockSpec((ROWS, width), lambda i, *_: (jnp.minimum(i, half - 1), 0)),
+                fixed((8, width)),
+            ],
+            scratch_shapes=[
+                pltpu.VMEM((width, 3 * width), bf16),
+                pltpu.SemaphoreType.DMA((n,)),
+            ],
+        ),
+        out_shape=[
+            shape((rows // 2, width), f32),
+            shape((rows // 2, width), bf16),
+            shape((8, width), f32),
+        ],
+        compiler_params=params(),
+        cost_estimate=cost(8 * rows * width * width, width * (14 * rows + 6 * width)),
+        name="in",
+    )(place, x, gm, gain, *grads, *slots)
+
+
+def local_swapped(
+    sizes, hidden_in, lengths, ln1_gain, ln1_bias, w_qkv, q_bias, v_bias, w_out, out_bias, ln2_gain, ln2_bias,
+    w_up, up_bias, w_down, down_bias, cotangent,
+):
+    ring = Ring(sizes)
+    blk = lax.axis_index("blk")
+    core = lax.axis_index("cell") % 2
+    genes, width = hidden_in.shape[1:]
+    height = w_qkv.shape[0]
+    units = w_up.shape[0]
+    shards = ring.cells
+    n = len(OFFSETS)
+
+    def vec(v):
+        return v.reshape(1, -1)
+
+    def pick(x, which):
+        return lax.dynamic_index_in_dim(x, which, 0, keepdims=False)
+
+    x_own, x_send = pick(hidden_in, blk), pick(hidden_in, 1 - blk)
+    x = jnp.concatenate([x_own, ring.swap_blk(x_send)], axis=0)
+    qkv_own = ring.gather(w_qkv, 2)
+    qkv_sib = [ring.swap_core(s) for s in qkv_own]
+    rest_own = ring.gather(jnp.concatenate([w_up, w_down, w_out], axis=0), 1)
+    g = jnp.concatenate([pick(cotangent, blk), ring.swap_blk(pick(cotangent, 1 - blk))], axis=0)
+    g_sib = ring.swap_core(g)
+    wo_own = jnp.concatenate([s[2 * units :] for s in rest_own], axis=0)
+    wo_sib = ring.swap_core(wo_own)
+
+    chips_own, chips_sib = ring.chips_of_slots(core), ring.chips_of_slots(1 - core)
+    shard_own = 2 * chips_own + core
+    shard_sib = 2 * chips_sib + 1 - core
+    place = jnp.concatenate([shard_own, shard_sib])
+    index = jnp.arange(genes, dtype=jnp.int32)
+    index = jnp.concatenate([blk * genes + index, (1 - blk) * genes + index])
+    keep = (index < pick(lengths, blk)).astype(f32)[:, None]
+    mask = jnp.where(keep > 0, 0.0, far_below)
+
+    a, q, k, v = qkv_call(
+        place, x, vec(ln1_gain), vec(ln1_bias), vec(q_bias), vec(v_bias), qkv_own + qkv_sib
+    )
+    pairs = width // 128
+    cuts = [(0, pairs // 2), (pairs // 2, pairs - pairs // 2)]
+    attended = [attend_call(mask, keep, q, k, v, first, count) for first, count in cuts]
+    o_parts = [t[0] for t in attended]
+    m, b = out_call(
+        place, x, o_parts, wo_own, wo_sib, vec(out_bias), vec(ln2_gain), vec(ln2_bias)
+    )
+    b_sib = ring.swap_core(b)
+    ub = up_bias.reshape(shards, units)[shard_own]
+    groups = ((0, 1, 2, 5), (3, 4, 6, 7))
+    acc = None
+    parts = [None] * n
+    up_sums = [None] * n
+    for group in groups:
+        res = ffn_call(
+            b, b_sib, g, g_sib, vec(jnp.concatenate([ub[s] for s in group])),
+            [rest_own[s] for s in group], acc,
+        )
+        h, gz, up_sum = res[:3]
+        acc = res[3:]
+        made = ffn_weights_call(gz, h, b, b_sib, g, g_sib, len(group))
+        for j, s in enumerate(group):
+            parts[s] = made[j]
+            up_sums[s] = up_sum[0, j * units : (j + 1) * units]
+    oo, gb_own, os_send, gs_send = acc
+    out_hidden, gm, gr, gatt, mid_sums = mid_call(
+        place, oo, ring.swap_core(os_send), gb_own, ring.swap_core(gs_send), m, g, keep,
+        vec(down_bias), vec(ln2_gain), wo_own, wo_sib,
+    )
+    ffn_rows = ring.reduce(lambda s: [parts[s]], 2)
+
+    backs = [
+        attend_back_call(mask, q, k, v, o_parts[i], gatt, attended[i][1], first, count)
+        for i, (first, count) in enumerate(cuts)
+    ]
+    grads = [t[i] for i in range(3) for t in backs]
+    made = att_weights_call(
+        place, [a, jnp.concatenate(o_parts, axis=1)],
+        grads + [gr], [0] * len(grads) + [1],
+    )
+    att_sib = ring.swap_core(made[n])
+    att_rows = ring.reduce(lambda s: [made[s], att_sib[s]], 2)
+    in_own, in_send, in_sums = in_call(place, x, gm, vec(ln1_gain), grads, qkv_own + qkv_sib)
+
+    def home(own, sent):
+        got = ring.swap_blk(sent).astype(own.dtype)
+        return jnp.where(blk == 0, jnp.stack([own, got]), jnp.stack([got, own]))
+
+    hidden = home(out_hidden[:genes], out_hidden[genes:])
+    in_grad = home(in_own, in_send)
+    up_rows = jnp.zeros((shards, units), f32).at[shard_own].set(jnp.stack(up_sums))
+    early = ring.total(jnp.concatenate([mid_sums[:4].reshape(-1), up_rows.reshape(-1)]))
+    late = ring.total(
+        jnp.concatenate(
+            [in_sums[:2].reshape(-1)]
+            + [t[3].reshape(-1) for t in backs]
+            + [t[4].reshape(-1) for t in backs]
+        )
+    )
+    ln2_gain_g, ln2_bias_g, out_bias_g, down_bias_g = jnp.split(early[: 4 * width], 4)
+    ln1_gain_g, ln1_bias_g, q_bias_g, v_bias_g = jnp.split(late, 4)
+    return (
+        hidden,
+        in_grad,
+        ln1_gain_g,
+        ln1_bias_g,
+        att_rows[:, : 3 * width],
+        q_bias_g,
+        v_bias_g,
+        att_rows[:, 3 * width :],
+        out_bias_g,
+        ln2_gain_g,
+        ln2_bias_g,
+        ffn_rows[:units],
+        early[4 * width :],
+        ffn_rows[units:],
+        down_bias_g,
+    )
+
+
 def solution(mesh):
     placed = (
         P("cell", "blk", None),
@@ -302,7 +1175,7 @@
         P("cell", "blk", None),
     )
     return jax.shard_map(
-        local,
+        partial(local_swapped, dict(mesh.shape)) if swappable(mesh) else local,
         mesh=mesh,
         in_specs=placed,
         out_specs=(

time: 1760 us -> 776 us (0.44)
  waiting for transfers between devices: 869 us -> 311 us
  matrix products: 500 us -> 0 us
  Pallas kernels: 0 us -> 325 us
  local copies, waits for them, and re-layouts: 168 us -> 41.2 us
  other arithmetic: 143 us -> 29.7 us
  starting transfers between devices: 10.3 us -> 62.8 us
  blocking collectives: 42.4 us -> 0 us
    dot_general x26 -> x0, matrix products: 500 us -> none  [the longest x4 73.7 us: block_scores(): jnp.einsum('cqhd,ckhd->chqk', queries, key_block, preferred_element_type=...]
    reduce_scatter x1 -> x0, waiting for transfers between devices: 330 us -> none  [local(): lax.psum_scatter(jnp.concatenate([qkv_term, out_term, ffn_term], axis=1)....]
    pallas_call x0 -> x13, Pallas kernels: none -> 325 us  [the longest x2 78.8 us: ffn_call(): pl.pallas_call(partial(ffn_kernel, n, later), grid=(2 * half,), in_specs=...]
    ppermute x10 -> x58, waiting for transfers between devices: 437 us -> 311 us  [permute(): return lax.ppermute(x, AXES, pairs)]
    all_gather x4 -> x0, waiting for transfers between devices: 81.1 us -> none  [the longest x1 81.1 us: local(): lax.all_gather(w_qkv, 'cell', axis=0, tiled=True)]
    reshape x9 -> x14, local copies, waits for them, and re-layouts: 65.4 us -> 6.16 us  [the longest x10 5.98 us: vec(): return v.reshape(1, -1)]
    ppermute x10 -> x58, starting transfers between devices: 10.1 us -> 62.8 us  [permute(): return lax.ppermute(x, AXES, pairs)]
    reduce_sum x10 -> x0, other arithmetic: 44.4 us -> none  [the longest x1 27.2 us: stats_turn(): jnp.sum(raised, axis=-1)]
  transfers between devices with their start and end apart: 16 -> 58, of which waited for: 12 -> 23; matrix products, arithmetic and copies ran while one was open for 19% -> 8% of each run, Pallas kernels for 0% -> 18%
where the time goes in v1:
time: 776 us; the launch traced here: 772 us
  Pallas kernels  325 us (42%)
  waiting for transfers between devices  311 us (40%)
  starting transfers between devices  62.8 us (8%)
  local copies, waits for them, and re-layouts  41.2 us (5%)
  other arithmetic  29.7 us (4%)
    ppermute x58, waiting for transfers between devices, permute(): return lax.ppermute(x, AXES, pairs)  311 us
    pallas_call x2, Pallas kernels, ffn_call(): pl.pallas_call(partial(ffn_kernel, n, later), grid=(2 * half,), in_specs=...  78.8 us
    pallas_call x2, Pallas kernels, attend_back_call(): pl.pallas_call(partial(attend_back_kernel, qrows), grid=(count,), in_spec...  63.3 us
    ppermute x58, starting transfers between devices, permute(): return lax.ppermute(x, AXES, pairs)  62.8 us
    pallas_call x2, Pallas kernels, ffn_weights_call(): pl.pallas_call(partial(ffn_weights_kernel, n), in_specs=[ANY] * 6, out_sp...  41.7 us
    pallas_call x2, Pallas kernels, attend_call(): pl.pallas_call(partial(attend_kernel, qrows), grid=(count,), in_specs=[fi...  39.5 us
    pallas_call x1, Pallas kernels, att_weights_call(): pl.pallas_call(partial(att_weights_kernel, n, (len(lefts), len(rights), t...  29 us
    pallas_call x1, Pallas kernels, in_call(): pl.pallas_call(partial(in_kernel, n, len(grads)), grid_spec=pltpu.Prefetc...  24.5 us
  transfers between devices with their start and end apart: 58, of which 23 were waited for; matrix products, arithmetic and copies ran while one was open for 8% of the time, Pallas kernels for 18%

profile of v1, /device:TPU:0, one launch (start us, length us, event | category | flops | bytes accessed | tf_op | source)
XLA Modules:
  0.0 772.1 jit_solution(17078598217483005985)
XLA Ops:
  7.6 21.5 %collective-permute-done.1.refs_6_ = bf16[720,1280]{1,0:T(8,128)(2,1)} collective-permute-done((bf16[720,1280]{1,0:T(8,128)(2,1)}, bf16[720,1280]{1,0:T(8,128)(2,1)}, u32[]{:S(2)}, u32[]{:S(2)}) %collective-permute-start.1) | collective-permute-done | bytes 1843232 | tf_op jit(solution)/shard_map/ppermute | solution.py:345
  38.3 27.7 %collective-permute-done.9.refs_1_.refs_7_ = bf16[80,3840]{1,0:T(8,128)(2,1)} collective-permute-done((bf16[80,3840]{1,0:T(8,128)(2,1)S(1)}, bf16[80,3840]{1,0:T(8,128)(2,1)}, u32[]{:S(2)}, u32[]{:S(2)}) %collective-permute-start.9) | collective-permute-done | bytes 614432 | tf_op jit(solution)/shard_map/ppermute | solution.py:345
  72.9 9.3 %collective-permute-done.10.refs_2_.refs_8_ = bf16[80,3840]{1,0:T(8,128)(2,1)} collective-permute-done((bf16[80,3840]{1,0:T(8,128)(2,1)}, bf16[80,3840]{1,0:T(8,128)(2,1)}, u32[]{:S(2)}, u32[]{:S(2)}) %collective-permute-start.10) | collective-permute-done | bytes 614432 | tf_op jit(solution)/shard_map/ppermute | solution.py:345
  90.4 4.9 collective-permute-done.11.refs_3_.refs_9_
  105.9 8.5 %collective-permute-done.25 = bf16[512,1280]{1,0:T(8,128)(2,1)} collective-permute-done((bf16[512,1280]{1,0:T(8,128)(2,1)}, bf16[512,1280]{1,0:T(8,128)(2,1)}, u32[]{:S(2)}, u32[]{:S(2)}) %collective-permute-start.25) | collective-permute-done | bytes 1310752 | tf_op jit(solution)/shard_map/ppermute | solution.py:345
  114.9 6.7 collective-permute-done.12.refs_4_.refs_10_
  130.1 19.0 %qkv.1 = (bf16[1024,1280]{1,0:T(8,128)(2,1)}, bf16[1024,1280]{1,0:T(8,128)(2,1)}, bf16[1024,1280]{1,0:T(8,128)(2,1)}, bf16[1024,1280]{1,0:T(8,128)(2,1)}) custom-call(s32[16]{0:T(128)} %pad_add_fusion.place_ref, bf16[1024,1280]{1,0:T(8,128)(2,1)} %pad_maximum_fusion.x_ref, f32[1,1280]{1,0:T(1,128)} %reshape.170.gain_ref, f32[1,1280]{1,0:T(1,128)} %reshape.171.bias_ref, ...), custom_call_target="tpu_custom_call" | custom-call | flops 10066329600 | bytes 22937600 | tf_op jit(solution)/shard_map/qkv/pallas_call | solution.py:473
  154.4 13.6 %collective-permute-done.4.refs_6_ = bf16[720,1280]{1,0:T(8,128)(2,1)} collective-permute-done((bf16[720,1280]{1,0:T(8,128)(2,1)}, bf16[720,1280]{1,0:T(8,128)(2,1)}, u32[]{:S(2)}, u32[]{:S(2)}) %collective-permute-start.4) | collective-permute-done | bytes 1843232 | tf_op jit(solution)/shard_map/ppermute | solution.py:345
  171.3 21.1 %collective-permute-done.6.refs_7_ = bf16[720,1280]{1,0:T(8,128)(2,1)S(1)} collective-permute-done((bf16[720,1280]{1,0:T(8,128)(2,1)}, bf16[720,1280]{1,0:T(8,128)(2,1)S(1)}, u32[]{:S(2)}, u32[]{:S(2)}) %collective-permute-start.6) | collective-permute-done | bytes 1843232 | tf_op jit(solution)/shard_map/ppermute | solution.py:345
  194.4 36.2 %collective-permute-done.7.refs_8_ = bf16[720,1280]{1,0:T(8,128)(2,1)S(1)} collective-permute-done((bf16[720,1280]{1,0:T(8,128)(2,1)}, bf16[720,1280]{1,0:T(8,128)(2,1)S(1)}, u32[]{:S(2)}, u32[]{:S(2)}) %collective-permute-start.7) | collective-permute-done | bytes 1843232 | tf_op jit(solution)/shard_map/ppermute | solution.py:345
  232.6 19.8 %attend.3 = (bf16[1024,640]{1,0:T(8,128)(2,1)}, f32[10,1,1024]{2,1,0:T(1,128)}) custom-call(f32[1024,1]{1,0:T(8,128)} %compare_select_fusion.mask_ref, f32[1024,1]{1,0:T(8,128)} %convert_element_type.201.keep_ref, bf16[1024,1280]{1,0:T(8,128)(2,1)} %get-tuple-element.72.q_ref, bf16[1024,1280]{1,0:T(8,128)(2,1)} %get-tuple-element.73.k_ref, ...), custom_call_target="tpu_custom_call" | custom-call | flops 13421772800 | bytes 5242880 | tf_op jit(solution)/shard_map/attend/pallas_call | solution.py:523
  252.3 19.7 %attend.2 = (bf16[1024,640]{1,0:T(8,128)(2,1)}, f32[10,1,1024]{2,1,0:T(1,128)}) custom-call(f32[1024,1]{1,0:T(8,128)} %compare_select_fusion.mask_ref, f32[1024,1]{1,0:T(8,128)} %convert_element_type.201.keep_ref, bf16[1024,1280]{1,0:T(8,128)(2,1)} %get-tuple-element.72.q_ref, bf16[1024,1280]{1,0:T(8,128)(2,1)} %get-tuple-element.73.k_ref, ...), custom_call_target="tpu_custom_call" | custom-call | flops 13421772800 | bytes 5242880 | tf_op jit(solution)/shard_map/attend/pallas_call | solution.py:523
  272.1 11.4 %out.1 = (f32[1024,1280]{1,0:T(8,128)}, bf16[1024,1280]{1,0:T(8,128)(2,1)}) custom-call(s32[16]{0:T(128)} %pad_add_fusion.place_ref, bf16[1024,1280]{1,0:T(8,128)(2,1)} %pad_maximum_fusion.x_ref, f32[1,1280]{1,0:T(1,128)} %reshape.167.bias_ref, f32[1,1280]{1,0:T(1,128)} %reshape.168.gain_ref, f32[1,1280]{1,0:T(1,128)} %reshape.169.shift_ref, ...), custom_call_target="tpu_custom_call" | custom-call | flops 6710886400 | bytes 16384000 | tf_op jit(solution)/shard_map/out/pallas_call | solution.py:639
  288.9 37.7 %ffn.2 = (bf16[2048,1280]{1,0:T(8,128)(2,1)}, bf16[2048,1280]{1,0:T(8,128)(2,1)}, f32[1,1280]{1,0:T(1,128)}, f32[2048,1280]{1,0:T(8,128)}, f32[2048,1280]{1,0:T(8,128)}) custom-call(bf16[1024,1280]{1,0:T(8,128)(2,1)} %get-tuple-element.77.refs_0_.b_own, bf16[1024,1280]{1,0:T(8,128)(2,1)} %collective-permute-done.24.refs_1_.b_sib, ...), custom_call_target="tpu_custom_call" | custom-call | flops 40265318400 | bytes 31457280 | tf_op jit(solution)/shard_map/ffn/pallas_call | solution.py:746
  326.7 41.1 %ffn.3 = (bf16[2048,1280]{1,0:T(8,128)(2,1)}, bf16[2048,1280]{1,0:T(8,128)(2,1)}, f32[1,1280]{1,0:T(1,128)}, f32[1024,1280]{1,0:T(8,128)}, f32[1024,1280]{1,0:T(...) custom-call(bf16[1024,1280]{1,0:T(8,128)(2,1)} %get-tuple-element.77.refs_0_.b_own, ...), custom_call_target="tpu_custom_call" | custom-call | flops 40265318400 | bytes 52428800 | tf_op jit(solution)/shard_map/ffn/pallas_call | solution.py:746
  377.1 18.0 %mid.1 = (bf16[1024,1280]{1,0:T(8,128)(2,1)}, f32[1024,1280]{1,0:T(8,128)}, bf16[1024,1280]{1,0:T(8,128)(2,1)}, bf16[1024,1280]{1,0:T(8,128)(2,1)}, f32[8,1280]{1,0:T(8,128)}) custom-call(s32[16]{0:T(128)} %pad_add_fusion.place_ref, f32[1024,1280]{1,0:T(8,128)} %get-tuple-element.80.oo_ref, bf16[1024,1280]{1,0:T(8,128)(2,1)} %copy-done.3, ...), custom_call_target="tpu_custom_call" | custom-call | flops 6710886400 | bytes 42598400 | tf_op jit(solution)/shard_map/mid/pallas_call | solution.py:862
  395.1 31.5 %attend_back.3 = (bf16[1024,640]{1,0:T(8,128)(2,1)}, bf16[1024,640]{1,0:T(8,128)(2,1)}, bf16[1024,640]{1,0:T(8,128)(2,1)}, f32[1,640]{1,0:T(1,128)}, f32[1,640]{1,0:T(1,128)}) custom-call(f32[1024,1]{1,0:T(8,128)} %compare_select_fusion.mask_ref, bf16[1024,1280]{1,0:T(8,128)(2,1)} %get-tuple-element.72.q_ref, bf16[1024,1280]{1,0:T(8,128)(2,1)} %get-tuple-element.73.k_ref, ...), custom_call_target="tpu_custom_call" | custom-call | flops 21474836480 | bytes 10485760 | tf_op jit(solution)/shard_map/attend_back/pallas_call | solution.py:586
  426.6 31.7 %attend_back.2 = (bf16[1024,640]{1,0:T(8,128)(2,1)}, bf16[1024,640]{1,0:T(8,128)(2,1)}, bf16[1024,640]{1,0:T(8,128)(2,1)}, f32[1,640]{1,0:T(1,128)}, f32[1,640]{1,0:T(1,128)}) custom-call(f32[1024,1]{1,0:T(8,128)} %compare_select_fusion.mask_ref, bf16[1024,1280]{1,0:T(8,128)(2,1)} %get-tuple-element.72.q_ref, bf16[1024,1280]{1,0:T(8,128)(2,1)} %get-tuple-element.73.k_ref, ...), custom_call_target="tpu_custom_call" | custom-call | flops 21474836480 | bytes 10485760 | tf_op jit(solution)/shard_map/attend_back/pallas_call | solution.py:586
  458.4 29.0 %att_weights.1 = (bf16[80,5120]{1,0:T(8,128)(2,1)}, bf16[80,5120]{1,0:T(8,128)(2,1)}, bf16[80,5120]{1,0:T(8,128)(2,1)}, bf16[80,5120]{1,0:T(8,128)(2,1)}, bf16[8...) custom-call(s32[16]{0:T(128)} %pad_add_fusion.place_ref, ...), custom_call_target="tpu_custom_call" | custom-call | flops 20132659200 | bytes 23592960 | tf_op jit(solution)/shard_map/att_weights/pallas_call | solution.py:941
  487.8 20.8 %ffn_weights.2 = (bf16[640,1280]{1,0:T(8,128)(2,1)}, bf16[640,1280]{1,0:T(8,128)(2,1)}, bf16[640,1280]{1,0:T(8,128)(2,1)}, bf16[640,1280]{1,0:T(8,128)(2,1)}) custom-call(bf16[2048,1280]{1,0:T(8,128)(2,1)} %get-tuple-element.117.gz, bf16[2048,1280]{1,0:T(8,128)(2,1)} %get-tuple-element.118.h, bf16[1024,1280]{1,0:T(8,128)(2,1)} %get-tuple-element.77.refs_0_.b_own, ...), custom_call_target="tpu_custom_call" | custom-call | flops 20132659200 | bytes 20971520 | tf_op jit(solution)/shard_map/ffn_weights/pallas_call | solution.py:809
  513.4 24.5 %in.1 = (f32[512,1280]{1,0:T(8,128)}, bf16[512,1280]{1,0:T(8,128)(2,1)}, f32[8,1280]{1,0:T(8,128)}) custom-call(s32[16]{0:T(128)} %pad_add_fusion.place_ref, bf16[1024,1280]{1,0:T(8,128)(2,1)} %pad_maximum_fusion.x_ref, f32[1024,1280]{1,0:T(8,128)} %get-tuple-element.86.gm_ref, f32[1,1280]{1,0:T(1,128)} %reshape.170.gain_ref, ...), custom_call_target="tpu_custom_call" | custom-call | flops 13421772800 | bytes 28180480 | tf_op jit(solution)/shard_map/in/pallas_call | solution.py:1008
  540.7 7.1 collective-permute-done.31
  550.0 20.9 %ffn_weights.3 = (bf16[640,1280]{1,0:T(8,128)(2,1)}, bf16[640,1280]{1,0:T(8,128)(2,1)}, bf16[640,1280]{1,0:T(8,128)(2,1)}, bf16[640,1280]{1,0:T(8,128)(2,1)}) custom-call(bf16[2048,1280]{1,0:T(8,128)(2,1)} %get-tuple-element.122.gz, bf16[2048,1280]{1,0:T(8,128)(2,1)} %get-tuple-element.123.h, bf16[1024,1280]{1,0:T(8,128)(2,1)} %get-tuple-element.77.refs_0_.b_own, ...), custom_call_target="tpu_custom_call" | custom-call | flops 20132659200 | bytes 20971520 | tf_op jit(solution)/shard_map/ffn_weights/pallas_call | solution.py:809
  579.2 17.9 %collective-permute-done.34 = f32[5120]{0:T(1024)S(1)} collective-permute-done((f32[5120]{0:T(1024)S(1)}, f32[5120]{0:T(1024)S(1)}, u32[]{:S(2)}, u32[]{:S(2)}) %collective-permute-start.34) | collective-permute-done | bytes 20512 | tf_op jit(solution)/shard_map/ppermute | solution.py:345
  607.0 22.5 %collective-permute-done.49 = f32[10240]{0:T(1024)S(1)} collective-permute-done((f32[10240]{0:T(1024)S(1)}, f32[10240]{0:T(1024)S(1)}, u32[]{:S(2)}, u32[]{:S(2)}) %collective-permute-start.49) | collective-permute-done | bytes 40992 | tf_op jit(solution)/shard_map/ppermute | solution.py:345
  629.4 4.2 collective-permute-start.30
  638.6 24.2 %collective-permute-done.30 = bf16[512,1280]{1,0:T(8,128)(2,1)S(1)} collective-permute-done((bf16[512,1280]{1,0:T(8,128)(2,1)S(1)}, bf16[512,1280]{1,0:T(8,128)(2,1)S(1)}, u32[]{:S(2)}, u32[]{:S(2)}) %collective-permute-start.30) | collective-permute-done | bytes 1310752 | tf_op jit(solution)/shard_map/ppermute | solution.py:345
  672.5 13.0 %collective-permute-done.40 = bf16[80,5120]{1,0:T(8,128)(2,1)S(1)} collective-permute-done((bf16[80,5120]{1,0:T(8,128)(2,1)S(1)}, bf16[80,5120]{1,0:T(8,128)(2,1)S(1)}, u32[]{:S(2)}, u32[]{:S(2)}) %collective-permute-start.40) | collective-permute-done | bytes 819232 | tf_op jit(solution)/shard_map/ppermute | solution.py:345
  692.7 20.0 %collective-permute-done.54 = bf16[640,1280]{1,0:T(8,128)(2,1)S(1)} collective-permute-done((bf16[640,1280]{1,0:T(8,128)(2,1)S(1)}, bf16[640,1280]{1,0:T(8,128)(2,1)S(1)}, u32[]{:S(2)}, u32[]{:S(2)}) %collective-permute-start.54) | collective-permute-done | bytes 1638432 | tf_op jit(solution)/shard_map/ppermute | solution.py:345
  717.5 4.0 collective-permute-done.41
  725.5 26.8 %collective-permute-done.57 = bf16[640,1280]{1,0:T(8,128)(2,1)S(1)} collective-permute-done((bf16[640,1280]{1,0:T(8,128)(2,1)S(1)}, bf16[640,1280]{1,0:T(8,128)(2,1)S(1)}, u32[]{:S(2)}, u32[]{:S(2)}) %collective-permute-start.57) | collective-permute-done | bytes 1638432 | tf_op jit(solution)/shard_map/ppermute | solution.py:345
  754.7 14.9 %collective-permute-done.44 = bf16[80,5120]{1,0:T(8,128)(2,1)S(1)} collective-permute-done((bf16[80,5120]{1,0:T(8,128)(2,1)S(1)}, bf16[80,5120]{1,0:T(8,128)(2,1)S(1)}, u32[]{:S(2)}, u32[]{:S(2)}) %collective-permute-start.44) | collective-permute-done | bytes 819232 | tf_op jit(solution)/shard_map/ppermute | solution.py:345
  (292 shorter events, 140.8 us)
Async XLA Ops:
  4.6 24.5 %collective-permute-start.1 = (bf16[720,1280]{1,0:T(8,128)(2,1)}, bf16[720,1280]{1,0:T(8,128)(2,1)}, u32[]{:S(2)}, u32[]{:S(2)}) collective-permute-start(bf16[720,1280]{1,0:T(8,128)(2,1)} %get-tuple-element.153.refs_5_), channel_id=1, source_target_pairs={{0,8},{1,5},{2,6},{3,11},{4,0},{5,13},{6,14},{7,3},{8,16},{9,1},{1... | collective-permute-start | bytes 5529608 | tf_op jit(solution)/shard_map/ppermute | solution.py:345
  29.2 57.6 %collective-permute-start.2 = (bf16[720,1280]{1,0:T(8,128)(2,1)}, bf16[720,1280]{1,0:T(8,128)(2,1)}, u32[]{:S(2)}, u32[]{:S(2)}) collective-permute-start(bf16[720,1280]{1,0:T(8,128)(2,1)} %collective-permute-done.1.refs_6_), channel_id=1, source_target_pairs={{0,8},{1,5},{2,6},{3,11},{4,0},{5,13},{6,14},{7,3},{8,16},{9,1},{1... | collective-permute-start | bytes 5529608 | tf_op jit(solution)/shard_map/ppermute | solution.py:345
  31.3 34.7 %collective-permute-start.9 = (bf16[80,3840]{1,0:T(8,128)(2,1)S(1)}, bf16[80,3840]{1,0:T(8,128)(2,1)}, u32[]{:S(2)}, u32[]{:S(2)}) collective-permute-start(bf16[80,3840]{1,0:T(8,128)(2,1)S(1)} %copy-done.42), channel_id=1, source_target_pairs={{0,8},{1,5},{2,6},{3,11},{4,0},{5,13},{6,14},{7,3},{8,16},{9,1},{1... | collective-permute-start | bytes 1843208 | tf_op jit(solution)/shard_map/ppermute | solution.py:345
  32.9 34.4 %collective-permute-start.13 = (bf16[80,3840]{1,0:T(8,128)(2,1)S(1)}, bf16[80,3840]{1,0:T(8,128)(2,1)}, u32[]{:S(2)}, u32[]{:S(2)}) collective-permute-start(bf16[80,3840]{1,0:T(8,128)(2,1)S(1)} %copy-done.42), channel_id=1, source_target_pairs={{0,4},{1,9},{2,10},{3,7},{4,12},{5,1},{6,2},{7,15},{8,0},{9,17},{1... | collective-permute-start | bytes 1843208 | tf_op jit(solution)/shard_map/ppermute | solution.py:345
  33.3 33.9 %collective-permute-start.16 = (bf16[80,3840]{1,0:T(8,128)(2,1)S(1)}, bf16[80,3840]{1,0:T(8,128)(2,1)}, u32[]{:S(2)}, u32[]{:S(2)}) collective-permute-start(bf16[80,3840]{1,0:T(8,128)(2,1)S(1)} %copy-done.42), channel_id=1, source_target_pairs={{0,2},{1,3},{2,0},{3,1},{4,6},{5,7},{6,4},{7,5},{8,10},{9,11},{10,... | collective-permute-start | bytes 1843208 | tf_op jit(solution)/shard_map/ppermute | solution.py:345
  36.3 60.9 %collective-permute-start = (bf16[512,1280]{1,0:T(8,128)(2,1)}, bf16[512,1280]{1,0:T(8,128)(2,1)S(1)}, u32[]{:S(2)}, u32[]{:S(2)}) collective-permute-start(bf16[512,1280]{1,0:T(8,128)(2,1)} %get-tuple-element.152), channel_id=1, source_target_pairs={{0,1},{1,0},{2,3},{3,2},{4,5},{5,4},{6,7},{7,6},{8,9},{9,8},{10,11... | collective-permute-start | bytes 3932168 | tf_op jit(solution)/shard_map/ppermute | solution.py:345
  82.2 32.2 %collective-permute-start.25 = (bf16[512,1280]{1,0:T(8,128)(2,1)}, bf16[512,1280]{1,0:T(8,128)(2,1)}, u32[]{:S(2)}, u32[]{:S(2)}) collective-permute-start(bf16[512,1280]{1,0:T(8,128)(2,1)} %get-tuple-element.150), channel_id=1, source_target_pairs={{0,1},{1,0},{2,3},{3,2},{4,5},{5,4},{6,7},{7,6},{8,9},{9,8},{10,11... | collective-permute-start | bytes 3932168 | tf_op jit(solution)/shard_map/ppermute | solution.py:345
  86.7 41.7 %collective-permute-start.3 = (bf16[720,1280]{1,0:T(8,128)(2,1)}, bf16[720,1280]{1,0:T(8,128)(2,1)}, u32[]{:S(2)}, u32[]{:S(2)}) collective-permute-start(bf16[720,1280]{1,0:T(8,128)(2,1)} %collective-permute-done.2.refs_7_), channel_id=1, source_target_pairs={{0,8},{1,5},{2,6},{3,11},{4,0},{5,13},{6,14},{7,3},{8,16},{9,1},{1... | collective-permute-start | bytes 5529608 | tf_op jit(solution)/shard_map/ppermute | solution.py:345
  95.3 26.3 %collective-permute-start.12 = (bf16[80,3840]{1,0:T(8,128)(2,1)}, bf16[80,3840]{1,0:T(8,128)(2,1)}, u32[]{:S(2)}, u32[]{:S(2)}) collective-permute-start(bf16[80,3840]{1,0:T(8,128)(2,1)} %collective-permute-done.11.refs_3_.refs_9_), channel_id=1, source_target_pairs={{0,8},{1,5},{2,6},{3,11},{4,0},{5,13},{6,14},{7,3},{8,16},{9,1},{1... | collective-permute-start | bytes 1843208 | tf_op jit(solution)/shard_map/ppermute | solution.py:345
  125.5 44.1 %collective-permute-start.5 = (bf16[720,1280]{1,0:T(8,128)(2,1)}, bf16[720,1280]{1,0:T(8,128)(2,1)}, u32[]{:S(2)}, u32[]{:S(2)}) collective-permute-start(bf16[720,1280]{1,0:T(8,128)(2,1)} %get-tuple-element.153.refs_5_), channel_id=1, source_target_pairs={{0,4},{1,9},{2,10},{3,7},{4,12},{5,1},{6,2},{7,15},{8,0},{9,17},{1... | collective-permute-start | bytes 5529608 | tf_op jit(solution)/shard_map/ppermute | solution.py:345
  127.7 158.4 %collective-permute-start.26 = (bf16[1024,1280]{1,0:T(8,128)(2,1)S(1)}, bf16[1024,1280]{1,0:T(8,128)(2,1)}, u32[]{:S(2)}, u32[]{:S(2)}) collective-permute-start(bf16[1024,1280]{1,0:T(8,128)(2,1)S(1)} %pad_maximum_fusion.1.refs_2_.g_ref.g_own), channel_id=1, source_target_pairs={{0,2},{1,3},{2,0},{3,1},{4,6},{5,7},{6,4},{7,5},{8,10},{9,11},{10,... | collective-permute-start | bytes 7864328 | tf_op jit(solution)/shard_map/ppermute | solution.py:345
  128.4 39.6 %collective-permute-start.4 = (bf16[720,1280]{1,0:T(8,128)(2,1)}, bf16[720,1280]{1,0:T(8,128)(2,1)}, u32[]{:S(2)}, u32[]{:S(2)}) collective-permute-start(bf16[720,1280]{1,0:T(8,128)(2,1)} %collective-permute-done.3.refs_5_), channel_id=1, source_target_pairs={{0,8},{1,5},{2,6},{3,11},{4,0},{5,13},{6,14},{7,3},{8,16},{9,1},{1... | collective-permute-start | bytes 5529608 | tf_op jit(solution)/shard_map/ppermute | solution.py:345
  149.0 43.4 %collective-permute-start.6 = (bf16[720,1280]{1,0:T(8,128)(2,1)}, bf16[720,1280]{1,0:T(8,128)(2,1)S(1)}, u32[]{:S(2)}, u32[]{:S(2)}) collective-permute-start(bf16[720,1280]{1,0:T(8,128)(2,1)} %collective-permute-done.2.refs_7_), channel_id=1, source_target_pairs={{0,1},{1,0},{2,3},{3,2},{4,5},{5,4},{6,7},{7,6},{8,9},{9,8},{10,11... | collective-permute-start | bytes 5529608 | tf_op jit(solution)/shard_map/ppermute | solution.py:345
  152.2 78.4 %collective-permute-start.7 = (bf16[720,1280]{1,0:T(8,128)(2,1)}, bf16[720,1280]{1,0:T(8,128)(2,1)S(1)}, u32[]{:S(2)}, u32[]{:S(2)}) collective-permute-start(bf16[720,1280]{1,0:T(8,128)(2,1)} %collective-permute-done.3.refs_5_), channel_id=1, source_target_pairs={{0,1},{1,0},{2,3},{3,2},{4,5},{5,4},{6,7},{7,6},{8,9},{9,8},{10,11... | collective-permute-start | bytes 5529608 | tf_op jit(solution)/shard_map/ppermute | solution.py:345
  232.5 39.5 %collective-permute-start.8 = (bf16[640,1280]{1,0:T(8,128)(2,1)}, bf16[640,1280]{1,0:T(8,128)(2,1)}, u32[]{:S(2)}, u32[]{:S(2)}) collective-permute-start(bf16[640,1280]{1,0:T(8,128)(2,1)} %slice_dynamic-update-slice_fusion.own_ref), channel_id=1, source_target_pairs={{0,2},{1,3},{2,0},{3,1},{4,6},{5,7},{6,4},{7,5},{8,10},{9,11},{10,... | collective-permute-start | bytes 4915208 | tf_op jit(solution)/shard_map/ppermute | solution.py:345
  487.4 112.4 %collective-permute-start.36 = (bf16[8,80,5120]{2,1,0:T(8,128)(2,1)}, bf16[8,80,5120]{2,1,0:T(8,128)(2,1)}, u32[]{:S(2)}, u32[]{:S(2)}) collective-permute-start(bf16[8,80,5120]{2,1,0:T(8,128)(2,1)} %get-tuple-element.106), channel_id=1, source_target_pairs={{0,2},{1,3},{2,0},{3,1},{4,6},{5,7},{6,4},{7,5},{8,10},{9,11},{10,... | collective-permute-start | bytes 19660808 | tf_op jit(solution)/shard_map/ppermute | solution.py:345
  508.6 64.2 %collective-permute-start.50 = (bf16[640,1280]{1,0:T(8,128)(2,1)}, bf16[640,1280]{1,0:T(8,128)(2,1)}, u32[]{:S(2)}, u32[]{:S(2)}) collective-permute-start(bf16[640,1280]{1,0:T(8,128)(2,1)} %get-tuple-element.119), channel_id=1, source_target_pairs={{0,4},{1,9},{2,10},{3,7},{4,12},{5,1},{6,2},{7,15},{8,0},{9,17},{1... | collective-permute-start | bytes 4915208 | tf_op jit(solution)/shard_map/ppermute | solution.py:345
  510.2 62.7 %collective-permute-start.51 = (bf16[640,1280]{1,0:T(8,128)(2,1)}, bf16[640,1280]{1,0:T(8,128)(2,1)}, u32[]{:S(2)}, u32[]{:S(2)}) collective-permute-start(bf16[640,1280]{1,0:T(8,128)(2,1)} %get-tuple-element.121), channel_id=1, source_target_pairs={{0,1},{1,0},{2,3},{3,2},{4,5},{5,4},{6,7},{7,6},{8,9},{9,8},{10,11... | collective-permute-start | bytes 4915208 | tf_op jit(solution)/shard_map/ppermute | solution.py:345
  511.4 67.4 %collective-permute-start.55 = (bf16[640,1280]{1,0:T(8,128)(2,1)}, bf16[640,1280]{1,0:T(8,128)(2,1)S(1)}, u32[]{:S(2)}, u32[]{:S(2)}) collective-permute-start(bf16[640,1280]{1,0:T(8,128)(2,1)} %get-tuple-element.126), channel_id=1, source_target_pairs={{0,8},{1,5},{2,6},{3,11},{4,0},{5,13},{6,14},{7,3},{8,16},{9,1},{1... | collective-permute-start | bytes 4915208 | tf_op jit(solution)/shard_map/ppermute | solution.py:345
  575.6 62.5 %collective-permute-start.52 = (bf16[640,1280]{1,0:T(8,128)(2,1)S(1)}, bf16[640,1280]{1,0:T(8,128)(2,1)S(1)}, u32[]{:S(2)}, u32[]{:S(2)}) collective-permute-start(bf16[640,1280]{1,0:T(8,128)(2,1)S(1)} %add_convert_fusion.4), channel_id=1, source_target_pairs={{0,4},{1,9},{2,10},{3,7},{4,12},{5,1},{6,2},{7,15},{8,0},{9,17},{1... | collective-permute-start | bytes 4915208 | tf_op jit(solution)/shard_map/ppermute | solution.py:345
  601.8 33.1 %collective-permute-start.37 = (bf16[80,5120]{1,0:T(8,128)(2,1)S(1)}, bf16[80,5120]{1,0:T(8,128)(2,1)S(1)}, u32[]{:S(2)}, u32[]{:S(2)}) collective-permute-start(bf16[80,5120]{1,0:T(8,128)(2,1)S(1)} %get-tuple-element.143), channel_id=1, source_target_pairs={{0,4},{1,9},{2,10},{3,7},{4,12},{5,1},{6,2},{7,15},{8,0},{9,17},{1... | collective-permute-start | bytes 2457608 | tf_op jit(solution)/shard_map/ppermute | solution.py:345
  603.1 31.8 %collective-permute-start.38 = (bf16[80,5120]{1,0:T(8,128)(2,1)S(1)}, bf16[80,5120]{1,0:T(8,128)(2,1)S(1)}, u32[]{:S(2)}, u32[]{:S(2)}) collective-permute-start(bf16[80,5120]{1,0:T(8,128)(2,1)S(1)} %get-tuple-element.144), channel_id=1, source_target_pairs={{0,1},{1,0},{2,3},{3,2},{4,5},{5,4},{6,7},{7,6},{8,9},{9,8},{10,11... | collective-permute-start | bytes 2457608 | tf_op jit(solution)/shard_map/ppermute | solution.py:345
  603.5 89.2 %collective-permute-start.56 = (bf16[640,1280]{1,0:T(8,128)(2,1)S(1)}, bf16[640,1280]{1,0:T(8,128)(2,1)S(1)}, u32[]{:S(2)}, u32[]{:S(2)}) collective-permute-start(bf16[640,1280]{1,0:T(8,128)(2,1)S(1)} %add_convert_fusion.1), channel_id=1, source_target_pairs={{0,8},{1,5},{2,6},{3,11},{4,0},{5,13},{6,14},{7,3},{8,16},{9,1},{1... | collective-permute-start | bytes 4915208 | tf_op jit(solution)/shard_map/ppermute | solution.py:345
  629.4 33.3 %collective-permute-start.30 = (bf16[512,1280]{1,0:T(8,128)(2,1)S(1)}, bf16[512,1280]{1,0:T(8,128)(2,1)S(1)}, u32[]{:S(2)}, u32[]{:S(2)}) collective-permute-start(bf16[512,1280]{1,0:T(8,128)(2,1)S(1)} %copy-done.41), channel_id=1, source_target_pairs={{0,1},{1,0},{2,3},{3,2},{4,5},{5,4},{6,7},{7,6},{8,9},{9,8},{10,11... | collective-permute-start | bytes 3932168 | tf_op jit(solution)/shard_map/ppermute | solution.py:345
  634.9 80.9 %collective-permute-start.29 = (bf16[512,1280]{1,0:T(8,128)(2,1)S(1)}, bf16[512,1280]{1,0:T(8,128)(2,1)S(1)}, u32[]{:S(2)}, u32[]{:S(2)}) collective-permute-start(bf16[512,1280]{1,0:T(8,128)(2,1)S(1)} %get-tuple-element.148), channel_id=1, source_target_pairs={{0,1},{1,0},{2,3},{3,2},{4,5},{5,4},{6,7},{7,6},{8,9},{9,8},{10,11... | collective-permute-start | bytes 3932168 | tf_op jit(solution)/shard_map/ppermute | solution.py:345
  636.6 26.4 %collective-permute-start.39 = (bf16[80,5120]{1,0:T(8,128)(2,1)S(1)}, bf16[80,5120]{1,0:T(8,128)(2,1)S(1)}, u32[]{:S(2)}, u32[]{:S(2)}) collective-permute-start(bf16[80,5120]{1,0:T(8,128)(2,1)S(1)} %fusion.7), channel_id=1, source_target_pairs={{0,4},{1,9},{2,10},{3,7},{4,12},{5,1},{6,2},{7,15},{8,0},{9,17},{1... | collective-permute-start | bytes 2457608 | tf_op jit(solution)/shard_map/ppermute | solution.py:345
  638.5 28.8 %collective-permute-start.53 = (bf16[640,1280]{1,0:T(8,128)(2,1)S(1)}, bf16[640,1280]{1,0:T(8,128)(2,1)S(1)}, u32[]{:S(2)}, u32[]{:S(2)}) collective-permute-start(bf16[640,1280]{1,0:T(8,128)(2,1)S(1)} %add_convert_fusion.3), channel_id=1, source_target_pairs={{0,4},{1,9},{2,10},{3,7},{4,12},{5,1},{6,2},{7,15},{8,0},{9,17},{1... | collective-permute-start | bytes 4915208 | tf_op jit(solution)/shard_map/ppermute | solution.py:345
  667.7 45.0 %collective-permute-start.54 = (bf16[640,1280]{1,0:T(8,128)(2,1)S(1)}, bf16[640,1280]{1,0:T(8,128)(2,1)S(1)}, u32[]{:S(2)}, u32[]{:S(2)}) collective-permute-start(bf16[640,1280]{1,0:T(8,128)(2,1)S(1)} %add_convert_fusion.2), channel_id=1, source_target_pairs={{0,4},{1,9},{2,10},{3,7},{4,12},{5,1},{6,2},{7,15},{8,0},{9,17},{1... | collective-permute-start | bytes 4915208 | tf_op jit(solution)/shard_map/ppermute | solution.py:345
  690.7 30.8 %collective-permute-start.41 = (bf16[80,5120]{1,0:T(8,128)(2,1)S(1)}, bf16[80,5120]{1,0:T(8,128)(2,1)S(1)}, u32[]{:S(2)}, u32[]{:S(2)}) collective-permute-start(bf16[80,5120]{1,0:T(8,128)(2,1)S(1)} %get-tuple-element.139), channel_id=1, source_target_pairs={{0,4},{1,9},{2,10},{3,7},{4,12},{5,1},{6,2},{7,15},{8,0},{9,17},{1... | collective-permute-start | bytes 2457608 | tf_op jit(solution)/shard_map/ppermute | solution.py:345
  690.8 30.7 %collective-permute-start.43 = (bf16[80,5120]{1,0:T(8,128)(2,1)S(1)}, bf16[80,5120]{1,0:T(8,128)(2,1)S(1)}, u32[]{:S(2)}, u32[]{:S(2)}) collective-permute-start(bf16[80,5120]{1,0:T(8,128)(2,1)S(1)} %get-tuple-element.140), channel_id=1, source_target_pairs={{0,8},{1,5},{2,6},{3,11},{4,0},{5,13},{6,14},{7,3},{8,16},{9,1},{1... | collective-permute-start | bytes 2457608 | tf_op jit(solution)/shard_map/ppermute | solution.py:345
  713.3 39.0 %collective-permute-start.57 = (bf16[640,1280]{1,0:T(8,128)(2,1)S(1)}, bf16[640,1280]{1,0:T(8,128)(2,1)S(1)}, u32[]{:S(2)}, u32[]{:S(2)}) collective-permute-start(bf16[640,1280]{1,0:T(8,128)(2,1)S(1)} %add_convert_fusion), channel_id=1, source_target_pairs={{0,1},{1,0},{2,3},{3,2},{4,5},{5,4},{6,7},{7,6},{8,9},{9,8},{10,11... | collective-permute-start | bytes 4915208 | tf_op jit(solution)/shard_map/ppermute | solution.py:345
  723.0 46.5 %collective-permute-start.44 = (bf16[80,5120]{1,0:T(8,128)(2,1)S(1)}, bf16[80,5120]{1,0:T(8,128)(2,1)S(1)}, u32[]{:S(2)}, u32[]{:S(2)}) collective-permute-start(bf16[80,5120]{1,0:T(8,128)(2,1)S(1)} %fusion), channel_id=1, source_target_pairs={{0,1},{1,0},{2,3},{3,2},{4,5},{5,4},{6,7},{7,6},{8,9},{9,8},{10,11... | collective-permute-start | bytes 2457608 | tf_op jit(solution)/shard_map/ppermute | solution.py:345
  (74 other events, 1448.0 us)

commit v2 on v1

--- a/solution.py
+++ b/solution.py
@@ -292,6 +292,7 @@
 AXES = ("cell", "blk")
 VMEM_LIMIT = 60 * 2**20
 ROWS = 256
+COST_PART = 50
 OFFSETS = (0, -1, -2, -3, -4, 1, 2, 3)
 
 
@@ -309,7 +310,9 @@
 
 def cost(flops, nbytes, trans=0):
     return pl.CostEstimate(
-        flops=int(flops), bytes_accessed=int(nbytes), transcendentals=int(trans)
+        flops=int(flops) // COST_PART,
+        bytes_accessed=int(nbytes) // COST_PART,
+        transcendentals=int(trans) // COST_PART,
     )
 
 
@@ -367,51 +370,52 @@
         ]
 
     def gather(self, x, back):
-        ahead = [x]
-        for _ in range(4):
-            ahead.append(self.shift(ahead[-1], 1))
-        behind = []
-        for k in range(1, 4):
+        slots = [x] + [None] * 7
+        for k in range(1, 5):
+            slots[k] = self.shift(slots[k - 1], 1)
             if k <= back:
-                behind.append(self.shift(behind[-1] if behind else x, -1))
-            else:
-                behind.append(self.swap_blk(ahead[k]))
-        return ahead + behind
+                slots[4 + k] = self.shift(slots[3 + k] if k > 1 else slots[0], -1)
+            if k > back + 1:
+                slots[3 + k] = self.swap_blk(slots[k - 1])
+            slots = yield slots
 
     def reduce(self, parts, back):
         def added(terms):
             total = terms[0].astype(f32)
             for t in terms[1:]:
                 total = total + t.astype(f32)
-            return total
-
-        across = {}
-        for k in range(back + 1, 4):
-            across[k] = self.swap_blk(added(parts(4 + k)).astype(bf16))
-        run = added(parts(4)).astype(bf16)
+            return total.astype(bf16)
+
+        ahead, behind = parts[4], [] if back == 0 else parts[4 + back]
+        way = {"ahead": self.shift(added(ahead), -1)}
+        if back:
+            way["behind"] = self.shift(added(behind), 1)
+        for k in range(3, back, -1):
+            way[f"over{k}"] = self.swap_blk(added(parts[4 + k]))
+        way = yield way
         for k in (3, 2, 1):
-            extra = [across[k]] if k in across else []
-            run = added([self.shift(run, -1)] + parts(k) + extra).astype(bf16)
-        last = [self.shift(run, -1)]
-        run = None
-        for k in range(back, 0, -1):
-            moved = [] if run is None else [self.shift(run, 1)]
-            run = added(moved + parts(4 + k)).astype(bf16)
-        if run is not None:
-            last.append(self.shift(run, 1))
-        total = added(last + parts(0)).astype(bf16)
-        return total.astype(f32) + self.swap_blk(total).astype(f32)
+            extra = [way.pop(f"over{k}")] if f"over{k}" in way else []
+            terms = [way["ahead"]] + parts[k] + extra
+            way["ahead"] = self.shift(added(terms), -1)
+            if back - (4 - k) >= 1:
+                way["behind"] = self.shift(added([way["behind"]] + parts[4 + back - (4 - k)]), 1)
+            way = yield way
+        ends = [way["ahead"]] + ([way["behind"]] if back else [])
+        total = added(ends + parts[0])
+        way = yield {"own": total, "other": self.swap_blk(total)}
+        yield way["own"].astype(f32) + way["other"].astype(f32)
 
     def total(self, x):
         bit = 1
         while bit < self.cells * self.blks:
             other = bit
-            x = x + self.permute(
-                x,
-                lambda cell, blk: divmod((cell * self.blks + blk) ^ other, self.blks),
+            moved = self.permute(
+                x, lambda cell, blk: divmod((cell * self.blks + blk) ^ other, self.blks)
             )
+            x, moved = yield x, moved
+            x = x + moved
             bit *= 2
-        return x
+        yield x
 
 
 def norm_parts(x):
@@ -433,12 +437,13 @@
     return jnp.sum(x, axis=0, keepdims=True)
 
 
-def place_rows(slots, target, place_ref, sem, height, first=0):
+def place_rows(slots, target, place_ref, sem, height, cols=None):
+    cols = slice(None) if cols is None else cols
     return [
         pltpu.make_async_copy(
-            slot,
-            target.at[pl.ds(pl.multiple_of(place_ref[first + i] * height, 16), height), :],
-            sem.at[first + i],
+            slot.at[:, cols],
+            target.at[pl.ds(pl.multiple_of(place_ref[i] * height, 16), height), cols],
+            sem.at[i],
         )
         for i, slot in enumerate(slots)
     ]
@@ -448,21 +453,31 @@
     slots, (a_ref, q_ref, k_ref, v_ref, w, sem) = refs[:n], refs[n:]
     height = slots[0].shape[0]
     width = x_ref.shape[1]
-    copies = place_rows(slots, w, place_ref, sem, height)
-
-    @pl.when(pl.program_id(0) == 0)
+    first = pl.program_id(0) == 0
+    copies = [
+        place_rows(slots, w, place_ref, sem.at[j], height, pl.ds(j * width, width))
+        for j in range(3)
+    ]
+
+    @pl.when(first)
     def _():
-        for c in copies:
-            c.start()
-        for c in copies:
-            c.wait()
+        for group in copies:
+            for c in group:
+                c.start()
 
     xh, _ = norm_parts(x_ref[...].astype(f32))
-    a = (xh * gain_ref[...] + bias_ref[...]).astype(bf16)
-    a_ref[...] = a
-    q_ref[...] = (dot(a, w[:, :width], NN) + qb_ref[...]).astype(bf16)
-    k_ref[...] = dot(a, w[:, width : 2 * width], NN).astype(bf16)
-    v_ref[...] = (dot(a, w[:, 2 * width :], NN) + vb_ref[...]).astype(bf16)
+    a_ref[...] = (xh * gain_ref[...] + bias_ref[...]).astype(bf16)
+    for j, (res_ref, add_ref) in enumerate(((q_ref, qb_ref), (k_ref, None), (v_ref, vb_ref))):
+
+        @pl.when(first)
+        def _(group=copies[j]):
+            for c in group:
+                c.wait()
+
+        res = dot(a_ref[...], w[:, j * width : (j + 1) * width], NN)
+        if add_ref is not None:
+            res = res + add_ref[...]
+        res_ref[...] = res.astype(bf16)
 
 
 def qkv_call(place, x, gain, bias, qb, vb, slots):
@@ -479,7 +494,7 @@
             out_specs=[block] * 4,
             scratch_shapes=[
                 pltpu.VMEM((width, 3 * width), bf16),
-                pltpu.SemaphoreType.DMA((n,)),
+                pltpu.SemaphoreType.DMA((3, n)),
             ],
         ),
         out_shape=[shape((rows, width), bf16)] * 4,
@@ -599,60 +614,33 @@
     )(mask, q, k, v, o, go, lse)
 
 
-def out_kernel(parts, place_ref, x_ref, bias_ref, gain_ref, shift_ref, own_ref, sib_ref, *refs):
-    o_refs, (m_ref, b_ref, w, sem) = refs[:parts], refs[parts:]
-    copies = wout_copies(own_ref, sib_ref, w, place_ref, sem)
-
-    @pl.when(pl.program_id(0) == 0)
-    def _():
-        for c in copies:
-            c.start()
-        for c in copies:
-            c.wait()
-
+def out_kernel(x_ref, bias_ref, gain_ref, shift_ref, w_ref, *refs):
+    o_refs, (m_ref, b_ref) = refs[:-2], refs[-2:]
     m = x_ref[...].astype(f32) + bias_ref[...]
     first = 0
     for o_ref in o_refs:
-        m = m + dot(o_ref[...], w[first : first + o_ref.shape[1], :], NN)
+        m = m + dot(o_ref[...], w_ref[first : first + o_ref.shape[1], :], NN)
         first += o_ref.shape[1]
     m_ref[...] = m
     xh, _ = norm_parts(m)
     b_ref[...] = (xh * gain_ref[...] + shift_ref[...]).astype(bf16)
 
 
-def wout_copies(own_ref, sib_ref, w, place_ref, sem):
-    n = len(OFFSETS)
-    height = own_ref.shape[0] // n
-    return place_rows(
-        [ref.at[pl.ds(height * i, height), :] for ref in (own_ref, sib_ref) for i in range(n)],
-        w,
-        place_ref,
-        sem,
-        height,
-    )
-
-
-def out_call(place, x, o_parts, own, sib, bias, gain, shift):
+def out_call(x, o_parts, w, bias, gain, shift):
     rows, width = x.shape
     vec = fixed((1, width))
     block = rowed(ROWS, width)
     return pl.pallas_call(
-        partial(out_kernel, len(o_parts)),
-        grid_spec=pltpu.PrefetchScalarGridSpec(
-            num_scalar_prefetch=1,
-            grid=(rows // ROWS,),
-            in_specs=[block, vec, vec, vec, ANY, ANY] + [rowed(ROWS, o.shape[1]) for o in o_parts],
-            out_specs=[block, block],
-            scratch_shapes=[
-                pltpu.VMEM((width, width), bf16),
-                pltpu.SemaphoreType.DMA((2 * len(OFFSETS),)),
-            ],
-        ),
+        out_kernel,
+        grid=(rows // ROWS,),
+        in_specs=[block, vec, vec, vec, fixed((width, width))]
+        + [rowed(ROWS, o.shape[1]) for o in o_parts],
+        out_specs=[block, block],
         out_shape=[shape((rows, width), f32), shape((rows, width), bf16)],
         compiler_params=params(),
         cost_estimate=cost(4 * rows * width * width, width * (10 * rows + 2 * width)),
         name="out",
-    )(place, x, bias, gain, shift, own, sib, *o_parts)
+    )(x, bias, gain, shift, w, *o_parts)
 
 
 def gelu_both(z, gh):
@@ -716,8 +704,8 @@
 
     @pl.when(near)
     def _():
-        oo_ref[...] = out
-        go_ref[...] = back
+        oo_ref[...] = out.astype(bf16)
+        go_ref[...] = back.astype(bf16)
 
     @pl.when(jnp.logical_not(near))
     def _():
@@ -739,7 +727,7 @@
     out_shape = [shape((2 * rows, units), bf16)] * 2 + [shape((1, units), f32)]
     if later:
         out_specs += [near, near, far, far]
-        out_shape += [shape((rows, width), f32)] * 2 + [shape((rows, width), bf16)] * 2
+        out_shape += [shape((rows, width), bf16)] * 4
     else:
         out_specs += [both, both]
         out_shape += [shape((2 * rows, width), f32)] * 2
@@ -826,54 +814,40 @@
 
 
 def mid_kernel(
-    place_ref, oo_ref, os_ref, go_ref, gs_ref, m_ref, g_ref, keep_ref, db_ref, gain_ref, own_ref, sib_ref,
-    hid_ref, gm_ref, gr_ref, gatt_ref, sums_ref, w, sem,
+    oo_ref, os_ref, go_ref, gs_ref, m_ref, g_ref, keep_ref, db_ref, gain_ref, w_ref,
+    hid_ref, gr_ref, gatt_ref, sums_ref,
 ):
-    copies = wout_copies(own_ref, sib_ref, w, place_ref, sem)
-
     @pl.when(pl.program_id(0) == 0)
     def _():
-        for c in copies:
-            c.start()
-        for c in copies:
-            c.wait()
         sums_ref[...] = jnp.zeros_like(sums_ref)
 
     m = m_ref[...]
     g = g_ref[...].astype(f32)
-    hid_ref[...] = (m + oo_ref[...] + os_ref[...].astype(f32) + db_ref[...]).astype(bf16)
-    gb = go_ref[...] + gs_ref[...].astype(f32)
+    ff = oo_ref[...].astype(f32) + os_ref[...].astype(f32)
+    hid_ref[...] = (m + ff + db_ref[...]).astype(bf16)
+    gb = go_ref[...].astype(f32) + gs_ref[...].astype(f32)
     xh, scale = norm_parts(m)
     gm = g + norm_back(xh, scale, gain_ref[...], gb)
     gr = gm.astype(bf16)
-    gm_ref[...] = gm
     gr_ref[...] = gr
-    gatt_ref[...] = (dot(gr, w[...], NT) * keep_ref[...]).astype(bf16)
+    gatt_ref[...] = (dot(gr, w_ref[...], NT) * keep_ref[...]).astype(bf16)
     sums_ref[0:1, :] += colsum(gb * xh)
     sums_ref[1:2, :] += colsum(gb)
     sums_ref[2:3, :] += colsum(gr.astype(f32))
     sums_ref[3:4, :] += colsum(g)
 
 
-def mid_call(place, oo, os, go, gs, m, g, keep, db, gain, own, sib):
+def mid_call(oo, os, go, gs, m, g, keep, db, gain, w):
     rows, width = m.shape
     block = rowed(ROWS, width)
     vec = fixed((1, width))
     return pl.pallas_call(
         mid_kernel,
-        grid_spec=pltpu.PrefetchScalarGridSpec(
-            num_scalar_prefetch=1,
-            grid=(rows // ROWS,),
-            in_specs=[block] * 6 + [rowed(ROWS, 1), vec, vec, ANY, ANY],
-            out_specs=[block] * 4 + [fixed((8, width))],
-            scratch_shapes=[
-                pltpu.VMEM((width, width), bf16),
-                pltpu.SemaphoreType.DMA((2 * len(OFFSETS),)),
-            ],
-        ),
+        grid=(rows // ROWS,),
+        in_specs=[block] * 6 + [rowed(ROWS, 1), vec, vec, fixed((width, width))],
+        out_specs=[block] * 3 + [fixed((8, width))],
         out_shape=[
             shape((rows, width), bf16),
-            shape((rows, width), f32),
             shape((rows, width), bf16),
             shape((rows, width), bf16),
             shape((8, width), f32),
@@ -881,14 +855,14 @@
         compiler_params=params(),
         cost_estimate=cost(4 * rows * width * width, width * (30 * rows + 2 * width)),
         name="mid",
-    )(place, oo, os, go, gs, m, g, keep, db, gain, own, sib)
+    )(oo, os, go, gs, m, g, keep, db, gain, w)
 
 
 def att_weights_kernel(n, jobs, place_ref, *refs):
     lefts, rights = refs[: jobs[0]], refs[jobs[0] : jobs[0] + jobs[1]]
     refs = refs[jobs[0] + jobs[1] :]
     outs, refs = refs[: n + 1], refs[n + 1 :]
-    lv, rv, ov, lsem, rsem, osem = refs
+    lv, tv, rv, ov, lsem, rsem, osem = refs
     table = jobs[2]
     height = outs[0].shape[0]
     loads = [pltpu.make_async_copy(r, lv.at[i], lsem.at[i]) for i, r in enumerate(lefts)]
@@ -910,6 +884,7 @@
     for step, (left, r) in enumerate(zip(table, rights, strict=True)):
         if left not in have:
             loads[left].wait()
+            tv[left] = jnp.transpose(lv[left])
             have.add(left)
         right_loads[step].wait()
         slot = step % 2
@@ -918,7 +893,7 @@
                 c.wait()
         wide = r.shape[1]
         cols = pl.ds(col, wide)
-        ov[slot, :, pl.ds(0, wide)] = dot(lv[left], rv[:, cols], TN).astype(bf16)
+        ov[slot, :, pl.ds(0, wide)] = dot(tv[left], rv[:, cols], NN).astype(bf16)
         stores.append([])
         for i in range(2 * n):
             rows = pl.ds(pl.multiple_of(place_ref[i] * height, 16), height)
@@ -947,6 +922,7 @@
             out_specs=[ANY] * (n + 1),
             scratch_shapes=[
                 pltpu.VMEM((len(lefts), rows, width), bf16),
+                pltpu.VMEM((len(lefts), width, rows), bf16),
                 pltpu.VMEM((rows, total), bf16),
                 pltpu.VMEM((2, width, wide), bf16),
                 pltpu.SemaphoreType.DMA((len(lefts),)),
@@ -961,14 +937,13 @@
     )(place, *lefts, *rights)
 
 
-def in_kernel(n, pieces, place_ref, x_ref, gm_ref, gain_ref, *refs):
+def in_kernel(n, pieces, place_ref, x_ref, gr_ref, gain_ref, *refs):
     grads, slots = refs[:pieces], refs[pieces : pieces + n]
-    own_ref, send_ref, sums_ref, w, sem = refs[pieces + n :]
+    res_ref, sums_ref, w, sem = refs[pieces + n :]
     height = slots[0].shape[0]
     copies = place_rows(slots, w, place_ref, sem, height)
-    i = pl.program_id(0)
-
-    @pl.when(i == 0)
+
+    @pl.when(pl.program_id(0) == 0)
     def _():
         for c in copies:
             c.start()
@@ -983,55 +958,43 @@
         ga = part if ga is None else ga + part
         col += r.shape[1]
     xh, scale = norm_parts(x_ref[...].astype(f32))
-    res = gm_ref[...] + norm_back(xh, scale, gain_ref[...], ga)
+    res = gr_ref[...].astype(f32) + norm_back(xh, scale, gain_ref[...], ga)
     sums_ref[0:1, :] += colsum(ga * xh)
     sums_ref[1:2, :] += colsum(ga)
-    half = pl.num_programs(0) // 2
-
-    @pl.when(i < half)
-    def _():
-        send_ref[...] = res.astype(bf16)
-
-    @pl.when(i >= half)
-    def _():
-        own_ref[...] = res
-
-
-def in_call(place, x, gm, gain, grads, slots):
+    res_ref[...] = res.astype(res_ref.dtype)
+
+
+def in_call(place, x, gr, gain, grads, slots, part, dtype):
     rows, width = x.shape
     n = len(slots)
     half = rows // ROWS // 2
 
-    def turned(w):
-        return pl.BlockSpec((ROWS, w), lambda i, *_: ((i + half) % (2 * half), 0))
+    def piece(w):
+        return pl.BlockSpec((ROWS, w), lambda i, *_: (i + part * half, 0))
 
     return pl.pallas_call(
         partial(in_kernel, n, len(grads)),
         grid_spec=pltpu.PrefetchScalarGridSpec(
             num_scalar_prefetch=1,
-            grid=(2 * half,),
-            in_specs=[turned(width), turned(width), fixed((1, width))]
-            + [turned(g.shape[1]) for g in grads]
+            grid=(half,),
+            in_specs=[piece(width), piece(width), fixed((1, width))]
+            + [piece(g.shape[1]) for g in grads]
             + [ANY] * n,
-            out_specs=[
-                pl.BlockSpec((ROWS, width), lambda i, *_: (jnp.maximum(i - half, 0), 0)),
-                pl.BlockSpec((ROWS, width), lambda i, *_: (jnp.minimum(i, half - 1), 0)),
-                fixed((8, width)),
-            ],
+            out_specs=[rowed(ROWS, width), fixed((8, width))],
             scratch_shapes=[
                 pltpu.VMEM((width, 3 * width), bf16),
                 pltpu.SemaphoreType.DMA((n,)),
             ],
         ),
-        out_shape=[
-            shape((rows // 2, width), f32),
-            shape((rows // 2, width), bf16),
-            shape((8, width), f32),
-        ],
+        out_shape=[shape((rows // 2, width), dtype), shape((8, width), f32)],
         compiler_params=params(),
-        cost_estimate=cost(8 * rows * width * width, width * (14 * rows + 6 * width)),
+        cost_estimate=cost(4 * rows * width * width, width * (7 * rows + 6 * width)),
         name="in",
-    )(place, x, gm, gain, *grads, *slots)
+    )(place, x, gr, gain, *grads, *slots)
+
+
+def fence(*trees):
+    return lax.optimization_barrier(trees)
 
 
 def local_swapped(
@@ -1042,7 +1005,6 @@
     blk = lax.axis_index("blk")
     core = lax.axis_index("cell") % 2
     genes, width = hidden_in.shape[1:]
-    height = w_qkv.shape[0]
     units = w_up.shape[0]
     shards = ring.cells
     n = len(OFFSETS)
@@ -1052,16 +1014,6 @@
 
     def pick(x, which):
         return lax.dynamic_index_in_dim(x, which, 0, keepdims=False)
-
-    x_own, x_send = pick(hidden_in, blk), pick(hidden_in, 1 - blk)
-    x = jnp.concatenate([x_own, ring.swap_blk(x_send)], axis=0)
-    qkv_own = ring.gather(w_qkv, 2)
-    qkv_sib = [ring.swap_core(s) for s in qkv_own]
-    rest_own = ring.gather(jnp.concatenate([w_up, w_down, w_out], axis=0), 1)
-    g = jnp.concatenate([pick(cotangent, blk), ring.swap_blk(pick(cotangent, 1 - blk))], axis=0)
-    g_sib = ring.swap_core(g)
-    wo_own = jnp.concatenate([s[2 * units :] for s in rest_own], axis=0)
-    wo_sib = ring.swap_core(wo_own)
 
     chips_own, chips_sib = ring.chips_of_slots(core), ring.chips_of_slots(1 - core)
     shard_own = 2 * chips_own + core
@@ -1072,84 +1024,184 @@
     keep = (index < pick(lengths, blk)).astype(f32)[:, None]
     mask = jnp.where(keep > 0, 0.0, far_below)
 
+    x_got = ring.swap_blk(pick(hidden_in, 1 - blk))
+    steps = ring.gather(w_qkv, 2)
+    qkv_own = next(steps)
+    w_pair = jnp.concatenate([w_up, w_down], axis=0)
+    qkv_own[1], qkv_own[5] = fence(qkv_own[1], qkv_own[5])
+    qkv_own = steps.send(qkv_own)
+    qkv_own[2], qkv_own[6], x_got = fence(qkv_own[2], qkv_own[6], x_got)
+    qkv_own = steps.send(qkv_own)
+    x = jnp.concatenate([pick(hidden_in, blk), x_got], axis=0)
+    qkv_own[3], x = fence(qkv_own[3], x)
+    qkv_own = steps.send(qkv_own)
+    qkv_own[4], w_pair, w_out = fence(qkv_own[4], w_pair, w_out)
+    pair = [w_pair, ring.shift(w_pair, 1)] + [None] * 6
+    w_out = lax.all_gather(w_out, "cell", axis=0, tiled=True)
+    qkv_sib = [ring.swap_core(s) for s in qkv_own]
+    g_send, qkv_sib[7] = fence(cotangent, qkv_sib[7])
+    g_got = ring.swap_blk(pick(g_send, 1 - blk))
+
     a, q, k, v = qkv_call(
         place, x, vec(ln1_gain), vec(ln1_bias), vec(q_bias), vec(v_bias), qkv_own + qkv_sib
     )
     pairs = width // 128
-    cuts = [(0, pairs // 2), (pairs // 2, pairs - pairs // 2)]
-    attended = [attend_call(mask, keep, q, k, v, first, count) for first, count in cuts]
+    cuts = [(0, 4 * pairs // 10), (4 * pairs // 10, 2 * pairs // 10)]
+    cuts.append((sum(cuts[1]), pairs - sum(cuts[1])))
+    q, k, v, pair[1], g_got = fence(q, k, v, pair[1], g_got)
+    pair[2] = ring.shift(pair[1], 1)
+    attended = [attend_call(mask, keep, q, k, v, *cuts[0])]
+    q, k, v, attended, pair[2] = fence(q, k, v, attended, pair[2])
+    g = jnp.concatenate([pick(cotangent, blk), g_got], axis=0)
+    g_sib = ring.swap_core(g)
+    pair[3] = ring.shift(pair[2], 1)
+    pair[6] = ring.swap_blk(pair[2])
+    attended += [attend_call(mask, keep, q, k, v, *cut) for cut in cuts[1:]]
+    attended, pair[0], pair[3] = fence(attended, pair[0], pair[3])
     o_parts = [t[0] for t in attended]
-    m, b = out_call(
-        place, x, o_parts, wo_own, wo_sib, vec(out_bias), vec(ln2_gain), vec(ln2_bias)
-    )
+    pair[4] = ring.shift(pair[3], 1)
+    pair[5] = ring.shift(pair[0], -1)
+    pair[7] = ring.swap_blk(pair[3])
+    m, b = out_call(x, o_parts, w_out, vec(out_bias), vec(ln2_gain), vec(ln2_bias))
+    m, b, pair[6], g_sib = fence(m, b, pair[6], g_sib)
     b_sib = ring.swap_core(b)
+
     ub = up_bias.reshape(shards, units)[shard_own]
-    groups = ((0, 1, 2, 5), (3, 4, 6, 7))
-    acc = None
+    near, far = (0, 1, 2, 3), (4, 5, 6, 7)
+    ub_near, ub_far = [vec(jnp.concatenate([ub[s] for s in group])) for group in (near, far)]
+    h_near, gz_near, sum_near, *acc = ffn_call(
+        b, b_sib, g, g_sib, ub_near, [pair[s] for s in near]
+    )
+    h_far, gz_far, sum_far, oo, gb_own, os_send, gs_send = ffn_call(
+        b, b_sib, g, g_sib, ub_far, [pair[s] for s in far], acc
+    )
+    up_sums = dict(
+        zip(near + far, jnp.split(sum_near[0], 4) + jnp.split(sum_far[0], 4), strict=True)
+    )
+    mine = shard_own[None, :] == jnp.arange(shards, dtype=jnp.int32)[:, None]
+    up_rows = jnp.sum(
+        jnp.where(mine[:, :, None], jnp.stack([up_sums[s] for s in range(n)])[None], 0.0), axis=1
+    )
     parts = [None] * n
-    up_sums = [None] * n
-    for group in groups:
-        res = ffn_call(
-            b, b_sib, g, g_sib, vec(jnp.concatenate([ub[s] for s in group])),
-            [rest_own[s] for s in group], acc,
-        )
-        h, gz, up_sum = res[:3]
-        acc = res[3:]
-        made = ffn_weights_call(gz, h, b, b_sib, g, g_sib, len(group))
-        for j, s in enumerate(group):
-            parts[s] = made[j]
-            up_sums[s] = up_sum[0, j * units : (j + 1) * units]
-    oo, gb_own, os_send, gs_send = acc
-    out_hidden, gm, gr, gatt, mid_sums = mid_call(
-        place, oo, ring.swap_core(os_send), gb_own, ring.swap_core(gs_send), m, g, keep,
-        vec(down_bias), vec(ln2_gain), wo_own, wo_sib,
-    )
-    ffn_rows = ring.reduce(lambda s: [parts[s]], 2)
-
-    backs = [
-        attend_back_call(mask, q, k, v, o_parts[i], gatt, attended[i][1], first, count)
-        for i, (first, count) in enumerate(cuts)
+    made = ffn_weights_call(gz_far, h_far, b, b_sib, g, g_sib, len(far))
+    os_got, gs_got = ring.swap_core(os_send), ring.swap_core(gs_send)
+    made, oo, os_got, gs_got = fence(made, oo, os_got, gs_got)
+    for s, t in zip(far, made, strict=True):
+        parts[s] = [t]
+    steps = ring.reduce(parts, 1)
+    way = next(steps)
+    out_hidden, gr, gatt, mid_sums = mid_call(
+        oo, os_got, gb_own, gs_got, m, g, keep, vec(down_bias), vec(ln2_gain), w_out
+    )
+    gr, gatt, gz_near = fence(gr, gatt, gz_near)
+    hid_got = ring.swap_blk(out_hidden[genes:])
+    made = ffn_weights_call(gz_near, h_near, b, b_sib, g, g_sib, len(near))
+    made, gatt, way["ahead"], way["over3"] = fence(made, gatt, way["ahead"], way["over3"])
+    for s, t in zip(near, made, strict=True):
+        parts[s] = [t]
+    way = steps.send(way)
+
+    def back(part, gatt):
+        return attend_back_call(mask, q, k, v, o_parts[part], gatt, attended[part][1], *cuts[part])
+
+    backs = [back(0, gatt)]
+    backs, gatt = fence(backs, gatt)
+    backs.append(back(1, gatt))
+    backs, gatt, way = fence(backs, gatt, way)
+    way = steps.send(way)
+    first = att_weights_call(
+        place, [a, jnp.concatenate(o_parts, axis=1)],
+        [t[i] for i in range(3) for t in backs] + [gr], [0] * 6 + [1],
+    )
+    first, gatt, way = fence(first, gatt, way)
+    way = steps.send(way)
+    first_sib = ring.swap_core(first[n])
+    backs.append(back(2, gatt))
+    backs, way, first, first_sib, hid_got, up_rows = fence(
+        backs, way, first, first_sib, hid_got, up_rows
+    )
+    way = steps.send(way)
+    steps_first = ring.reduce([[first[s], first_sib[s]] for s in range(n)], 3)
+    way_first = next(steps_first)
+    second = att_weights_call(place, [a], list(backs[2][:3]), [0] * 3)
+    second_sib = ring.swap_core(second[n])
+    grads = [t[i] for i in range(3) for t in backs]
+    second, grads, way_first = fence(second, grads, way_first)
+    way_first = steps_first.send(way_first)
+    steps_second = ring.reduce([[second[s], second_sib[s]] for s in range(n)], 3)
+    way_second = next(steps_second)
+    weights = qkv_own + qkv_sib
+    in_send, in_sums_send = in_call(place, x, gr, vec(ln1_gain), grads, weights, 1, bf16)
+    in_send, grads, way_first, way_second = fence(in_send, grads, way_first, way_second)
+    way_first = steps_first.send(way_first)
+    way_second = steps_second.send(way_second)
+    in_got = ring.swap_blk(in_send)
+    in_own, in_sums = in_call(place, x, gr, vec(ln1_gain), grads, weights, 0, f32)
+    in_own, in_sums, in_sums_send, way_first, way_second = fence(
+        in_own, in_sums, in_sums_send, way_first, way_second
+    )
+    way_first = steps_first.send(way_first)
+    way_second = steps_second.send(way_second)
+    ln1_sums = (in_sums + in_sums_send)[:2].reshape(-1)
+    steps_sums = ring.total(
+        jnp.concatenate(
+            [mid_sums[:4].reshape(-1), ln1_sums, up_rows.reshape(-1)]
+            + [t[i].reshape(-1) for i in (3, 4) for t in backs]
+        )
+    )
+    sums = next(steps_sums)
+    sums = steps_sums.send(sums)
+    way_first, way_second, sums, in_got = fence(way_first, way_second, sums, in_got)
+    way_first = steps_first.send(way_first)
+    way_second = steps_second.send(way_second)
+    sums = steps_sums.send(sums)
+    sums = steps_sums.send(sums)
+    way_first, way_second, sums = fence(way_first, way_second, sums)
+    ffn_rows = steps.send(way)
+    first_rows = steps_first.send(way_first)
+    way_second = steps_second.send(way_second)
+    sums = steps_sums.send(sums)
+    sums = steps_sums.send(sums)
+    second_rows = steps_second.send(way_second)
+
+    def home(own, got):
+        got = got.astype(own.dtype)
+        return jnp.where(blk == 0, jnp.stack([own, got]), jnp.stack([got, own]))
+
+    hidden = home(out_hidden[:genes], hid_got)
+    in_grad = home(in_own, in_got)
+    ln2_gain_g, ln2_bias_g, out_bias_g, down_bias_g, ln1_gain_g, ln1_bias_g = [
+        sums[i * width : (i + 1) * width] for i in range(6)
     ]
-    grads = [t[i] for i in range(3) for t in backs]
-    made = att_weights_call(
-        place, [a, jnp.concatenate(o_parts, axis=1)],
-        grads + [gr], [0] * len(grads) + [1],
-    )
-    att_sib = ring.swap_core(made[n])
-    att_rows = ring.reduce(lambda s: [made[s], att_sib[s]], 2)
-    in_own, in_send, in_sums = in_call(place, x, gm, vec(ln1_gain), grads, qkv_own + qkv_sib)
-
-    def home(own, sent):
-        got = ring.swap_blk(sent).astype(own.dtype)
-        return jnp.where(blk == 0, jnp.stack([own, got]), jnp.stack([got, own]))
-
-    hidden = home(out_hidden[:genes], out_hidden[genes:])
-    in_grad = home(in_own, in_send)
-    up_rows = jnp.zeros((shards, units), f32).at[shard_own].set(jnp.stack(up_sums))
-    early = ring.total(jnp.concatenate([mid_sums[:4].reshape(-1), up_rows.reshape(-1)]))
-    late = ring.total(
-        jnp.concatenate(
-            [in_sums[:2].reshape(-1)]
-            + [t[3].reshape(-1) for t in backs]
-            + [t[4].reshape(-1) for t in backs]
-        )
-    )
-    ln2_gain_g, ln2_bias_g, out_bias_g, down_bias_g = jnp.split(early[: 4 * width], 4)
-    ln1_gain_g, ln1_bias_g, q_bias_g, v_bias_g = jnp.split(late, 4)
+    up_bias_g = sums[6 * width : 6 * width + shards * units]
+    q_bias_g, v_bias_g = jnp.split(sums[6 * width + shards * units :], 2)
+    wide = cuts[2][0] * 128
+    rest = width - wide
+    w_qkv_grad = jnp.concatenate(
+        [
+            t
+            for i in range(3)
+            for t in (
+                first_rows[:, i * wide : (i + 1) * wide],
+                second_rows[:, i * rest : (i + 1) * rest],
+            )
+        ],
+        axis=1,
+    )
     return (
         hidden,
         in_grad,
         ln1_gain_g,
         ln1_bias_g,
-        att_rows[:, : 3 * width],
+        w_qkv_grad,
         q_bias_g,
         v_bias_g,
-        att_rows[:, 3 * width :],
+        first_rows[:, 3 * wide :],
         out_bias_g,
         ln2_gain_g,
         ln2_bias_g,
         ffn_rows[:units],
-        early[4 * width :],
+        up_bias_g,
         ffn_rows[units:],
         down_bias_g,
     )

time: 776 us -> 580 us (0.75)
  waiting for transfers between devices: 311 us -> 96.4 us
  other arithmetic: 29.7 us -> 51.2 us
  local copies, waits for them, and re-layouts: 41.2 us -> 25.3 us
  between operations: 1.91 us -> 15.6 us
  starting transfers between devices: 62.8 us -> 52.4 us
    ppermute x58 -> x61, waiting for transfers between devices: 311 us -> 96.4 us  [permute(): return lax.ppermute(x, AXES, pairs)]
    convert_element_type x10 -> x14, other arithmetic: 14.2 us -> 30.8 us  [added(): return total.astype(bf16)]
    ppermute x58 -> x61, starting transfers between devices: 62.8 us -> 52.4 us  [permute(): return lax.ppermute(x, AXES, pairs)]
    unnamed x109 -> x141, local copies, waits for them, and re-layouts: 16.1 us -> 6.41 us
    pallas_call x1 -> x2, Pallas kernels: 24.5 us -> 29.6 us  [in_call(): pl.pallas_call(partial(in_kernel, n, len(grads)), grid_spec=pltpu.Prefetc...]
    pallas_call x2 -> x3, Pallas kernels: 39.5 us -> 41.7 us  [attend_call(): pl.pallas_call(partial(attend_kernel, qrows), grid=(count,), in_specs=[fi...]
    pallas_call x2 -> x3, Pallas kernels: 63.3 us -> 65.2 us  [attend_back_call(): pl.pallas_call(partial(attend_back_kernel, qrows), grid=(count,), in_spec...]
    pallas_call x1 -> x2, Pallas kernels: 29 us -> 30.7 us  [att_weights_call(): pl.pallas_call(partial(att_weights_kernel, n, (len(lefts), len(rights), t...]
  transfers between devices with their start and end apart: 58 -> 62, of which waited for: 23 -> 17; matrix products, arithmetic and copies ran while one was open for 8% -> 11% of each run, Pallas kernels for 18% -> 49%
where the time goes in v2:
time: 580 us; the launch traced here: 572 us
  Pallas kernels  331 us (57%)
  waiting for transfers between devices  96.4 us (17%)
  starting transfers between devices  52.4 us (9%)
  other arithmetic  51.2 us (9%)
  local copies, waits for them, and re-layouts  25.3 us (4%)
  between operations  15.6 us (3%)
    ppermute x61, waiting for transfers between devices, permute(): return lax.ppermute(x, AXES, pairs)  96.4 us
    pallas_call x2, Pallas kernels, ffn_call(): pl.pallas_call(partial(ffn_kernel, n, later), grid=(2 * half,), in_specs=...  78 us
    pallas_call x3, Pallas kernels, attend_back_call(): pl.pallas_call(partial(attend_back_kernel, qrows), grid=(count,), in_spec...  65.2 us
    ppermute x61, starting transfers between devices, permute(): return lax.ppermute(x, AXES, pairs)  52.4 us
    pallas_call x3, Pallas kernels, attend_call(): pl.pallas_call(partial(attend_kernel, qrows), grid=(count,), in_specs=[fi...  41.7 us
    pallas_call x2, Pallas kernels, ffn_weights_call(): pl.pallas_call(partial(ffn_weights_kernel, n), in_specs=[ANY] * 6, out_sp...  41.7 us
    convert_element_type x14, other arithmetic, added(): return total.astype(bf16)  30.8 us
    pallas_call x2, Pallas kernels, att_weights_call(): pl.pallas_call(partial(att_weights_kernel, n, (len(lefts), len(rights), t...  30.7 us
  transfers between devices with their start and end apart: 62, of which 17 were waited for; matrix products, arithmetic and copies ran while one was open for 11% of the time, Pallas kernels for 49%

profile of v2, /device:TPU:0, one launch (start us, length us, event | category | flops | bytes accessed | tf_op | source)
XLA Modules:
  0.0 572.0 jit_solution(7963982877971000724)
XLA Ops:
  9.3 3.0 collective-permute-start.4
  14.4 14.6 %collective-permute-done.refs_1_.refs_10_ = bf16[80,3840]{1,0:T(8,128)(2,1)} collective-permute-done((bf16[80,3840]{1,0:T(8,128)(2,1)S(1)}, bf16[80,3840]{1,0:T(8,128)(2,1)}, u32[]{:S(2)}, u32[]{:S(2)}) %collective-permute-start) | collective-permute-done | bytes 614432 | tf_op jit(solution)/shard_map/ppermute | solution.py:348
  31.0 14.7 %collective-permute-done.2.refs_2_.refs_11_ = bf16[80,3840]{1,0:T(8,128)(2,1)} collective-permute-done((bf16[80,3840]{1,0:T(8,128)(2,1)}, bf16[80,3840]{1,0:T(8,128)(2,1)}, u32[]{:S(2)}, u32[]{:S(2)}) %collective-permute-start.2) | collective-permute-done | bytes 614432 | tf_op jit(solution)/shard_map/ppermute | solution.py:348
  48.1 8.0 %collective-permute-done.5.refs_3_.refs_12_ = bf16[80,3840]{1,0:T(8,128)(2,1)S(1)} collective-permute-done((bf16[80,3840]{1,0:T(8,128)(2,1)}, bf16[80,3840]{1,0:T(8,128)(2,1)S(1)}, u32[]{:S(2)}, u32[]{:S(2)}) %collective-permute-start.5) | collective-permute-done | bytes 614432 | tf_op jit(solution)/shard_map/ppermute | solution.py:348
  58.1 8.3 %collective-permute-done.6.refs_4_.refs_13_ = bf16[80,3840]{1,0:T(8,128)(2,1)} collective-permute-done((bf16[80,3840]{1,0:T(8,128)(2,1)S(1)}, bf16[80,3840]{1,0:T(8,128)(2,1)}, u32[]{:S(2)}, u32[]{:S(2)}) %collective-permute-start.6) | collective-permute-done | bytes 614432 | tf_op jit(solution)/shard_map/ppermute | solution.py:348
  66.6 14.2 %collective-permute-done.7.refs_7_.refs_16_ = bf16[80,3840]{1,0:T(8,128)(2,1)S(1)} collective-permute-done((bf16[80,3840]{1,0:T(8,128)(2,1)}, bf16[80,3840]{1,0:T(8,128)(2,1)S(1)}, u32[]{:S(2)}, u32[]{:S(2)}) %collective-permute-start.7) | collective-permute-done | bytes 614432 | tf_op jit(solution)/shard_map/ppermute | solution.py:348
  93.8 20.4 %qkv.1 = (bf16[1024,1280]{1,0:T(8,128)(2,1)}, bf16[1024,1280]{1,0:T(8,128)(2,1)}, bf16[1024,1280]{1,0:T(8,128)(2,1)}, bf16[1024,1280]{1,0:T(8,128)(2,1)}) custom-call(s32[16]{0:T(128)} %pad_add_fusion.place_ref, bf16[1024,1280]{1,0:T(8,128)(2,1)} %pad_maximum_fusion.x_ref, f32[1,1280]{1,0:T(1,128)} %reshape.233.gain_ref, f32[1,1280]{1,0:T(1,128)} %reshape.234.bias_ref, ...), custom_call_target="tpu_custom_call" | custom-call | flops 201326592 | bytes 458752 | tf_op jit(solution)/shard_map/qkv/pallas_call | solution.py:488
  122.5 16.2 %attend.3 = (bf16[1024,512]{1,0:T(8,128)(2,1)}, f32[8,1,1024]{2,1,0:T(1,128)}) custom-call(f32[1024,1]{1,0:T(8,128)} %compare_select_fusion.mask_ref, f32[1024,1]{1,0:T(8,128)} %convert_element_type.320.keep_ref, bf16[1024,1280]{1,0:T(8,128)(2,1)} %get-tuple-element.276.q_ref, bf16[1024,1280]{1,0:T(8,128)(2,1)} %get-tuple-element.277.k_ref, ...), custom_call_target="tpu_custom_call" | custom-call | flops 214748368 | bytes 83886 | tf_op jit(solution)/shard_map/attend/pallas_call | solution.py:538
  143.8 9.2 %attend.4 = (bf16[1024,256]{1,0:T(8,128)(2,1)}, f32[4,1,1024]{2,1,0:T(1,128)}) custom-call(f32[1024,1]{1,0:T(8,128)} %compare_select_fusion.mask_ref, f32[1024,1]{1,0:T(8,128)} %convert_element_type.320.keep_ref, bf16[1024,1280]{1,0:T(8,128)(2,1)} %get-tuple-element.276.q_ref, bf16[1024,1280]{1,0:T(8,128)(2,1)} %get-tuple-element.277.k_ref, ...), custom_call_target="tpu_custom_call" | custom-call | flops 107374184 | bytes 41943 | tf_op jit(solution)/shard_map/attend/pallas_call | solution.py:538
  153.1 16.3 %attend.5 = (bf16[1024,512]{1,0:T(8,128)(2,1)}, f32[8,1,1024]{2,1,0:T(1,128)}) custom-call(f32[1024,1]{1,0:T(8,128)} %compare_select_fusion.mask_ref, f32[1024,1]{1,0:T(8,128)} %convert_element_type.320.keep_ref, bf16[1024,1280]{1,0:T(8,128)(2,1)} %get-tuple-element.276.q_ref, bf16[1024,1280]{1,0:T(8,128)(2,1)} %get-tuple-element.277.k_ref, ...), custom_call_target="tpu_custom_call" | custom-call | flops 214748368 | bytes 83886 | tf_op jit(solution)/shard_map/attend/pallas_call | solution.py:538
  169.4 9.3 %out.1 = (f32[1024,1280]{1,0:T(8,128)}, bf16[1024,1280]{1,0:T(8,128)(2,1)}) custom-call(bf16[1024,1280]{1,0:T(8,128)(2,1)} %pad_maximum_fusion.x_ref, f32[1,1280]{1,0:T(1,128)} %reshape.230.bias_ref, f32[1,1280]{1,0:T(1,128)} %reshape.231.gain_ref, f32[1,1280]{1,0:T(1,128)} %reshape.232.shift_ref, bf16[1280,1280]{1,0:T(8,128)(2,1)} %all-gather.2.cloned.1.call-done.w_ref, ...), custom_call_target="tpu_custom_call" | custom-call | flops 134217728 | bytes 327680 | tf_op jit(solution)/shard_map/out/pallas_call | solution.py:633
  185.7 37.3 %ffn.2 = (bf16[2048,1280]{1,0:T(8,128)(2,1)}, bf16[2048,1280]{1,0:T(8,128)(2,1)}, f32[1,1280]{1,0:T(1,128)}, f32[2048,1280]{1,0:T(8,128)}, f32[2048,1280]{1,0:T(8,128)}) custom-call(bf16[1024,1280]{1,0:T(8,128)(2,1)} %get-tuple-element.290.refs_0_.b_own, bf16[1024,1280]{1,0:T(8,128)(2,1)} %copy-done.4, bf16[1024,1280]{1,0:T(8,128)(2,1)} %copy-done.3, ...), custom_call_target="tpu_custom_call" | custom-call | flops 805306368 | bytes 629145 | tf_op jit(solution)/shard_map/ffn/pallas_call | solution.py:734
  223.1 40.6 %ffn.3 = (bf16[2048,1280]{1,0:T(8,128)(2,1)}, bf16[2048,1280]{1,0:T(8,128)(2,1)}, f32[1,1280]{1,0:T(1,128)}, bf16[1024,1280]{1,0:T(8,128)(2,1)}, bf16[1024,1280]...) custom-call(bf16[1024,1280]{1,0:T(8,128)(2,1)} %get-tuple-element.290.refs_0_.b_own, ...), custom_call_target="tpu_custom_call" | custom-call | flops 805306368 | bytes 1048576 | tf_op jit(solution)/shard_map/ffn/pallas_call | solution.py:734
  264.3 20.9 %ffn_weights.2 = (bf16[640,1280]{1,0:T(8,128)(2,1)}, bf16[640,1280]{1,0:T(8,128)(2,1)}, bf16[640,1280]{1,0:T(8,128)(2,1)}, bf16[640,1280]{1,0:T(8,128)(2,1)}) custom-call(bf16[2048,1280]{1,0:T(8,128)(2,1)} %get-tuple-element.297.gz, bf16[2048,1280]{1,0:T(8,128)(2,1)} %get-tuple-element.298.h, bf16[1024,1280]{1,0:T(8,128)(2,1)} %get-tuple-element.290.refs_0_.b_own, ...), custom_call_target="tpu_custom_call" | custom-call | flops 402653184 | bytes 419430 | tf_op jit(solution)/shard_map/ffn_weights/pallas_call | solution.py:797
  287.2 14.5 %mid.1 = (bf16[1024,1280]{1,0:T(8,128)(2,1)}, bf16[1024,1280]{1,0:T(8,128)(2,1)}, bf16[1024,1280]{1,0:T(8,128)(2,1)}, f32[8,1280]{1,0:T(8,128)}) custom-call(bf16[1024,1280]{1,0:T(8,128)(2,1)} %get-tuple-element.306.oo_ref, bf16[1024,1280]{1,0:T(8,128)(2,1)} %copy-done.17, bf16[1024,1280]{1,0:T(8,128)(2,1)} %get-tuple-element.308.go_ref, ...), custom_call_target="tpu_custom_call" | custom-call | flops 134217728 | bytes 851968 | tf_op jit(solution)/shard_map/mid/pallas_call | solution.py:844
  305.0 20.8 %ffn_weights.3 = (bf16[640,1280]{1,0:T(8,128)(2,1)}, bf16[640,1280]{1,0:T(8,128)(2,1)}, bf16[640,1280]{1,0:T(8,128)(2,1)}, bf16[640,1280]{1,0:T(8,128)(2,1)}) custom-call(bf16[2048,1280]{1,0:T(8,128)(2,1)} %get-tuple-element.315.gz, bf16[2048,1280]{1,0:T(8,128)(2,1)} %get-tuple-element.316.h, bf16[1024,1280]{1,0:T(8,128)(2,1)} %get-tuple-element.290.refs_0_.b_own, ...), custom_call_target="tpu_custom_call" | custom-call | flops 402653184 | bytes 419430 | tf_op jit(solution)/shard_map/ffn_weights/pallas_call | solution.py:797
  325.8 4.2 add_convert_fusion.3
  331.2 25.6 %attend_back.3 = (bf16[1024,512]{1,0:T(8,128)(2,1)}, bf16[1024,512]{1,0:T(8,128)(2,1)}, bf16[1024,512]{1,0:T(8,128)(2,1)}, f32[1,512]{1,0:T(1,128)}, f32[1,512]{1,0:T(1,128)}) custom-call(f32[1024,1]{1,0:T(8,128)} %compare_select_fusion.mask_ref, bf16[1024,1280]{1,0:T(8,128)(2,1)} %get-tuple-element.276.q_ref, bf16[1024,1280]{1,0:T(8,128)(2,1)} %get-tuple-element.277.k_ref, ...), custom_call_target="tpu_custom_call" | custom-call | flops 343597376 | bytes 167772 | tf_op jit(solution)/shard_map/attend_back/pallas_call | solution.py:601
  356.8 14.0 %attend_back.4 = (bf16[1024,256]{1,0:T(8,128)(2,1)}, bf16[1024,256]{1,0:T(8,128)(2,1)}, bf16[1024,256]{1,0:T(8,128)(2,1)}, f32[1,256]{1,0:T(1,128)}, f32[1,256]{1,0:T(1,128)}) custom-call(f32[1024,1]{1,0:T(8,128)} %compare_select_fusion.mask_ref, bf16[1024,1280]{1,0:T(8,128)(2,1)} %get-tuple-element.276.q_ref, bf16[1024,1280]{1,0:T(8,128)(2,1)} %get-tuple-element.277.k_ref, ...), custom_call_target="tpu_custom_call" | custom-call | flops 171798688 | bytes 83886 | tf_op jit(solution)/shard_map/attend_back/pallas_call | solution.py:601
  372.0 4.3 add_convert_fusion.2
  379.3 20.8 %att_weights.2 = (bf16[80,3584]{1,0:T(8,128)(2,1)}, bf16[80,3584]{1,0:T(8,128)(2,1)}, bf16[80,3584]{1,0:T(8,128)(2,1)}, bf16[80,3584]{1,0:T(8,128)(2,1)}, bf16[8...) custom-call(s32[16]{0:T(128)} %pad_add_fusion.place_ref, ...), custom_call_target="tpu_custom_call" | custom-call | flops 281857216 | bytes 330301 | tf_op jit(solution)/shard_map/att_weights/pallas_call | solution.py:916
  400.3 3.6 add_convert_fusion.1
  408.0 25.6 %attend_back.5 = (bf16[1024,512]{1,0:T(8,128)(2,1)}, bf16[1024,512]{1,0:T(8,128)(2,1)}, bf16[1024,512]{1,0:T(8,128)(2,1)}, f32[1,512]{1,0:T(1,128)}, f32[1,512]{1,0:T(1,128)}) custom-call(f32[1024,1]{1,0:T(8,128)} %compare_select_fusion.mask_ref, bf16[1024,1280]{1,0:T(8,128)(2,1)} %get-tuple-element.276.q_ref, bf16[1024,1280]{1,0:T(8,128)(2,1)} %get-tuple-element.277.k_ref, ...), custom_call_target="tpu_custom_call" | custom-call | flops 343597376 | bytes 167772 | tf_op jit(solution)/shard_map/attend_back/pallas_call | solution.py:601
  433.6 4.1 collective-permute-done.36
  437.7 9.9 %att_weights.3 = (bf16[80,1536]{1,0:T(8,128)(2,1)}, bf16[80,1536]{1,0:T(8,128)(2,1)}, bf16[80,1536]{1,0:T(8,128)(2,1)}, bf16[80,1536]{1,0:T(8,128)(2,1)}, bf16[8...) custom-call(s32[16]{0:T(128)} %pad_add_fusion.place_ref, ...), custom_call_target="tpu_custom_call" | custom-call | flops 120795952 | bytes 141557 | tf_op jit(solution)/shard_map/att_weights/pallas_call | solution.py:916
  454.0 11.0 %collective-permute-done.37 = bf16[80,3584]{1,0:T(8,128)(2,1)S(1)} collective-permute-done((bf16[80,3584]{1,0:T(8,128)(2,1)S(1)}, bf16[80,3584]{1,0:T(8,128)(2,1)S(1)}, u32[]{:S(2)}, u32[]{:S(2)}) %collective-permute-start.37) | collective-permute-done | bytes 573472 | tf_op jit(solution)/shard_map/ppermute | solution.py:348
  465.0 2.8 fusion.4
  476.1 14.8 %in.2 = (bf16[512,1280]{1,0:T(8,128)(2,1)}, f32[8,1280]{1,0:T(8,128)}) custom-call(s32[16]{0:T(128)} %pad_add_fusion.place_ref, bf16[1024,1280]{1,0:T(8,128)(2,1)} %pad_maximum_fusion.x_ref, bf16[1024,1280]{1,0:T(8,128)(2,1)} %get-tuple-element.359.refs_8_.gr_ref, f32[1,1280]{1,0:T(1,128)} %reshape.233.gain_ref, ...), custom_call_target="tpu_custom_call" | custom-call | flops 134217728 | bytes 380108 | tf_op jit(solution)/shard_map/in/pallas_call | solution.py:975
  499.9 3.5 convert_add_fusion
  503.9 14.8 %in.3 = (f32[512,1280]{1,0:T(8,128)}, f32[8,1280]{1,0:T(8,128)}) custom-call(s32[16]{0:T(128)} %pad_add_fusion.place_ref, bf16[1024,1280]{1,0:T(8,128)(2,1)} %pad_maximum_fusion.x_ref, bf16[1024,1280]{1,0:T(8,128)(2,1)} %get-tuple-element.359.refs_8_.gr_ref, f32[1,1280]{1,0:T(1,128)} %reshape.233.gain_ref, ...), custom_call_target="tpu_custom_call" | custom-call | flops 134217728 | bytes 380108 | tf_op jit(solution)/shard_map/in/pallas_call | solution.py:975
  527.9 6.0 %collective-permute-done.51 = f32[15360]{0:T(1024)S(1)} collective-permute-done((f32[15360]{0:T(1024)S(1)}, f32[15360]{0:T(1024)S(1)}, u32[]{:S(2)}, u32[]{:S(2)}) %collective-permute-start.51) | collective-permute-done | bytes 61472 | tf_op jit(solution)/shard_map/ppermute | solution.py:348
  547.5 7.8 %collective-permute-done.54 = bf16[80,3584]{1,0:T(8,128)(2,1)S(1)} collective-permute-done((bf16[80,3584]{1,0:T(8,128)(2,1)S(1)}, bf16[80,3584]{1,0:T(8,128)(2,1)S(1)}, u32[]{:S(2)}, u32[]{:S(2)}) %collective-permute-start.54) | collective-permute-done | bytes 573472 | tf_op jit(solution)/shard_map/ppermute | solution.py:348
  (331 shorter events, 115.2 us)
Async XLA Ops:
  7.2 162.2 %all-gather.2.cloned.1.call-start = ((), (), s32[]{:S(2)}) async-start(), calls=%async_computation | async-start | bytes 3481600 | tf_op jit(solution)/shard_map/all_gather | solution.py:1040
  9.3 36.4 %collective-permute-start.4 = (bf16[512,1280]{1,0:T(8,128)(2,1)S(1)}, bf16[512,1280]{1,0:T(8,128)(2,1)S(1)}, u32[]{:S(2)}, u32[]{:S(2)}) collective-permute-start(bf16[512,1280]{1,0:T(8,128)(2,1)S(1)} %get-tuple-element.512), channel_id=1, source_target_pairs={{0,1},{1,0},{2,3},{3,2},{4,5},{5,4},{6,7},{7,6},{8,9},{9,8},{10,11... | collective-permute-start | bytes 3932168 | tf_op jit(solution)/shard_map/ppermute | solution.py:348
  81.7 33.2 %collective-permute-start.16 = (bf16[640,1280]{1,0:T(8,128)(2,1)}, bf16[640,1280]{1,0:T(8,128)(2,1)}, u32[]{:S(2)}, u32[]{:S(2)}) collective-permute-start(bf16[640,1280]{1,0:T(8,128)(2,1)} %pad_maximum_fusion.3.refs_5_), channel_id=1, source_target_pairs={{0,8},{1,5},{2,6},{3,11},{4,0},{5,13},{6,14},{7,3},{8,16},{9,1},{1... | collective-permute-start | bytes 4915208 | tf_op jit(solution)/shard_map/ppermute | solution.py:348
  85.0 31.1 %collective-permute-start.17 = (bf16[512,1280]{1,0:T(8,128)(2,1)}, bf16[512,1280]{1,0:T(8,128)(2,1)}, u32[]{:S(2)}, u32[]{:S(2)}) collective-permute-start(bf16[512,1280]{1,0:T(8,128)(2,1)} %dynamic-slice_bitcast_fusion.1), channel_id=1, source_target_pairs={{0,1},{1,0},{2,3},{3,2},{4,5},{5,4},{6,7},{7,6},{8,9},{9,8},{10,11... | collective-permute-start | bytes 3932168 | tf_op jit(solution)/shard_map/ppermute | solution.py:348
  116.2 22.6 %collective-permute-start.18 = (bf16[640,1280]{1,0:T(8,128)(2,1)}, bf16[640,1280]{1,0:T(8,128)(2,1)}, u32[]{:S(2)}, u32[]{:S(2)}) collective-permute-start(bf16[640,1280]{1,0:T(8,128)(2,1)} %collective-permute-done.16.refs_6_), channel_id=1, source_target_pairs={{0,8},{1,5},{2,6},{3,11},{4,0},{5,13},{6,14},{7,3},{8,16},{9,1},{1... | collective-permute-start | bytes 4915208 | tf_op jit(solution)/shard_map/ppermute | solution.py:348
  119.0 59.7 %collective-permute-start.21 = (bf16[1024,1280]{1,0:T(8,128)(2,1)S(1)}, bf16[1024,1280]{1,0:T(8,128)(2,1)}, u32[]{:S(2)}, u32[]{:S(2)}) collective-permute-start(bf16[1024,1280]{1,0:T(8,128)(2,1)S(1)} %pad_maximum_fusion.1.refs_2_.g_own.g_ref), channel_id=1, source_target_pairs={{0,2},{1,3},{2,0},{3,1},{4,6},{5,7},{6,4},{7,5},{8,10},{9,11},{10,... | collective-permute-start | bytes 7864328 | tf_op jit(solution)/shard_map/ppermute | solution.py:348
  138.8 30.6 %collective-permute-start.19 = (bf16[640,1280]{1,0:T(8,128)(2,1)}, bf16[640,1280]{1,0:T(8,128)(2,1)}, u32[]{:S(2)}, u32[]{:S(2)}) collective-permute-start(bf16[640,1280]{1,0:T(8,128)(2,1)} %collective-permute-done.18.refs_7_), channel_id=1, source_target_pairs={{0,8},{1,5},{2,6},{3,11},{4,0},{5,13},{6,14},{7,3},{8,16},{9,1},{1... | collective-permute-start | bytes 4915208 | tf_op jit(solution)/shard_map/ppermute | solution.py:348
  140.5 38.2 %collective-permute-start.20 = (bf16[640,1280]{1,0:T(8,128)(2,1)}, bf16[640,1280]{1,0:T(8,128)(2,1)}, u32[]{:S(2)}, u32[]{:S(2)}) collective-permute-start(bf16[640,1280]{1,0:T(8,128)(2,1)} %collective-permute-done.18.refs_7_), channel_id=1, source_target_pairs={{0,1},{1,0},{2,3},{3,2},{4,5},{5,4},{6,7},{7,6},{8,9},{9,8},{10,11... | collective-permute-start | bytes 4915208 | tf_op jit(solution)/shard_map/ppermute | solution.py:348
  178.8 44.3 %collective-permute-start.23 = (bf16[640,1280]{1,0:T(8,128)(2,1)}, bf16[640,1280]{1,0:T(8,128)(2,1)}, u32[]{:S(2)}, u32[]{:S(2)}) collective-permute-start(bf16[640,1280]{1,0:T(8,128)(2,1)} %collective-permute-done.19.refs_8_), channel_id=1, source_target_pairs={{0,8},{1,5},{2,6},{3,11},{4,0},{5,13},{6,14},{7,3},{8,16},{9,1},{1... | collective-permute-start | bytes 4915208 | tf_op jit(solution)/shard_map/ppermute | solution.py:348
  179.1 44.0 %collective-permute-start.24 = (bf16[640,1280]{1,0:T(8,128)(2,1)}, bf16[640,1280]{1,0:T(8,128)(2,1)}, u32[]{:S(2)}, u32[]{:S(2)}) collective-permute-start(bf16[640,1280]{1,0:T(8,128)(2,1)} %pad_maximum_fusion.3.refs_5_), channel_id=1, source_target_pairs={{0,4},{1,9},{2,10},{3,7},{4,12},{5,1},{6,2},{7,15},{8,0},{9,17},{1... | collective-permute-start | bytes 4915208 | tf_op jit(solution)/shard_map/ppermute | solution.py:348
  181.2 41.8 %collective-permute-start.25 = (bf16[640,1280]{1,0:T(8,128)(2,1)}, bf16[640,1280]{1,0:T(8,128)(2,1)}, u32[]{:S(2)}, u32[]{:S(2)}) collective-permute-start(bf16[640,1280]{1,0:T(8,128)(2,1)} %collective-permute-done.19.refs_8_), channel_id=1, source_target_pairs={{0,1},{1,0},{2,3},{3,2},{4,5},{5,4},{6,7},{7,6},{8,9},{9,8},{10,11... | collective-permute-start | bytes 4915208 | tf_op jit(solution)/shard_map/ppermute | solution.py:348
  263.7 21.4 %collective-permute-start.26 = (bf16[1024,1280]{1,0:T(8,128)(2,1)}, bf16[1024,1280]{1,0:T(8,128)(2,1)S(1)}, u32[]{:S(2)}, u32[]{:S(2)}) collective-permute-start(bf16[1024,1280]{1,0:T(8,128)(2,1)} %get-tuple-element.304), channel_id=1, source_target_pairs={{0,2},{1,3},{2,0},{3,1},{4,6},{5,7},{6,4},{7,5},{8,10},{9,11},{10,... | collective-permute-start | bytes 7864328 | tf_op jit(solution)/shard_map/ppermute | solution.py:348
  263.8 21.4 %collective-permute-start.27 = (bf16[1024,1280]{1,0:T(8,128)(2,1)}, bf16[1024,1280]{1,0:T(8,128)(2,1)}, u32[]{:S(2)}, u32[]{:S(2)}) collective-permute-start(bf16[1024,1280]{1,0:T(8,128)(2,1)} %get-tuple-element.305), channel_id=1, source_target_pairs={{0,2},{1,3},{2,0},{3,1},{4,6},{5,7},{6,4},{7,5},{8,10},{9,11},{10,... | collective-permute-start | bytes 7864328 | tf_op jit(solution)/shard_map/ppermute | solution.py:348
  285.2 40.6 %collective-permute-start.28 = (bf16[640,1280]{1,0:T(8,128)(2,1)}, bf16[640,1280]{1,0:T(8,128)(2,1)}, u32[]{:S(2)}, u32[]{:S(2)}) collective-permute-start(bf16[640,1280]{1,0:T(8,128)(2,1)} %get-tuple-element.322), channel_id=1, source_target_pairs={{0,4},{1,9},{2,10},{3,7},{4,12},{5,1},{6,2},{7,15},{8,0},{9,17},{1... | collective-permute-start | bytes 4915208 | tf_op jit(solution)/shard_map/ppermute | solution.py:348
  285.9 39.8 %collective-permute-start.29 = (bf16[640,1280]{1,0:T(8,128)(2,1)}, bf16[640,1280]{1,0:T(8,128)(2,1)}, u32[]{:S(2)}, u32[]{:S(2)}) collective-permute-start(bf16[640,1280]{1,0:T(8,128)(2,1)} %get-tuple-element.323), channel_id=1, source_target_pairs={{0,1},{1,0},{2,3},{3,2},{4,5},{5,4},{6,7},{7,6},{8,9},{9,8},{10,11... | collective-permute-start | bytes 4915208 | tf_op jit(solution)/shard_map/ppermute | solution.py:348
  301.8 69.1 %collective-permute-start.31 = (bf16[640,1280]{1,0:T(8,128)(2,1)}, bf16[640,1280]{1,0:T(8,128)(2,1)S(1)}, u32[]{:S(2)}, u32[]{:S(2)}) collective-permute-start(bf16[640,1280]{1,0:T(8,128)(2,1)} %get-tuple-element.346), channel_id=1, source_target_pairs={{0,8},{1,5},{2,6},{3,11},{4,0},{5,13},{6,14},{7,3},{8,16},{9,1},{1... | collective-permute-start | bytes 4915208 | tf_op jit(solution)/shard_map/ppermute | solution.py:348
  303.4 67.5 %collective-permute-start.32 = (bf16[640,1280]{1,0:T(8,128)(2,1)}, bf16[640,1280]{1,0:T(8,128)(2,1)}, u32[]{:S(2)}, u32[]{:S(2)}) collective-permute-start(bf16[640,1280]{1,0:T(8,128)(2,1)} %get-tuple-element.347), channel_id=1, source_target_pairs={{0,1},{1,0},{2,3},{3,2},{4,5},{5,4},{6,7},{7,6},{8,9},{9,8},{10,11... | collective-permute-start | bytes 4915208 | tf_op jit(solution)/shard_map/ppermute | solution.py:348
  330.0 40.9 %collective-permute-start.30 = (bf16[640,1280]{1,0:T(8,128)(2,1)}, bf16[640,1280]{1,0:T(8,128)(2,1)}, u32[]{:S(2)}, u32[]{:S(2)}) collective-permute-start(bf16[640,1280]{1,0:T(8,128)(2,1)} %add_convert_fusion.3), channel_id=1, source_target_pairs={{0,4},{1,9},{2,10},{3,7},{4,12},{5,1},{6,2},{7,15},{8,0},{9,17},{1... | collective-permute-start | bytes 4915208 | tf_op jit(solution)/shard_map/ppermute | solution.py:348
  376.4 23.8 %collective-permute-start.33 = (bf16[640,1280]{1,0:T(8,128)(2,1)}, bf16[640,1280]{1,0:T(8,128)(2,1)}, u32[]{:S(2)}, u32[]{:S(2)}) collective-permute-start(bf16[640,1280]{1,0:T(8,128)(2,1)} %add_convert_fusion.2), channel_id=1, source_target_pairs={{0,4},{1,9},{2,10},{3,7},{4,12},{5,1},{6,2},{7,15},{8,0},{9,17},{1... | collective-permute-start | bytes 4915208 | tf_op jit(solution)/shard_map/ppermute | solution.py:348
  400.2 37.5 %collective-permute-start.35 = (bf16[8,80,3584]{2,1,0:T(8,128)(2,1)}, bf16[8,80,3584]{2,1,0:T(8,128)(2,1)}, u32[]{:S(2)}, u32[]{:S(2)}) collective-permute-start(bf16[8,80,3584]{2,1,0:T(8,128)(2,1)} %get-tuple-element.392), channel_id=1, source_target_pairs={{0,2},{1,3},{2,0},{3,1},{4,6},{5,7},{6,4},{7,5},{8,10},{9,11},{10,... | collective-permute-start | bytes 13762568 | tf_op jit(solution)/shard_map/ppermute | solution.py:348
  403.9 33.8 %collective-permute-start.34 = (bf16[640,1280]{1,0:T(8,128)(2,1)}, bf16[640,1280]{1,0:T(8,128)(2,1)}, u32[]{:S(2)}, u32[]{:S(2)}) collective-permute-start(bf16[640,1280]{1,0:T(8,128)(2,1)} %add_convert_fusion.1), channel_id=1, source_target_pairs={{0,4},{1,9},{2,10},{3,7},{4,12},{5,1},{6,2},{7,15},{8,0},{9,17},{1... | collective-permute-start | bytes 4915208 | tf_op jit(solution)/shard_map/ppermute | solution.py:348
  406.6 31.1 %collective-permute-start.36 = (bf16[512,1280]{1,0:T(8,128)(2,1)}, bf16[512,1280]{1,0:T(8,128)(2,1)S(1)}, u32[]{:S(2)}, u32[]{:S(2)}) collective-permute-start(bf16[512,1280]{1,0:T(8,128)(2,1)} %get-tuple-element.510), channel_id=1, source_target_pairs={{0,1},{1,0},{2,3},{3,2},{4,5},{5,4},{6,7},{7,6},{8,9},{9,8},{10,11... | collective-permute-start | bytes 3932168 | tf_op jit(solution)/shard_map/ppermute | solution.py:348
  447.6 22.2 %collective-permute-start.41 = (bf16[8,80,1536]{2,1,0:T(8,128)(2,1)}, bf16[8,80,1536]{2,1,0:T(8,128)(2,1)S(1)}, u32[]{:S(2)}, u32[]{:S(2)}) collective-permute-start(bf16[8,80,1536]{2,1,0:T(8,128)(2,1)} %get-tuple-element.407), channel_id=1, source_target_pairs={{0,2},{1,3},{2,0},{3,1},{4,6},{5,7},{6,4},{7,5},{8,10},{9,11},{10,... | collective-permute-start | bytes 5898248 | tf_op jit(solution)/shard_map/ppermute | solution.py:348
  453.5 46.5 %collective-permute-start.60 = (bf16[640,1280]{1,0:T(8,128)(2,1)S(1)}, bf16[640,1280]{1,0:T(8,128)(2,1)}, u32[]{:S(2)}, u32[]{:S(2)}) collective-permute-start(bf16[640,1280]{1,0:T(8,128)(2,1)S(1)} %add_convert_fusion), channel_id=1, source_target_pairs={{0,1},{1,0},{2,3},{3,2},{4,5},{5,4},{6,7},{7,6},{8,9},{9,8},{10,11... | collective-permute-start | bytes 4915208 | tf_op jit(solution)/shard_map/ppermute | solution.py:348
  467.8 23.1 %collective-permute-start.39 = (bf16[80,3584]{1,0:T(8,128)(2,1)}, bf16[80,3584]{1,0:T(8,128)(2,1)S(1)}, u32[]{:S(2)}, u32[]{:S(2)}) collective-permute-start(bf16[80,3584]{1,0:T(8,128)(2,1)} %get-tuple-element.504), channel_id=1, source_target_pairs={{0,4},{1,9},{2,10},{3,7},{4,12},{5,1},{6,2},{7,15},{8,0},{9,17},{1... | collective-permute-start | bytes 1720328 | tf_op jit(solution)/shard_map/ppermute | solution.py:348
  469.1 21.8 %collective-permute-start.40 = (bf16[80,3584]{1,0:T(8,128)(2,1)}, bf16[80,3584]{1,0:T(8,128)(2,1)}, u32[]{:S(2)}, u32[]{:S(2)}) collective-permute-start(bf16[80,3584]{1,0:T(8,128)(2,1)} %get-tuple-element.503), channel_id=1, source_target_pairs={{0,8},{1,5},{2,6},{3,11},{4,0},{5,13},{6,14},{7,3},{8,16},{9,1},{1... | collective-permute-start | bytes 1720328 | tf_op jit(solution)/shard_map/ppermute | solution.py:348
  472.0 18.9 %collective-permute-start.42 = (bf16[80,1536]{1,0:T(8,128)(2,1)}, bf16[80,1536]{1,0:T(8,128)(2,1)S(1)}, u32[]{:S(2)}, u32[]{:S(2)}) collective-permute-start(bf16[80,1536]{1,0:T(8,128)(2,1)} %get-tuple-element.518), channel_id=1, source_target_pairs={{0,4},{1,9},{2,10},{3,7},{4,12},{5,1},{6,2},{7,15},{8,0},{9,17},{1... | collective-permute-start | bytes 737288 | tf_op jit(solution)/shard_map/ppermute | solution.py:348
  493.2 25.6 %collective-permute-start.46 = (bf16[80,1536]{1,0:T(8,128)(2,1)}, bf16[80,1536]{1,0:T(8,128)(2,1)}, u32[]{:S(2)}, u32[]{:S(2)}) collective-permute-start(bf16[80,1536]{1,0:T(8,128)(2,1)} %get-tuple-element.516), channel_id=1, source_target_pairs={{0,4},{1,9},{2,10},{3,7},{4,12},{5,1},{6,2},{7,15},{8,0},{9,17},{1... | collective-permute-start | bytes 737288 | tf_op jit(solution)/shard_map/ppermute | solution.py:348
  494.5 24.3 %collective-permute-start.47 = (bf16[80,1536]{1,0:T(8,128)(2,1)}, bf16[80,1536]{1,0:T(8,128)(2,1)}, u32[]{:S(2)}, u32[]{:S(2)}) collective-permute-start(bf16[80,1536]{1,0:T(8,128)(2,1)} %get-tuple-element.515), channel_id=1, source_target_pairs={{0,8},{1,5},{2,6},{3,11},{4,0},{5,13},{6,14},{7,3},{8,16},{9,1},{1... | collective-permute-start | bytes 737288 | tf_op jit(solution)/shard_map/ppermute | solution.py:348
  497.9 20.9 %collective-permute-start.44 = (bf16[80,3584]{1,0:T(8,128)(2,1)}, bf16[80,3584]{1,0:T(8,128)(2,1)S(1)}, u32[]{:S(2)}, u32[]{:S(2)}) collective-permute-start(bf16[80,3584]{1,0:T(8,128)(2,1)} %get-tuple-element.502), channel_id=1, source_target_pairs={{0,4},{1,9},{2,10},{3,7},{4,12},{5,1},{6,2},{7,15},{8,0},{9,17},{1... | collective-permute-start | bytes 1720328 | tf_op jit(solution)/shard_map/ppermute | solution.py:348
  499.2 19.6 %collective-permute-start.45 = (bf16[80,3584]{1,0:T(8,128)(2,1)S(1)}, bf16[80,3584]{1,0:T(8,128)(2,1)S(1)}, u32[]{:S(2)}, u32[]{:S(2)}) collective-permute-start(bf16[80,3584]{1,0:T(8,128)(2,1)S(1)} %get-tuple-element.501), channel_id=1, source_target_pairs={{0,8},{1,5},{2,6},{3,11},{4,0},{5,13},{6,14},{7,3},{8,16},{9,1},{1... | collective-permute-start | bytes 1720328 | tf_op jit(solution)/shard_map/ppermute | solution.py:348
  503.4 32.9 %collective-permute-start.53 = (bf16[512,1280]{1,0:T(8,128)(2,1)}, bf16[512,1280]{1,0:T(8,128)(2,1)S(1)}, u32[]{:S(2)}, u32[]{:S(2)}) collective-permute-start(bf16[512,1280]{1,0:T(8,128)(2,1)} %get-tuple-element.471), channel_id=1, source_target_pairs={{0,1},{1,0},{2,3},{3,2},{4,5},{5,4},{6,7},{7,6},{8,9},{9,8},{10,11... | collective-permute-start | bytes 3932168 | tf_op jit(solution)/shard_map/ppermute | solution.py:348
  (94 other events, 1039.1 us)
Sparse Core Ops, SparseCore 0:
  66.5 48.2 all-gather.1

commit v3 on v2

--- a/solution.py
+++ b/solution.py
@@ -379,42 +379,41 @@
                 slots[3 + k] = self.swap_blk(slots[k - 1])
             slots = yield slots
 
-    def reduce(self, parts, back):
+    def reduce(self, parts, back, alone=False):
         def added(terms):
             total = terms[0].astype(f32)
             for t in terms[1:]:
                 total = total + t.astype(f32)
             return total.astype(bf16)
 
-        ahead, behind = parts[4], [] if back == 0 else parts[4 + back]
-        way = {"ahead": self.shift(added(ahead), -1)}
+        way = {"ahead": self.shift(added(parts[4]), -1)}
         if back:
-            way["behind"] = self.shift(added(behind), 1)
+            way["behind"] = self.shift(added(parts[4 + back]), 1)
         for k in range(3, back, -1):
             way[f"over{k}"] = self.swap_blk(added(parts[4 + k]))
         way = yield way
         for k in (3, 2, 1):
             extra = [way.pop(f"over{k}")] if f"over{k}" in way else []
-            terms = [way["ahead"]] + parts[k] + extra
-            way["ahead"] = self.shift(added(terms), -1)
-            if back - (4 - k) >= 1:
-                way["behind"] = self.shift(added([way["behind"]] + parts[4 + back - (4 - k)]), 1)
+            way["ahead"] = self.shift(added([way["ahead"]] + parts[k] + extra), -1)
+            if k < back and not (alone and k == 1):
+                way["behind"] = self.shift(added([way["behind"]] + parts[4 + k]), 1)
+            way = yield way
+        if alone:
+            way["behind"] = self.shift(added([way["behind"]] + parts[5]), 1)
             way = yield way
         ends = [way["ahead"]] + ([way["behind"]] if back else [])
-        total = added(ends + parts[0])
-        way = yield {"own": total, "other": self.swap_blk(total)}
-        yield way["own"].astype(f32) + way["other"].astype(f32)
+        yield added(ends + parts[0])
 
     def total(self, x):
-        bit = 1
-        while bit < self.cells * self.blks:
+        count = self.cells * self.blks
+        bits = [1 << i for i in range(count.bit_length() - 1)]
+        for bit in [b for b in bits if b >= self.blks] + [b for b in bits if b < self.blks]:
             other = bit
             moved = self.permute(
                 x, lambda cell, blk: divmod((cell * self.blks + blk) ^ other, self.blks)
             )
             x, moved = yield x, moved
             x = x + moved
-            bit *= 2
         yield x
 
 
@@ -437,12 +436,16 @@
     return jnp.sum(x, axis=0, keepdims=True)
 
 
-def place_rows(slots, target, place_ref, sem, height, cols=None):
-    cols = slice(None) if cols is None else cols
+def place_rows(slots, target, place_ref, sem, first=0, cols=None):
+    height = slots[0].shape[0]
+    start, wide = cols or (0, slots[0].shape[1])
     return [
         pltpu.make_async_copy(
-            slot.at[:, cols],
-            target.at[pl.ds(pl.multiple_of(place_ref[i] * height, 16), height), cols],
+            slot.at[:, pl.ds(start, wide)],
+            target.at[
+                pl.ds(pl.multiple_of(place_ref[i] * height, 16), height),
+                pl.ds(first + start, wide),
+            ],
             sem.at[i],
         )
         for i, slot in enumerate(slots)
@@ -451,12 +454,10 @@
 
 def qkv_kernel(n, place_ref, x_ref, gain_ref, bias_ref, qb_ref, vb_ref, *refs):
     slots, (a_ref, q_ref, k_ref, v_ref, w, sem) = refs[:n], refs[n:]
-    height = slots[0].shape[0]
     width = x_ref.shape[1]
     first = pl.program_id(0) == 0
     copies = [
-        place_rows(slots, w, place_ref, sem.at[j], height, pl.ds(j * width, width))
-        for j in range(3)
+        place_rows(slots, w, place_ref, sem.at[j], cols=(j * width, width)) for j in range(3)
     ]
 
     @pl.when(first)
@@ -504,39 +505,62 @@
     )(place, x, gain, bias, qb, vb, *slots)
 
 
-def attend_kernel(qrows, mask_ref, keep_ref, q_ref, k_ref, v_ref, o_ref, lse_ref):
+def head_keys(low, k, v, mask, fill):
+    res = []
+    for half in range(2):
+        mine = low if half == 0 else jnp.logical_not(low)
+        res.append(
+            (
+                jnp.where(mine, k.astype(f32), mask).astype(bf16),
+                jnp.where(mine, v.astype(f32), fill).astype(bf16),
+            )
+        )
+    return res
+
+
+def head_query(low, lane, half, q):
+    mine = low if half == 0 else jnp.logical_not(low)
+    one = lane == (HEAD_DIM if half == 0 else 0)
+    q = q.astype(f32) * (1.0 / math.sqrt(HEAD_DIM))
+    return jnp.where(mine, q, jnp.where(one, 1.0, 0.0)).astype(bf16)
+
+
+def attend_kernel(qrows, ahead, mask_ref, keep_ref, q_ref, k_ref, v_ref, o_ref, lse_ref):
     n = q_ref.shape[0]
     lane = lax.broadcasted_iota(jnp.int32, (n, 128), 1)
-    k, v, mask = k_ref[...], v_ref[...], mask_ref[...]
-    for half in range(2):
-        mine = (lane < HEAD_DIM) if half == 0 else (lane >= HEAD_DIM)
-        here = mine[:qrows]
-        one = ((lane == HEAD_DIM) if half == 0 else (lane == 0))[:qrows]
-        keys = jnp.where(mine, k.astype(f32), mask).astype(bf16)
-        vals = jnp.where(mine, v.astype(f32), 1.0).astype(bf16)
-        for i in range(n // qrows):
-            rows = pl.ds(i * qrows, qrows)
-            q = q_ref[rows, :].astype(f32) * (1.0 / math.sqrt(HEAD_DIM))
-            q = jnp.where(here, q, jnp.where(one, 1.0, 0.0)).astype(bf16)
-            s = dot(q, keys, NT)
-            top = jnp.max(s, axis=1, keepdims=True)
-            mixed = dot(jnp.exp(s - top).astype(bf16), vals, NN)
-            total = pltpu.roll(mixed, HEAD_DIM, 1)
-            o = (mixed / total * keep_ref[rows, :]).astype(bf16)
-            if half == 0:
-                o_ref[rows, :] = o
-            else:
-                o_ref[rows, :] = jnp.where(here, o, o_ref[rows, :])
-            lse = jnp.transpose(top + jnp.log(total))
-            first = half * HEAD_DIM
-            lse_ref[half, :, rows] = lse[first : first + 1, :]
-
-
-def attend_call(mask, keep, q, k, v, first, count, qrows=512):
-    n = q.shape[0]
+    pair = head_keys(lane < HEAD_DIM, k_ref[...], v_ref[...], mask_ref[...], 1.0)
+    lane = lane[:qrows]
+    low = lane < HEAD_DIM
+    items = [(i, half) for i in range(n // qrows) for half in range(2)]
+
+    def scores(i, half):
+        q = head_query(low, lane, half, q_ref[pl.ds(i * qrows, qrows), :])
+        return dot(q, pair[half][0], NT)
+
+    waiting = [scores(*item) for item in items[:ahead]]
+    for at, (i, half) in enumerate(items):
+        if at + ahead < len(items):
+            waiting.append(scores(*items[at + ahead]))
+        s = waiting.pop(0)
+        rows = pl.ds(i * qrows, qrows)
+        top = jnp.max(s, axis=1, keepdims=True)
+        mixed = dot(jnp.exp(s - top).astype(bf16), pair[half][1], NN)
+        total = pltpu.roll(mixed, HEAD_DIM, 1)
+        o, lse = mixed / total, top + jnp.log(total)
+        if half == 0:
+            o_first, lse_first = o, lse
+            continue
+        o_ref[rows, :] = (jnp.where(low, o_first, o) * keep_ref[rows, :]).astype(bf16)
+        lse = jnp.transpose(jnp.where(low, lse_first, lse))
+        lse_ref[0, :, rows] = lse[:1, :]
+        lse_ref[1, :, rows] = lse[HEAD_DIM : HEAD_DIM + 1, :]
+
+
+def attend_call(mask, keep, qkv, first, count, qrows=256, ahead=2):
+    n = qkv[0].shape[0]
     block = pl.BlockSpec((n, 128), lambda h: (0, h + first))
     return pl.pallas_call(
-        partial(attend_kernel, qrows),
+        partial(attend_kernel, qrows, ahead),
         grid=(count,),
         in_specs=[fixed((n, 1)), fixed((n, 1)), block, block, block],
         out_specs=[
@@ -547,7 +571,7 @@
         compiler_params=params(),
         cost_estimate=cost(20 * count * n * n * 128, 8 * n * 128 * count, 2 * count * n * n),
         name="attend",
-    )(mask, keep, q, k, v)
+    )(mask, keep, *qkv)
 
 
 def attend_back_kernel(
@@ -556,23 +580,22 @@
 ):
     n = q_ref.shape[0]
     lane = lax.broadcasted_iota(jnp.int32, (n, 128), 1)
-    k, v, mask = k_ref[...], v_ref[...], mask_ref[...]
+    k = k_ref[...]
     scale = 1.0 / math.sqrt(HEAD_DIM)
+    pair = head_keys(lane < HEAD_DIM, k, v_ref[...], mask_ref[...], 0.0)
+    k_turned = jnp.transpose(k)
     prod = jnp.transpose(o_ref[...].astype(f32) * go_ref[...].astype(f32))
-    for half in range(2):
-        mine = (lane < HEAD_DIM) if half == 0 else (lane >= HEAD_DIM)
-        here = mine[:qrows]
-        one = ((lane == HEAD_DIM) if half == 0 else (lane == 0))[:qrows]
-        keys = jnp.where(mine, k.astype(f32), mask).astype(bf16)
-        vals = jnp.where(mine, v, jnp.zeros_like(v))
-        delta = colsum(prod[half * HEAD_DIM : (half + 1) * HEAD_DIM, :])
-        for i in range(n // qrows):
-            rows = pl.ds(i * qrows, qrows)
+    delta = [colsum(prod[half * HEAD_DIM : (half + 1) * HEAD_DIM, :]) for half in range(2)]
+    top = lane[:qrows]
+    for i in range(n // qrows):
+        rows = pl.ds(i * qrows, qrows)
+        gq = []
+        for half in range(2):
             q_raw, go = q_ref[rows, :], go_ref[rows, :]
-            q = jnp.where(here, q_raw.astype(f32) * scale, jnp.where(one, 1.0, 0.0)).astype(bf16)
-            p = jnp.exp(dot(keys, q, NT) - lse_ref[half, :, rows])
-            gp = dot(vals, go, NT)
-            gs = (p * (gp - delta[:, i * qrows : (i + 1) * qrows])).astype(bf16)
+            q = head_query(top < HEAD_DIM, top, half, q_raw)
+            p = jnp.exp(dot(pair[half][0], q, NT) - lse_ref[half, :, rows])
+            gp = dot(pair[half][1], go, NT)
+            gs = (p * (gp - delta[half][:, i * qrows : (i + 1) * qrows])).astype(bf16)
             gv = dot(p.astype(bf16), go, NN)
             gk = dot(gs, q_raw, NN)
             if i == 0:
@@ -580,11 +603,9 @@
             else:
                 gv_sum[half] += gv
                 gk_sum[half] += gk
-            gq = (dot(gs, k, TN) * scale).astype(bf16)
-            if half == 0:
-                gq_ref[rows, :] = gq
-            else:
-                gq_ref[rows, :] = jnp.where(here, gq, gq_ref[rows, :])
+            gq.append(dot(k_turned, gs, NN))
+        turned = jnp.concatenate([gq[0][:HEAD_DIM], gq[1][HEAD_DIM:]], axis=0)
+        gq_ref[rows, :] = jnp.transpose(turned * scale).astype(bf16)
     low = lane < HEAD_DIM
     gk_ref[...] = (jnp.where(low, gk_sum[0], gk_sum[1]) * scale).astype(bf16)
     gv = jnp.where(low, gv_sum[0], gv_sum[1]).astype(bf16)
@@ -593,54 +614,76 @@
     sv_ref[...] = colsum(gv.astype(f32))
 
 
-def attend_back_call(mask, q, k, v, o, go, lse, first, count, qrows=512):
-    n = q.shape[0]
-    block = pl.BlockSpec((n, 128), lambda h: (0, h + first))
-    own = pl.BlockSpec((n, 128), lambda h: (0, h))
-    vec = pl.BlockSpec((1, 128), lambda h: (0, h))
+def attend_back_call(mask, qkv, o, go, lse, count, firsts, qrows=512):
+    n = go.shape[0]
+
+    def block(first):
+        return pl.BlockSpec((n, 128), lambda h: (0, h + first))
+
+    own, vec = block(0), pl.BlockSpec((1, 128), lambda h: (0, h))
+    at_qkv, at_o, at_go = firsts
     return pl.pallas_call(
         partial(attend_back_kernel, qrows),
         grid=(count,),
-        in_specs=[
-            fixed((n, 1)), block, block, block, own, block,
-            pl.BlockSpec((2, 1, n), lambda h: (h, 0, 0)),
-        ],
+        in_specs=[fixed((n, 1))]
+        + [block(at_qkv)] * 3
+        + [block(at_o), block(at_go), pl.BlockSpec((2, 1, n), lambda h: (h + at_o, 0, 0))],
         out_specs=[own, own, own, vec, vec],
         out_shape=[shape((n, 128 * count), bf16)] * 3 + [shape((1, 128 * count), f32)] * 2,
         scratch_shapes=[pltpu.VMEM((2, n, 128), f32)] * 2,
         compiler_params=params(),
         cost_estimate=cost(32 * count * n * n * 128, 16 * n * 128 * count, 2 * count * n * n),
         name="attend_back",
-    )(mask, q, k, v, o, go, lse)
-
-
-def out_kernel(x_ref, bias_ref, gain_ref, shift_ref, w_ref, *refs):
-    o_refs, (m_ref, b_ref) = refs[:-2], refs[-2:]
+    )(mask, *qkv, o, go, lse)
+
+
+def load_wout(slots, place_ref, w, sem):
+    wide = w.shape[1]
+    start = slots[0].shape[1] - wide
+    copies = place_rows(slots, w, place_ref, sem, -start, (start, wide))
+
+    @pl.when(pl.program_id(0) == 0)
+    def _():
+        for c in copies:
+            c.start()
+        for c in copies:
+            c.wait()
+
+
+def out_kernel(n, place_ref, x_ref, bias_ref, gain_ref, shift_ref, *refs):
+    slots, o_refs, (m_ref, b_ref, w, sem) = refs[:n], refs[n:-4], refs[-4:]
+    load_wout(slots, place_ref, w, sem)
     m = x_ref[...].astype(f32) + bias_ref[...]
     first = 0
     for o_ref in o_refs:
-        m = m + dot(o_ref[...], w_ref[first : first + o_ref.shape[1], :], NN)
+        m = m + dot(o_ref[...], w[first : first + o_ref.shape[1], :], NN)
         first += o_ref.shape[1]
     m_ref[...] = m
     xh, _ = norm_parts(m)
     b_ref[...] = (xh * gain_ref[...] + shift_ref[...]).astype(bf16)
 
 
-def out_call(x, o_parts, w, bias, gain, shift):
+def out_call(place, x, o_parts, slots, bias, gain, shift):
     rows, width = x.shape
+    n = len(slots)
     vec = fixed((1, width))
     block = rowed(ROWS, width)
     return pl.pallas_call(
-        out_kernel,
-        grid=(rows // ROWS,),
-        in_specs=[block, vec, vec, vec, fixed((width, width))]
-        + [rowed(ROWS, o.shape[1]) for o in o_parts],
-        out_specs=[block, block],
+        partial(out_kernel, n),
+        grid_spec=pltpu.PrefetchScalarGridSpec(
+            num_scalar_prefetch=1,
+            grid=(rows // ROWS,),
+            in_specs=[block, vec, vec, vec]
+            + [ANY] * n
+            + [rowed(ROWS, o.shape[1]) for o in o_parts],
+            out_specs=[block, block],
+            scratch_shapes=[pltpu.VMEM((width, width), bf16), pltpu.SemaphoreType.DMA((n,))],
+        ),
         out_shape=[shape((rows, width), f32), shape((rows, width), bf16)],
         compiler_params=params(),
         cost_estimate=cost(4 * rows * width * width, width * (10 * rows + 2 * width)),
         name="out",
-    )(x, bias, gain, shift, w, *o_parts)
+    )(place, x, bias, gain, shift, *slots, *o_parts)
 
 
 def gelu_both(z, gh):
@@ -814,9 +857,11 @@
 
 
 def mid_kernel(
-    oo_ref, os_ref, go_ref, gs_ref, m_ref, g_ref, keep_ref, db_ref, gain_ref, w_ref,
-    hid_ref, gr_ref, gatt_ref, sums_ref,
+    n, place_ref, oo_ref, os_ref, go_ref, gs_ref, m_ref, g_ref, keep_ref, db_ref, gain_ref, *refs
 ):
+    slots, (hid_ref, gr_ref, gatt_ref, sums_ref, w, sem) = refs[:n], refs[n:]
+    load_wout(slots, place_ref, w, sem)
+
     @pl.when(pl.program_id(0) == 0)
     def _():
         sums_ref[...] = jnp.zeros_like(sums_ref)
@@ -830,69 +875,64 @@
     gm = g + norm_back(xh, scale, gain_ref[...], gb)
     gr = gm.astype(bf16)
     gr_ref[...] = gr
-    gatt_ref[...] = (dot(gr, w_ref[...], NT) * keep_ref[...]).astype(bf16)
+    gatt_ref[...] = (dot(gr, w[...], NT) * keep_ref[...]).astype(bf16)
     sums_ref[0:1, :] += colsum(gb * xh)
     sums_ref[1:2, :] += colsum(gb)
     sums_ref[2:3, :] += colsum(gr.astype(f32))
     sums_ref[3:4, :] += colsum(g)
 
 
-def mid_call(oo, os, go, gs, m, g, keep, db, gain, w):
+def mid_call(place, oo, os, go, gs, m, g, keep, db, gain, slots):
     rows, width = m.shape
+    n = len(slots)
     block = rowed(ROWS, width)
     vec = fixed((1, width))
     return pl.pallas_call(
-        mid_kernel,
-        grid=(rows // ROWS,),
-        in_specs=[block] * 6 + [rowed(ROWS, 1), vec, vec, fixed((width, width))],
-        out_specs=[block] * 3 + [fixed((8, width))],
-        out_shape=[
-            shape((rows, width), bf16),
-            shape((rows, width), bf16),
-            shape((rows, width), bf16),
-            shape((8, width), f32),
-        ],
+        partial(mid_kernel, n),
+        grid_spec=pltpu.PrefetchScalarGridSpec(
+            num_scalar_prefetch=1,
+            grid=(rows // ROWS,),
+            in_specs=[block] * 6 + [rowed(ROWS, 1), vec, vec] + [ANY] * n,
+            out_specs=[block] * 3 + [fixed((8, width))],
+            scratch_shapes=[pltpu.VMEM((width, width), bf16), pltpu.SemaphoreType.DMA((n,))],
+        ),
+        out_shape=[shape((rows, width), bf16)] * 3 + [shape((8, width), f32)],
         compiler_params=params(),
         cost_estimate=cost(4 * rows * width * width, width * (30 * rows + 2 * width)),
         name="mid",
-    )(oo, os, go, gs, m, g, keep, db, gain, w)
-
-
-def att_weights_kernel(n, jobs, place_ref, *refs):
-    lefts, rights = refs[: jobs[0]], refs[jobs[0] : jobs[0] + jobs[1]]
-    refs = refs[jobs[0] + jobs[1] :]
-    outs, refs = refs[: n + 1], refs[n + 1 :]
-    lv, tv, rv, ov, lsem, rsem, osem = refs
-    table = jobs[2]
+    )(place, oo, os, go, gs, m, g, keep, db, gain, *slots)
+
+
+def att_weights_kernel(n, counts, blocks, place_ref, *refs):
+    lefts, rights = refs[: counts[0]], refs[counts[0] : sum(counts)]
+    refs = refs[sum(counts) :]
+    outs, (lv, tv, rv, ov, lsem, rsem, osem) = refs[: n + 1], refs[n + 1 :]
     height = outs[0].shape[0]
     loads = [pltpu.make_async_copy(r, lv.at[i], lsem.at[i]) for i, r in enumerate(lefts)]
-    col = 0
-    right_loads = []
+    ends, right_loads = [], []
     for i, r in enumerate(rights):
+        start = ends[-1] if ends else 0
+        ends.append(start + r.shape[1])
         right_loads.append(
-            pltpu.make_async_copy(r, rv.at[:, pl.ds(col, r.shape[1])], rsem.at[i])
+            pltpu.make_async_copy(r, rv.at[:, pl.ds(start, r.shape[1])], rsem.at[i])
         )
-        col += r.shape[1]
-    loads[0].start()
-    for c in right_loads:
+    for c in loads[:1] + right_loads + loads[1:]:
         c.start()
-    for c in loads[1:]:
-        c.start()
-    have = set()
+    have, arrived = set(), 0
     stores = []
-    col = 0
-    for step, (left, r) in enumerate(zip(table, rights, strict=True)):
+    for step, (left, start, wide) in enumerate(blocks):
         if left not in have:
             loads[left].wait()
             tv[left] = jnp.transpose(lv[left])
             have.add(left)
-        right_loads[step].wait()
+        while arrived < len(ends) and (arrived == 0 or ends[arrived - 1] < start + wide):
+            right_loads[arrived].wait()
+            arrived += 1
         slot = step % 2
         if step >= 2:
             for c in stores[step - 2]:
                 c.wait()
-        wide = r.shape[1]
-        cols = pl.ds(col, wide)
+        cols = pl.ds(start, wide)
         ov[slot, :, pl.ds(0, wide)] = dot(tv[left], rv[:, cols], NN).astype(bf16)
         stores.append([])
         for i in range(2 * n):
@@ -901,20 +941,19 @@
             c = pltpu.make_async_copy(ov.at[slot, rows, pl.ds(0, wide)], goal, osem.at[slot, i])
             c.start()
             stores[-1].append(c)
-        col += wide
     for group in stores[-2:]:
         for c in group:
             c.wait()
 
 
-def att_weights_call(place, lefts, rights, table):
+def att_weights_call(place, lefts, rights, blocks):
     rows, width = lefts[0].shape
     n = len(OFFSETS)
     total = sum(r.shape[1] for r in rights)
-    wide = max(r.shape[1] for r in rights)
+    wide = max(b[2] for b in blocks)
     height = width // (2 * n)
     return pl.pallas_call(
-        partial(att_weights_kernel, n, (len(lefts), len(rights), table)),
+        partial(att_weights_kernel, n, (len(lefts), len(rights)), blocks),
         grid_spec=pltpu.PrefetchScalarGridSpec(
             num_scalar_prefetch=1,
             grid=(1,),
@@ -940,8 +979,7 @@
 def in_kernel(n, pieces, place_ref, x_ref, gr_ref, gain_ref, *refs):
     grads, slots = refs[:pieces], refs[pieces : pieces + n]
     res_ref, sums_ref, w, sem = refs[pieces + n :]
-    height = slots[0].shape[0]
-    copies = place_rows(slots, w, place_ref, sem, height)
+    copies = place_rows(slots, w, place_ref, sem, cols=(0, w.shape[1]))
 
     @pl.when(pl.program_id(0) == 0)
     def _():
@@ -997,6 +1035,16 @@
     return lax.optimization_barrier(trees)
 
 
+def side_by_side(vectors):
+    total = sum(v.shape[0] for v in vectors)
+    res, at = None, 0
+    for v in vectors:
+        wide = jnp.pad(v, (at, total - at - v.shape[0]))
+        at += v.shape[0]
+        res = wide if res is None else res + wide
+    return res
+
+
 def local_swapped(
     sizes, hidden_in, lengths, ln1_gain, ln1_bias, w_qkv, q_bias, v_bias, w_out, out_bias, ln2_gain, ln2_bias,
     w_up, up_bias, w_down, down_bias, cotangent,
@@ -1025,46 +1073,50 @@
     mask = jnp.where(keep > 0, 0.0, far_below)
 
     x_got = ring.swap_blk(pick(hidden_in, 1 - blk))
-    steps = ring.gather(w_qkv, 2)
-    qkv_own = next(steps)
+    steps = ring.gather(jnp.concatenate([w_qkv, w_out], axis=1), 2)
+    slots, sib = next(steps), [None] * n
     w_pair = jnp.concatenate([w_up, w_down], axis=0)
-    qkv_own[1], qkv_own[5] = fence(qkv_own[1], qkv_own[5])
-    qkv_own = steps.send(qkv_own)
-    qkv_own[2], qkv_own[6], x_got = fence(qkv_own[2], qkv_own[6], x_got)
-    qkv_own = steps.send(qkv_own)
+    g_send = pick(cotangent, 1 - blk)
+    small = [vec(v) for v in (ln1_gain, ln1_bias, q_bias, v_bias, out_bias, ln2_gain, ln2_bias)]
+    small += [place, mask, keep]
+    slots[1], slots[5] = fence(slots[1], slots[5])
+    slots = steps.send(slots)
+    slots[2], slots[6], small, x_got, w_pair = fence(slots[2], slots[6], small, x_got, w_pair)
+    ln1_gain, ln1_bias, q_bias, v_bias, out_bias, ln2_gain, ln2_bias, place, mask, keep = small
+    slots = steps.send(slots)
+    for s in (0, 1, 5, 2, 6):
+        sib[s] = ring.swap_core(slots[s])
     x = jnp.concatenate([pick(hidden_in, blk), x_got], axis=0)
-    qkv_own[3], x = fence(qkv_own[3], x)
-    qkv_own = steps.send(qkv_own)
-    qkv_own[4], w_pair, w_out = fence(qkv_own[4], w_pair, w_out)
+    slots[3], x, sib, g_send = fence(slots[3], x, sib, g_send)
+    slots = steps.send(slots)
+    for s in (3, 4, 7):
+        sib[s] = ring.swap_core(slots[s])
+    slots[4], w_pair = fence(slots[4], w_pair)
     pair = [w_pair, ring.shift(w_pair, 1)] + [None] * 6
-    w_out = lax.all_gather(w_out, "cell", axis=0, tiled=True)
-    qkv_sib = [ring.swap_core(s) for s in qkv_own]
-    g_send, qkv_sib[7] = fence(cotangent, qkv_sib[7])
-    g_got = ring.swap_blk(pick(g_send, 1 - blk))
-
-    a, q, k, v = qkv_call(
-        place, x, vec(ln1_gain), vec(ln1_bias), vec(q_bias), vec(v_bias), qkv_own + qkv_sib
-    )
+    g_send, slots[7] = fence(g_send, slots[7])
+    g_send = [g_send[: genes // 2], g_send[genes // 2 :]]
+    g_got = [ring.swap_blk(g_send[0])]
+
+    weights = slots + sib
+    a, *qkv = qkv_call(place, x, ln1_gain, ln1_bias, q_bias, v_bias, weights)
+    qkv, pair[1], g_got, g_send = fence(qkv, pair[1], g_got, g_send)
+    g_got.append(ring.swap_blk(g_send[1]))
+    pair[2] = ring.shift(pair[1], 1)
     pairs = width // 128
-    cuts = [(0, 4 * pairs // 10), (4 * pairs // 10, 2 * pairs // 10)]
-    cuts.append((sum(cuts[1]), pairs - sum(cuts[1])))
-    q, k, v, pair[1], g_got = fence(q, k, v, pair[1], g_got)
-    pair[2] = ring.shift(pair[1], 1)
-    attended = [attend_call(mask, keep, q, k, v, *cuts[0])]
-    q, k, v, attended, pair[2] = fence(q, k, v, attended, pair[2])
-    g = jnp.concatenate([pick(cotangent, blk), g_got], axis=0)
+    cut = 6 * pairs // 10
+    attended = [attend_call(mask, keep, qkv, 0, cut)]
+    attended, qkv, pair[2], g_got = fence(attended, qkv, pair[2], g_got)
+    pair[3] = ring.shift(pair[2], 1)
+    g = jnp.concatenate([pick(cotangent, blk)] + g_got, axis=0)
     g_sib = ring.swap_core(g)
-    pair[3] = ring.shift(pair[2], 1)
-    pair[6] = ring.swap_blk(pair[2])
-    attended += [attend_call(mask, keep, q, k, v, *cut) for cut in cuts[1:]]
-    attended, pair[0], pair[3] = fence(attended, pair[0], pair[3])
+    attended.append(attend_call(mask, keep, qkv, cut, pairs - cut))
     o_parts = [t[0] for t in attended]
+    m, b = out_call(place, x, o_parts, weights, out_bias, ln2_gain, ln2_bias)
+    b, g_sib, pair[0], pair[3] = fence(b, g_sib, pair[0], pair[3])
+    b_sib = ring.swap_core(b)
     pair[4] = ring.shift(pair[3], 1)
     pair[5] = ring.shift(pair[0], -1)
     pair[7] = ring.swap_blk(pair[3])
-    m, b = out_call(x, o_parts, w_out, vec(out_bias), vec(ln2_gain), vec(ln2_bias))
-    m, b, pair[6], g_sib = fence(m, b, pair[6], g_sib)
-    b_sib = ring.swap_core(b)
 
     ub = up_bias.reshape(shards, units)[shard_own]
     near, far = (0, 1, 2, 3), (4, 5, 6, 7)
@@ -1072,6 +1124,13 @@
     h_near, gz_near, sum_near, *acc = ffn_call(
         b, b_sib, g, g_sib, ub_near, [pair[s] for s in near]
     )
+    h_near, gz_near, acc, pair[5] = fence(h_near, gz_near, acc, pair[5])
+    pair[6] = ring.shift(pair[5], -1)
+    parts = [None] * n
+    made = ffn_weights_call(gz_near, h_near, b, b_sib, g, g_sib, len(near))
+    made, acc = fence(made, acc)
+    for s, t in zip(near, made, strict=True):
+        parts[s] = [t]
     h_far, gz_far, sum_far, oo, gb_own, os_send, gs_send = ffn_call(
         b, b_sib, g, g_sib, ub_far, [pair[s] for s in far], acc
     )
@@ -1082,7 +1141,6 @@
     up_rows = jnp.sum(
         jnp.where(mine[:, :, None], jnp.stack([up_sums[s] for s in range(n)])[None], 0.0), axis=1
     )
-    parts = [None] * n
     made = ffn_weights_call(gz_far, h_far, b, b_sib, g, g_sib, len(far))
     os_got, gs_got = ring.swap_core(os_send), ring.swap_core(gs_send)
     made, oo, os_got, gs_got = fence(made, oo, os_got, gs_got)
@@ -1091,99 +1149,112 @@
     steps = ring.reduce(parts, 1)
     way = next(steps)
     out_hidden, gr, gatt, mid_sums = mid_call(
-        oo, os_got, gb_own, gs_got, m, g, keep, vec(down_bias), vec(ln2_gain), w_out
-    )
-    gr, gatt, gz_near = fence(gr, gatt, gz_near)
-    hid_got = ring.swap_blk(out_hidden[genes:])
-    made = ffn_weights_call(gz_near, h_near, b, b_sib, g, g_sib, len(near))
-    made, gatt, way["ahead"], way["over3"] = fence(made, gatt, way["ahead"], way["over3"])
-    for s, t in zip(near, made, strict=True):
-        parts[s] = [t]
-    way = steps.send(way)
-
-    def back(part, gatt):
-        return attend_back_call(mask, q, k, v, o_parts[part], gatt, attended[part][1], *cuts[part])
-
-    backs = [back(0, gatt)]
-    backs, gatt = fence(backs, gatt)
-    backs.append(back(1, gatt))
-    backs, gatt, way = fence(backs, gatt, way)
+        place, oo, os_got, gb_own, gs_got, m, g, keep, vec(down_bias), ln2_gain, weights
+    )
+    hid_send = [out_hidden[genes : genes + genes // 2], out_hidden[genes + genes // 2 :]]
+
+    def back(first, count, gatt):
+        o, lse = attended[0 if first < cut else 1]
+        at = first if first < cut else first - cut
+        return attend_back_call(mask, qkv, o, gatt, lse, count, (first, at, first))
+
+    early, half = 128 * cut, width // 2
+    late = width - early
+    backs = [back(0, cut, gatt)]
+    backs, gatt, way["ahead"], way["over3"], hid_send = fence(
+        backs, gatt, way["ahead"], way["over3"], hid_send
+    )
     way = steps.send(way)
     first = att_weights_call(
-        place, [a, jnp.concatenate(o_parts, axis=1)],
-        [t[i] for i in range(3) for t in backs] + [gr], [0] * 6 + [1],
-    )
-    first, gatt, way = fence(first, gatt, way)
+        place, [a, jnp.concatenate(o_parts, axis=1)], list(backs[0][:3]) + [gr],
+        [(0, i * early, early) for i in range(3)] + [(1, 3 * early + i * half, half) for i in range(2)],
+    )
+    first, gatt, way, hid_send = fence(first, gatt, way, hid_send)
     way = steps.send(way)
+    hid_got = [ring.swap_blk(hid_send[0])]
     first_sib = ring.swap_core(first[n])
-    backs.append(back(2, gatt))
-    backs, way, first, first_sib, hid_got, up_rows = fence(
-        backs, way, first, first_sib, hid_got, up_rows
-    )
-    way = steps.send(way)
+    one = (pairs - cut) // 4
+    backs.append(back(cut, one, gatt))
+    backs, gatt, first, first_sib, up_rows = fence(backs, gatt, first, first_sib, up_rows)
     steps_first = ring.reduce([[first[s], first_sib[s]] for s in range(n)], 3)
     way_first = next(steps_first)
-    second = att_weights_call(place, [a], list(backs[2][:3]), [0] * 3)
+    backs.append(back(cut + one, pairs - cut - one, gatt))
+    backs, way_first, way, hid_got, hid_send = fence(backs, way_first, way, hid_got, hid_send)
+    way_first = steps_first.send(way_first)
+    hid_got.append(ring.swap_blk(hid_send[1]))
+    way = steps.send(way)
+    grads = [t[i] for i in range(3) for t in backs]
+    in_send, in_sums_send = in_call(place, x, gr, ln1_gain, grads, weights, 1, bf16)
+    sums_early = side_by_side(
+        [mid_sums[:4].reshape(-1), up_rows.reshape(-1)]
+        + [t[i].reshape(-1) for i in (3, 4) for t in backs]
+    )
+    in_send, backs, way_first, hid_got = fence(in_send, backs, way_first, hid_got)
+    way_first = steps_first.send(way_first)
+    in_got = ring.swap_blk(in_send)
+    second = att_weights_call(
+        place, [a], [t[i] for i in range(3) for t in backs[1:]],
+        [(0, i * late, late) for i in range(3)],
+    )
+    second, way, way_first, grads, sums_early = fence(second, way, way_first, grads, sums_early)
+    way_first = steps_first.send(way_first)
+    ffn_sum = steps.send(way)
+    ffn_got = ring.swap_blk(ffn_sum)
     second_sib = ring.swap_core(second[n])
-    grads = [t[i] for i in range(3) for t in backs]
-    second, grads, way_first = fence(second, grads, way_first)
-    way_first = steps_first.send(way_first)
     steps_second = ring.reduce([[second[s], second_sib[s]] for s in range(n)], 3)
     way_second = next(steps_second)
-    weights = qkv_own + qkv_sib
-    in_send, in_sums_send = in_call(place, x, gr, vec(ln1_gain), grads, weights, 1, bf16)
-    in_send, grads, way_first, way_second = fence(in_send, grads, way_first, way_second)
-    way_first = steps_first.send(way_first)
-    way_second = steps_second.send(way_second)
-    in_got = ring.swap_blk(in_send)
-    in_own, in_sums = in_call(place, x, gr, vec(ln1_gain), grads, weights, 0, f32)
+    in_own, in_sums = in_call(place, x, gr, ln1_gain, grads, weights, 0, f32)
     in_own, in_sums, in_sums_send, way_first, way_second = fence(
         in_own, in_sums, in_sums_send, way_first, way_second
     )
-    way_first = steps_first.send(way_first)
+    first_sum = steps_first.send(way_first)
+    first_got = ring.swap_blk(first_sum)
     way_second = steps_second.send(way_second)
     ln1_sums = (in_sums + in_sums_send)[:2].reshape(-1)
-    steps_sums = ring.total(
-        jnp.concatenate(
-            [mid_sums[:4].reshape(-1), ln1_sums, up_rows.reshape(-1)]
-            + [t[i].reshape(-1) for i in (3, 4) for t in backs]
-        )
-    )
+    steps_sums = ring.total(side_by_side([sums_early, ln1_sums]))
     sums = next(steps_sums)
     sums = steps_sums.send(sums)
-    way_first, way_second, sums, in_got = fence(way_first, way_second, sums, in_got)
-    way_first = steps_first.send(way_first)
+    way_second, sums = fence(way_second, sums)
     way_second = steps_second.send(way_second)
     sums = steps_sums.send(sums)
-    sums = steps_sums.send(sums)
-    way_first, way_second, sums = fence(way_first, way_second, sums)
-    ffn_rows = steps.send(way)
-    first_rows = steps_first.send(way_first)
+    way_second, sums = fence(way_second, sums)
     way_second = steps_second.send(way_second)
     sums = steps_sums.send(sums)
+    way_second, sums = fence(way_second, sums)
+    second_sum = steps_second.send(way_second)
+    second_got = ring.swap_blk(second_sum)
     sums = steps_sums.send(sums)
-    second_rows = steps_second.send(way_second)
+    sums = steps_sums.send(sums)
+    ffn_sum, ffn_got, first_sum, first_got, in_got = fence(
+        ffn_sum, ffn_got, first_sum, first_got, in_got
+    )
+    ffn_rows, first_rows, second_rows = [
+        a.astype(f32) + b.astype(f32)
+        for a, b in ((ffn_sum, ffn_got), (first_sum, first_got), (second_sum, second_got))
+    ]
 
     def home(own, got):
         got = got.astype(own.dtype)
         return jnp.where(blk == 0, jnp.stack([own, got]), jnp.stack([got, own]))
 
-    hidden = home(out_hidden[:genes], hid_got)
+    hidden = home(out_hidden[:genes], jnp.concatenate(hid_got))
     in_grad = home(in_own, in_got)
-    ln2_gain_g, ln2_bias_g, out_bias_g, down_bias_g, ln1_gain_g, ln1_bias_g = [
-        sums[i * width : (i + 1) * width] for i in range(6)
-    ]
-    up_bias_g = sums[6 * width : 6 * width + shards * units]
-    q_bias_g, v_bias_g = jnp.split(sums[6 * width + shards * units :], 2)
-    wide = cuts[2][0] * 128
-    rest = width - wide
+    marks = [width] * 4 + [shards * units]
+    marks += 2 * [128 * c for c in (cut, one, pairs - cut - one)] + [width] * 2
+    pieces, at = [], 0
+    for size in marks:
+        pieces.append(sums[at : at + size])
+        at += size
+    ln2_gain_g, ln2_bias_g, out_bias_g, down_bias_g, up_bias_g = pieces[:5]
+    q_bias_g, v_bias_g = jnp.concatenate(pieces[5:8]), jnp.concatenate(pieces[8:11])
+    ln1_gain_g, ln1_bias_g = pieces[11:]
     w_qkv_grad = jnp.concatenate(
         [
             t
             for i in range(3)
             for t in (
-                first_rows[:, i * wide : (i + 1) * wide],
-                second_rows[:, i * rest : (i + 1) * rest],
+                first_rows[:, i * early : (i + 1) * early],
+                second_rows[:, i * late : (i + 1) * late],
             )
         ],
         axis=1,
@@ -1196,7 +1267,7 @@
         w_qkv_grad,
         q_bias_g,
         v_bias_g,
-        first_rows[:, 3 * wide :],
+        first_rows[:, 3 * early :],
         out_bias_g,
         ln2_gain_g,
         ln2_bias_g,

time: 580 us -> 560 us (0.966)
  between operations: 15.6 us -> 2.33 us
  waiting for transfers between devices: 96.4 us -> 84.9 us
  Pallas kernels: 331 us -> 323 us
  local copies, waits for them, and re-layouts: 25.3 us -> 32.3 us
    ppermute x61 -> x63, waiting for transfers between devices: 96.4 us -> 84.9 us  [permute(): return lax.ppermute(x, AXES, pairs)]
    ppermute x61 -> x63, starting transfers between devices: 52.4 us -> 57 us  [permute(): return lax.ppermute(x, AXES, pairs)]
    pallas_call x7 -> x6, Pallas kernels: 96.3 us -> 91.7 us  [the longest x2 34.1 us: attend_call(): pl.pallas_call(partial(attend_kernel, qrows, ahead), grid=(count,), in_sp...]
  transfers between devices with their start and end apart: 62 -> 63, of which waited for: 17 -> 18; matrix products, arithmetic and copies ran while one was open for 11% -> 13% of each run, Pallas kernels for 49% -> 51%
where the time goes in v3:
time: 560 us; the launch traced here: 552 us
  Pallas kernels  323 us (58%)
  waiting for transfers between devices  84.9 us (15%)
  starting transfers between devices  57 us (10%)
  other arithmetic  52 us (9%)
  local copies, waits for them, and re-layouts  32.3 us (6%)
    ppermute x63, waiting for transfers between devices, permute(): return lax.ppermute(x, AXES, pairs)  84.9 us
    pallas_call x2, Pallas kernels, ffn_call(): pl.pallas_call(partial(ffn_kernel, n, later), grid=(2 * half,), in_specs=...  77.9 us
    pallas_call x3, Pallas kernels, attend_back_call(): pl.pallas_call(partial(attend_back_kernel, qrows), grid=(count,), in_spec...  60.5 us
    ppermute x63, starting transfers between devices, permute(): return lax.ppermute(x, AXES, pairs)  57 us
    pallas_call x2, Pallas kernels, ffn_weights_call(): pl.pallas_call(partial(ffn_weights_kernel, n), in_specs=[ANY] * 6, out_sp...  41.6 us
    pallas_call x2, Pallas kernels, attend_call(): pl.pallas_call(partial(attend_kernel, qrows, ahead), grid=(count,), in_sp...  34.1 us
    pallas_call x2, Pallas kernels, in_call(): pl.pallas_call(partial(in_kernel, n, len(grads)), grid_spec=pltpu.Prefetc...  31.2 us
    pallas_call x2, Pallas kernels, att_weights_call(): pl.pallas_call(partial(att_weights_kernel, n, (len(lefts), len(rights)),...  30.1 us
  transfers between devices with their start and end apart: 63, of which 18 were waited for; matrix products, arithmetic and copies ran while one was open for 13% of the time, Pallas kernels for 51%

profile of v3, /device:TPU:0, one launch (start us, length us, event | category | flops | bytes accessed | tf_op | source)
XLA Modules:
  0.0 551.7 jit_solution(18372603678055313863)
XLA Ops:
  2.7 3.1 collective-permute-start
  5.9 3.4 dynamic-slice_bitcast_fusion.2
  20.5 3.8 collective-permute-done.refs_1_.refs_10_
  30.9 10.2 %collective-permute-done.4 = bf16[512,1280]{1,0:T(8,128)(2,1)} collective-permute-done((bf16[512,1280]{1,0:T(8,128)(2,1)}, bf16[512,1280]{1,0:T(8,128)(2,1)}, u32[]{:S(2)}, u32[]{:S(2)}) %collective-permute-start.4) | collective-permute-done | bytes 1310752 | tf_op jit(solution)/shard_map/ppermute | solution.py:348
  41.1 3.6 collective-permute-done.2.refs_2_.refs_11_
  51.8 6.2 %collective-permute-done.5.refs_3_.refs_12_ = bf16[80,5120]{1,0:T(8,128)(2,1)S(1)} collective-permute-done((bf16[80,5120]{1,0:T(8,128)(2,1)S(1)}, bf16[80,5120]{1,0:T(8,128)(2,1)S(1)}, u32[]{:S(2)}, u32[]{:S(2)}) %collective-permute-start.5) | collective-permute-done | bytes 819232 | tf_op jit(solution)/shard_map/ppermute | solution.py:348
  60.9 9.5 %collective-permute-done.11.refs_4_.refs_13_ = bf16[80,5120]{1,0:T(8,128)(2,1)S(1)} collective-permute-done((bf16[80,5120]{1,0:T(8,128)(2,1)S(1)}, bf16[80,5120]{1,0:T(8,128)(2,1)S(1)}, u32[]{:S(2)}, u32[]{:S(2)}) %collective-permute-start.11) | collective-permute-done | bytes 819232 | tf_op jit(solution)/shard_map/ppermute | solution.py:348
  71.7 7.5 %collective-permute-done.12.refs_7_.refs_16_ = bf16[80,5120]{1,0:T(8,128)(2,1)S(1)} collective-permute-done((bf16[80,5120]{1,0:T(8,128)(2,1)S(1)}, bf16[80,5120]{1,0:T(8,128)(2,1)S(1)}, u32[]{:S(2)}, u32[]{:S(2)}) %collective-permute-start.12) | collective-permute-done | bytes 819232 | tf_op jit(solution)/shard_map/ppermute | solution.py:348
  83.7 20.4 %qkv.1 = (bf16[1024,1280]{1,0:T(8,128)(2,1)}, bf16[1024,1280]{1,0:T(8,128)(2,1)}, bf16[1024,1280]{1,0:T(8,128)(2,1)}, bf16[1024,1280]{1,0:T(8,128)(2,1)}) custom-call(s32[16]{0:T(128)} %pad_add_fusion.2.place_ref, bf16[1024,1280]{1,0:T(8,128)(2,1)} %pad_maximum_fusion.x_ref, f32[1,1280]{1,0:T(1,128)} %reshape.227.gain_ref, f32[1,1280]{1,0:T(1,128)} %reshape.228.bias_ref, ...), custom_call_target="tpu_custom_call" | custom-call | flops 201326592 | bytes 458752 | tf_op jit(solution)/shard_map/qkv/pallas_call | solution.py:489
  106.2 20.0 %attend.2 = (bf16[1024,768]{1,0:T(8,128)(2,1)}, f32[12,1,1024]{2,1,0:T(1,128)}) custom-call(f32[1024,1]{1,0:T(8,128)} %compare_select_fusion.mask_ref, f32[1024,1]{1,0:T(8,128)} %convert_element_type.340.keep_ref, bf16[1024,1280]{1,0:T(8,128)(2,1)} %get-tuple-element.315.q_ref, bf16[1024,1280]{1,0:T(8,128)(2,1)} %get-tuple-element.316.k_ref, ...), custom_call_target="tpu_custom_call" | custom-call | flops 322122560 | bytes 125829 | tf_op jit(solution)/shard_map/attend/pallas_call | solution.py:562
  131.0 14.0 %attend.3 = (bf16[1024,512]{1,0:T(8,128)(2,1)}, f32[8,1,1024]{2,1,0:T(1,128)}) custom-call(f32[1024,1]{1,0:T(8,128)} %compare_select_fusion.mask_ref, f32[1024,1]{1,0:T(8,128)} %convert_element_type.340.keep_ref, bf16[1024,1280]{1,0:T(8,128)(2,1)} %get-tuple-element.315.q_ref, bf16[1024,1280]{1,0:T(8,128)(2,1)} %get-tuple-element.316.k_ref, ...), custom_call_target="tpu_custom_call" | custom-call | flops 214748368 | bytes 83886 | tf_op jit(solution)/shard_map/attend/pallas_call | solution.py:562
  145.1 10.9 %out.1 = (f32[1024,1280]{1,0:T(8,128)}, bf16[1024,1280]{1,0:T(8,128)(2,1)}) custom-call(s32[16]{0:T(128)} %pad_add_fusion.2.place_ref, bf16[1024,1280]{1,0:T(8,128)(2,1)} %pad_maximum_fusion.x_ref, f32[1,1280]{1,0:T(1,128)} %reshape.231.bias_ref, f32[1,1280]{1,0:T(1,128)} %reshape.232.gain_ref, f32[1,1280]{1,0:T(1,128)} %reshape.233.shift_ref, ...), custom_call_target="tpu_custom_call" | custom-call | flops 134217728 | bytes 327680 | tf_op jit(solution)/shard_map/out/pallas_call | solution.py:671
  162.8 37.3 %ffn.2 = (bf16[2048,1280]{1,0:T(8,128)(2,1)}, bf16[2048,1280]{1,0:T(8,128)(2,1)}, f32[1,1280]{1,0:T(1,128)}, f32[2048,1280]{1,0:T(8,128)}, f32[2048,1280]{1,0:T(8,128)}) custom-call(bf16[1024,1280]{1,0:T(8,128)(2,1)} %get-tuple-element.323.refs_0_.b_own, bf16[1024,1280]{1,0:T(8,128)(2,1)} %copy-done.2, bf16[1024,1280]{1,0:T(8,128)(2,1)} %copy-done.1, ...), custom_call_target="tpu_custom_call" | custom-call | flops 805306368 | bytes 629145 | tf_op jit(solution)/shard_map/ffn/pallas_call | solution.py:777
  201.7 20.8 %ffn_weights.2 = (bf16[640,1280]{1,0:T(8,128)(2,1)}, bf16[640,1280]{1,0:T(8,128)(2,1)}, bf16[640,1280]{1,0:T(8,128)(2,1)}, bf16[640,1280]{1,0:T(8,128)(2,1)}) custom-call(bf16[2048,1280]{1,0:T(8,128)(2,1)} %get-tuple-element.332.gz, bf16[2048,1280]{1,0:T(8,128)(2,1)} %get-tuple-element.333.h, bf16[1024,1280]{1,0:T(8,128)(2,1)} %get-tuple-element.323.refs_0_.b_own, ...), custom_call_target="tpu_custom_call" | custom-call | flops 402653184 | bytes 419430 | tf_op jit(solution)/shard_map/ffn_weights/pallas_call | solution.py:840
  223.7 40.6 %ffn.3 = (bf16[2048,1280]{1,0:T(8,128)(2,1)}, bf16[2048,1280]{1,0:T(8,128)(2,1)}, f32[1,1280]{1,0:T(1,128)}, bf16[1024,1280]{1,0:T(8,128)(2,1)}, bf16[1024,1280]...) custom-call(bf16[1024,1280]{1,0:T(8,128)(2,1)} %get-tuple-element.323.refs_0_.b_own, ...), custom_call_target="tpu_custom_call" | custom-call | flops 805306368 | bytes 1048576 | tf_op jit(solution)/shard_map/ffn/pallas_call | solution.py:777
  264.9 20.8 %ffn_weights.3 = (bf16[640,1280]{1,0:T(8,128)(2,1)}, bf16[640,1280]{1,0:T(8,128)(2,1)}, bf16[640,1280]{1,0:T(8,128)(2,1)}, bf16[640,1280]{1,0:T(8,128)(2,1)}) custom-call(bf16[2048,1280]{1,0:T(8,128)(2,1)} %get-tuple-element.342.gz, bf16[2048,1280]{1,0:T(8,128)(2,1)} %get-tuple-element.343.h, bf16[1024,1280]{1,0:T(8,128)(2,1)} %get-tuple-element.323.refs_0_.b_own, ...), custom_call_target="tpu_custom_call" | custom-call | flops 402653184 | bytes 419430 | tf_op jit(solution)/shard_map/ffn_weights/pallas_call | solution.py:840
  290.6 16.6 %mid.1 = (bf16[1024,1280]{1,0:T(8,128)(2,1)}, bf16[1024,1280]{1,0:T(8,128)(2,1)}, bf16[1024,1280]{1,0:T(8,128)(2,1)}, f32[8,1280]{1,0:T(8,128)}) custom-call(s32[16]{0:T(128)} %pad_add_fusion.2.place_ref, bf16[1024,1280]{1,0:T(8,128)(2,1)} %get-tuple-element.351.oo_ref, bf16[1024,1280]{1,0:T(8,128)(2,1)} %copy-done.23, ...), custom_call_target="tpu_custom_call" | custom-call | flops 134217728 | bytes 851968 | tf_op jit(solution)/shard_map/mid/pallas_call | solution.py:890
  307.2 34.6 %attend_back.3 = (bf16[1024,768]{1,0:T(8,128)(2,1)}, bf16[1024,768]{1,0:T(8,128)(2,1)}, bf16[1024,768]{1,0:T(8,128)(2,1)}, f32[1,768]{1,0:T(1,128)}, f32[1,768]{1,0:T(1,128)}) custom-call(f32[1024,1]{1,0:T(8,128)} %compare_select_fusion.mask_ref, bf16[1024,1280]{1,0:T(8,128)(2,1)} %get-tuple-element.315.q_ref, bf16[1024,1280]{1,0:T(8,128)(2,1)} %get-tuple-element.316.k_ref, ...), custom_call_target="tpu_custom_call" | custom-call | flops 515396064 | bytes 251658 | tf_op jit(solution)/shard_map/attend_back/pallas_call | solution.py:625
  343.7 3.8 add_convert_fusion.3
  351.2 20.2 %att_weights.2 = (bf16[80,3584]{1,0:T(8,128)(2,1)}, bf16[80,3584]{1,0:T(8,128)(2,1)}, bf16[80,3584]{1,0:T(8,128)(2,1)}, bf16[80,3584]{1,0:T(8,128)(2,1)}, bf16[8...) custom-call(s32[16]{0:T(128)} %pad_add_fusion.2.place_ref, ...), custom_call_target="tpu_custom_call" | custom-call | flops 281857216 | bytes 330301 | tf_op jit(solution)/shard_map/att_weights/pallas_call | solution.py:955
  371.8 3.2 add_convert_fusion.2
  376.6 7.5 %attend_back.4 = (bf16[1024,128]{1,0:T(8,128)(2,1)}, bf16[1024,128]{1,0:T(8,128)(2,1)}, bf16[1024,128]{1,0:T(8,128)(2,1)}, f32[1,128]{1,0:T(1,128)}, f32[1,128]{1,0:T(1,128)}) custom-call(f32[1024,1]{1,0:T(8,128)} %compare_select_fusion.mask_ref, bf16[1024,1280]{1,0:T(8,128)(2,1)} %get-tuple-element.315.q_ref, bf16[1024,1280]{1,0:T(8,128)(2,1)} %get-tuple-element.316.k_ref, ...), custom_call_target="tpu_custom_call" | custom-call | flops 85899344 | bytes 41943 | tf_op jit(solution)/shard_map/attend_back/pallas_call | solution.py:625
  388.7 18.4 %attend_back.5 = (bf16[1024,384]{1,0:T(8,128)(2,1)}, bf16[1024,384]{1,0:T(8,128)(2,1)}, bf16[1024,384]{1,0:T(8,128)(2,1)}, f32[1,384]{1,0:T(1,128)}, f32[1,384]{1,0:T(1,128)}) custom-call(f32[1024,1]{1,0:T(8,128)} %compare_select_fusion.mask_ref, bf16[1024,1280]{1,0:T(8,128)(2,1)} %get-tuple-element.315.q_ref, bf16[1024,1280]{1,0:T(8,128)(2,1)} %get-tuple-element.316.k_ref, ...), custom_call_target="tpu_custom_call" | custom-call | flops 257698032 | bytes 125829 | tf_op jit(solution)/shard_map/attend_back/pallas_call | solution.py:625
  414.6 15.4 %in.2 = (bf16[512,1280]{1,0:T(8,128)(2,1)}, f32[8,1280]{1,0:T(8,128)}) custom-call(s32[16]{0:T(128)} %pad_add_fusion.2.place_ref, bf16[1024,1280]{1,0:T(8,128)(2,1)} %pad_maximum_fusion.x_ref, bf16[1024,1280]{1,0:T(8,128)(2,1)} %get-tuple-element.357.refs_5_.gr_ref, f32[1,1280]{1,0:T(1,128)} %reshape.227.gain_ref, ...), custom_call_target="tpu_custom_call" | custom-call | flops 134217728 | bytes 380108 | tf_op jit(solution)/shard_map/in/pallas_call | solution.py:1013
  430.1 3.2 fusion.3
  436.2 9.8 %att_weights.3 = (bf16[80,1536]{1,0:T(8,128)(2,1)}, bf16[80,1536]{1,0:T(8,128)(2,1)}, bf16[80,1536]{1,0:T(8,128)(2,1)}, bf16[80,1536]{1,0:T(8,128)(2,1)}, bf16[8...) custom-call(s32[16]{0:T(128)} %pad_add_fusion.2.place_ref, ...), custom_call_target="tpu_custom_call" | custom-call | flops 120795952 | bytes 141557 | tf_op jit(solution)/shard_map/att_weights/pallas_call | solution.py:955
  446.1 4.9 collective-permute-done.42
  456.8 3.0 fusion.1
  467.2 15.8 %in.3 = (f32[512,1280]{1,0:T(8,128)}, f32[8,1280]{1,0:T(8,128)}) custom-call(s32[16]{0:T(128)} %pad_add_fusion.2.place_ref, bf16[1024,1280]{1,0:T(8,128)(2,1)} %pad_maximum_fusion.x_ref, bf16[1024,1280]{1,0:T(8,128)(2,1)} %get-tuple-element.357.refs_5_.gr_ref, f32[1,1280]{1,0:T(1,128)} %reshape.227.gain_ref, ...), custom_call_target="tpu_custom_call" | custom-call | flops 134217728 | bytes 380108 | tf_op jit(solution)/shard_map/in/pallas_call | solution.py:1013
  508.1 13.8 %collective-permute-done.49 = bf16[640,1280]{1,0:T(8,128)(2,1)} collective-permute-done((bf16[640,1280]{1,0:T(8,128)(2,1)S(1)}, bf16[640,1280]{1,0:T(8,128)(2,1)}, u32[]{:S(2)}, u32[]{:S(2)}) %collective-permute-start.49) | collective-permute-done | bytes 1638432 | tf_op jit(solution)/shard_map/ppermute | solution.py:348
  521.9 10.5 %collective-permute-done.50 = bf16[80,3584]{1,0:T(8,128)(2,1)S(1)} collective-permute-done((bf16[80,3584]{1,0:T(8,128)(2,1)S(1)}, bf16[80,3584]{1,0:T(8,128)(2,1)S(1)}, u32[]{:S(2)}, u32[]{:S(2)}) %collective-permute-start.50) | collective-permute-done | bytes 573472 | tf_op jit(solution)/shard_map/ppermute | solution.py:348
  544.1 4.7 collective-permute-done.61
  (356 shorter events, 131.7 us)
Async XLA Ops:
  2.7 21.5 %collective-permute-start = (bf16[80,5120]{1,0:T(8,128)(2,1)S(1)}, bf16[80,5120]{1,0:T(8,128)(2,1)S(1)}, u32[]{:S(2)}, u32[]{:S(2)}) collective-permute-start(bf16[80,5120]{1,0:T(8,128)(2,1)S(1)} %constant_dynamic-update-slice_fusion.refs_0_.refs_9_), channel_id=1, source_target_pairs={{0,8},{1,5},{2,6},{3,11},{4,0},{5,13},{6,14},{7,3},{8,16},{9,1},{1... | collective-permute-start | bytes 2457608 | tf_op jit(solution)/shard_map/ppermute | solution.py:348
  5.8 41.2 %collective-permute-start.6 = (bf16[80,5120]{1,0:T(8,128)(2,1)S(1)}, bf16[80,5120]{1,0:T(8,128)(2,1)S(1)}, u32[]{:S(2)}, u32[]{:S(2)}) collective-permute-start(bf16[80,5120]{1,0:T(8,128)(2,1)S(1)} %constant_dynamic-update-slice_fusion.refs_0_.refs_9_), channel_id=1, source_target_pairs={{0,2},{1,3},{2,0},{3,1},{4,6},{5,7},{6,4},{7,5},{8,10},{9,11},{10,... | collective-permute-start | bytes 2457608 | tf_op jit(solution)/shard_map/ppermute | solution.py:348
  9.3 31.8 %collective-permute-start.4 = (bf16[512,1280]{1,0:T(8,128)(2,1)}, bf16[512,1280]{1,0:T(8,128)(2,1)}, u32[]{:S(2)}, u32[]{:S(2)}) collective-permute-start(bf16[512,1280]{1,0:T(8,128)(2,1)} %get-tuple-element.558), channel_id=1, source_target_pairs={{0,1},{1,0},{2,3},{3,2},{4,5},{5,4},{6,7},{7,6},{8,9},{9,8},{10,11... | collective-permute-start | bytes 3932168 | tf_op jit(solution)/shard_map/ppermute | solution.py:348
  70.4 33.7 %collective-permute-start.16 = (bf16[640,1280]{1,0:T(8,128)(2,1)}, bf16[640,1280]{1,0:T(8,128)(2,1)}, u32[]{:S(2)}, u32[]{:S(2)}) collective-permute-start(bf16[640,1280]{1,0:T(8,128)(2,1)} %pad_maximum_fusion.3.refs_5_), channel_id=1, source_target_pairs={{0,8},{1,5},{2,6},{3,11},{4,0},{5,13},{6,14},{7,3},{8,16},{9,1},{1... | collective-permute-start | bytes 4915208 | tf_op jit(solution)/shard_map/ppermute | solution.py:348
  80.9 23.2 %collective-permute-start.17 = (bf16[256,1280]{1,0:T(8,128)(2,1)}, bf16[256,1280]{1,0:T(8,128)(2,1)}, u32[]{:S(2)}, u32[]{:S(2)}) collective-permute-start(bf16[256,1280]{1,0:T(8,128)(2,1)} %get-tuple-element.566), channel_id=1, source_target_pairs={{0,1},{1,0},{2,3},{3,2},{4,5},{5,4},{6,7},{7,6},{8,9},{9,8},{10,11... | collective-permute-start | bytes 1966088 | tf_op jit(solution)/shard_map/ppermute | solution.py:348
  104.2 22.1 %collective-permute-start.18 = (bf16[640,1280]{1,0:T(8,128)(2,1)}, bf16[640,1280]{1,0:T(8,128)(2,1)}, u32[]{:S(2)}, u32[]{:S(2)}) collective-permute-start(bf16[640,1280]{1,0:T(8,128)(2,1)} %collective-permute-done.16.refs_6_), channel_id=1, source_target_pairs={{0,8},{1,5},{2,6},{3,11},{4,0},{5,13},{6,14},{7,3},{8,16},{9,1},{1... | collective-permute-start | bytes 4915208 | tf_op jit(solution)/shard_map/ppermute | solution.py:348
  128.5 27.5 %collective-permute-start.20 = (bf16[1024,1280]{1,0:T(8,128)(2,1)S(1)}, bf16[1024,1280]{1,0:T(8,128)(2,1)}, u32[]{:S(2)}, u32[]{:S(2)}) collective-permute-start(bf16[1024,1280]{1,0:T(8,128)(2,1)S(1)} %pad_maximum_fusion.1.refs_2_.g_own.g_ref), channel_id=1, source_target_pairs={{0,2},{1,3},{2,0},{3,1},{4,6},{5,7},{6,4},{7,5},{8,10},{9,11},{10,... | collective-permute-start | bytes 7864328 | tf_op jit(solution)/shard_map/ppermute | solution.py:348
  129.3 26.7 %collective-permute-start.21 = (bf16[640,1280]{1,0:T(8,128)(2,1)}, bf16[640,1280]{1,0:T(8,128)(2,1)}, u32[]{:S(2)}, u32[]{:S(2)}) collective-permute-start(bf16[640,1280]{1,0:T(8,128)(2,1)} %collective-permute-done.18.refs_7_), channel_id=1, source_target_pairs={{0,8},{1,5},{2,6},{3,11},{4,0},{5,13},{6,14},{7,3},{8,16},{9,1},{1... | collective-permute-start | bytes 4915208 | tf_op jit(solution)/shard_map/ppermute | solution.py:348
  156.1 44.0 %collective-permute-start.24 = (bf16[640,1280]{1,0:T(8,128)(2,1)}, bf16[640,1280]{1,0:T(8,128)(2,1)}, u32[]{:S(2)}, u32[]{:S(2)}) collective-permute-start(bf16[640,1280]{1,0:T(8,128)(2,1)} %pad_maximum_fusion.3.refs_5_), channel_id=1, source_target_pairs={{0,4},{1,9},{2,10},{3,7},{4,12},{5,1},{6,2},{7,15},{8,0},{9,17},{1... | collective-permute-start | bytes 4915208 | tf_op jit(solution)/shard_map/ppermute | solution.py:348
  158.0 64.5 %collective-permute-start.23 = (bf16[640,1280]{1,0:T(8,128)(2,1)}, bf16[640,1280]{1,0:T(8,128)(2,1)}, u32[]{:S(2)}, u32[]{:S(2)}) collective-permute-start(bf16[640,1280]{1,0:T(8,128)(2,1)} %collective-permute-done.21.refs_8_), channel_id=1, source_target_pairs={{0,8},{1,5},{2,6},{3,11},{4,0},{5,13},{6,14},{7,3},{8,16},{9,1},{1... | collective-permute-start | bytes 4915208 | tf_op jit(solution)/shard_map/ppermute | solution.py:348
  159.6 62.9 %collective-permute-start.26 = (bf16[640,1280]{1,0:T(8,128)(2,1)}, bf16[640,1280]{1,0:T(8,128)(2,1)}, u32[]{:S(2)}, u32[]{:S(2)}) collective-permute-start(bf16[640,1280]{1,0:T(8,128)(2,1)} %collective-permute-done.21.refs_8_), channel_id=1, source_target_pairs={{0,1},{1,0},{2,3},{3,2},{4,5},{5,4},{6,7},{7,6},{8,9},{9,8},{10,11... | collective-permute-start | bytes 4915208 | tf_op jit(solution)/shard_map/ppermute | solution.py:348
  200.1 22.4 %collective-permute-start.25 = (bf16[640,1280]{1,0:T(8,128)(2,1)}, bf16[640,1280]{1,0:T(8,128)(2,1)S(1)}, u32[]{:S(2)}, u32[]{:S(2)}) collective-permute-start(bf16[640,1280]{1,0:T(8,128)(2,1)} %collective-permute-done.24.refs_6_), channel_id=1, source_target_pairs={{0,4},{1,9},{2,10},{3,7},{4,12},{5,1},{6,2},{7,15},{8,0},{9,17},{1... | collective-permute-start | bytes 4915208 | tf_op jit(solution)/shard_map/ppermute | solution.py:348
  264.3 21.4 %collective-permute-start.27 = (bf16[1024,1280]{1,0:T(8,128)(2,1)}, bf16[1024,1280]{1,0:T(8,128)(2,1)S(1)}, u32[]{:S(2)}, u32[]{:S(2)}) collective-permute-start(bf16[1024,1280]{1,0:T(8,128)(2,1)} %get-tuple-element.349), channel_id=1, source_target_pairs={{0,2},{1,3},{2,0},{3,1},{4,6},{5,7},{6,4},{7,5},{8,10},{9,11},{10,... | collective-permute-start | bytes 7864328 | tf_op jit(solution)/shard_map/ppermute | solution.py:348
  264.7 21.0 %collective-permute-start.28 = (bf16[1024,1280]{1,0:T(8,128)(2,1)}, bf16[1024,1280]{1,0:T(8,128)(2,1)}, u32[]{:S(2)}, u32[]{:S(2)}) collective-permute-start(bf16[1024,1280]{1,0:T(8,128)(2,1)} %get-tuple-element.350), channel_id=1, source_target_pairs={{0,2},{1,3},{2,0},{3,1},{4,6},{5,7},{6,4},{7,5},{8,10},{9,11},{10,... | collective-permute-start | bytes 7864328 | tf_op jit(solution)/shard_map/ppermute | solution.py:348
  285.7 57.2 %collective-permute-start.29 = (bf16[640,1280]{1,0:T(8,128)(2,1)}, bf16[640,1280]{1,0:T(8,128)(2,1)}, u32[]{:S(2)}, u32[]{:S(2)}) collective-permute-start(bf16[640,1280]{1,0:T(8,128)(2,1)} %get-tuple-element.365), channel_id=1, source_target_pairs={{0,4},{1,9},{2,10},{3,7},{4,12},{5,1},{6,2},{7,15},{8,0},{9,17},{1... | collective-permute-start | bytes 4915208 | tf_op jit(solution)/shard_map/ppermute | solution.py:348
  286.8 56.2 %collective-permute-start.30 = (bf16[640,1280]{1,0:T(8,128)(2,1)}, bf16[640,1280]{1,0:T(8,128)(2,1)}, u32[]{:S(2)}, u32[]{:S(2)}) collective-permute-start(bf16[640,1280]{1,0:T(8,128)(2,1)} %get-tuple-element.366), channel_id=1, source_target_pairs={{0,1},{1,0},{2,3},{3,2},{4,5},{5,4},{6,7},{7,6},{8,9},{9,8},{10,11... | collective-permute-start | bytes 4915208 | tf_op jit(solution)/shard_map/ppermute | solution.py:348
  288.9 82.6 %collective-permute-start.32 = (bf16[640,1280]{1,0:T(8,128)(2,1)}, bf16[640,1280]{1,0:T(8,128)(2,1)}, u32[]{:S(2)}, u32[]{:S(2)}) collective-permute-start(bf16[640,1280]{1,0:T(8,128)(2,1)} %get-tuple-element.386), channel_id=1, source_target_pairs={{0,8},{1,5},{2,6},{3,11},{4,0},{5,13},{6,14},{7,3},{8,16},{9,1},{1... | collective-permute-start | bytes 4915208 | tf_op jit(solution)/shard_map/ppermute | solution.py:348
  289.4 82.1 %collective-permute-start.33 = (bf16[640,1280]{1,0:T(8,128)(2,1)}, bf16[640,1280]{1,0:T(8,128)(2,1)}, u32[]{:S(2)}, u32[]{:S(2)}) collective-permute-start(bf16[640,1280]{1,0:T(8,128)(2,1)} %get-tuple-element.387), channel_id=1, source_target_pairs={{0,1},{1,0},{2,3},{3,2},{4,5},{5,4},{6,7},{7,6},{8,9},{9,8},{10,11... | collective-permute-start | bytes 4915208 | tf_op jit(solution)/shard_map/ppermute | solution.py:348
  347.5 24.0 %collective-permute-start.31 = (bf16[640,1280]{1,0:T(8,128)(2,1)}, bf16[640,1280]{1,0:T(8,128)(2,1)S(1)}, u32[]{:S(2)}, u32[]{:S(2)}) collective-permute-start(bf16[640,1280]{1,0:T(8,128)(2,1)} %add_convert_fusion.3), channel_id=1, source_target_pairs={{0,4},{1,9},{2,10},{3,7},{4,12},{5,1},{6,2},{7,15},{8,0},{9,17},{1... | collective-permute-start | bytes 4915208 | tf_op jit(solution)/shard_map/ppermute | solution.py:348
  375.1 32.0 %collective-permute-start.37 = (bf16[640,1280]{1,0:T(8,128)(2,1)}, bf16[640,1280]{1,0:T(8,128)(2,1)S(1)}, u32[]{:S(2)}, u32[]{:S(2)}) collective-permute-start(bf16[640,1280]{1,0:T(8,128)(2,1)} %add_convert_fusion.2), channel_id=1, source_target_pairs={{0,4},{1,9},{2,10},{3,7},{4,12},{5,1},{6,2},{7,15},{8,0},{9,17},{1... | collective-permute-start | bytes 4915208 | tf_op jit(solution)/shard_map/ppermute | solution.py:348
  376.1 31.0 %collective-permute-start.38 = (bf16[256,1280]{1,0:T(8,128)(2,1)}, bf16[256,1280]{1,0:T(8,128)(2,1)S(1)}, u32[]{:S(2)}, u32[]{:S(2)}) collective-permute-start(bf16[256,1280]{1,0:T(8,128)(2,1)} %get-tuple-element.431), channel_id=1, source_target_pairs={{0,1},{1,0},{2,3},{3,2},{4,5},{5,4},{6,7},{7,6},{8,9},{9,8},{10,11... | collective-permute-start | bytes 1966088 | tf_op jit(solution)/shard_map/ppermute | solution.py:348
  386.6 22.2 %collective-permute-start.35 = (bf16[80,3584]{1,0:T(8,128)(2,1)}, bf16[80,3584]{1,0:T(8,128)(2,1)S(1)}, u32[]{:S(2)}, u32[]{:S(2)}) collective-permute-start(bf16[80,3584]{1,0:T(8,128)(2,1)} %get-tuple-element.550), channel_id=1, source_target_pairs={{0,4},{1,9},{2,10},{3,7},{4,12},{5,1},{6,2},{7,15},{8,0},{9,17},{1... | collective-permute-start | bytes 1720328 | tf_op jit(solution)/shard_map/ppermute | solution.py:348
  413.1 37.9 %collective-permute-start.41 = (bf16[640,1280]{1,0:T(8,128)(2,1)S(1)}, bf16[640,1280]{1,0:T(8,128)(2,1)S(1)}, u32[]{:S(2)}, u32[]{:S(2)}) collective-permute-start(bf16[640,1280]{1,0:T(8,128)(2,1)S(1)} %add_convert_fusion.1), channel_id=1, source_target_pairs={{0,4},{1,9},{2,10},{3,7},{4,12},{5,1},{6,2},{7,15},{8,0},{9,17},{1... | collective-permute-start | bytes 4915208 | tf_op jit(solution)/shard_map/ppermute | solution.py:348
  453.6 53.8 %collective-permute-start.51 = (bf16[512,1280]{1,0:T(8,128)(2,1)}, bf16[512,1280]{1,0:T(8,128)(2,1)}, u32[]{:S(2)}, u32[]{:S(2)}) collective-permute-start(bf16[512,1280]{1,0:T(8,128)(2,1)} %get-tuple-element.506), channel_id=1, source_target_pairs={{0,1},{1,0},{2,3},{3,2},{4,5},{5,4},{6,7},{7,6},{8,9},{9,8},{10,11... | collective-permute-start | bytes 3932168 | tf_op jit(solution)/shard_map/ppermute | solution.py:348
  459.8 23.1 %collective-permute-start.44 = (bf16[80,3584]{1,0:T(8,128)(2,1)}, bf16[80,3584]{1,0:T(8,128)(2,1)}, u32[]{:S(2)}, u32[]{:S(2)}) collective-permute-start(bf16[80,3584]{1,0:T(8,128)(2,1)} %get-tuple-element.546), channel_id=1, source_target_pairs={{0,4},{1,9},{2,10},{3,7},{4,12},{5,1},{6,2},{7,15},{8,0},{9,17},{1... | collective-permute-start | bytes 1720328 | tf_op jit(solution)/shard_map/ppermute | solution.py:348
  460.8 23.6 %collective-permute-start.45 = (bf16[80,3584]{1,0:T(8,128)(2,1)S(1)}, bf16[80,3584]{1,0:T(8,128)(2,1)}, u32[]{:S(2)}, u32[]{:S(2)}) collective-permute-start(bf16[80,3584]{1,0:T(8,128)(2,1)S(1)} %get-tuple-element.545), channel_id=1, source_target_pairs={{0,8},{1,5},{2,6},{3,11},{4,0},{5,13},{6,14},{7,3},{8,16},{9,1},{1... | collective-permute-start | bytes 1720328 | tf_op jit(solution)/shard_map/ppermute | solution.py:348
  462.9 21.5 %collective-permute-start.47 = (bf16[80,1536]{1,0:T(8,128)(2,1)}, bf16[80,1536]{1,0:T(8,128)(2,1)}, u32[]{:S(2)}, u32[]{:S(2)}) collective-permute-start(bf16[80,1536]{1,0:T(8,128)(2,1)} %get-tuple-element.564), channel_id=1, source_target_pairs={{0,4},{1,9},{2,10},{3,7},{4,12},{5,1},{6,2},{7,15},{8,0},{9,17},{1... | collective-permute-start | bytes 737288 | tf_op jit(solution)/shard_map/ppermute | solution.py:348
  483.0 38.9 %collective-permute-start.49 = (bf16[640,1280]{1,0:T(8,128)(2,1)S(1)}, bf16[640,1280]{1,0:T(8,128)(2,1)}, u32[]{:S(2)}, u32[]{:S(2)}) collective-permute-start(bf16[640,1280]{1,0:T(8,128)(2,1)S(1)} %add_convert_fusion), channel_id=1, source_target_pairs={{0,1},{1,0},{2,3},{3,2},{4,5},{5,4},{6,7},{7,6},{8,9},{9,8},{10,11... | collective-permute-start | bytes 4915208 | tf_op jit(solution)/shard_map/ppermute | solution.py:348
  492.3 40.2 %collective-permute-start.50 = (bf16[80,3584]{1,0:T(8,128)(2,1)S(1)}, bf16[80,3584]{1,0:T(8,128)(2,1)S(1)}, u32[]{:S(2)}, u32[]{:S(2)}) collective-permute-start(bf16[80,3584]{1,0:T(8,128)(2,1)S(1)} %fusion), channel_id=1, source_target_pairs={{0,1},{1,0},{2,3},{3,2},{4,5},{5,4},{6,7},{7,6},{8,9},{9,8},{10,11... | collective-permute-start | bytes 1720328 | tf_op jit(solution)/shard_map/ppermute | solution.py:348
  504.9 36.0 %collective-permute-start.60 = (f32[15360]{0:T(1024)S(1)}, f32[15360]{0:T(1024)S(1)}, u32[]{:S(2)}, u32[]{:S(2)}) collective-permute-start(f32[15360]{0:T(1024)S(1)} %add.370), channel_id=1, source_target_pairs={{0,16},{1,17},{2,18},{3,19},{4,20},{5,21},{6,22},{7,23},{8,24},{9,... | collective-permute-start | bytes 184328 | tf_op jit(solution)/shard_map/ppermute | solution.py:348
  505.9 35.0 %collective-permute-start.58 = (bf16[80,1536]{1,0:T(8,128)(2,1)S(1)}, bf16[80,1536]{1,0:T(8,128)(2,1)S(1)}, u32[]{:S(2)}, u32[]{:S(2)}) collective-permute-start(bf16[80,1536]{1,0:T(8,128)(2,1)S(1)} %get-tuple-element.560), channel_id=1, source_target_pairs={{0,4},{1,9},{2,10},{3,7},{4,12},{5,1},{6,2},{7,15},{8,0},{9,17},{1... | collective-permute-start | bytes 737288 | tf_op jit(solution)/shard_map/ppermute | solution.py:348
  507.4 33.5 %collective-permute-start.59 = (bf16[80,1536]{1,0:T(8,128)(2,1)S(1)}, bf16[80,1536]{1,0:T(8,128)(2,1)S(1)}, u32[]{:S(2)}, u32[]{:S(2)}) collective-permute-start(bf16[80,1536]{1,0:T(8,128)(2,1)S(1)} %get-tuple-element.559), channel_id=1, source_target_pairs={{0,8},{1,5},{2,6},{3,11},{4,0},{5,13},{6,14},{7,3},{8,16},{9,1},{1... | collective-permute-start | bytes 737288 | tf_op jit(solution)/shard_map/ppermute | solution.py:348
  (107 other events, 1024.8 us)

commit v4 on v3

--- a/solution.py
+++ b/solution.py
@@ -904,11 +904,23 @@
 
 
 def att_weights_kernel(n, counts, blocks, place_ref, *refs):
-    lefts, rights = refs[: counts[0]], refs[counts[0] : sum(counts)]
-    refs = refs[sum(counts) :]
+    lefts, at = [], 0
+    for count in counts[:-1]:
+        lefts.append(refs[at : at + count])
+        at += count
+    rights, refs = refs[at : at + counts[-1]], refs[at + counts[-1] :]
     outs, (lv, tv, rv, ov, lsem, rsem, osem) = refs[: n + 1], refs[n + 1 :]
     height = outs[0].shape[0]
-    loads = [pltpu.make_async_copy(r, lv.at[i], lsem.at[i]) for i, r in enumerate(lefts)]
+    loads = []
+    for i, pieces in enumerate(lefts):
+        loads.append([])
+        at = 0
+        for j, r in enumerate(pieces):
+            wide = r.shape[1]
+            loads[-1].append(
+                pltpu.make_async_copy(r, lv.at[i, :, pl.ds(at, wide)], lsem.at[i, j])
+            )
+            at += wide
     ends, right_loads = [], []
     for i, r in enumerate(rights):
         start = ends[-1] if ends else 0
@@ -916,13 +928,14 @@
         right_loads.append(
             pltpu.make_async_copy(r, rv.at[:, pl.ds(start, r.shape[1])], rsem.at[i])
         )
-    for c in loads[:1] + right_loads + loads[1:]:
+    for c in loads[0] + right_loads + [c for group in loads[1:] for c in group]:
         c.start()
     have, arrived = set(), 0
     stores = []
     for step, (left, start, wide) in enumerate(blocks):
         if left not in have:
-            loads[left].wait()
+            for c in loads[left]:
+                c.wait()
             tv[left] = jnp.transpose(lv[left])
             have.add(left)
         while arrived < len(ends) and (arrived == 0 or ends[arrived - 1] < start + wide):
@@ -947,24 +960,24 @@
 
 
 def att_weights_call(place, lefts, rights, blocks):
-    rows, width = lefts[0].shape
+    rows, width = lefts[0][0].shape[0], sum(l.shape[1] for l in lefts[0])
     n = len(OFFSETS)
     total = sum(r.shape[1] for r in rights)
     wide = max(b[2] for b in blocks)
     height = width // (2 * n)
     return pl.pallas_call(
-        partial(att_weights_kernel, n, (len(lefts), len(rights)), blocks),
+        partial(att_weights_kernel, n, [len(l) for l in lefts] + [len(rights)], blocks),
         grid_spec=pltpu.PrefetchScalarGridSpec(
             num_scalar_prefetch=1,
             grid=(1,),
-            in_specs=[ANY] * (len(lefts) + len(rights)),
+            in_specs=[ANY] * (sum(len(l) for l in lefts) + len(rights)),
             out_specs=[ANY] * (n + 1),
             scratch_shapes=[
                 pltpu.VMEM((len(lefts), rows, width), bf16),
                 pltpu.VMEM((len(lefts), width, rows), bf16),
                 pltpu.VMEM((rows, total), bf16),
                 pltpu.VMEM((2, width, wide), bf16),
-                pltpu.SemaphoreType.DMA((len(lefts),)),
+                pltpu.SemaphoreType.DMA((len(lefts), max(len(l) for l in lefts))),
                 pltpu.SemaphoreType.DMA((len(rights),)),
                 pltpu.SemaphoreType.DMA((2, 2 * n)),
             ],
@@ -973,7 +986,7 @@
         compiler_params=params(),
         cost_estimate=cost(3 * rows * width * total, 2 * (rows + width) * total),
         name="att_weights",
-    )(place, *lefts, *rights)
+    )(place, *[a for l in lefts for a in l], *rights)
 
 
 def in_kernel(n, pieces, place_ref, x_ref, gr_ref, gain_ref, *refs):
@@ -1166,7 +1179,7 @@
     )
     way = steps.send(way)
     first = att_weights_call(
-        place, [a, jnp.concatenate(o_parts, axis=1)], list(backs[0][:3]) + [gr],
+        place, [[a], o_parts], list(backs[0][:3]) + [gr],
         [(0, i * early, early) for i in range(3)] + [(1, 3 * early + i * half, half) for i in range(2)],
     )
     first, gatt, way, hid_send = fence(first, gatt, way, hid_send)
@@ -1189,17 +1202,21 @@
         [mid_sums[:4].reshape(-1), up_rows.reshape(-1)]
         + [t[i].reshape(-1) for i in (3, 4) for t in backs]
     )
-    in_send, backs, way_first, hid_got = fence(in_send, backs, way_first, hid_got)
+    in_send, backs, way_first, hid_got, way = fence(in_send, backs, way_first, hid_got, way)
+    ffn_sum = steps.send(way)
+    ffn_sum = [ffn_sum[:units], ffn_sum[units:]]
+    ffn_got = [ring.swap_blk(ffn_sum[0])]
     way_first = steps_first.send(way_first)
     in_got = ring.swap_blk(in_send)
     second = att_weights_call(
-        place, [a], [t[i] for i in range(3) for t in backs[1:]],
+        place, [[a]], [t[i] for i in range(3) for t in backs[1:]],
         [(0, i * late, late) for i in range(3)],
     )
-    second, way, way_first, grads, sums_early = fence(second, way, way_first, grads, sums_early)
+    second, way_first, grads, sums_early, ffn_got, ffn_sum = fence(
+        second, way_first, grads, sums_early, ffn_got, ffn_sum
+    )
+    ffn_got.append(ring.swap_blk(ffn_sum[1]))
     way_first = steps_first.send(way_first)
-    ffn_sum = steps.send(way)
-    ffn_got = ring.swap_blk(ffn_sum)
     second_sib = ring.swap_core(second[n])
     steps_second = ring.reduce([[second[s], second_sib[s]] for s in range(n)], 3)
     way_second = next(steps_second)
@@ -1228,9 +1245,9 @@
     ffn_sum, ffn_got, first_sum, first_got, in_got = fence(
         ffn_sum, ffn_got, first_sum, first_got, in_got
     )
-    ffn_rows, first_rows, second_rows = [
-        a.astype(f32) + b.astype(f32)
-        for a, b in ((ffn_sum, ffn_got), (first_sum, first_got), (second_sum, second_got))
+    sums_own, sums_got = ffn_sum + [first_sum, second_sum], ffn_got + [first_got, second_got]
+    w_up_grad, w_down_grad, first_rows, second_rows = [
+        a.astype(f32) + b.astype(f32) for a, b in zip(sums_own, sums_got, strict=True)
     ]
 
     def home(own, got):
@@ -1271,9 +1288,9 @@
         out_bias_g,
         ln2_gain_g,
         ln2_bias_g,
-        ffn_rows[:units],
+        w_up_grad,
         up_bias_g,
-        ffn_rows[units:],
+        w_down_grad,
         down_bias_g,
     )
 

time: 560 us -> 550 us (0.982)
  waiting for transfers between devices: 84.9 us -> 73.4 us
    ppermute x63 -> x64, waiting for transfers between devices: 84.9 us -> 73.4 us  [permute(): return lax.ppermute(x, AXES, pairs)]
    ppermute x63 -> x64, starting transfers between devices: 57 us -> 60.3 us  [permute(): return lax.ppermute(x, AXES, pairs)]
  transfers between devices with their start and end apart: 63 -> 64, of which waited for: 18 -> 19; matrix products, arithmetic and copies ran while one was open for 13% -> 12% of each run, Pallas kernels for 51% -> 52%
where the time goes in v4:
time: 550 us; the launch traced here: 542 us
  Pallas kernels  323 us (59%)
  waiting for transfers between devices  73.4 us (13%)
  starting transfers between devices  60.3 us (11%)
  other arithmetic  51.6 us (9%)
  local copies, waits for them, and re-layouts  31.6 us (6%)
    pallas_call x2, Pallas kernels, ffn_call(): pl.pallas_call(partial(ffn_kernel, n, later), grid=(2 * half,), in_specs=...  77.9 us
    ppermute x64, waiting for transfers between devices, permute(): return lax.ppermute(x, AXES, pairs)  73.4 us
    pallas_call x3, Pallas kernels, attend_back_call(): pl.pallas_call(partial(attend_back_kernel, qrows), grid=(count,), in_spec...  60.5 us
    ppermute x64, starting transfers between devices, permute(): return lax.ppermute(x, AXES, pairs)  60.3 us
    pallas_call x2, Pallas kernels, ffn_weights_call(): pl.pallas_call(partial(ffn_weights_kernel, n), in_specs=[ANY] * 6, out_sp...  41.6 us
    pallas_call x2, Pallas kernels, attend_call(): pl.pallas_call(partial(attend_kernel, qrows, ahead), grid=(count,), in_sp...  34.1 us
    pallas_call x2, Pallas kernels, in_call(): pl.pallas_call(partial(in_kernel, n, len(grads)), grid_spec=pltpu.Prefetc...  31.2 us
    convert_element_type x14, other arithmetic, added(): return total.astype(bf16)  29.9 us
  transfers between devices with their start and end apart: 64, of which 19 were waited for; matrix products, arithmetic and copies ran while one was open for 12% of the time, Pallas kernels for 52%

profile of v4, /device:TPU:0, one launch (start us, length us, event | category | flops | bytes accessed | tf_op | source)
XLA Modules:
  0.0 541.9 jit_solution(17005713187368496158)
XLA Ops:
  2.7 3.1 collective-permute-start
  5.9 3.4 dynamic-slice_bitcast_fusion.2
  20.5 3.8 collective-permute-done.refs_1_.refs_10_
  30.9 10.2 %collective-permute-done.4 = bf16[512,1280]{1,0:T(8,128)(2,1)} collective-permute-done((bf16[512,1280]{1,0:T(8,128)(2,1)}, bf16[512,1280]{1,0:T(8,128)(2,1)}, u32[]{:S(2)}, u32[]{:S(2)}) %collective-permute-start.4) | collective-permute-done | bytes 1310752 | tf_op jit(solution)/shard_map/ppermute | solution.py:348
  41.1 3.6 collective-permute-done.2.refs_2_.refs_11_
  48.8 3.0 pad_maximum_fusion.x_ref
  51.8 6.2 %collective-permute-done.5.refs_3_.refs_12_ = bf16[80,5120]{1,0:T(8,128)(2,1)S(1)} collective-permute-done((bf16[80,5120]{1,0:T(8,128)(2,1)S(1)}, bf16[80,5120]{1,0:T(8,128)(2,1)S(1)}, u32[]{:S(2)}, u32[]{:S(2)}) %collective-permute-start.5) | collective-permute-done | bytes 819232 | tf_op jit(solution)/shard_map/ppermute | solution.py:348
  60.9 9.5 %collective-permute-done.11.refs_4_.refs_13_ = bf16[80,5120]{1,0:T(8,128)(2,1)S(1)} collective-permute-done((bf16[80,5120]{1,0:T(8,128)(2,1)S(1)}, bf16[80,5120]{1,0:T(8,128)(2,1)S(1)}, u32[]{:S(2)}, u32[]{:S(2)}) %collective-permute-start.11) | collective-permute-done | bytes 819232 | tf_op jit(solution)/shard_map/ppermute | solution.py:348
  71.7 7.5 %collective-permute-done.12.refs_7_.refs_16_ = bf16[80,5120]{1,0:T(8,128)(2,1)S(1)} collective-permute-done((bf16[80,5120]{1,0:T(8,128)(2,1)S(1)}, bf16[80,5120]{1,0:T(8,128)(2,1)S(1)}, u32[]{:S(2)}, u32[]{:S(2)}) %collective-permute-start.12) | collective-permute-done | bytes 819232 | tf_op jit(solution)/shard_map/ppermute | solution.py:348
  83.7 20.4 %qkv.1 = (bf16[1024,1280]{1,0:T(8,128)(2,1)}, bf16[1024,1280]{1,0:T(8,128)(2,1)}, bf16[1024,1280]{1,0:T(8,128)(2,1)}, bf16[1024,1280]{1,0:T(8,128)(2,1)}) custom-call(s32[16]{0:T(128)} %pad_add_fusion.2.place_ref, bf16[1024,1280]{1,0:T(8,128)(2,1)} %pad_maximum_fusion.x_ref, f32[1,1280]{1,0:T(1,128)} %reshape.227.gain_ref, f32[1,1280]{1,0:T(1,128)} %reshape.228.bias_ref, ...), custom_call_target="tpu_custom_call" | custom-call | flops 201326592 | bytes 458752 | tf_op jit(solution)/shard_map/qkv/pallas_call | solution.py:489
  106.2 20.0 %attend.2 = (bf16[1024,768]{1,0:T(8,128)(2,1)}, f32[12,1,1024]{2,1,0:T(1,128)}) custom-call(f32[1024,1]{1,0:T(8,128)} %compare_select_fusion.mask_ref, f32[1024,1]{1,0:T(8,128)} %convert_element_type.346.keep_ref, bf16[1024,1280]{1,0:T(8,128)(2,1)} %get-tuple-element.320.q_ref, bf16[1024,1280]{1,0:T(8,128)(2,1)} %get-tuple-element.321.k_ref, ...), custom_call_target="tpu_custom_call" | custom-call | flops 322122560 | bytes 125829 | tf_op jit(solution)/shard_map/attend/pallas_call | solution.py:562
  131.0 14.0 %attend.3 = (bf16[1024,512]{1,0:T(8,128)(2,1)}, f32[8,1,1024]{2,1,0:T(1,128)}) custom-call(f32[1024,1]{1,0:T(8,128)} %compare_select_fusion.mask_ref, f32[1024,1]{1,0:T(8,128)} %convert_element_type.346.keep_ref, bf16[1024,1280]{1,0:T(8,128)(2,1)} %get-tuple-element.320.q_ref, bf16[1024,1280]{1,0:T(8,128)(2,1)} %get-tuple-element.321.k_ref, ...), custom_call_target="tpu_custom_call" | custom-call | flops 214748368 | bytes 83886 | tf_op jit(solution)/shard_map/attend/pallas_call | solution.py:562
  145.1 10.9 %out.1 = (f32[1024,1280]{1,0:T(8,128)}, bf16[1024,1280]{1,0:T(8,128)(2,1)}) custom-call(s32[16]{0:T(128)} %pad_add_fusion.2.place_ref, bf16[1024,1280]{1,0:T(8,128)(2,1)} %pad_maximum_fusion.x_ref, f32[1,1280]{1,0:T(1,128)} %reshape.231.bias_ref, f32[1,1280]{1,0:T(1,128)} %reshape.232.gain_ref, f32[1,1280]{1,0:T(1,128)} %reshape.233.shift_ref, ...), custom_call_target="tpu_custom_call" | custom-call | flops 134217728 | bytes 327680 | tf_op jit(solution)/shard_map/out/pallas_call | solution.py:671
  162.8 37.3 %ffn.2 = (bf16[2048,1280]{1,0:T(8,128)(2,1)}, bf16[2048,1280]{1,0:T(8,128)(2,1)}, f32[1,1280]{1,0:T(1,128)}, f32[2048,1280]{1,0:T(8,128)}, f32[2048,1280]{1,0:T(8,128)}) custom-call(bf16[1024,1280]{1,0:T(8,128)(2,1)} %get-tuple-element.328.refs_0_.b_own, bf16[1024,1280]{1,0:T(8,128)(2,1)} %copy-done.2, bf16[1024,1280]{1,0:T(8,128)(2,1)} %copy-done.1, ...), custom_call_target="tpu_custom_call" | custom-call | flops 805306368 | bytes 629145 | tf_op jit(solution)/shard_map/ffn/pallas_call | solution.py:777
  201.7 20.8 %ffn_weights.2 = (bf16[640,1280]{1,0:T(8,128)(2,1)}, bf16[640,1280]{1,0:T(8,128)(2,1)}, bf16[640,1280]{1,0:T(8,128)(2,1)}, bf16[640,1280]{1,0:T(8,128)(2,1)}) custom-call(bf16[2048,1280]{1,0:T(8,128)(2,1)} %get-tuple-element.337.gz, bf16[2048,1280]{1,0:T(8,128)(2,1)} %get-tuple-element.338.h, bf16[1024,1280]{1,0:T(8,128)(2,1)} %get-tuple-element.328.refs_0_.b_own, ...), custom_call_target="tpu_custom_call" | custom-call | flops 402653184 | bytes 419430 | tf_op jit(solution)/shard_map/ffn_weights/pallas_call | solution.py:840
  223.7 40.6 %ffn.3 = (bf16[2048,1280]{1,0:T(8,128)(2,1)}, bf16[2048,1280]{1,0:T(8,128)(2,1)}, f32[1,1280]{1,0:T(1,128)}, bf16[1024,1280]{1,0:T(8,128)(2,1)}, bf16[1024,1280]...) custom-call(bf16[1024,1280]{1,0:T(8,128)(2,1)} %get-tuple-element.328.refs_0_.b_own, ...), custom_call_target="tpu_custom_call" | custom-call | flops 805306368 | bytes 1048576 | tf_op jit(solution)/shard_map/ffn/pallas_call | solution.py:777
  264.9 20.8 %ffn_weights.3 = (bf16[640,1280]{1,0:T(8,128)(2,1)}, bf16[640,1280]{1,0:T(8,128)(2,1)}, bf16[640,1280]{1,0:T(8,128)(2,1)}, bf16[640,1280]{1,0:T(8,128)(2,1)}) custom-call(bf16[2048,1280]{1,0:T(8,128)(2,1)} %get-tuple-element.347.gz, bf16[2048,1280]{1,0:T(8,128)(2,1)} %get-tuple-element.348.h, bf16[1024,1280]{1,0:T(8,128)(2,1)} %get-tuple-element.328.refs_0_.b_own, ...), custom_call_target="tpu_custom_call" | custom-call | flops 402653184 | bytes 419430 | tf_op jit(solution)/shard_map/ffn_weights/pallas_call | solution.py:840
  290.6 16.6 %mid.1 = (bf16[1024,1280]{1,0:T(8,128)(2,1)}, bf16[1024,1280]{1,0:T(8,128)(2,1)}, bf16[1024,1280]{1,0:T(8,128)(2,1)}, f32[8,1280]{1,0:T(8,128)}) custom-call(s32[16]{0:T(128)} %pad_add_fusion.2.place_ref, bf16[1024,1280]{1,0:T(8,128)(2,1)} %get-tuple-element.356.oo_ref, bf16[1024,1280]{1,0:T(8,128)(2,1)} %copy-done.21, ...), custom_call_target="tpu_custom_call" | custom-call | flops 134217728 | bytes 851968 | tf_op jit(solution)/shard_map/mid/pallas_call | solution.py:890
  307.2 34.6 %attend_back.3 = (bf16[1024,768]{1,0:T(8,128)(2,1)}, bf16[1024,768]{1,0:T(8,128)(2,1)}, bf16[1024,768]{1,0:T(8,128)(2,1)}, f32[1,768]{1,0:T(1,128)}, f32[1,768]{1,0:T(1,128)}) custom-call(f32[1024,1]{1,0:T(8,128)} %compare_select_fusion.mask_ref, bf16[1024,1280]{1,0:T(8,128)(2,1)} %get-tuple-element.320.q_ref, bf16[1024,1280]{1,0:T(8,128)(2,1)} %get-tuple-element.321.k_ref, ...), custom_call_target="tpu_custom_call" | custom-call | flops 515396064 | bytes 251658 | tf_op jit(solution)/shard_map/attend_back/pallas_call | solution.py:625
  343.7 3.7 add_convert_fusion.3
  349.4 19.8 %att_weights.2 = (bf16[80,3584]{1,0:T(8,128)(2,1)}, bf16[80,3584]{1,0:T(8,128)(2,1)}, bf16[80,3584]{1,0:T(8,128)(2,1)}, bf16[80,3584]{1,0:T(8,128)(2,1)}, bf16[8...) custom-call(s32[16]{0:T(128)} %pad_add_fusion.2.place_ref, ...), custom_call_target="tpu_custom_call" | custom-call | flops 281857216 | bytes 330301 | tf_op jit(solution)/shard_map/att_weights/pallas_call | solution.py:968
  369.5 3.2 add_convert_fusion.2
  375.2 7.5 %attend_back.4 = (bf16[1024,128]{1,0:T(8,128)(2,1)}, bf16[1024,128]{1,0:T(8,128)(2,1)}, bf16[1024,128]{1,0:T(8,128)(2,1)}, f32[1,128]{1,0:T(1,128)}, f32[1,128]{1,0:T(1,128)}) custom-call(f32[1024,1]{1,0:T(8,128)} %compare_select_fusion.mask_ref, bf16[1024,1280]{1,0:T(8,128)(2,1)} %get-tuple-element.320.q_ref, bf16[1024,1280]{1,0:T(8,128)(2,1)} %get-tuple-element.321.k_ref, ...), custom_call_target="tpu_custom_call" | custom-call | flops 85899344 | bytes 41943 | tf_op jit(solution)/shard_map/attend_back/pallas_call | solution.py:625
  387.3 18.4 %attend_back.5 = (bf16[1024,384]{1,0:T(8,128)(2,1)}, bf16[1024,384]{1,0:T(8,128)(2,1)}, bf16[1024,384]{1,0:T(8,128)(2,1)}, f32[1,384]{1,0:T(1,128)}, f32[1,384]{1,0:T(1,128)}) custom-call(f32[1024,1]{1,0:T(8,128)} %compare_select_fusion.mask_ref, bf16[1024,1280]{1,0:T(8,128)(2,1)} %get-tuple-element.320.q_ref, bf16[1024,1280]{1,0:T(8,128)(2,1)} %get-tuple-element.321.k_ref, ...), custom_call_target="tpu_custom_call" | custom-call | flops 257698032 | bytes 125829 | tf_op jit(solution)/shard_map/attend_back/pallas_call | solution.py:625
  413.3 15.4 %in.2 = (bf16[512,1280]{1,0:T(8,128)(2,1)}, f32[8,1280]{1,0:T(8,128)}) custom-call(s32[16]{0:T(128)} %pad_add_fusion.2.place_ref, bf16[1024,1280]{1,0:T(8,128)(2,1)} %pad_maximum_fusion.x_ref, bf16[1024,1280]{1,0:T(8,128)(2,1)} %get-tuple-element.362.refs_6_.gr_ref, f32[1,1280]{1,0:T(1,128)} %reshape.227.gain_ref, ...), custom_call_target="tpu_custom_call" | custom-call | flops 134217728 | bytes 380108 | tf_op jit(solution)/shard_map/in/pallas_call | solution.py:1026
  428.7 7.0 %collective-permute-done.39 = bf16[80,3584]{1,0:T(8,128)(2,1)} collective-permute-done((bf16[80,3584]{1,0:T(8,128)(2,1)}, bf16[80,3584]{1,0:T(8,128)(2,1)}, u32[]{:S(2)}, u32[]{:S(2)}) %collective-permute-start.39) | collective-permute-done | bytes 573472 | tf_op jit(solution)/shard_map/ppermute | solution.py:348
  439.8 3.0 fusion.3
  445.2 9.9 %att_weights.3 = (bf16[80,1536]{1,0:T(8,128)(2,1)}, bf16[80,1536]{1,0:T(8,128)(2,1)}, bf16[80,1536]{1,0:T(8,128)(2,1)}, bf16[80,1536]{1,0:T(8,128)(2,1)}, bf16[8...) custom-call(s32[16]{0:T(128)} %pad_add_fusion.2.place_ref, ...), custom_call_target="tpu_custom_call" | custom-call | flops 120795952 | bytes 141557 | tf_op jit(solution)/shard_map/att_weights/pallas_call | solution.py:968
  470.6 15.8 %in.3 = (f32[512,1280]{1,0:T(8,128)}, f32[8,1280]{1,0:T(8,128)}) custom-call(s32[16]{0:T(128)} %pad_add_fusion.2.place_ref, bf16[1024,1280]{1,0:T(8,128)(2,1)} %pad_maximum_fusion.x_ref, bf16[1024,1280]{1,0:T(8,128)(2,1)} %get-tuple-element.362.refs_6_.gr_ref, f32[1,1280]{1,0:T(1,128)} %reshape.227.gain_ref, ...), custom_call_target="tpu_custom_call" | custom-call | flops 134217728 | bytes 380108 | tf_op jit(solution)/shard_map/in/pallas_call | solution.py:1026
  503.0 3.4 collective-permute-done.56
  512.6 8.2 %collective-permute-done.51 = bf16[80,3584]{1,0:T(8,128)(2,1)S(1)} collective-permute-done((bf16[80,3584]{1,0:T(8,128)(2,1)S(1)}, bf16[80,3584]{1,0:T(8,128)(2,1)S(1)}, u32[]{:S(2)}, u32[]{:S(2)}) %collective-permute-start.51) | collective-permute-done | bytes 573472 | tf_op jit(solution)/shard_map/ppermute | solution.py:348
  534.0 5.0 collective-permute-done.62
  (356 shorter events, 133.3 us)
Async XLA Ops:
  2.7 21.5 %collective-permute-start = (bf16[80,5120]{1,0:T(8,128)(2,1)S(1)}, bf16[80,5120]{1,0:T(8,128)(2,1)S(1)}, u32[]{:S(2)}, u32[]{:S(2)}) collective-permute-start(bf16[80,5120]{1,0:T(8,128)(2,1)S(1)} %constant_dynamic-update-slice_fusion.refs_0_.refs_9_), channel_id=1, source_target_pairs={{0,8},{1,5},{2,6},{3,11},{4,0},{5,13},{6,14},{7,3},{8,16},{9,1},{1... | collective-permute-start | bytes 2457608 | tf_op jit(solution)/shard_map/ppermute | solution.py:348
  5.8 41.2 %collective-permute-start.6 = (bf16[80,5120]{1,0:T(8,128)(2,1)S(1)}, bf16[80,5120]{1,0:T(8,128)(2,1)S(1)}, u32[]{:S(2)}, u32[]{:S(2)}) collective-permute-start(bf16[80,5120]{1,0:T(8,128)(2,1)S(1)} %constant_dynamic-update-slice_fusion.refs_0_.refs_9_), channel_id=1, source_target_pairs={{0,2},{1,3},{2,0},{3,1},{4,6},{5,7},{6,4},{7,5},{8,10},{9,11},{10,... | collective-permute-start | bytes 2457608 | tf_op jit(solution)/shard_map/ppermute | solution.py:348
  9.3 31.8 %collective-permute-start.4 = (bf16[512,1280]{1,0:T(8,128)(2,1)}, bf16[512,1280]{1,0:T(8,128)(2,1)}, u32[]{:S(2)}, u32[]{:S(2)}) collective-permute-start(bf16[512,1280]{1,0:T(8,128)(2,1)} %get-tuple-element.566), channel_id=1, source_target_pairs={{0,1},{1,0},{2,3},{3,2},{4,5},{5,4},{6,7},{7,6},{8,9},{9,8},{10,11... | collective-permute-start | bytes 3932168 | tf_op jit(solution)/shard_map/ppermute | solution.py:348
  30.9 20.9 %collective-permute-start.7 = (bf16[80,5120]{1,0:T(8,128)(2,1)S(1)}, bf16[80,5120]{1,0:T(8,128)(2,1)S(1)}, u32[]{:S(2)}, u32[]{:S(2)}) collective-permute-start(bf16[80,5120]{1,0:T(8,128)(2,1)S(1)} %collective-permute-done.refs_1_.refs_10_), channel_id=1, source_target_pairs={{0,2},{1,3},{2,0},{3,1},{4,6},{5,7},{6,4},{7,5},{8,10},{9,11},{10,... | collective-permute-start | bytes 2457608 | tf_op jit(solution)/shard_map/ppermute | solution.py:348
  70.4 33.7 %collective-permute-start.16 = (bf16[640,1280]{1,0:T(8,128)(2,1)}, bf16[640,1280]{1,0:T(8,128)(2,1)}, u32[]{:S(2)}, u32[]{:S(2)}) collective-permute-start(bf16[640,1280]{1,0:T(8,128)(2,1)} %pad_maximum_fusion.2.refs_5_), channel_id=1, source_target_pairs={{0,8},{1,5},{2,6},{3,11},{4,0},{5,13},{6,14},{7,3},{8,16},{9,1},{1... | collective-permute-start | bytes 4915208 | tf_op jit(solution)/shard_map/ppermute | solution.py:348
  80.9 23.2 %collective-permute-start.17 = (bf16[256,1280]{1,0:T(8,128)(2,1)}, bf16[256,1280]{1,0:T(8,128)(2,1)}, u32[]{:S(2)}, u32[]{:S(2)}) collective-permute-start(bf16[256,1280]{1,0:T(8,128)(2,1)} %get-tuple-element.576), channel_id=1, source_target_pairs={{0,1},{1,0},{2,3},{3,2},{4,5},{5,4},{6,7},{7,6},{8,9},{9,8},{10,11... | collective-permute-start | bytes 1966088 | tf_op jit(solution)/shard_map/ppermute | solution.py:348
  104.2 22.1 %collective-permute-start.18 = (bf16[640,1280]{1,0:T(8,128)(2,1)}, bf16[640,1280]{1,0:T(8,128)(2,1)}, u32[]{:S(2)}, u32[]{:S(2)}) collective-permute-start(bf16[640,1280]{1,0:T(8,128)(2,1)} %collective-permute-done.16.refs_6_), channel_id=1, source_target_pairs={{0,8},{1,5},{2,6},{3,11},{4,0},{5,13},{6,14},{7,3},{8,16},{9,1},{1... | collective-permute-start | bytes 4915208 | tf_op jit(solution)/shard_map/ppermute | solution.py:348
  128.6 27.5 %collective-permute-start.20 = (bf16[1024,1280]{1,0:T(8,128)(2,1)S(1)}, bf16[1024,1280]{1,0:T(8,128)(2,1)}, u32[]{:S(2)}, u32[]{:S(2)}) collective-permute-start(bf16[1024,1280]{1,0:T(8,128)(2,1)S(1)} %pad_maximum_fusion.1.refs_2_.g_own.g_ref), channel_id=1, source_target_pairs={{0,2},{1,3},{2,0},{3,1},{4,6},{5,7},{6,4},{7,5},{8,10},{9,11},{10,... | collective-permute-start | bytes 7864328 | tf_op jit(solution)/shard_map/ppermute | solution.py:348
  129.3 26.7 %collective-permute-start.21 = (bf16[640,1280]{1,0:T(8,128)(2,1)}, bf16[640,1280]{1,0:T(8,128)(2,1)}, u32[]{:S(2)}, u32[]{:S(2)}) collective-permute-start(bf16[640,1280]{1,0:T(8,128)(2,1)} %collective-permute-done.18.refs_7_), channel_id=1, source_target_pairs={{0,8},{1,5},{2,6},{3,11},{4,0},{5,13},{6,14},{7,3},{8,16},{9,1},{1... | collective-permute-start | bytes 4915208 | tf_op jit(solution)/shard_map/ppermute | solution.py:348
  156.1 44.0 %collective-permute-start.24 = (bf16[640,1280]{1,0:T(8,128)(2,1)}, bf16[640,1280]{1,0:T(8,128)(2,1)}, u32[]{:S(2)}, u32[]{:S(2)}) collective-permute-start(bf16[640,1280]{1,0:T(8,128)(2,1)} %pad_maximum_fusion.2.refs_5_), channel_id=1, source_target_pairs={{0,4},{1,9},{2,10},{3,7},{4,12},{5,1},{6,2},{7,15},{8,0},{9,17},{1... | collective-permute-start | bytes 4915208 | tf_op jit(solution)/shard_map/ppermute | solution.py:348
  158.0 64.5 %collective-permute-start.23 = (bf16[640,1280]{1,0:T(8,128)(2,1)}, bf16[640,1280]{1,0:T(8,128)(2,1)}, u32[]{:S(2)}, u32[]{:S(2)}) collective-permute-start(bf16[640,1280]{1,0:T(8,128)(2,1)} %collective-permute-done.21.refs_8_), channel_id=1, source_target_pairs={{0,8},{1,5},{2,6},{3,11},{4,0},{5,13},{6,14},{7,3},{8,16},{9,1},{1... | collective-permute-start | bytes 4915208 | tf_op jit(solution)/shard_map/ppermute | solution.py:348
  159.6 62.9 %collective-permute-start.26 = (bf16[640,1280]{1,0:T(8,128)(2,1)}, bf16[640,1280]{1,0:T(8,128)(2,1)}, u32[]{:S(2)}, u32[]{:S(2)}) collective-permute-start(bf16[640,1280]{1,0:T(8,128)(2,1)} %collective-permute-done.21.refs_8_), channel_id=1, source_target_pairs={{0,1},{1,0},{2,3},{3,2},{4,5},{5,4},{6,7},{7,6},{8,9},{9,8},{10,11... | collective-permute-start | bytes 4915208 | tf_op jit(solution)/shard_map/ppermute | solution.py:348
  200.1 22.4 %collective-permute-start.25 = (bf16[640,1280]{1,0:T(8,128)(2,1)}, bf16[640,1280]{1,0:T(8,128)(2,1)S(1)}, u32[]{:S(2)}, u32[]{:S(2)}) collective-permute-start(bf16[640,1280]{1,0:T(8,128)(2,1)} %collective-permute-done.24.refs_6_), channel_id=1, source_target_pairs={{0,4},{1,9},{2,10},{3,7},{4,12},{5,1},{6,2},{7,15},{8,0},{9,17},{1... | collective-permute-start | bytes 4915208 | tf_op jit(solution)/shard_map/ppermute | solution.py:348
  264.3 21.4 %collective-permute-start.27 = (bf16[1024,1280]{1,0:T(8,128)(2,1)}, bf16[1024,1280]{1,0:T(8,128)(2,1)S(1)}, u32[]{:S(2)}, u32[]{:S(2)}) collective-permute-start(bf16[1024,1280]{1,0:T(8,128)(2,1)} %get-tuple-element.354), channel_id=1, source_target_pairs={{0,2},{1,3},{2,0},{3,1},{4,6},{5,7},{6,4},{7,5},{8,10},{9,11},{10,... | collective-permute-start | bytes 7864328 | tf_op jit(solution)/shard_map/ppermute | solution.py:348
  264.7 21.0 %collective-permute-start.28 = (bf16[1024,1280]{1,0:T(8,128)(2,1)}, bf16[1024,1280]{1,0:T(8,128)(2,1)}, u32[]{:S(2)}, u32[]{:S(2)}) collective-permute-start(bf16[1024,1280]{1,0:T(8,128)(2,1)} %get-tuple-element.355), channel_id=1, source_target_pairs={{0,2},{1,3},{2,0},{3,1},{4,6},{5,7},{6,4},{7,5},{8,10},{9,11},{10,... | collective-permute-start | bytes 7864328 | tf_op jit(solution)/shard_map/ppermute | solution.py:348
  285.7 57.2 %collective-permute-start.29 = (bf16[640,1280]{1,0:T(8,128)(2,1)}, bf16[640,1280]{1,0:T(8,128)(2,1)}, u32[]{:S(2)}, u32[]{:S(2)}) collective-permute-start(bf16[640,1280]{1,0:T(8,128)(2,1)} %get-tuple-element.370), channel_id=1, source_target_pairs={{0,4},{1,9},{2,10},{3,7},{4,12},{5,1},{6,2},{7,15},{8,0},{9,17},{1... | collective-permute-start | bytes 4915208 | tf_op jit(solution)/shard_map/ppermute | solution.py:348
  286.8 56.2 %collective-permute-start.30 = (bf16[640,1280]{1,0:T(8,128)(2,1)}, bf16[640,1280]{1,0:T(8,128)(2,1)}, u32[]{:S(2)}, u32[]{:S(2)}) collective-permute-start(bf16[640,1280]{1,0:T(8,128)(2,1)} %get-tuple-element.371), channel_id=1, source_target_pairs={{0,1},{1,0},{2,3},{3,2},{4,5},{5,4},{6,7},{7,6},{8,9},{9,8},{10,11... | collective-permute-start | bytes 4915208 | tf_op jit(solution)/shard_map/ppermute | solution.py:348
  288.9 80.3 %collective-permute-start.32 = (bf16[640,1280]{1,0:T(8,128)(2,1)}, bf16[640,1280]{1,0:T(8,128)(2,1)}, u32[]{:S(2)}, u32[]{:S(2)}) collective-permute-start(bf16[640,1280]{1,0:T(8,128)(2,1)} %get-tuple-element.391), channel_id=1, source_target_pairs={{0,8},{1,5},{2,6},{3,11},{4,0},{5,13},{6,14},{7,3},{8,16},{9,1},{1... | collective-permute-start | bytes 4915208 | tf_op jit(solution)/shard_map/ppermute | solution.py:348
  289.4 79.8 %collective-permute-start.33 = (bf16[640,1280]{1,0:T(8,128)(2,1)}, bf16[640,1280]{1,0:T(8,128)(2,1)}, u32[]{:S(2)}, u32[]{:S(2)}) collective-permute-start(bf16[640,1280]{1,0:T(8,128)(2,1)} %get-tuple-element.392), channel_id=1, source_target_pairs={{0,1},{1,0},{2,3},{3,2},{4,5},{5,4},{6,7},{7,6},{8,9},{9,8},{10,11... | collective-permute-start | bytes 4915208 | tf_op jit(solution)/shard_map/ppermute | solution.py:348
  347.4 21.9 %collective-permute-start.31 = (bf16[640,1280]{1,0:T(8,128)(2,1)}, bf16[640,1280]{1,0:T(8,128)(2,1)S(1)}, u32[]{:S(2)}, u32[]{:S(2)}) collective-permute-start(bf16[640,1280]{1,0:T(8,128)(2,1)} %add_convert_fusion.3), channel_id=1, source_target_pairs={{0,4},{1,9},{2,10},{3,7},{4,12},{5,1},{6,2},{7,15},{8,0},{9,17},{1... | collective-permute-start | bytes 4915208 | tf_op jit(solution)/shard_map/ppermute | solution.py:348
  372.7 33.0 %collective-permute-start.37 = (bf16[640,1280]{1,0:T(8,128)(2,1)}, bf16[640,1280]{1,0:T(8,128)(2,1)S(1)}, u32[]{:S(2)}, u32[]{:S(2)}) collective-permute-start(bf16[640,1280]{1,0:T(8,128)(2,1)} %add_convert_fusion.2), channel_id=1, source_target_pairs={{0,4},{1,9},{2,10},{3,7},{4,12},{5,1},{6,2},{7,15},{8,0},{9,17},{1... | collective-permute-start | bytes 4915208 | tf_op jit(solution)/shard_map/ppermute | solution.py:348
  374.4 31.3 %collective-permute-start.38 = (bf16[256,1280]{1,0:T(8,128)(2,1)}, bf16[256,1280]{1,0:T(8,128)(2,1)S(1)}, u32[]{:S(2)}, u32[]{:S(2)}) collective-permute-start(bf16[256,1280]{1,0:T(8,128)(2,1)} %get-tuple-element.436), channel_id=1, source_target_pairs={{0,1},{1,0},{2,3},{3,2},{4,5},{5,4},{6,7},{7,6},{8,9},{9,8},{10,11... | collective-permute-start | bytes 1966088 | tf_op jit(solution)/shard_map/ppermute | solution.py:348
  385.2 21.3 %collective-permute-start.35 = (bf16[80,3584]{1,0:T(8,128)(2,1)}, bf16[80,3584]{1,0:T(8,128)(2,1)}, u32[]{:S(2)}, u32[]{:S(2)}) collective-permute-start(bf16[80,3584]{1,0:T(8,128)(2,1)} %get-tuple-element.560), channel_id=1, source_target_pairs={{0,4},{1,9},{2,10},{3,7},{4,12},{5,1},{6,2},{7,15},{8,0},{9,17},{1... | collective-permute-start | bytes 1720328 | tf_op jit(solution)/shard_map/ppermute | solution.py:348
  408.1 27.6 %collective-permute-start.41 = (bf16[640,1280]{1,0:T(8,128)(2,1)}, bf16[640,1280]{1,0:T(8,128)(2,1)S(1)}, u32[]{:S(2)}, u32[]{:S(2)}) collective-permute-start(bf16[640,1280]{1,0:T(8,128)(2,1)} %add_convert_fusion.1), channel_id=1, source_target_pairs={{0,4},{1,9},{2,10},{3,7},{4,12},{5,1},{6,2},{7,15},{8,0},{9,17},{1... | collective-permute-start | bytes 4915208 | tf_op jit(solution)/shard_map/ppermute | solution.py:348
  409.6 26.1 %collective-permute-start.40 = (bf16[256,1280]{1,0:T(8,128)(2,1)}, bf16[256,1280]{1,0:T(8,128)(2,1)S(1)}, u32[]{:S(2)}, u32[]{:S(2)}) collective-permute-start(bf16[256,1280]{1,0:T(8,128)(2,1)} %get-tuple-element.458), channel_id=1, source_target_pairs={{0,1},{1,0},{2,3},{3,2},{4,5},{5,4},{6,7},{7,6},{8,9},{9,8},{10,11... | collective-permute-start | bytes 1966088 | tf_op jit(solution)/shard_map/ppermute | solution.py:348
  412.5 23.2 %collective-permute-start.39 = (bf16[80,3584]{1,0:T(8,128)(2,1)}, bf16[80,3584]{1,0:T(8,128)(2,1)}, u32[]{:S(2)}, u32[]{:S(2)}) collective-permute-start(bf16[80,3584]{1,0:T(8,128)(2,1)} %fusion.5), channel_id=1, source_target_pairs={{0,4},{1,9},{2,10},{3,7},{4,12},{5,1},{6,2},{7,15},{8,0},{9,17},{1... | collective-permute-start | bytes 1720328 | tf_op jit(solution)/shard_map/ppermute | solution.py:348
  460.4 51.3 %collective-permute-start.52 = (bf16[512,1280]{1,0:T(8,128)(2,1)}, bf16[512,1280]{1,0:T(8,128)(2,1)}, u32[]{:S(2)}, u32[]{:S(2)}) collective-permute-start(bf16[512,1280]{1,0:T(8,128)(2,1)} %get-tuple-element.514), channel_id=1, source_target_pairs={{0,1},{1,0},{2,3},{3,2},{4,5},{5,4},{6,7},{7,6},{8,9},{9,8},{10,11... | collective-permute-start | bytes 3932168 | tf_op jit(solution)/shard_map/ppermute | solution.py:348
  464.3 22.1 %collective-permute-start.45 = (bf16[80,3584]{1,0:T(8,128)(2,1)}, bf16[80,3584]{1,0:T(8,128)(2,1)}, u32[]{:S(2)}, u32[]{:S(2)}) collective-permute-start(bf16[80,3584]{1,0:T(8,128)(2,1)} %get-tuple-element.556), channel_id=1, source_target_pairs={{0,4},{1,9},{2,10},{3,7},{4,12},{5,1},{6,2},{7,15},{8,0},{9,17},{1... | collective-permute-start | bytes 1720328 | tf_op jit(solution)/shard_map/ppermute | solution.py:348
  465.4 22.1 %collective-permute-start.46 = (bf16[80,3584]{1,0:T(8,128)(2,1)S(1)}, bf16[80,3584]{1,0:T(8,128)(2,1)}, u32[]{:S(2)}, u32[]{:S(2)}) collective-permute-start(bf16[80,3584]{1,0:T(8,128)(2,1)S(1)} %get-tuple-element.555), channel_id=1, source_target_pairs={{0,8},{1,5},{2,6},{3,11},{4,0},{5,13},{6,14},{7,3},{8,16},{9,1},{1... | collective-permute-start | bytes 1720328 | tf_op jit(solution)/shard_map/ppermute | solution.py:348
  486.4 26.2 %collective-permute-start.50 = (bf16[320,1280]{1,0:T(8,128)(2,1)}, bf16[320,1280]{1,0:T(8,128)(2,1)}, u32[]{:S(2)}, u32[]{:S(2)}) collective-permute-start(bf16[320,1280]{1,0:T(8,128)(2,1)} %get-tuple-element.543), channel_id=1, source_target_pairs={{0,1},{1,0},{2,3},{3,2},{4,5},{5,4},{6,7},{7,6},{8,9},{9,8},{10,11... | collective-permute-start | bytes 2457608 | tf_op jit(solution)/shard_map/ppermute | solution.py:348
  493.9 26.9 %collective-permute-start.51 = (bf16[80,3584]{1,0:T(8,128)(2,1)S(1)}, bf16[80,3584]{1,0:T(8,128)(2,1)S(1)}, u32[]{:S(2)}, u32[]{:S(2)}) collective-permute-start(bf16[80,3584]{1,0:T(8,128)(2,1)S(1)} %fusion), channel_id=1, source_target_pairs={{0,1},{1,0},{2,3},{3,2},{4,5},{5,4},{6,7},{7,6},{8,9},{9,8},{10,11... | collective-permute-start | bytes 1720328 | tf_op jit(solution)/shard_map/ppermute | solution.py:348
  507.7 22.2 %collective-permute-start.61 = (f32[15360]{0:T(1024)S(1)}, f32[15360]{0:T(1024)S(1)}, u32[]{:S(2)}, u32[]{:S(2)}) collective-permute-start(f32[15360]{0:T(1024)S(1)} %add.373), channel_id=1, source_target_pairs={{0,16},{1,17},{2,18},{3,19},{4,20},{5,21},{6,22},{7,23},{8,24},{9,... | collective-permute-start | bytes 184328 | tf_op jit(solution)/shard_map/ppermute | solution.py:348
  (107 other events, 1031.3 us)

commit v5 on v4

--- a/solution.py
+++ b/solution.py
@@ -1221,8 +1221,9 @@
     steps_second = ring.reduce([[second[s], second_sib[s]] for s in range(n)], 3)
     way_second = next(steps_second)
     in_own, in_sums = in_call(place, x, gr, ln1_gain, grads, weights, 0, f32)
-    in_own, in_sums, in_sums_send, way_first, way_second = fence(
-        in_own, in_sums, in_sums_send, way_first, way_second
+    w_up_grad = ffn_sum[0].astype(f32) + ffn_got[0].astype(f32)
+    in_own, in_sums, in_sums_send, way_first, way_second, w_up_grad = fence(
+        in_own, in_sums, in_sums_send, way_first, way_second, w_up_grad
     )
     first_sum = steps_first.send(way_first)
     first_got = ring.swap_blk(first_sum)
@@ -1241,13 +1242,13 @@
     second_sum = steps_second.send(way_second)
     second_got = ring.swap_blk(second_sum)
     sums = steps_sums.send(sums)
+    down_sum, down_got, first_sum, first_got, in_got, second_sum, _ = fence(
+        ffn_sum[1], ffn_got[1], first_sum, first_got, in_got, second_sum, sums[0]
+    )
     sums = steps_sums.send(sums)
-    ffn_sum, ffn_got, first_sum, first_got, in_got = fence(
-        ffn_sum, ffn_got, first_sum, first_got, in_got
-    )
-    sums_own, sums_got = ffn_sum + [first_sum, second_sum], ffn_got + [first_got, second_got]
-    w_up_grad, w_down_grad, first_rows, second_rows = [
-        a.astype(f32) + b.astype(f32) for a, b in zip(sums_own, sums_got, strict=True)
+    w_down_grad, first_rows, second_rows = [
+        a.astype(f32) + b.astype(f32)
+        for a, b in ((down_sum, down_got), (first_sum, first_got), (second_sum, second_got))
     ]
 
     def home(own, got):

time: 550 us -> 545 us (level)
  transfers between devices with their start and end apart: 64 -> 64, of which waited for: 19 -> 20; matrix products, arithmetic and copies ran while one was open for 12% -> 12% of each run, Pallas kernels for 52% -> 53%
where the time goes in v5:
time: 545 us; the launch traced here: 536 us
  Pallas kernels  323 us (59%)
  waiting for transfers between devices  68.5 us (13%)
  starting transfers between devices  59.7 us (11%)
  other arithmetic  51 us (9%)
  local copies, waits for them, and re-layouts  31.9 us (6%)
    pallas_call x2, Pallas kernels, ffn_call(): pl.pallas_call(partial(ffn_kernel, n, later), grid=(2 * half,), in_specs=...  77.9 us
    ppermute x64, waiting for transfers between devices, permute(): return lax.ppermute(x, AXES, pairs)  68.5 us
    pallas_call x3, Pallas kernels, attend_back_call(): pl.pallas_call(partial(attend_back_kernel, qrows), grid=(count,), in_spec...  60.5 us
    ppermute x64, starting transfers between devices, permute(): return lax.ppermute(x, AXES, pairs)  59.7 us
    pallas_call x2, Pallas kernels, ffn_weights_call(): pl.pallas_call(partial(ffn_weights_kernel, n), in_specs=[ANY] * 6, out_sp...  41.6 us
    pallas_call x2, Pallas kernels, attend_call(): pl.pallas_call(partial(attend_kernel, qrows, ahead), grid=(count,), in_sp...  34.1 us
    pallas_call x2, Pallas kernels, in_call(): pl.pallas_call(partial(in_kernel, n, len(grads)), grid_spec=pltpu.Prefetc...  31.3 us
    convert_element_type x14, other arithmetic, added(): return total.astype(bf16)  29.7 us
  transfers between devices with their start and end apart: 64, of which 20 were waited for; matrix products, arithmetic and copies ran while one was open for 12% of the time, Pallas kernels for 53%

profile of v5, /device:TPU:0, one launch (start us, length us, event | category | flops | bytes accessed | tf_op | source)
XLA Modules:
  0.0 536.2 jit_solution(2240321042913184842)
XLA Ops:
  2.7 3.1 collective-permute-start
  5.9 3.4 dynamic-slice_bitcast_fusion.2
  20.5 3.8 collective-permute-done.refs_1_.refs_10_
  30.9 10.2 %collective-permute-done.4 = bf16[512,1280]{1,0:T(8,128)(2,1)} collective-permute-done((bf16[512,1280]{1,0:T(8,128)(2,1)}, bf16[512,1280]{1,0:T(8,128)(2,1)}, u32[]{:S(2)}, u32[]{:S(2)}) %collective-permute-start.4) | collective-permute-done | bytes 1310752 | tf_op jit(solution)/shard_map/ppermute | solution.py:348
  41.1 3.6 collective-permute-done.2.refs_2_.refs_11_
  48.8 3.0 pad_maximum_fusion.x_ref
  51.8 6.2 %collective-permute-done.5.refs_3_.refs_12_ = bf16[80,5120]{1,0:T(8,128)(2,1)S(1)} collective-permute-done((bf16[80,5120]{1,0:T(8,128)(2,1)S(1)}, bf16[80,5120]{1,0:T(8,128)(2,1)S(1)}, u32[]{:S(2)}, u32[]{:S(2)}) %collective-permute-start.5) | collective-permute-done | bytes 819232 | tf_op jit(solution)/shard_map/ppermute | solution.py:348
  60.9 9.5 %collective-permute-done.11.refs_4_.refs_13_ = bf16[80,5120]{1,0:T(8,128)(2,1)S(1)} collective-permute-done((bf16[80,5120]{1,0:T(8,128)(2,1)S(1)}, bf16[80,5120]{1,0:T(8,128)(2,1)S(1)}, u32[]{:S(2)}, u32[]{:S(2)}) %collective-permute-start.11) | collective-permute-done | bytes 819232 | tf_op jit(solution)/shard_map/ppermute | solution.py:348
  71.7 7.5 %collective-permute-done.12.refs_7_.refs_16_ = bf16[80,5120]{1,0:T(8,128)(2,1)S(1)} collective-permute-done((bf16[80,5120]{1,0:T(8,128)(2,1)S(1)}, bf16[80,5120]{1,0:T(8,128)(2,1)S(1)}, u32[]{:S(2)}, u32[]{:S(2)}) %collective-permute-start.12) | collective-permute-done | bytes 819232 | tf_op jit(solution)/shard_map/ppermute | solution.py:348
  83.7 20.4 %qkv.1 = (bf16[1024,1280]{1,0:T(8,128)(2,1)}, bf16[1024,1280]{1,0:T(8,128)(2,1)}, bf16[1024,1280]{1,0:T(8,128)(2,1)}, bf16[1024,1280]{1,0:T(8,128)(2,1)}) custom-call(s32[16]{0:T(128)} %pad_add_fusion.2.place_ref, bf16[1024,1280]{1,0:T(8,128)(2,1)} %pad_maximum_fusion.x_ref, f32[1,1280]{1,0:T(1,128)} %reshape.227.gain_ref, f32[1,1280]{1,0:T(1,128)} %reshape.228.bias_ref, ...), custom_call_target="tpu_custom_call" | custom-call | flops 201326592 | bytes 458752 | tf_op jit(solution)/shard_map/qkv/pallas_call | solution.py:489
  106.2 20.0 %attend.2 = (bf16[1024,768]{1,0:T(8,128)(2,1)}, f32[12,1,1024]{2,1,0:T(1,128)}) custom-call(f32[1024,1]{1,0:T(8,128)} %compare_select_fusion.mask_ref, f32[1024,1]{1,0:T(8,128)} %convert_element_type.346.keep_ref, bf16[1024,1280]{1,0:T(8,128)(2,1)} %get-tuple-element.320.q_ref, bf16[1024,1280]{1,0:T(8,128)(2,1)} %get-tuple-element.321.k_ref, ...), custom_call_target="tpu_custom_call" | custom-call | flops 322122560 | bytes 125829 | tf_op jit(solution)/shard_map/attend/pallas_call | solution.py:562
  131.0 14.0 %attend.3 = (bf16[1024,512]{1,0:T(8,128)(2,1)}, f32[8,1,1024]{2,1,0:T(1,128)}) custom-call(f32[1024,1]{1,0:T(8,128)} %compare_select_fusion.mask_ref, f32[1024,1]{1,0:T(8,128)} %convert_element_type.346.keep_ref, bf16[1024,1280]{1,0:T(8,128)(2,1)} %get-tuple-element.320.q_ref, bf16[1024,1280]{1,0:T(8,128)(2,1)} %get-tuple-element.321.k_ref, ...), custom_call_target="tpu_custom_call" | custom-call | flops 214748368 | bytes 83886 | tf_op jit(solution)/shard_map/attend/pallas_call | solution.py:562
  145.1 10.9 %out.1 = (f32[1024,1280]{1,0:T(8,128)}, bf16[1024,1280]{1,0:T(8,128)(2,1)}) custom-call(s32[16]{0:T(128)} %pad_add_fusion.2.place_ref, bf16[1024,1280]{1,0:T(8,128)(2,1)} %pad_maximum_fusion.x_ref, f32[1,1280]{1,0:T(1,128)} %reshape.231.bias_ref, f32[1,1280]{1,0:T(1,128)} %reshape.232.gain_ref, f32[1,1280]{1,0:T(1,128)} %reshape.233.shift_ref, ...), custom_call_target="tpu_custom_call" | custom-call | flops 134217728 | bytes 327680 | tf_op jit(solution)/shard_map/out/pallas_call | solution.py:671
  162.8 37.3 %ffn.2 = (bf16[2048,1280]{1,0:T(8,128)(2,1)}, bf16[2048,1280]{1,0:T(8,128)(2,1)}, f32[1,1280]{1,0:T(1,128)}, f32[2048,1280]{1,0:T(8,128)}, f32[2048,1280]{1,0:T(8,128)}) custom-call(bf16[1024,1280]{1,0:T(8,128)(2,1)} %get-tuple-element.328.refs_0_.b_own, bf16[1024,1280]{1,0:T(8,128)(2,1)} %copy-done.2, bf16[1024,1280]{1,0:T(8,128)(2,1)} %copy-done.1, ...), custom_call_target="tpu_custom_call" | custom-call | flops 805306368 | bytes 629145 | tf_op jit(solution)/shard_map/ffn/pallas_call | solution.py:777
  201.7 20.8 %ffn_weights.2 = (bf16[640,1280]{1,0:T(8,128)(2,1)}, bf16[640,1280]{1,0:T(8,128)(2,1)}, bf16[640,1280]{1,0:T(8,128)(2,1)}, bf16[640,1280]{1,0:T(8,128)(2,1)}) custom-call(bf16[2048,1280]{1,0:T(8,128)(2,1)} %get-tuple-element.337.gz, bf16[2048,1280]{1,0:T(8,128)(2,1)} %get-tuple-element.338.h, bf16[1024,1280]{1,0:T(8,128)(2,1)} %get-tuple-element.328.refs_0_.b_own, ...), custom_call_target="tpu_custom_call" | custom-call | flops 402653184 | bytes 419430 | tf_op jit(solution)/shard_map/ffn_weights/pallas_call | solution.py:840
  223.7 40.6 %ffn.3 = (bf16[2048,1280]{1,0:T(8,128)(2,1)}, bf16[2048,1280]{1,0:T(8,128)(2,1)}, f32[1,1280]{1,0:T(1,128)}, bf16[1024,1280]{1,0:T(8,128)(2,1)}, bf16[1024,1280]...) custom-call(bf16[1024,1280]{1,0:T(8,128)(2,1)} %get-tuple-element.328.refs_0_.b_own, ...), custom_call_target="tpu_custom_call" | custom-call | flops 805306368 | bytes 1048576 | tf_op jit(solution)/shard_map/ffn/pallas_call | solution.py:777
  264.9 20.8 %ffn_weights.3 = (bf16[640,1280]{1,0:T(8,128)(2,1)}, bf16[640,1280]{1,0:T(8,128)(2,1)}, bf16[640,1280]{1,0:T(8,128)(2,1)}, bf16[640,1280]{1,0:T(8,128)(2,1)}) custom-call(bf16[2048,1280]{1,0:T(8,128)(2,1)} %get-tuple-element.347.gz, bf16[2048,1280]{1,0:T(8,128)(2,1)} %get-tuple-element.348.h, bf16[1024,1280]{1,0:T(8,128)(2,1)} %get-tuple-element.328.refs_0_.b_own, ...), custom_call_target="tpu_custom_call" | custom-call | flops 402653184 | bytes 419430 | tf_op jit(solution)/shard_map/ffn_weights/pallas_call | solution.py:840
  290.6 16.6 %mid.1 = (bf16[1024,1280]{1,0:T(8,128)(2,1)}, bf16[1024,1280]{1,0:T(8,128)(2,1)}, bf16[1024,1280]{1,0:T(8,128)(2,1)}, f32[8,1280]{1,0:T(8,128)}) custom-call(s32[16]{0:T(128)} %pad_add_fusion.2.place_ref, bf16[1024,1280]{1,0:T(8,128)(2,1)} %get-tuple-element.356.oo_ref, bf16[1024,1280]{1,0:T(8,128)(2,1)} %copy-done.20, ...), custom_call_target="tpu_custom_call" | custom-call | flops 134217728 | bytes 851968 | tf_op jit(solution)/shard_map/mid/pallas_call | solution.py:890
  307.2 34.6 %attend_back.3 = (bf16[1024,768]{1,0:T(8,128)(2,1)}, bf16[1024,768]{1,0:T(8,128)(2,1)}, bf16[1024,768]{1,0:T(8,128)(2,1)}, f32[1,768]{1,0:T(1,128)}, f32[1,768]{1,0:T(1,128)}) custom-call(f32[1024,1]{1,0:T(8,128)} %compare_select_fusion.mask_ref, bf16[1024,1280]{1,0:T(8,128)(2,1)} %get-tuple-element.320.q_ref, bf16[1024,1280]{1,0:T(8,128)(2,1)} %get-tuple-element.321.k_ref, ...), custom_call_target="tpu_custom_call" | custom-call | flops 515396064 | bytes 251658 | tf_op jit(solution)/shard_map/attend_back/pallas_call | solution.py:625
  343.7 3.7 add_convert_fusion.3
  349.4 19.8 %att_weights.2 = (bf16[80,3584]{1,0:T(8,128)(2,1)}, bf16[80,3584]{1,0:T(8,128)(2,1)}, bf16[80,3584]{1,0:T(8,128)(2,1)}, bf16[80,3584]{1,0:T(8,128)(2,1)}, bf16[8...) custom-call(s32[16]{0:T(128)} %pad_add_fusion.2.place_ref, ...), custom_call_target="tpu_custom_call" | custom-call | flops 281857216 | bytes 330301 | tf_op jit(solution)/shard_map/att_weights/pallas_call | solution.py:968
  369.5 3.2 add_convert_fusion.2
  375.2 7.5 %attend_back.4 = (bf16[1024,128]{1,0:T(8,128)(2,1)}, bf16[1024,128]{1,0:T(8,128)(2,1)}, bf16[1024,128]{1,0:T(8,128)(2,1)}, f32[1,128]{1,0:T(1,128)}, f32[1,128]{1,0:T(1,128)}) custom-call(f32[1024,1]{1,0:T(8,128)} %compare_select_fusion.mask_ref, bf16[1024,1280]{1,0:T(8,128)(2,1)} %get-tuple-element.320.q_ref, bf16[1024,1280]{1,0:T(8,128)(2,1)} %get-tuple-element.321.k_ref, ...), custom_call_target="tpu_custom_call" | custom-call | flops 85899344 | bytes 41943 | tf_op jit(solution)/shard_map/attend_back/pallas_call | solution.py:625
  387.3 18.4 %attend_back.5 = (bf16[1024,384]{1,0:T(8,128)(2,1)}, bf16[1024,384]{1,0:T(8,128)(2,1)}, bf16[1024,384]{1,0:T(8,128)(2,1)}, f32[1,384]{1,0:T(1,128)}, f32[1,384]{1,0:T(1,128)}) custom-call(f32[1024,1]{1,0:T(8,128)} %compare_select_fusion.mask_ref, bf16[1024,1280]{1,0:T(8,128)(2,1)} %get-tuple-element.320.q_ref, bf16[1024,1280]{1,0:T(8,128)(2,1)} %get-tuple-element.321.k_ref, ...), custom_call_target="tpu_custom_call" | custom-call | flops 257698032 | bytes 125829 | tf_op jit(solution)/shard_map/attend_back/pallas_call | solution.py:625
  413.3 15.5 %in.2 = (bf16[512,1280]{1,0:T(8,128)(2,1)}, f32[8,1280]{1,0:T(8,128)}) custom-call(s32[16]{0:T(128)} %pad_add_fusion.2.place_ref, bf16[1024,1280]{1,0:T(8,128)(2,1)} %pad_maximum_fusion.x_ref, bf16[1024,1280]{1,0:T(8,128)(2,1)} %get-tuple-element.362.refs_6_.gr_ref, f32[1,1280]{1,0:T(1,128)} %reshape.227.gain_ref, ...), custom_call_target="tpu_custom_call" | custom-call | flops 134217728 | bytes 380108 | tf_op jit(solution)/shard_map/in/pallas_call | solution.py:1026
  428.8 6.9 %collective-permute-done.39 = bf16[80,3584]{1,0:T(8,128)(2,1)} collective-permute-done((bf16[80,3584]{1,0:T(8,128)(2,1)}, bf16[80,3584]{1,0:T(8,128)(2,1)}, u32[]{:S(2)}, u32[]{:S(2)}) %collective-permute-start.39) | collective-permute-done | bytes 573472 | tf_op jit(solution)/shard_map/ppermute | solution.py:348
  439.8 3.1 fusion.3
  445.8 9.9 %att_weights.3 = (bf16[80,1536]{1,0:T(8,128)(2,1)}, bf16[80,1536]{1,0:T(8,128)(2,1)}, bf16[80,1536]{1,0:T(8,128)(2,1)}, bf16[80,1536]{1,0:T(8,128)(2,1)}, bf16[8...) custom-call(s32[16]{0:T(128)} %pad_add_fusion.2.place_ref, ...), custom_call_target="tpu_custom_call" | custom-call | flops 120795952 | bytes 141557 | tf_op jit(solution)/shard_map/att_weights/pallas_call | solution.py:968
  471.8 15.8 %in.3 = (f32[512,1280]{1,0:T(8,128)}, f32[8,1280]{1,0:T(8,128)}) custom-call(s32[16]{0:T(128)} %pad_add_fusion.2.place_ref, bf16[1024,1280]{1,0:T(8,128)(2,1)} %pad_maximum_fusion.x_ref, bf16[1024,1280]{1,0:T(8,128)(2,1)} %get-tuple-element.362.refs_6_.gr_ref, f32[1,1280]{1,0:T(1,128)} %reshape.227.gain_ref, ...), custom_call_target="tpu_custom_call" | custom-call | flops 134217728 | bytes 380108 | tf_op jit(solution)/shard_map/in/pallas_call | solution.py:1026
  493.3 2.9 collective-permute-done.55
  503.9 3.6 collective-permute-done.56
  516.2 3.7 collective-permute-done.60
  (356 shorter events, 134.0 us)
Async XLA Ops:
  2.7 21.5 %collective-permute-start = (bf16[80,5120]{1,0:T(8,128)(2,1)S(1)}, bf16[80,5120]{1,0:T(8,128)(2,1)S(1)}, u32[]{:S(2)}, u32[]{:S(2)}) collective-permute-start(bf16[80,5120]{1,0:T(8,128)(2,1)S(1)} %constant_dynamic-update-slice_fusion.refs_0_.refs_9_), channel_id=1, source_target_pairs={{0,8},{1,5},{2,6},{3,11},{4,0},{5,13},{6,14},{7,3},{8,16},{9,1},{1... | collective-permute-start | bytes 2457608 | tf_op jit(solution)/shard_map/ppermute | solution.py:348
  5.8 41.2 %collective-permute-start.6 = (bf16[80,5120]{1,0:T(8,128)(2,1)S(1)}, bf16[80,5120]{1,0:T(8,128)(2,1)S(1)}, u32[]{:S(2)}, u32[]{:S(2)}) collective-permute-start(bf16[80,5120]{1,0:T(8,128)(2,1)S(1)} %constant_dynamic-update-slice_fusion.refs_0_.refs_9_), channel_id=1, source_target_pairs={{0,2},{1,3},{2,0},{3,1},{4,6},{5,7},{6,4},{7,5},{8,10},{9,11},{10,... | collective-permute-start | bytes 2457608 | tf_op jit(solution)/shard_map/ppermute | solution.py:348
  9.3 31.8 %collective-permute-start.4 = (bf16[512,1280]{1,0:T(8,128)(2,1)}, bf16[512,1280]{1,0:T(8,128)(2,1)}, u32[]{:S(2)}, u32[]{:S(2)}) collective-permute-start(bf16[512,1280]{1,0:T(8,128)(2,1)} %get-tuple-element.566), channel_id=1, source_target_pairs={{0,1},{1,0},{2,3},{3,2},{4,5},{5,4},{6,7},{7,6},{8,9},{9,8},{10,11... | collective-permute-start | bytes 3932168 | tf_op jit(solution)/shard_map/ppermute | solution.py:348
  30.9 20.9 %collective-permute-start.7 = (bf16[80,5120]{1,0:T(8,128)(2,1)S(1)}, bf16[80,5120]{1,0:T(8,128)(2,1)S(1)}, u32[]{:S(2)}, u32[]{:S(2)}) collective-permute-start(bf16[80,5120]{1,0:T(8,128)(2,1)S(1)} %collective-permute-done.refs_1_.refs_10_), channel_id=1, source_target_pairs={{0,2},{1,3},{2,0},{3,1},{4,6},{5,7},{6,4},{7,5},{8,10},{9,11},{10,... | collective-permute-start | bytes 2457608 | tf_op jit(solution)/shard_map/ppermute | solution.py:348
  70.4 33.7 %collective-permute-start.16 = (bf16[640,1280]{1,0:T(8,128)(2,1)}, bf16[640,1280]{1,0:T(8,128)(2,1)}, u32[]{:S(2)}, u32[]{:S(2)}) collective-permute-start(bf16[640,1280]{1,0:T(8,128)(2,1)} %pad_maximum_fusion.2.refs_5_), channel_id=1, source_target_pairs={{0,8},{1,5},{2,6},{3,11},{4,0},{5,13},{6,14},{7,3},{8,16},{9,1},{1... | collective-permute-start | bytes 4915208 | tf_op jit(solution)/shard_map/ppermute | solution.py:348
  80.9 23.2 %collective-permute-start.17 = (bf16[256,1280]{1,0:T(8,128)(2,1)}, bf16[256,1280]{1,0:T(8,128)(2,1)}, u32[]{:S(2)}, u32[]{:S(2)}) collective-permute-start(bf16[256,1280]{1,0:T(8,128)(2,1)} %get-tuple-element.576), channel_id=1, source_target_pairs={{0,1},{1,0},{2,3},{3,2},{4,5},{5,4},{6,7},{7,6},{8,9},{9,8},{10,11... | collective-permute-start | bytes 1966088 | tf_op jit(solution)/shard_map/ppermute | solution.py:348
  104.2 22.1 %collective-permute-start.18 = (bf16[640,1280]{1,0:T(8,128)(2,1)}, bf16[640,1280]{1,0:T(8,128)(2,1)}, u32[]{:S(2)}, u32[]{:S(2)}) collective-permute-start(bf16[640,1280]{1,0:T(8,128)(2,1)} %collective-permute-done.16.refs_6_), channel_id=1, source_target_pairs={{0,8},{1,5},{2,6},{3,11},{4,0},{5,13},{6,14},{7,3},{8,16},{9,1},{1... | collective-permute-start | bytes 4915208 | tf_op jit(solution)/shard_map/ppermute | solution.py:348
  128.6 27.5 %collective-permute-start.20 = (bf16[1024,1280]{1,0:T(8,128)(2,1)S(1)}, bf16[1024,1280]{1,0:T(8,128)(2,1)}, u32[]{:S(2)}, u32[]{:S(2)}) collective-permute-start(bf16[1024,1280]{1,0:T(8,128)(2,1)S(1)} %pad_maximum_fusion.1.refs_2_.g_own.g_ref), channel_id=1, source_target_pairs={{0,2},{1,3},{2,0},{3,1},{4,6},{5,7},{6,4},{7,5},{8,10},{9,11},{10,... | collective-permute-start | bytes 7864328 | tf_op jit(solution)/shard_map/ppermute | solution.py:348
  129.3 26.7 %collective-permute-start.21 = (bf16[640,1280]{1,0:T(8,128)(2,1)}, bf16[640,1280]{1,0:T(8,128)(2,1)}, u32[]{:S(2)}, u32[]{:S(2)}) collective-permute-start(bf16[640,1280]{1,0:T(8,128)(2,1)} %collective-permute-done.18.refs_7_), channel_id=1, source_target_pairs={{0,8},{1,5},{2,6},{3,11},{4,0},{5,13},{6,14},{7,3},{8,16},{9,1},{1... | collective-permute-start | bytes 4915208 | tf_op jit(solution)/shard_map/ppermute | solution.py:348
  156.1 44.0 %collective-permute-start.24 = (bf16[640,1280]{1,0:T(8,128)(2,1)}, bf16[640,1280]{1,0:T(8,128)(2,1)}, u32[]{:S(2)}, u32[]{:S(2)}) collective-permute-start(bf16[640,1280]{1,0:T(8,128)(2,1)} %pad_maximum_fusion.2.refs_5_), channel_id=1, source_target_pairs={{0,4},{1,9},{2,10},{3,7},{4,12},{5,1},{6,2},{7,15},{8,0},{9,17},{1... | collective-permute-start | bytes 4915208 | tf_op jit(solution)/shard_map/ppermute | solution.py:348
  158.0 64.5 %collective-permute-start.23 = (bf16[640,1280]{1,0:T(8,128)(2,1)}, bf16[640,1280]{1,0:T(8,128)(2,1)}, u32[]{:S(2)}, u32[]{:S(2)}) collective-permute-start(bf16[640,1280]{1,0:T(8,128)(2,1)} %collective-permute-done.21.refs_8_), channel_id=1, source_target_pairs={{0,8},{1,5},{2,6},{3,11},{4,0},{5,13},{6,14},{7,3},{8,16},{9,1},{1... | collective-permute-start | bytes 4915208 | tf_op jit(solution)/shard_map/ppermute | solution.py:348
  159.6 62.9 %collective-permute-start.26 = (bf16[640,1280]{1,0:T(8,128)(2,1)}, bf16[640,1280]{1,0:T(8,128)(2,1)}, u32[]{:S(2)}, u32[]{:S(2)}) collective-permute-start(bf16[640,1280]{1,0:T(8,128)(2,1)} %collective-permute-done.21.refs_8_), channel_id=1, source_target_pairs={{0,1},{1,0},{2,3},{3,2},{4,5},{5,4},{6,7},{7,6},{8,9},{9,8},{10,11... | collective-permute-start | bytes 4915208 | tf_op jit(solution)/shard_map/ppermute | solution.py:348
  200.1 22.4 %collective-permute-start.25 = (bf16[640,1280]{1,0:T(8,128)(2,1)}, bf16[640,1280]{1,0:T(8,128)(2,1)S(1)}, u32[]{:S(2)}, u32[]{:S(2)}) collective-permute-start(bf16[640,1280]{1,0:T(8,128)(2,1)} %collective-permute-done.24.refs_6_), channel_id=1, source_target_pairs={{0,4},{1,9},{2,10},{3,7},{4,12},{5,1},{6,2},{7,15},{8,0},{9,17},{1... | collective-permute-start | bytes 4915208 | tf_op jit(solution)/shard_map/ppermute | solution.py:348
  264.3 21.4 %collective-permute-start.27 = (bf16[1024,1280]{1,0:T(8,128)(2,1)}, bf16[1024,1280]{1,0:T(8,128)(2,1)S(1)}, u32[]{:S(2)}, u32[]{:S(2)}) collective-permute-start(bf16[1024,1280]{1,0:T(8,128)(2,1)} %get-tuple-element.354), channel_id=1, source_target_pairs={{0,2},{1,3},{2,0},{3,1},{4,6},{5,7},{6,4},{7,5},{8,10},{9,11},{10,... | collective-permute-start | bytes 7864328 | tf_op jit(solution)/shard_map/ppermute | solution.py:348
  264.7 21.0 %collective-permute-start.28 = (bf16[1024,1280]{1,0:T(8,128)(2,1)}, bf16[1024,1280]{1,0:T(8,128)(2,1)}, u32[]{:S(2)}, u32[]{:S(2)}) collective-permute-start(bf16[1024,1280]{1,0:T(8,128)(2,1)} %get-tuple-element.355), channel_id=1, source_target_pairs={{0,2},{1,3},{2,0},{3,1},{4,6},{5,7},{6,4},{7,5},{8,10},{9,11},{10,... | collective-permute-start | bytes 7864328 | tf_op jit(solution)/shard_map/ppermute | solution.py:348
  285.7 57.2 %collective-permute-start.29 = (bf16[640,1280]{1,0:T(8,128)(2,1)}, bf16[640,1280]{1,0:T(8,128)(2,1)}, u32[]{:S(2)}, u32[]{:S(2)}) collective-permute-start(bf16[640,1280]{1,0:T(8,128)(2,1)} %get-tuple-element.370), channel_id=1, source_target_pairs={{0,4},{1,9},{2,10},{3,7},{4,12},{5,1},{6,2},{7,15},{8,0},{9,17},{1... | collective-permute-start | bytes 4915208 | tf_op jit(solution)/shard_map/ppermute | solution.py:348
  286.8 56.2 %collective-permute-start.30 = (bf16[640,1280]{1,0:T(8,128)(2,1)}, bf16[640,1280]{1,0:T(8,128)(2,1)}, u32[]{:S(2)}, u32[]{:S(2)}) collective-permute-start(bf16[640,1280]{1,0:T(8,128)(2,1)} %get-tuple-element.371), channel_id=1, source_target_pairs={{0,1},{1,0},{2,3},{3,2},{4,5},{5,4},{6,7},{7,6},{8,9},{9,8},{10,11... | collective-permute-start | bytes 4915208 | tf_op jit(solution)/shard_map/ppermute | solution.py:348
  288.9 80.3 %collective-permute-start.32 = (bf16[640,1280]{1,0:T(8,128)(2,1)}, bf16[640,1280]{1,0:T(8,128)(2,1)}, u32[]{:S(2)}, u32[]{:S(2)}) collective-permute-start(bf16[640,1280]{1,0:T(8,128)(2,1)} %get-tuple-element.391), channel_id=1, source_target_pairs={{0,8},{1,5},{2,6},{3,11},{4,0},{5,13},{6,14},{7,3},{8,16},{9,1},{1... | collective-permute-start | bytes 4915208 | tf_op jit(solution)/shard_map/ppermute | solution.py:348
  289.4 79.8 %collective-permute-start.33 = (bf16[640,1280]{1,0:T(8,128)(2,1)}, bf16[640,1280]{1,0:T(8,128)(2,1)}, u32[]{:S(2)}, u32[]{:S(2)}) collective-permute-start(bf16[640,1280]{1,0:T(8,128)(2,1)} %get-tuple-element.392), channel_id=1, source_target_pairs={{0,1},{1,0},{2,3},{3,2},{4,5},{5,4},{6,7},{7,6},{8,9},{9,8},{10,11... | collective-permute-start | bytes 4915208 | tf_op jit(solution)/shard_map/ppermute | solution.py:348
  347.4 21.9 %collective-permute-start.31 = (bf16[640,1280]{1,0:T(8,128)(2,1)}, bf16[640,1280]{1,0:T(8,128)(2,1)S(1)}, u32[]{:S(2)}, u32[]{:S(2)}) collective-permute-start(bf16[640,1280]{1,0:T(8,128)(2,1)} %add_convert_fusion.3), channel_id=1, source_target_pairs={{0,4},{1,9},{2,10},{3,7},{4,12},{5,1},{6,2},{7,15},{8,0},{9,17},{1... | collective-permute-start | bytes 4915208 | tf_op jit(solution)/shard_map/ppermute | solution.py:348
  372.7 33.0 %collective-permute-start.37 = (bf16[640,1280]{1,0:T(8,128)(2,1)}, bf16[640,1280]{1,0:T(8,128)(2,1)S(1)}, u32[]{:S(2)}, u32[]{:S(2)}) collective-permute-start(bf16[640,1280]{1,0:T(8,128)(2,1)} %add_convert_fusion.2), channel_id=1, source_target_pairs={{0,4},{1,9},{2,10},{3,7},{4,12},{5,1},{6,2},{7,15},{8,0},{9,17},{1... | collective-permute-start | bytes 4915208 | tf_op jit(solution)/shard_map/ppermute | solution.py:348
  374.4 31.3 %collective-permute-start.38 = (bf16[256,1280]{1,0:T(8,128)(2,1)}, bf16[256,1280]{1,0:T(8,128)(2,1)S(1)}, u32[]{:S(2)}, u32[]{:S(2)}) collective-permute-start(bf16[256,1280]{1,0:T(8,128)(2,1)} %get-tuple-element.436), channel_id=1, source_target_pairs={{0,1},{1,0},{2,3},{3,2},{4,5},{5,4},{6,7},{7,6},{8,9},{9,8},{10,11... | collective-permute-start | bytes 1966088 | tf_op jit(solution)/shard_map/ppermute | solution.py:348
  385.2 21.3 %collective-permute-start.35 = (bf16[80,3584]{1,0:T(8,128)(2,1)}, bf16[80,3584]{1,0:T(8,128)(2,1)}, u32[]{:S(2)}, u32[]{:S(2)}) collective-permute-start(bf16[80,3584]{1,0:T(8,128)(2,1)} %get-tuple-element.560), channel_id=1, source_target_pairs={{0,4},{1,9},{2,10},{3,7},{4,12},{5,1},{6,2},{7,15},{8,0},{9,17},{1... | collective-permute-start | bytes 1720328 | tf_op jit(solution)/shard_map/ppermute | solution.py:348
  385.8 20.7 %collective-permute-start.36 = (bf16[80,3584]{1,0:T(8,128)(2,1)}, bf16[80,3584]{1,0:T(8,128)(2,1)}, u32[]{:S(2)}, u32[]{:S(2)}) collective-permute-start(bf16[80,3584]{1,0:T(8,128)(2,1)} %get-tuple-element.559), channel_id=1, source_target_pairs={{0,8},{1,5},{2,6},{3,11},{4,0},{5,13},{6,14},{7,3},{8,16},{9,1},{1... | collective-permute-start | bytes 1720328 | tf_op jit(solution)/shard_map/ppermute | solution.py:348
  408.1 27.6 %collective-permute-start.41 = (bf16[640,1280]{1,0:T(8,128)(2,1)}, bf16[640,1280]{1,0:T(8,128)(2,1)S(1)}, u32[]{:S(2)}, u32[]{:S(2)}) collective-permute-start(bf16[640,1280]{1,0:T(8,128)(2,1)} %add_convert_fusion.1), channel_id=1, source_target_pairs={{0,4},{1,9},{2,10},{3,7},{4,12},{5,1},{6,2},{7,15},{8,0},{9,17},{1... | collective-permute-start | bytes 4915208 | tf_op jit(solution)/shard_map/ppermute | solution.py:348
  409.6 26.1 %collective-permute-start.40 = (bf16[256,1280]{1,0:T(8,128)(2,1)}, bf16[256,1280]{1,0:T(8,128)(2,1)S(1)}, u32[]{:S(2)}, u32[]{:S(2)}) collective-permute-start(bf16[256,1280]{1,0:T(8,128)(2,1)} %get-tuple-element.458), channel_id=1, source_target_pairs={{0,1},{1,0},{2,3},{3,2},{4,5},{5,4},{6,7},{7,6},{8,9},{9,8},{10,11... | collective-permute-start | bytes 1966088 | tf_op jit(solution)/shard_map/ppermute | solution.py:348
  412.5 23.2 %collective-permute-start.39 = (bf16[80,3584]{1,0:T(8,128)(2,1)}, bf16[80,3584]{1,0:T(8,128)(2,1)}, u32[]{:S(2)}, u32[]{:S(2)}) collective-permute-start(bf16[80,3584]{1,0:T(8,128)(2,1)} %fusion.5), channel_id=1, source_target_pairs={{0,4},{1,9},{2,10},{3,7},{4,12},{5,1},{6,2},{7,15},{8,0},{9,17},{1... | collective-permute-start | bytes 1720328 | tf_op jit(solution)/shard_map/ppermute | solution.py:348
  460.2 63.0 %collective-permute-start.52 = (bf16[512,1280]{1,0:T(8,128)(2,1)}, bf16[512,1280]{1,0:T(8,128)(2,1)}, u32[]{:S(2)}, u32[]{:S(2)}) collective-permute-start(bf16[512,1280]{1,0:T(8,128)(2,1)} %get-tuple-element.514), channel_id=1, source_target_pairs={{0,1},{1,0},{2,3},{3,2},{4,5},{5,4},{6,7},{7,6},{8,9},{9,8},{10,11... | collective-permute-start | bytes 3932168 | tf_op jit(solution)/shard_map/ppermute | solution.py:348
  464.2 23.5 %collective-permute-start.45 = (bf16[80,3584]{1,0:T(8,128)(2,1)}, bf16[80,3584]{1,0:T(8,128)(2,1)}, u32[]{:S(2)}, u32[]{:S(2)}) collective-permute-start(bf16[80,3584]{1,0:T(8,128)(2,1)} %get-tuple-element.556), channel_id=1, source_target_pairs={{0,4},{1,9},{2,10},{3,7},{4,12},{5,1},{6,2},{7,15},{8,0},{9,17},{1... | collective-permute-start | bytes 1720328 | tf_op jit(solution)/shard_map/ppermute | solution.py:348
  465.2 22.4 %collective-permute-start.46 = (bf16[80,3584]{1,0:T(8,128)(2,1)S(1)}, bf16[80,3584]{1,0:T(8,128)(2,1)}, u32[]{:S(2)}, u32[]{:S(2)}) collective-permute-start(bf16[80,3584]{1,0:T(8,128)(2,1)S(1)} %get-tuple-element.555), channel_id=1, source_target_pairs={{0,8},{1,5},{2,6},{3,11},{4,0},{5,13},{6,14},{7,3},{8,16},{9,1},{1... | collective-permute-start | bytes 1720328 | tf_op jit(solution)/shard_map/ppermute | solution.py:348
  492.5 30.7 %collective-permute-start.50 = (bf16[320,1280]{1,0:T(8,128)(2,1)S(1)}, bf16[320,1280]{1,0:T(8,128)(2,1)S(1)}, u32[]{:S(2)}, u32[]{:S(2)}) collective-permute-start(bf16[320,1280]{1,0:T(8,128)(2,1)S(1)} %get-tuple-element.543), channel_id=1, source_target_pairs={{0,1},{1,0},{2,3},{3,2},{4,5},{5,4},{6,7},{7,6},{8,9},{9,8},{10,11... | collective-permute-start | bytes 2457608 | tf_op jit(solution)/shard_map/ppermute | solution.py:348
  502.6 23.4 %collective-permute-start.51 = (bf16[80,3584]{1,0:T(8,128)(2,1)S(1)}, bf16[80,3584]{1,0:T(8,128)(2,1)S(1)}, u32[]{:S(2)}, u32[]{:S(2)}) collective-permute-start(bf16[80,3584]{1,0:T(8,128)(2,1)S(1)} %fusion), channel_id=1, source_target_pairs={{0,1},{1,0},{2,3},{3,2},{4,5},{5,4},{6,7},{7,6},{8,9},{9,8},{10,11... | collective-permute-start | bytes 1720328 | tf_op jit(solution)/shard_map/ppermute | solution.py:348
  (107 other events, 1017.7 us)

commit v6 on v5

--- a/solution.py
+++ b/solution.py
@@ -1193,7 +1193,6 @@
     way_first = next(steps_first)
     backs.append(back(cut + one, pairs - cut - one, gatt))
     backs, way_first, way, hid_got, hid_send = fence(backs, way_first, way, hid_got, hid_send)
-    way_first = steps_first.send(way_first)
     hid_got.append(ring.swap_blk(hid_send[1]))
     way = steps.send(way)
     grads = [t[i] for i in range(3) for t in backs]
@@ -1225,22 +1224,23 @@
     in_own, in_sums, in_sums_send, way_first, way_second, w_up_grad = fence(
         in_own, in_sums, in_sums_send, way_first, way_second, w_up_grad
     )
-    first_sum = steps_first.send(way_first)
-    first_got = ring.swap_blk(first_sum)
+    way_first = steps_first.send(way_first)
     way_second = steps_second.send(way_second)
     ln1_sums = (in_sums + in_sums_send)[:2].reshape(-1)
     steps_sums = ring.total(side_by_side([sums_early, ln1_sums]))
     sums = next(steps_sums)
-    sums = steps_sums.send(sums)
-    way_second, sums = fence(way_second, sums)
+    way_first, way_second, sums = fence(way_first, way_second, sums)
+    first_sum = steps_first.send(way_first)
+    first_got = ring.swap_blk(first_sum)
     way_second = steps_second.send(way_second)
     sums = steps_sums.send(sums)
     way_second, sums = fence(way_second, sums)
     way_second = steps_second.send(way_second)
     sums = steps_sums.send(sums)
-    way_second, sums = fence(way_second, sums)
+    way_second, sums, ffn_got = fence(way_second, sums, ffn_got)
     second_sum = steps_second.send(way_second)
     second_got = ring.swap_blk(second_sum)
+    sums = steps_sums.send(sums)
     sums = steps_sums.send(sums)
     down_sum, down_got, first_sum, first_got, in_got, second_sum, _ = fence(
         ffn_sum[1], ffn_got[1], first_sum, first_got, in_got, second_sum, sums[0]

time: 545 us -> 549 us (level)
  transfers between devices with their start and end apart: 64 -> 64, of which waited for: 20 -> 16; matrix products, arithmetic and copies ran while one was open for 12% -> 12% of each run, Pallas kernels for 53% -> 52%
where the time goes in v6:
time: 549 us; the launch traced here: 540 us
  Pallas kernels  323 us (59%)
  waiting for transfers between devices  72.1 us (13%)
  starting transfers between devices  61.9 us (11%)
  other arithmetic  50.2 us (9%)
  local copies, waits for them, and re-layouts  30.8 us (6%)
    pallas_call x2, Pallas kernels, ffn_call(): pl.pallas_call(partial(ffn_kernel, n, later), grid=(2 * half,), in_specs=...  77.9 us
    ppermute x64, waiting for transfers between devices, permute(): return lax.ppermute(x, AXES, pairs)  72.1 us
    ppermute x64, starting transfers between devices, permute(): return lax.ppermute(x, AXES, pairs)  61.9 us
    pallas_call x3, Pallas kernels, attend_back_call(): pl.pallas_call(partial(attend_back_kernel, qrows), grid=(count,), in_spec...  60.5 us
    pallas_call x2, Pallas kernels, ffn_weights_call(): pl.pallas_call(partial(ffn_weights_kernel, n), in_specs=[ANY] * 6, out_sp...  41.6 us
    pallas_call x2, Pallas kernels, attend_call(): pl.pallas_call(partial(attend_kernel, qrows, ahead), grid=(count,), in_sp...  34.1 us
    pallas_call x2, Pallas kernels, in_call(): pl.pallas_call(partial(in_kernel, n, len(grads)), grid_spec=pltpu.Prefetc...  31.3 us
    pallas_call x2, Pallas kernels, att_weights_call(): pl.pallas_call(partial(att_weights_kernel, n, [len(l) for l in lefts] + [...  29.6 us
  transfers between devices with their start and end apart: 64, of which 16 were waited for; matrix products, arithmetic and copies ran while one was open for 12% of the time, Pallas kernels for 52%

profile of v6, /device:TPU:0, one launch (start us, length us, event | category | flops | bytes accessed | tf_op | source)
XLA Modules:
  0.0 540.1 jit_solution(2850992349817816215)
XLA Ops:
  2.7 3.1 collective-permute-start
  5.9 3.4 dynamic-slice_bitcast_fusion.2
  20.5 3.8 collective-permute-done.refs_1_.refs_10_
  30.9 10.2 %collective-permute-done.4 = bf16[512,1280]{1,0:T(8,128)(2,1)} collective-permute-done((bf16[512,1280]{1,0:T(8,128)(2,1)}, bf16[512,1280]{1,0:T(8,128)(2,1)}, u32[]{:S(2)}, u32[]{:S(2)}) %collective-permute-start.4) | collective-permute-done | bytes 1310752 | tf_op jit(solution)/shard_map/ppermute | solution.py:348
  41.1 3.6 collective-permute-done.2.refs_2_.refs_11_
  48.8 3.0 pad_maximum_fusion.x_ref
  51.8 6.2 %collective-permute-done.5.refs_3_.refs_12_ = bf16[80,5120]{1,0:T(8,128)(2,1)S(1)} collective-permute-done((bf16[80,5120]{1,0:T(8,128)(2,1)S(1)}, bf16[80,5120]{1,0:T(8,128)(2,1)S(1)}, u32[]{:S(2)}, u32[]{:S(2)}) %collective-permute-start.5) | collective-permute-done | bytes 819232 | tf_op jit(solution)/shard_map/ppermute | solution.py:348
  60.9 9.5 %collective-permute-done.11.refs_4_.refs_13_ = bf16[80,5120]{1,0:T(8,128)(2,1)S(1)} collective-permute-done((bf16[80,5120]{1,0:T(8,128)(2,1)S(1)}, bf16[80,5120]{1,0:T(8,128)(2,1)S(1)}, u32[]{:S(2)}, u32[]{:S(2)}) %collective-permute-start.11) | collective-permute-done | bytes 819232 | tf_op jit(solution)/shard_map/ppermute | solution.py:348
  71.7 7.5 %collective-permute-done.12.refs_7_.refs_16_ = bf16[80,5120]{1,0:T(8,128)(2,1)S(1)} collective-permute-done((bf16[80,5120]{1,0:T(8,128)(2,1)S(1)}, bf16[80,5120]{1,0:T(8,128)(2,1)S(1)}, u32[]{:S(2)}, u32[]{:S(2)}) %collective-permute-start.12) | collective-permute-done | bytes 819232 | tf_op jit(solution)/shard_map/ppermute | solution.py:348
  83.7 20.4 %qkv.1 = (bf16[1024,1280]{1,0:T(8,128)(2,1)}, bf16[1024,1280]{1,0:T(8,128)(2,1)}, bf16[1024,1280]{1,0:T(8,128)(2,1)}, bf16[1024,1280]{1,0:T(8,128)(2,1)}) custom-call(s32[16]{0:T(128)} %pad_add_fusion.2.place_ref, bf16[1024,1280]{1,0:T(8,128)(2,1)} %pad_maximum_fusion.x_ref, f32[1,1280]{1,0:T(1,128)} %reshape.227.gain_ref, f32[1,1280]{1,0:T(1,128)} %reshape.228.bias_ref, ...), custom_call_target="tpu_custom_call" | custom-call | flops 201326592 | bytes 458752 | tf_op jit(solution)/shard_map/qkv/pallas_call | solution.py:489
  106.2 20.0 %attend.2 = (bf16[1024,768]{1,0:T(8,128)(2,1)}, f32[12,1,1024]{2,1,0:T(1,128)}) custom-call(f32[1024,1]{1,0:T(8,128)} %compare_select_fusion.mask_ref, f32[1024,1]{1,0:T(8,128)} %convert_element_type.346.keep_ref, bf16[1024,1280]{1,0:T(8,128)(2,1)} %get-tuple-element.323.q_ref, bf16[1024,1280]{1,0:T(8,128)(2,1)} %get-tuple-element.324.k_ref, ...), custom_call_target="tpu_custom_call" | custom-call | flops 322122560 | bytes 125829 | tf_op jit(solution)/shard_map/attend/pallas_call | solution.py:562
  131.0 14.0 %attend.3 = (bf16[1024,512]{1,0:T(8,128)(2,1)}, f32[8,1,1024]{2,1,0:T(1,128)}) custom-call(f32[1024,1]{1,0:T(8,128)} %compare_select_fusion.mask_ref, f32[1024,1]{1,0:T(8,128)} %convert_element_type.346.keep_ref, bf16[1024,1280]{1,0:T(8,128)(2,1)} %get-tuple-element.323.q_ref, bf16[1024,1280]{1,0:T(8,128)(2,1)} %get-tuple-element.324.k_ref, ...), custom_call_target="tpu_custom_call" | custom-call | flops 214748368 | bytes 83886 | tf_op jit(solution)/shard_map/attend/pallas_call | solution.py:562
  145.1 10.9 %out.1 = (f32[1024,1280]{1,0:T(8,128)}, bf16[1024,1280]{1,0:T(8,128)(2,1)}) custom-call(s32[16]{0:T(128)} %pad_add_fusion.2.place_ref, bf16[1024,1280]{1,0:T(8,128)(2,1)} %pad_maximum_fusion.x_ref, f32[1,1280]{1,0:T(1,128)} %reshape.231.bias_ref, f32[1,1280]{1,0:T(1,128)} %reshape.232.gain_ref, f32[1,1280]{1,0:T(1,128)} %reshape.233.shift_ref, ...), custom_call_target="tpu_custom_call" | custom-call | flops 134217728 | bytes 327680 | tf_op jit(solution)/shard_map/out/pallas_call | solution.py:671
  162.8 37.3 %ffn.2 = (bf16[2048,1280]{1,0:T(8,128)(2,1)}, bf16[2048,1280]{1,0:T(8,128)(2,1)}, f32[1,1280]{1,0:T(1,128)}, f32[2048,1280]{1,0:T(8,128)}, f32[2048,1280]{1,0:T(8,128)}) custom-call(bf16[1024,1280]{1,0:T(8,128)(2,1)} %get-tuple-element.331.refs_0_.b_own, bf16[1024,1280]{1,0:T(8,128)(2,1)} %copy-done.2, bf16[1024,1280]{1,0:T(8,128)(2,1)} %copy-done.1, ...), custom_call_target="tpu_custom_call" | custom-call | flops 805306368 | bytes 629145 | tf_op jit(solution)/shard_map/ffn/pallas_call | solution.py:777
  201.7 20.8 %ffn_weights.2 = (bf16[640,1280]{1,0:T(8,128)(2,1)}, bf16[640,1280]{1,0:T(8,128)(2,1)}, bf16[640,1280]{1,0:T(8,128)(2,1)}, bf16[640,1280]{1,0:T(8,128)(2,1)}) custom-call(bf16[2048,1280]{1,0:T(8,128)(2,1)} %get-tuple-element.340.gz, bf16[2048,1280]{1,0:T(8,128)(2,1)} %get-tuple-element.341.h, bf16[1024,1280]{1,0:T(8,128)(2,1)} %get-tuple-element.331.refs_0_.b_own, ...), custom_call_target="tpu_custom_call" | custom-call | flops 402653184 | bytes 419430 | tf_op jit(solution)/shard_map/ffn_weights/pallas_call | solution.py:840
  223.7 40.6 %ffn.3 = (bf16[2048,1280]{1,0:T(8,128)(2,1)}, bf16[2048,1280]{1,0:T(8,128)(2,1)}, f32[1,1280]{1,0:T(1,128)}, bf16[1024,1280]{1,0:T(8,128)(2,1)}, bf16[1024,1280]...) custom-call(bf16[1024,1280]{1,0:T(8,128)(2,1)} %get-tuple-element.331.refs_0_.b_own, ...), custom_call_target="tpu_custom_call" | custom-call | flops 805306368 | bytes 1048576 | tf_op jit(solution)/shard_map/ffn/pallas_call | solution.py:777
  264.9 20.8 %ffn_weights.3 = (bf16[640,1280]{1,0:T(8,128)(2,1)}, bf16[640,1280]{1,0:T(8,128)(2,1)}, bf16[640,1280]{1,0:T(8,128)(2,1)}, bf16[640,1280]{1,0:T(8,128)(2,1)}) custom-call(bf16[2048,1280]{1,0:T(8,128)(2,1)} %get-tuple-element.350.gz, bf16[2048,1280]{1,0:T(8,128)(2,1)} %get-tuple-element.351.h, bf16[1024,1280]{1,0:T(8,128)(2,1)} %get-tuple-element.331.refs_0_.b_own, ...), custom_call_target="tpu_custom_call" | custom-call | flops 402653184 | bytes 419430 | tf_op jit(solution)/shard_map/ffn_weights/pallas_call | solution.py:840
  290.6 16.6 %mid.1 = (bf16[1024,1280]{1,0:T(8,128)(2,1)}, bf16[1024,1280]{1,0:T(8,128)(2,1)}, bf16[1024,1280]{1,0:T(8,128)(2,1)}, f32[8,1280]{1,0:T(8,128)}) custom-call(s32[16]{0:T(128)} %pad_add_fusion.2.place_ref, bf16[1024,1280]{1,0:T(8,128)(2,1)} %get-tuple-element.359.oo_ref, bf16[1024,1280]{1,0:T(8,128)(2,1)} %copy-done.20, ...), custom_call_target="tpu_custom_call" | custom-call | flops 134217728 | bytes 851968 | tf_op jit(solution)/shard_map/mid/pallas_call | solution.py:890
  307.2 34.6 %attend_back.3 = (bf16[1024,768]{1,0:T(8,128)(2,1)}, bf16[1024,768]{1,0:T(8,128)(2,1)}, bf16[1024,768]{1,0:T(8,128)(2,1)}, f32[1,768]{1,0:T(1,128)}, f32[1,768]{1,0:T(1,128)}) custom-call(f32[1024,1]{1,0:T(8,128)} %compare_select_fusion.mask_ref, bf16[1024,1280]{1,0:T(8,128)(2,1)} %get-tuple-element.323.q_ref, bf16[1024,1280]{1,0:T(8,128)(2,1)} %get-tuple-element.324.k_ref, ...), custom_call_target="tpu_custom_call" | custom-call | flops 515396064 | bytes 251658 | tf_op jit(solution)/shard_map/attend_back/pallas_call | solution.py:625
  343.7 3.7 add_convert_fusion.3
  349.4 19.8 %att_weights.2 = (bf16[80,3584]{1,0:T(8,128)(2,1)}, bf16[80,3584]{1,0:T(8,128)(2,1)}, bf16[80,3584]{1,0:T(8,128)(2,1)}, bf16[80,3584]{1,0:T(8,128)(2,1)}, bf16[8...) custom-call(s32[16]{0:T(128)} %pad_add_fusion.2.place_ref, ...), custom_call_target="tpu_custom_call" | custom-call | flops 281857216 | bytes 330301 | tf_op jit(solution)/shard_map/att_weights/pallas_call | solution.py:968
  369.5 3.2 add_convert_fusion.2
  375.2 7.5 %attend_back.4 = (bf16[1024,128]{1,0:T(8,128)(2,1)}, bf16[1024,128]{1,0:T(8,128)(2,1)}, bf16[1024,128]{1,0:T(8,128)(2,1)}, f32[1,128]{1,0:T(1,128)}, f32[1,128]{1,0:T(1,128)}) custom-call(f32[1024,1]{1,0:T(8,128)} %compare_select_fusion.mask_ref, bf16[1024,1280]{1,0:T(8,128)(2,1)} %get-tuple-element.323.q_ref, bf16[1024,1280]{1,0:T(8,128)(2,1)} %get-tuple-element.324.k_ref, ...), custom_call_target="tpu_custom_call" | custom-call | flops 85899344 | bytes 41943 | tf_op jit(solution)/shard_map/attend_back/pallas_call | solution.py:625
  387.3 18.4 %attend_back.5 = (bf16[1024,384]{1,0:T(8,128)(2,1)}, bf16[1024,384]{1,0:T(8,128)(2,1)}, bf16[1024,384]{1,0:T(8,128)(2,1)}, f32[1,384]{1,0:T(1,128)}, f32[1,384]{1,0:T(1,128)}) custom-call(f32[1024,1]{1,0:T(8,128)} %compare_select_fusion.mask_ref, bf16[1024,1280]{1,0:T(8,128)(2,1)} %get-tuple-element.323.q_ref, bf16[1024,1280]{1,0:T(8,128)(2,1)} %get-tuple-element.324.k_ref, ...), custom_call_target="tpu_custom_call" | custom-call | flops 257698032 | bytes 125829 | tf_op jit(solution)/shard_map/attend_back/pallas_call | solution.py:625
  410.5 15.5 %in.2 = (bf16[512,1280]{1,0:T(8,128)(2,1)}, f32[8,1280]{1,0:T(8,128)}) custom-call(s32[16]{0:T(128)} %pad_add_fusion.2.place_ref, bf16[1024,1280]{1,0:T(8,128)(2,1)} %pad_maximum_fusion.x_ref, bf16[1024,1280]{1,0:T(8,128)(2,1)} %get-tuple-element.365.refs_6_.gr_ref, f32[1,1280]{1,0:T(1,128)} %reshape.227.gain_ref, ...), custom_call_target="tpu_custom_call" | custom-call | flops 134217728 | bytes 380108 | tf_op jit(solution)/shard_map/in/pallas_call | solution.py:1026
  426.0 3.7 collective-permute-done.40
  437.3 9.9 %att_weights.3 = (bf16[80,1536]{1,0:T(8,128)(2,1)}, bf16[80,1536]{1,0:T(8,128)(2,1)}, bf16[80,1536]{1,0:T(8,128)(2,1)}, bf16[80,1536]{1,0:T(8,128)(2,1)}, bf16[8...) custom-call(s32[16]{0:T(128)} %pad_add_fusion.2.place_ref, ...), custom_call_target="tpu_custom_call" | custom-call | flops 120795952 | bytes 141557 | tf_op jit(solution)/shard_map/att_weights/pallas_call | solution.py:968
  447.2 3.7 collective-permute-done.42
  454.0 2.8 fusion.3
  464.5 15.8 %in.3 = (f32[512,1280]{1,0:T(8,128)}, f32[8,1280]{1,0:T(8,128)}) custom-call(s32[16]{0:T(128)} %pad_add_fusion.2.place_ref, bf16[1024,1280]{1,0:T(8,128)(2,1)} %pad_maximum_fusion.x_ref, bf16[1024,1280]{1,0:T(8,128)(2,1)} %get-tuple-element.365.refs_6_.gr_ref, f32[1,1280]{1,0:T(1,128)} %reshape.227.gain_ref, ...), custom_call_target="tpu_custom_call" | custom-call | flops 134217728 | bytes 380108 | tf_op jit(solution)/shard_map/in/pallas_call | solution.py:1026
  489.7 13.1 %collective-permute-done.50 = bf16[80,1536]{1,0:T(8,128)(2,1)S(1)} collective-permute-done((bf16[80,1536]{1,0:T(8,128)(2,1)S(1)}, bf16[80,1536]{1,0:T(8,128)(2,1)S(1)}, u32[]{:S(2)}, u32[]{:S(2)}) %collective-permute-start.50) | collective-permute-done | bytes 245792 | tf_op jit(solution)/shard_map/ppermute | solution.py:348
  519.4 3.8 collective-permute-done.55
  (356 shorter events, 130.8 us)
Async XLA Ops:
  2.7 21.5 %collective-permute-start = (bf16[80,5120]{1,0:T(8,128)(2,1)S(1)}, bf16[80,5120]{1,0:T(8,128)(2,1)S(1)}, u32[]{:S(2)}, u32[]{:S(2)}) collective-permute-start(bf16[80,5120]{1,0:T(8,128)(2,1)S(1)} %constant_dynamic-update-slice_fusion.refs_0_.refs_9_), channel_id=1, source_target_pairs={{0,8},{1,5},{2,6},{3,11},{4,0},{5,13},{6,14},{7,3},{8,16},{9,1},{1... | collective-permute-start | bytes 2457608 | tf_op jit(solution)/shard_map/ppermute | solution.py:348
  5.8 41.2 %collective-permute-start.6 = (bf16[80,5120]{1,0:T(8,128)(2,1)S(1)}, bf16[80,5120]{1,0:T(8,128)(2,1)S(1)}, u32[]{:S(2)}, u32[]{:S(2)}) collective-permute-start(bf16[80,5120]{1,0:T(8,128)(2,1)S(1)} %constant_dynamic-update-slice_fusion.refs_0_.refs_9_), channel_id=1, source_target_pairs={{0,2},{1,3},{2,0},{3,1},{4,6},{5,7},{6,4},{7,5},{8,10},{9,11},{10,... | collective-permute-start | bytes 2457608 | tf_op jit(solution)/shard_map/ppermute | solution.py:348
  9.3 31.8 %collective-permute-start.4 = (bf16[512,1280]{1,0:T(8,128)(2,1)}, bf16[512,1280]{1,0:T(8,128)(2,1)}, u32[]{:S(2)}, u32[]{:S(2)}) collective-permute-start(bf16[512,1280]{1,0:T(8,128)(2,1)} %get-tuple-element.572), channel_id=1, source_target_pairs={{0,1},{1,0},{2,3},{3,2},{4,5},{5,4},{6,7},{7,6},{8,9},{9,8},{10,11... | collective-permute-start | bytes 3932168 | tf_op jit(solution)/shard_map/ppermute | solution.py:348
  24.3 20.4 %collective-permute-start.2 = (bf16[80,5120]{1,0:T(8,128)(2,1)S(1)}, bf16[80,5120]{1,0:T(8,128)(2,1)S(1)}, u32[]{:S(2)}, u32[]{:S(2)}) collective-permute-start(bf16[80,5120]{1,0:T(8,128)(2,1)S(1)} %collective-permute-done.refs_1_.refs_10_), channel_id=1, source_target_pairs={{0,8},{1,5},{2,6},{3,11},{4,0},{5,13},{6,14},{7,3},{8,16},{9,1},{1... | collective-permute-start | bytes 2457608 | tf_op jit(solution)/shard_map/ppermute | solution.py:348
  30.9 20.9 %collective-permute-start.7 = (bf16[80,5120]{1,0:T(8,128)(2,1)S(1)}, bf16[80,5120]{1,0:T(8,128)(2,1)S(1)}, u32[]{:S(2)}, u32[]{:S(2)}) collective-permute-start(bf16[80,5120]{1,0:T(8,128)(2,1)S(1)} %collective-permute-done.refs_1_.refs_10_), channel_id=1, source_target_pairs={{0,2},{1,3},{2,0},{3,1},{4,6},{5,7},{6,4},{7,5},{8,10},{9,11},{10,... | collective-permute-start | bytes 2457608 | tf_op jit(solution)/shard_map/ppermute | solution.py:348
  70.4 33.7 %collective-permute-start.16 = (bf16[640,1280]{1,0:T(8,128)(2,1)}, bf16[640,1280]{1,0:T(8,128)(2,1)}, u32[]{:S(2)}, u32[]{:S(2)}) collective-permute-start(bf16[640,1280]{1,0:T(8,128)(2,1)} %pad_maximum_fusion.2.refs_5_), channel_id=1, source_target_pairs={{0,8},{1,5},{2,6},{3,11},{4,0},{5,13},{6,14},{7,3},{8,16},{9,1},{1... | collective-permute-start | bytes 4915208 | tf_op jit(solution)/shard_map/ppermute | solution.py:348
  80.9 23.2 %collective-permute-start.17 = (bf16[256,1280]{1,0:T(8,128)(2,1)}, bf16[256,1280]{1,0:T(8,128)(2,1)}, u32[]{:S(2)}, u32[]{:S(2)}) collective-permute-start(bf16[256,1280]{1,0:T(8,128)(2,1)} %get-tuple-element.582), channel_id=1, source_target_pairs={{0,1},{1,0},{2,3},{3,2},{4,5},{5,4},{6,7},{7,6},{8,9},{9,8},{10,11... | collective-permute-start | bytes 1966088 | tf_op jit(solution)/shard_map/ppermute | solution.py:348
  104.2 22.1 %collective-permute-start.18 = (bf16[640,1280]{1,0:T(8,128)(2,1)}, bf16[640,1280]{1,0:T(8,128)(2,1)}, u32[]{:S(2)}, u32[]{:S(2)}) collective-permute-start(bf16[640,1280]{1,0:T(8,128)(2,1)} %collective-permute-done.16.refs_6_), channel_id=1, source_target_pairs={{0,8},{1,5},{2,6},{3,11},{4,0},{5,13},{6,14},{7,3},{8,16},{9,1},{1... | collective-permute-start | bytes 4915208 | tf_op jit(solution)/shard_map/ppermute | solution.py:348
  105.7 20.5 %collective-permute-start.19 = (bf16[256,1280]{1,0:T(8,128)(2,1)}, bf16[256,1280]{1,0:T(8,128)(2,1)S(1)}, u32[]{:S(2)}, u32[]{:S(2)}) collective-permute-start(bf16[256,1280]{1,0:T(8,128)(2,1)} %get-tuple-element.321), channel_id=1, source_target_pairs={{0,1},{1,0},{2,3},{3,2},{4,5},{5,4},{6,7},{7,6},{8,9},{9,8},{10,11... | collective-permute-start | bytes 1966088 | tf_op jit(solution)/shard_map/ppermute | solution.py:348
  128.6 27.5 %collective-permute-start.20 = (bf16[1024,1280]{1,0:T(8,128)(2,1)S(1)}, bf16[1024,1280]{1,0:T(8,128)(2,1)}, u32[]{:S(2)}, u32[]{:S(2)}) collective-permute-start(bf16[1024,1280]{1,0:T(8,128)(2,1)S(1)} %pad_maximum_fusion.1.refs_2_.g_own.g_ref), channel_id=1, source_target_pairs={{0,2},{1,3},{2,0},{3,1},{4,6},{5,7},{6,4},{7,5},{8,10},{9,11},{10,... | collective-permute-start | bytes 7864328 | tf_op jit(solution)/shard_map/ppermute | solution.py:348
  129.3 26.7 %collective-permute-start.21 = (bf16[640,1280]{1,0:T(8,128)(2,1)}, bf16[640,1280]{1,0:T(8,128)(2,1)}, u32[]{:S(2)}, u32[]{:S(2)}) collective-permute-start(bf16[640,1280]{1,0:T(8,128)(2,1)} %collective-permute-done.18.refs_7_), channel_id=1, source_target_pairs={{0,8},{1,5},{2,6},{3,11},{4,0},{5,13},{6,14},{7,3},{8,16},{9,1},{1... | collective-permute-start | bytes 4915208 | tf_op jit(solution)/shard_map/ppermute | solution.py:348
  156.1 44.0 %collective-permute-start.24 = (bf16[640,1280]{1,0:T(8,128)(2,1)}, bf16[640,1280]{1,0:T(8,128)(2,1)}, u32[]{:S(2)}, u32[]{:S(2)}) collective-permute-start(bf16[640,1280]{1,0:T(8,128)(2,1)} %pad_maximum_fusion.2.refs_5_), channel_id=1, source_target_pairs={{0,4},{1,9},{2,10},{3,7},{4,12},{5,1},{6,2},{7,15},{8,0},{9,17},{1... | collective-permute-start | bytes 4915208 | tf_op jit(solution)/shard_map/ppermute | solution.py:348
  158.0 64.5 %collective-permute-start.23 = (bf16[640,1280]{1,0:T(8,128)(2,1)}, bf16[640,1280]{1,0:T(8,128)(2,1)}, u32[]{:S(2)}, u32[]{:S(2)}) collective-permute-start(bf16[640,1280]{1,0:T(8,128)(2,1)} %collective-permute-done.21.refs_8_), channel_id=1, source_target_pairs={{0,8},{1,5},{2,6},{3,11},{4,0},{5,13},{6,14},{7,3},{8,16},{9,1},{1... | collective-permute-start | bytes 4915208 | tf_op jit(solution)/shard_map/ppermute | solution.py:348
  159.6 62.9 %collective-permute-start.26 = (bf16[640,1280]{1,0:T(8,128)(2,1)}, bf16[640,1280]{1,0:T(8,128)(2,1)}, u32[]{:S(2)}, u32[]{:S(2)}) collective-permute-start(bf16[640,1280]{1,0:T(8,128)(2,1)} %collective-permute-done.21.refs_8_), channel_id=1, source_target_pairs={{0,1},{1,0},{2,3},{3,2},{4,5},{5,4},{6,7},{7,6},{8,9},{9,8},{10,11... | collective-permute-start | bytes 4915208 | tf_op jit(solution)/shard_map/ppermute | solution.py:348
  200.1 22.4 %collective-permute-start.25 = (bf16[640,1280]{1,0:T(8,128)(2,1)}, bf16[640,1280]{1,0:T(8,128)(2,1)S(1)}, u32[]{:S(2)}, u32[]{:S(2)}) collective-permute-start(bf16[640,1280]{1,0:T(8,128)(2,1)} %collective-permute-done.24.refs_6_), channel_id=1, source_target_pairs={{0,4},{1,9},{2,10},{3,7},{4,12},{5,1},{6,2},{7,15},{8,0},{9,17},{1... | collective-permute-start | bytes 4915208 | tf_op jit(solution)/shard_map/ppermute | solution.py:348
  264.3 21.4 %collective-permute-start.27 = (bf16[1024,1280]{1,0:T(8,128)(2,1)}, bf16[1024,1280]{1,0:T(8,128)(2,1)S(1)}, u32[]{:S(2)}, u32[]{:S(2)}) collective-permute-start(bf16[1024,1280]{1,0:T(8,128)(2,1)} %get-tuple-element.357), channel_id=1, source_target_pairs={{0,2},{1,3},{2,0},{3,1},{4,6},{5,7},{6,4},{7,5},{8,10},{9,11},{10,... | collective-permute-start | bytes 7864328 | tf_op jit(solution)/shard_map/ppermute | solution.py:348
  264.7 21.0 %collective-permute-start.28 = (bf16[1024,1280]{1,0:T(8,128)(2,1)}, bf16[1024,1280]{1,0:T(8,128)(2,1)}, u32[]{:S(2)}, u32[]{:S(2)}) collective-permute-start(bf16[1024,1280]{1,0:T(8,128)(2,1)} %get-tuple-element.358), channel_id=1, source_target_pairs={{0,2},{1,3},{2,0},{3,1},{4,6},{5,7},{6,4},{7,5},{8,10},{9,11},{10,... | collective-permute-start | bytes 7864328 | tf_op jit(solution)/shard_map/ppermute | solution.py:348
  285.7 57.2 %collective-permute-start.29 = (bf16[640,1280]{1,0:T(8,128)(2,1)}, bf16[640,1280]{1,0:T(8,128)(2,1)}, u32[]{:S(2)}, u32[]{:S(2)}) collective-permute-start(bf16[640,1280]{1,0:T(8,128)(2,1)} %get-tuple-element.373), channel_id=1, source_target_pairs={{0,4},{1,9},{2,10},{3,7},{4,12},{5,1},{6,2},{7,15},{8,0},{9,17},{1... | collective-permute-start | bytes 4915208 | tf_op jit(solution)/shard_map/ppermute | solution.py:348
  286.8 56.2 %collective-permute-start.30 = (bf16[640,1280]{1,0:T(8,128)(2,1)}, bf16[640,1280]{1,0:T(8,128)(2,1)}, u32[]{:S(2)}, u32[]{:S(2)}) collective-permute-start(bf16[640,1280]{1,0:T(8,128)(2,1)} %get-tuple-element.374), channel_id=1, source_target_pairs={{0,1},{1,0},{2,3},{3,2},{4,5},{5,4},{6,7},{7,6},{8,9},{9,8},{10,11... | collective-permute-start | bytes 4915208 | tf_op jit(solution)/shard_map/ppermute | solution.py:348
  288.9 80.3 %collective-permute-start.32 = (bf16[640,1280]{1,0:T(8,128)(2,1)}, bf16[640,1280]{1,0:T(8,128)(2,1)}, u32[]{:S(2)}, u32[]{:S(2)}) collective-permute-start(bf16[640,1280]{1,0:T(8,128)(2,1)} %get-tuple-element.394), channel_id=1, source_target_pairs={{0,8},{1,5},{2,6},{3,11},{4,0},{5,13},{6,14},{7,3},{8,16},{9,1},{1... | collective-permute-start | bytes 4915208 | tf_op jit(solution)/shard_map/ppermute | solution.py:348
  289.4 79.8 %collective-permute-start.33 = (bf16[640,1280]{1,0:T(8,128)(2,1)}, bf16[640,1280]{1,0:T(8,128)(2,1)}, u32[]{:S(2)}, u32[]{:S(2)}) collective-permute-start(bf16[640,1280]{1,0:T(8,128)(2,1)} %get-tuple-element.395), channel_id=1, source_target_pairs={{0,1},{1,0},{2,3},{3,2},{4,5},{5,4},{6,7},{7,6},{8,9},{9,8},{10,11... | collective-permute-start | bytes 4915208 | tf_op jit(solution)/shard_map/ppermute | solution.py:348
  347.4 21.9 %collective-permute-start.31 = (bf16[640,1280]{1,0:T(8,128)(2,1)}, bf16[640,1280]{1,0:T(8,128)(2,1)S(1)}, u32[]{:S(2)}, u32[]{:S(2)}) collective-permute-start(bf16[640,1280]{1,0:T(8,128)(2,1)} %add_convert_fusion.3), channel_id=1, source_target_pairs={{0,4},{1,9},{2,10},{3,7},{4,12},{5,1},{6,2},{7,15},{8,0},{9,17},{1... | collective-permute-start | bytes 4915208 | tf_op jit(solution)/shard_map/ppermute | solution.py:348
  372.7 33.0 %collective-permute-start.37 = (bf16[640,1280]{1,0:T(8,128)(2,1)}, bf16[640,1280]{1,0:T(8,128)(2,1)S(1)}, u32[]{:S(2)}, u32[]{:S(2)}) collective-permute-start(bf16[640,1280]{1,0:T(8,128)(2,1)} %add_convert_fusion.2), channel_id=1, source_target_pairs={{0,4},{1,9},{2,10},{3,7},{4,12},{5,1},{6,2},{7,15},{8,0},{9,17},{1... | collective-permute-start | bytes 4915208 | tf_op jit(solution)/shard_map/ppermute | solution.py:348
  374.4 31.3 %collective-permute-start.38 = (bf16[256,1280]{1,0:T(8,128)(2,1)}, bf16[256,1280]{1,0:T(8,128)(2,1)S(1)}, u32[]{:S(2)}, u32[]{:S(2)}) collective-permute-start(bf16[256,1280]{1,0:T(8,128)(2,1)} %get-tuple-element.439), channel_id=1, source_target_pairs={{0,1},{1,0},{2,3},{3,2},{4,5},{5,4},{6,7},{7,6},{8,9},{9,8},{10,11... | collective-permute-start | bytes 1966088 | tf_op jit(solution)/shard_map/ppermute | solution.py:348
  385.3 21.3 %collective-permute-start.35 = (bf16[80,3584]{1,0:T(8,128)(2,1)}, bf16[80,3584]{1,0:T(8,128)(2,1)}, u32[]{:S(2)}, u32[]{:S(2)}) collective-permute-start(bf16[80,3584]{1,0:T(8,128)(2,1)} %get-tuple-element.566), channel_id=1, source_target_pairs={{0,4},{1,9},{2,10},{3,7},{4,12},{5,1},{6,2},{7,15},{8,0},{9,17},{1... | collective-permute-start | bytes 1720328 | tf_op jit(solution)/shard_map/ppermute | solution.py:348
  385.8 20.7 %collective-permute-start.36 = (bf16[80,3584]{1,0:T(8,128)(2,1)}, bf16[80,3584]{1,0:T(8,128)(2,1)}, u32[]{:S(2)}, u32[]{:S(2)}) collective-permute-start(bf16[80,3584]{1,0:T(8,128)(2,1)} %get-tuple-element.565), channel_id=1, source_target_pairs={{0,8},{1,5},{2,6},{3,11},{4,0},{5,13},{6,14},{7,3},{8,16},{9,1},{1... | collective-permute-start | bytes 1720328 | tf_op jit(solution)/shard_map/ppermute | solution.py:348
  408.1 21.5 %collective-permute-start.40 = (bf16[640,1280]{1,0:T(8,128)(2,1)}, bf16[640,1280]{1,0:T(8,128)(2,1)S(1)}, u32[]{:S(2)}, u32[]{:S(2)}) collective-permute-start(bf16[640,1280]{1,0:T(8,128)(2,1)} %add_convert_fusion.1), channel_id=1, source_target_pairs={{0,4},{1,9},{2,10},{3,7},{4,12},{5,1},{6,2},{7,15},{8,0},{9,17},{1... | collective-permute-start | bytes 4915208 | tf_op jit(solution)/shard_map/ppermute | solution.py:348
  453.3 76.6 %collective-permute-start.60 = (bf16[512,1280]{1,0:T(8,128)(2,1)}, bf16[512,1280]{1,0:T(8,128)(2,1)}, u32[]{:S(2)}, u32[]{:S(2)}) collective-permute-start(bf16[512,1280]{1,0:T(8,128)(2,1)} %get-tuple-element.538), channel_id=1, source_target_pairs={{0,1},{1,0},{2,3},{3,2},{4,5},{5,4},{6,7},{7,6},{8,9},{9,8},{10,11... | collective-permute-start | bytes 3932168 | tf_op jit(solution)/shard_map/ppermute | solution.py:348
  456.9 23.5 %collective-permute-start.43 = (bf16[80,3584]{1,0:T(8,128)(2,1)}, bf16[80,3584]{1,0:T(8,128)(2,1)}, u32[]{:S(2)}, u32[]{:S(2)}) collective-permute-start(bf16[80,3584]{1,0:T(8,128)(2,1)} %get-tuple-element.564), channel_id=1, source_target_pairs={{0,4},{1,9},{2,10},{3,7},{4,12},{5,1},{6,2},{7,15},{8,0},{9,17},{1... | collective-permute-start | bytes 1720328 | tf_op jit(solution)/shard_map/ppermute | solution.py:348
  458.3 22.1 %collective-permute-start.44 = (bf16[80,3584]{1,0:T(8,128)(2,1)S(1)}, bf16[80,3584]{1,0:T(8,128)(2,1)}, u32[]{:S(2)}, u32[]{:S(2)}) collective-permute-start(bf16[80,3584]{1,0:T(8,128)(2,1)S(1)} %get-tuple-element.563), channel_id=1, source_target_pairs={{0,8},{1,5},{2,6},{3,11},{4,0},{5,13},{6,14},{7,3},{8,16},{9,1},{1... | collective-permute-start | bytes 1720328 | tf_op jit(solution)/shard_map/ppermute | solution.py:348
  489.1 27.4 %collective-permute-start.58 = (bf16[320,1280]{1,0:T(8,128)(2,1)S(1)}, bf16[320,1280]{1,0:T(8,128)(2,1)S(1)}, u32[]{:S(2)}, u32[]{:S(2)}) collective-permute-start(bf16[320,1280]{1,0:T(8,128)(2,1)S(1)} %get-tuple-element.549), channel_id=1, source_target_pairs={{0,1},{1,0},{2,3},{3,2},{4,5},{5,4},{6,7},{7,6},{8,9},{9,8},{10,11... | collective-permute-start | bytes 2457608 | tf_op jit(solution)/shard_map/ppermute | solution.py:348
  508.7 21.2 %collective-permute-start.59 = (bf16[80,3584]{1,0:T(8,128)(2,1)S(1)}, bf16[80,3584]{1,0:T(8,128)(2,1)S(1)}, u32[]{:S(2)}, u32[]{:S(2)}) collective-permute-start(bf16[80,3584]{1,0:T(8,128)(2,1)S(1)} %fusion), channel_id=1, source_target_pairs={{0,1},{1,0},{2,3},{3,2},{4,5},{5,4},{6,7},{7,6},{8,9},{9,8},{10,11... | collective-permute-start | bytes 1720328 | tf_op jit(solution)/shard_map/ppermute | solution.py:348
  (107 other events, 1063.2 us)

commit v7 on v5

--- a/solution.py
+++ b/solution.py
@@ -1086,7 +1086,7 @@
     mask = jnp.where(keep > 0, 0.0, far_below)
 
     x_got = ring.swap_blk(pick(hidden_in, 1 - blk))
-    steps = ring.gather(jnp.concatenate([w_qkv, w_out], axis=1), 2)
+    steps = ring.gather(jnp.concatenate([w_qkv, w_out], axis=1), 1)
     slots, sib = next(steps), [None] * n
     w_pair = jnp.concatenate([w_up, w_down], axis=0)
     g_send = pick(cotangent, 1 - blk)
@@ -1094,15 +1094,15 @@
     small += [place, mask, keep]
     slots[1], slots[5] = fence(slots[1], slots[5])
     slots = steps.send(slots)
-    slots[2], slots[6], small, x_got, w_pair = fence(slots[2], slots[6], small, x_got, w_pair)
+    slots[2], small, w_pair = fence(slots[2], small, w_pair)
     ln1_gain, ln1_bias, q_bias, v_bias, out_bias, ln2_gain, ln2_bias, place, mask, keep = small
     slots = steps.send(slots)
-    for s in (0, 1, 5, 2, 6):
+    for s in (0, 1, 5, 2):
         sib[s] = ring.swap_core(slots[s])
     x = jnp.concatenate([pick(hidden_in, blk), x_got], axis=0)
     slots[3], x, sib, g_send = fence(slots[3], x, sib, g_send)
     slots = steps.send(slots)
-    for s in (3, 4, 7):
+    for s in (3, 4, 6, 7):
         sib[s] = ring.swap_core(slots[s])
     slots[4], w_pair = fence(slots[4], w_pair)
     pair = [w_pair, ring.shift(w_pair, 1)] + [None] * 6

time: 545 us -> 553 us (1.015)
  waiting for transfers between devices: 68.5 us -> 75.6 us
    ppermute x64, waiting for transfers between devices: 68.5 us -> 75.6 us  [permute(): return lax.ppermute(x, AXES, pairs)]
  transfers between devices with their start and end apart: 64 -> 64, of which waited for: 20 -> 18; matrix products, arithmetic and copies ran while one was open for 12% -> 12% of each run, Pallas kernels for 53% -> 52%
where the time goes in v7:
time: 553 us; the launch traced here: 545 us
  Pallas kernels  323 us (58%)
  waiting for transfers between devices  75.6 us (14%)
  starting transfers between devices  60.7 us (11%)
  other arithmetic  51 us (9%)
  local copies, waits for them, and re-layouts  32.3 us (6%)
    pallas_call x2, Pallas kernels, ffn_call(): pl.pallas_call(partial(ffn_kernel, n, later), grid=(2 * half,), in_specs=...  77.9 us
    ppermute x64, waiting for transfers between devices, permute(): return lax.ppermute(x, AXES, pairs)  75.6 us
    ppermute x64, starting transfers between devices, permute(): return lax.ppermute(x, AXES, pairs)  60.7 us
    pallas_call x3, Pallas kernels, attend_back_call(): pl.pallas_call(partial(attend_back_kernel, qrows), grid=(count,), in_spec...  60.5 us
    pallas_call x2, Pallas kernels, ffn_weights_call(): pl.pallas_call(partial(ffn_weights_kernel, n), in_specs=[ANY] * 6, out_sp...  41.6 us
    pallas_call x2, Pallas kernels, attend_call(): pl.pallas_call(partial(attend_kernel, qrows, ahead), grid=(count,), in_sp...  34.1 us
    pallas_call x2, Pallas kernels, in_call(): pl.pallas_call(partial(in_kernel, n, len(grads)), grid_spec=pltpu.Prefetc...  31.3 us
    convert_element_type x14, other arithmetic, added(): return total.astype(bf16)  29.7 us
  transfers between devices with their start and end apart: 64, of which 18 were waited for; matrix products, arithmetic and copies ran while one was open for 12% of the time, Pallas kernels for 52%

profile of v7, /device:TPU:0, one launch (start us, length us, event | category | flops | bytes accessed | tf_op | source)
XLA Modules:
  0.0 544.7 jit_solution(13800306157960245524)
XLA Ops:
  2.7 3.1 collective-permute-start
  5.9 3.4 dynamic-slice_bitcast_fusion.3
  20.5 3.8 collective-permute-done.refs_1_.refs_10_
  30.9 6.1 %collective-permute-done.2.refs_2_.refs_11_ = bf16[80,5120]{1,0:T(8,128)(2,1)S(1)} collective-permute-done((bf16[80,5120]{1,0:T(8,128)(2,1)S(1)}, bf16[80,5120]{1,0:T(8,128)(2,1)S(1)}, u32[]{:S(2)}, u32[]{:S(2)}) %collective-permute-start.2) | collective-permute-done | bytes 819232 | tf_op jit(solution)/shard_map/ppermute | solution.py:348
  42.3 3.0 pad_maximum_fusion.x_ref
  45.4 4.0 collective-permute-done.3.refs_3_.refs_12_
  52.7 9.1 %collective-permute-done.9.refs_4_.refs_13_ = bf16[80,5120]{1,0:T(8,128)(2,1)S(1)} collective-permute-done((bf16[80,5120]{1,0:T(8,128)(2,1)S(1)}, bf16[80,5120]{1,0:T(8,128)(2,1)S(1)}, u32[]{:S(2)}, u32[]{:S(2)}) %collective-permute-start.9) | collective-permute-done | bytes 819232 | tf_op jit(solution)/shard_map/ppermute | solution.py:348
  63.0 8.8 %collective-permute-done.10.refs_6_.refs_15_ = bf16[80,5120]{1,0:T(8,128)(2,1)S(1)} collective-permute-done((bf16[80,5120]{1,0:T(8,128)(2,1)S(1)}, bf16[80,5120]{1,0:T(8,128)(2,1)S(1)}, u32[]{:S(2)}, u32[]{:S(2)}) %collective-permute-start.10) | collective-permute-done | bytes 819232 | tf_op jit(solution)/shard_map/ppermute | solution.py:348
  71.9 15.8 %collective-permute-done.11.refs_7_.refs_16_ = bf16[80,5120]{1,0:T(8,128)(2,1)S(1)} collective-permute-done((bf16[80,5120]{1,0:T(8,128)(2,1)S(1)}, bf16[80,5120]{1,0:T(8,128)(2,1)S(1)}, u32[]{:S(2)}, u32[]{:S(2)}) %collective-permute-start.11) | collective-permute-done | bytes 819232 | tf_op jit(solution)/shard_map/ppermute | solution.py:348
  92.8 20.4 %qkv.1 = (bf16[1024,1280]{1,0:T(8,128)(2,1)}, bf16[1024,1280]{1,0:T(8,128)(2,1)}, bf16[1024,1280]{1,0:T(8,128)(2,1)}, bf16[1024,1280]{1,0:T(8,128)(2,1)}) custom-call(s32[16]{0:T(128)} %pad_add_fusion.2.place_ref, bf16[1024,1280]{1,0:T(8,128)(2,1)} %pad_maximum_fusion.x_ref, f32[1,1280]{1,0:T(1,128)} %reshape.227.gain_ref, f32[1,1280]{1,0:T(1,128)} %reshape.228.bias_ref, ...), custom_call_target="tpu_custom_call" | custom-call | flops 201326592 | bytes 458752 | tf_op jit(solution)/shard_map/qkv/pallas_call | solution.py:489
  115.3 20.0 %attend.2 = (bf16[1024,768]{1,0:T(8,128)(2,1)}, f32[12,1,1024]{2,1,0:T(1,128)}) custom-call(f32[1024,1]{1,0:T(8,128)} %compare_select_fusion.mask_ref, f32[1024,1]{1,0:T(8,128)} %convert_element_type.346.keep_ref, bf16[1024,1280]{1,0:T(8,128)(2,1)} %get-tuple-element.314.q_ref, bf16[1024,1280]{1,0:T(8,128)(2,1)} %get-tuple-element.315.k_ref, ...), custom_call_target="tpu_custom_call" | custom-call | flops 322122560 | bytes 125829 | tf_op jit(solution)/shard_map/attend/pallas_call | solution.py:562
  139.1 14.0 %attend.3 = (bf16[1024,512]{1,0:T(8,128)(2,1)}, f32[8,1,1024]{2,1,0:T(1,128)}) custom-call(f32[1024,1]{1,0:T(8,128)} %compare_select_fusion.mask_ref, f32[1024,1]{1,0:T(8,128)} %convert_element_type.346.keep_ref, bf16[1024,1280]{1,0:T(8,128)(2,1)} %get-tuple-element.314.q_ref, bf16[1024,1280]{1,0:T(8,128)(2,1)} %get-tuple-element.315.k_ref, ...), custom_call_target="tpu_custom_call" | custom-call | flops 214748368 | bytes 83886 | tf_op jit(solution)/shard_map/attend/pallas_call | solution.py:562
  153.2 10.9 %out.1 = (f32[1024,1280]{1,0:T(8,128)}, bf16[1024,1280]{1,0:T(8,128)(2,1)}) custom-call(s32[16]{0:T(128)} %pad_add_fusion.2.place_ref, bf16[1024,1280]{1,0:T(8,128)(2,1)} %pad_maximum_fusion.x_ref, f32[1,1280]{1,0:T(1,128)} %reshape.231.bias_ref, f32[1,1280]{1,0:T(1,128)} %reshape.232.gain_ref, f32[1,1280]{1,0:T(1,128)} %reshape.233.shift_ref, ...), custom_call_target="tpu_custom_call" | custom-call | flops 134217728 | bytes 327680 | tf_op jit(solution)/shard_map/out/pallas_call | solution.py:671
  171.3 37.3 %ffn.2 = (bf16[2048,1280]{1,0:T(8,128)(2,1)}, bf16[2048,1280]{1,0:T(8,128)(2,1)}, f32[1,1280]{1,0:T(1,128)}, f32[2048,1280]{1,0:T(8,128)}, f32[2048,1280]{1,0:T(8,128)}) custom-call(bf16[1024,1280]{1,0:T(8,128)(2,1)} %get-tuple-element.322.refs_0_.b_own, bf16[1024,1280]{1,0:T(8,128)(2,1)} %copy-done.2, bf16[1024,1280]{1,0:T(8,128)(2,1)} %copy-done.1, ...), custom_call_target="tpu_custom_call" | custom-call | flops 805306368 | bytes 629145 | tf_op jit(solution)/shard_map/ffn/pallas_call | solution.py:777
  210.3 20.8 %ffn_weights.2 = (bf16[640,1280]{1,0:T(8,128)(2,1)}, bf16[640,1280]{1,0:T(8,128)(2,1)}, bf16[640,1280]{1,0:T(8,128)(2,1)}, bf16[640,1280]{1,0:T(8,128)(2,1)}) custom-call(bf16[2048,1280]{1,0:T(8,128)(2,1)} %get-tuple-element.331.gz, bf16[2048,1280]{1,0:T(8,128)(2,1)} %get-tuple-element.332.h, bf16[1024,1280]{1,0:T(8,128)(2,1)} %get-tuple-element.322.refs_0_.b_own, ...), custom_call_target="tpu_custom_call" | custom-call | flops 402653184 | bytes 419430 | tf_op jit(solution)/shard_map/ffn_weights/pallas_call | solution.py:840
  232.3 40.6 %ffn.3 = (bf16[2048,1280]{1,0:T(8,128)(2,1)}, bf16[2048,1280]{1,0:T(8,128)(2,1)}, f32[1,1280]{1,0:T(1,128)}, bf16[1024,1280]{1,0:T(8,128)(2,1)}, bf16[1024,1280]...) custom-call(bf16[1024,1280]{1,0:T(8,128)(2,1)} %get-tuple-element.322.refs_0_.b_own, ...), custom_call_target="tpu_custom_call" | custom-call | flops 805306368 | bytes 1048576 | tf_op jit(solution)/shard_map/ffn/pallas_call | solution.py:777
  273.5 20.8 %ffn_weights.3 = (bf16[640,1280]{1,0:T(8,128)(2,1)}, bf16[640,1280]{1,0:T(8,128)(2,1)}, bf16[640,1280]{1,0:T(8,128)(2,1)}, bf16[640,1280]{1,0:T(8,128)(2,1)}) custom-call(bf16[2048,1280]{1,0:T(8,128)(2,1)} %get-tuple-element.341.gz, bf16[2048,1280]{1,0:T(8,128)(2,1)} %get-tuple-element.342.h, bf16[1024,1280]{1,0:T(8,128)(2,1)} %get-tuple-element.322.refs_0_.b_own, ...), custom_call_target="tpu_custom_call" | custom-call | flops 402653184 | bytes 419430 | tf_op jit(solution)/shard_map/ffn_weights/pallas_call | solution.py:840
  298.8 16.6 %mid.1 = (bf16[1024,1280]{1,0:T(8,128)(2,1)}, bf16[1024,1280]{1,0:T(8,128)(2,1)}, bf16[1024,1280]{1,0:T(8,128)(2,1)}, f32[8,1280]{1,0:T(8,128)}) custom-call(s32[16]{0:T(128)} %pad_add_fusion.2.place_ref, bf16[1024,1280]{1,0:T(8,128)(2,1)} %get-tuple-element.350.oo_ref, bf16[1024,1280]{1,0:T(8,128)(2,1)} %copy-done.20, ...), custom_call_target="tpu_custom_call" | custom-call | flops 134217728 | bytes 851968 | tf_op jit(solution)/shard_map/mid/pallas_call | solution.py:890
  315.4 34.6 %attend_back.3 = (bf16[1024,768]{1,0:T(8,128)(2,1)}, bf16[1024,768]{1,0:T(8,128)(2,1)}, bf16[1024,768]{1,0:T(8,128)(2,1)}, f32[1,768]{1,0:T(1,128)}, f32[1,768]{1,0:T(1,128)}) custom-call(f32[1024,1]{1,0:T(8,128)} %compare_select_fusion.mask_ref, bf16[1024,1280]{1,0:T(8,128)(2,1)} %get-tuple-element.314.q_ref, bf16[1024,1280]{1,0:T(8,128)(2,1)} %get-tuple-element.315.k_ref, ...), custom_call_target="tpu_custom_call" | custom-call | flops 515396064 | bytes 251658 | tf_op jit(solution)/shard_map/attend_back/pallas_call | solution.py:625
  351.9 3.7 add_convert_fusion.3
  357.3 19.8 %att_weights.2 = (bf16[80,3584]{1,0:T(8,128)(2,1)}, bf16[80,3584]{1,0:T(8,128)(2,1)}, bf16[80,3584]{1,0:T(8,128)(2,1)}, bf16[80,3584]{1,0:T(8,128)(2,1)}, bf16[8...) custom-call(s32[16]{0:T(128)} %pad_add_fusion.2.place_ref, ...), custom_call_target="tpu_custom_call" | custom-call | flops 281857216 | bytes 330301 | tf_op jit(solution)/shard_map/att_weights/pallas_call | solution.py:968
  377.5 3.2 add_convert_fusion.2
  383.8 7.5 %attend_back.4 = (bf16[1024,128]{1,0:T(8,128)(2,1)}, bf16[1024,128]{1,0:T(8,128)(2,1)}, bf16[1024,128]{1,0:T(8,128)(2,1)}, f32[1,128]{1,0:T(1,128)}, f32[1,128]{1,0:T(1,128)}) custom-call(f32[1024,1]{1,0:T(8,128)} %compare_select_fusion.mask_ref, bf16[1024,1280]{1,0:T(8,128)(2,1)} %get-tuple-element.314.q_ref, bf16[1024,1280]{1,0:T(8,128)(2,1)} %get-tuple-element.315.k_ref, ...), custom_call_target="tpu_custom_call" | custom-call | flops 85899344 | bytes 41943 | tf_op jit(solution)/shard_map/attend_back/pallas_call | solution.py:625
  395.8 18.4 %attend_back.5 = (bf16[1024,384]{1,0:T(8,128)(2,1)}, bf16[1024,384]{1,0:T(8,128)(2,1)}, bf16[1024,384]{1,0:T(8,128)(2,1)}, f32[1,384]{1,0:T(1,128)}, f32[1,384]{1,0:T(1,128)}) custom-call(f32[1024,1]{1,0:T(8,128)} %compare_select_fusion.mask_ref, bf16[1024,1280]{1,0:T(8,128)(2,1)} %get-tuple-element.314.q_ref, bf16[1024,1280]{1,0:T(8,128)(2,1)} %get-tuple-element.315.k_ref, ...), custom_call_target="tpu_custom_call" | custom-call | flops 257698032 | bytes 125829 | tf_op jit(solution)/shard_map/attend_back/pallas_call | solution.py:625
  422.2 15.5 %in.2 = (bf16[512,1280]{1,0:T(8,128)(2,1)}, f32[8,1280]{1,0:T(8,128)}) custom-call(s32[16]{0:T(128)} %pad_add_fusion.2.place_ref, bf16[1024,1280]{1,0:T(8,128)(2,1)} %pad_maximum_fusion.x_ref, bf16[1024,1280]{1,0:T(8,128)(2,1)} %get-tuple-element.356.refs_6_.gr_ref, f32[1,1280]{1,0:T(1,128)} %reshape.227.gain_ref, ...), custom_call_target="tpu_custom_call" | custom-call | flops 134217728 | bytes 380108 | tf_op jit(solution)/shard_map/in/pallas_call | solution.py:1026
  437.7 6.0 %collective-permute-done.39 = bf16[80,3584]{1,0:T(8,128)(2,1)} collective-permute-done((bf16[80,3584]{1,0:T(8,128)(2,1)}, bf16[80,3584]{1,0:T(8,128)(2,1)}, u32[]{:S(2)}, u32[]{:S(2)}) %collective-permute-start.39) | collective-permute-done | bytes 573472 | tf_op jit(solution)/shard_map/ppermute | solution.py:348
  448.5 3.1 fusion.3
  454.4 9.9 %att_weights.3 = (bf16[80,1536]{1,0:T(8,128)(2,1)}, bf16[80,1536]{1,0:T(8,128)(2,1)}, bf16[80,1536]{1,0:T(8,128)(2,1)}, bf16[80,1536]{1,0:T(8,128)(2,1)}, bf16[8...) custom-call(s32[16]{0:T(128)} %pad_add_fusion.2.place_ref, ...), custom_call_target="tpu_custom_call" | custom-call | flops 120795952 | bytes 141557 | tf_op jit(solution)/shard_map/att_weights/pallas_call | solution.py:968
  480.8 15.8 %in.3 = (f32[512,1280]{1,0:T(8,128)}, f32[8,1280]{1,0:T(8,128)}) custom-call(s32[16]{0:T(128)} %pad_add_fusion.2.place_ref, bf16[1024,1280]{1,0:T(8,128)(2,1)} %pad_maximum_fusion.x_ref, bf16[1024,1280]{1,0:T(8,128)(2,1)} %get-tuple-element.356.refs_6_.gr_ref, f32[1,1280]{1,0:T(1,128)} %reshape.227.gain_ref, ...), custom_call_target="tpu_custom_call" | custom-call | flops 134217728 | bytes 380108 | tf_op jit(solution)/shard_map/in/pallas_call | solution.py:1026
  501.8 3.5 collective-permute-done.55
  512.4 3.2 collective-permute-done.56
  525.2 3.7 collective-permute-done.60
  (356 shorter events, 136.3 us)
Async XLA Ops:
  2.7 21.5 %collective-permute-start = (bf16[80,5120]{1,0:T(8,128)(2,1)S(1)}, bf16[80,5120]{1,0:T(8,128)(2,1)S(1)}, u32[]{:S(2)}, u32[]{:S(2)}) collective-permute-start(bf16[80,5120]{1,0:T(8,128)(2,1)S(1)} %constant_dynamic-update-slice_fusion.refs_0_.refs_9_), channel_id=1, source_target_pairs={{0,8},{1,5},{2,6},{3,11},{4,0},{5,13},{6,14},{7,3},{8,16},{9,1},{1... | collective-permute-start | bytes 2457608 | tf_op jit(solution)/shard_map/ppermute | solution.py:348
  5.8 39.5 %collective-permute-start.5 = (bf16[80,5120]{1,0:T(8,128)(2,1)S(1)}, bf16[80,5120]{1,0:T(8,128)(2,1)S(1)}, u32[]{:S(2)}, u32[]{:S(2)}) collective-permute-start(bf16[80,5120]{1,0:T(8,128)(2,1)S(1)} %constant_dynamic-update-slice_fusion.refs_0_.refs_9_), channel_id=1, source_target_pairs={{0,2},{1,3},{2,0},{3,1},{4,6},{5,7},{6,4},{7,5},{8,10},{9,11},{10,... | collective-permute-start | bytes 2457608 | tf_op jit(solution)/shard_map/ppermute | solution.py:348
  9.3 31.8 %collective-permute-start.4 = (bf16[512,1280]{1,0:T(8,128)(2,1)}, bf16[512,1280]{1,0:T(8,128)(2,1)}, u32[]{:S(2)}, u32[]{:S(2)}) collective-permute-start(bf16[512,1280]{1,0:T(8,128)(2,1)} %get-tuple-element.560), channel_id=1, source_target_pairs={{0,1},{1,0},{2,3},{3,2},{4,5},{5,4},{6,7},{7,6},{8,9},{9,8},{10,11... | collective-permute-start | bytes 3932168 | tf_op jit(solution)/shard_map/ppermute | solution.py:348
  50.7 21.2 %collective-permute-start.10 = (bf16[80,5120]{1,0:T(8,128)(2,1)S(1)}, bf16[80,5120]{1,0:T(8,128)(2,1)S(1)}, u32[]{:S(2)}, u32[]{:S(2)}) collective-permute-start(bf16[80,5120]{1,0:T(8,128)(2,1)S(1)} %collective-permute-done.2.refs_2_.refs_11_), channel_id=1, source_target_pairs={{0,1},{1,0},{2,3},{3,2},{4,5},{5,4},{6,7},{7,6},{8,9},{9,8},{10,11... | collective-permute-start | bytes 2457608 | tf_op jit(solution)/shard_map/ppermute | solution.py:348
  52.3 35.3 %collective-permute-start.11 = (bf16[80,5120]{1,0:T(8,128)(2,1)S(1)}, bf16[80,5120]{1,0:T(8,128)(2,1)S(1)}, u32[]{:S(2)}, u32[]{:S(2)}) collective-permute-start(bf16[80,5120]{1,0:T(8,128)(2,1)S(1)} %collective-permute-done.3.refs_3_.refs_12_), channel_id=1, source_target_pairs={{0,1},{1,0},{2,3},{3,2},{4,5},{5,4},{6,7},{7,6},{8,9},{9,8},{10,11... | collective-permute-start | bytes 2457608 | tf_op jit(solution)/shard_map/ppermute | solution.py:348
  61.8 51.4 %collective-permute-start.16 = (bf16[640,1280]{1,0:T(8,128)(2,1)}, bf16[640,1280]{1,0:T(8,128)(2,1)}, u32[]{:S(2)}, u32[]{:S(2)}) collective-permute-start(bf16[640,1280]{1,0:T(8,128)(2,1)} %pad_maximum_fusion.2.refs_5_), channel_id=1, source_target_pairs={{0,8},{1,5},{2,6},{3,11},{4,0},{5,13},{6,14},{7,3},{8,16},{9,1},{1... | collective-permute-start | bytes 4915208 | tf_op jit(solution)/shard_map/ppermute | solution.py:348
  63.0 26.3 %collective-permute-start.12 = (bf16[80,5120]{1,0:T(8,128)(2,1)S(1)}, bf16[80,5120]{1,0:T(8,128)(2,1)S(1)}, u32[]{:S(2)}, u32[]{:S(2)}) collective-permute-start(bf16[80,5120]{1,0:T(8,128)(2,1)S(1)} %collective-permute-done.3.refs_3_.refs_12_), channel_id=1, source_target_pairs={{0,2},{1,3},{2,0},{3,1},{4,6},{5,7},{6,4},{7,5},{8,10},{9,11},{10,... | collective-permute-start | bytes 2457608 | tf_op jit(solution)/shard_map/ppermute | solution.py:348
  89.3 23.9 %collective-permute-start.17 = (bf16[256,1280]{1,0:T(8,128)(2,1)}, bf16[256,1280]{1,0:T(8,128)(2,1)}, u32[]{:S(2)}, u32[]{:S(2)}) collective-permute-start(bf16[256,1280]{1,0:T(8,128)(2,1)} %get-tuple-element.570), channel_id=1, source_target_pairs={{0,1},{1,0},{2,3},{3,2},{4,5},{5,4},{6,7},{7,6},{8,9},{9,8},{10,11... | collective-permute-start | bytes 1966088 | tf_op jit(solution)/shard_map/ppermute | solution.py:348
  113.2 22.1 %collective-permute-start.18 = (bf16[640,1280]{1,0:T(8,128)(2,1)}, bf16[640,1280]{1,0:T(8,128)(2,1)}, u32[]{:S(2)}, u32[]{:S(2)}) collective-permute-start(bf16[640,1280]{1,0:T(8,128)(2,1)} %collective-permute-done.16.refs_6_), channel_id=1, source_target_pairs={{0,8},{1,5},{2,6},{3,11},{4,0},{5,13},{6,14},{7,3},{8,16},{9,1},{1... | collective-permute-start | bytes 4915208 | tf_op jit(solution)/shard_map/ppermute | solution.py:348
  137.6 26.5 %collective-permute-start.20 = (bf16[1024,1280]{1,0:T(8,128)(2,1)S(1)}, bf16[1024,1280]{1,0:T(8,128)(2,1)}, u32[]{:S(2)}, u32[]{:S(2)}) collective-permute-start(bf16[1024,1280]{1,0:T(8,128)(2,1)S(1)} %pad_maximum_fusion.1.refs_2_.g_own.g_ref), channel_id=1, source_target_pairs={{0,2},{1,3},{2,0},{3,1},{4,6},{5,7},{6,4},{7,5},{8,10},{9,11},{10,... | collective-permute-start | bytes 7864328 | tf_op jit(solution)/shard_map/ppermute | solution.py:348
  137.7 26.4 %collective-permute-start.21 = (bf16[640,1280]{1,0:T(8,128)(2,1)}, bf16[640,1280]{1,0:T(8,128)(2,1)}, u32[]{:S(2)}, u32[]{:S(2)}) collective-permute-start(bf16[640,1280]{1,0:T(8,128)(2,1)} %collective-permute-done.18.refs_7_), channel_id=1, source_target_pairs={{0,8},{1,5},{2,6},{3,11},{4,0},{5,13},{6,14},{7,3},{8,16},{9,1},{1... | collective-permute-start | bytes 4915208 | tf_op jit(solution)/shard_map/ppermute | solution.py:348
  164.8 43.9 %collective-permute-start.24 = (bf16[640,1280]{1,0:T(8,128)(2,1)}, bf16[640,1280]{1,0:T(8,128)(2,1)}, u32[]{:S(2)}, u32[]{:S(2)}) collective-permute-start(bf16[640,1280]{1,0:T(8,128)(2,1)} %pad_maximum_fusion.2.refs_5_), channel_id=1, source_target_pairs={{0,4},{1,9},{2,10},{3,7},{4,12},{5,1},{6,2},{7,15},{8,0},{9,17},{1... | collective-permute-start | bytes 4915208 | tf_op jit(solution)/shard_map/ppermute | solution.py:348
  166.6 64.5 %collective-permute-start.23 = (bf16[640,1280]{1,0:T(8,128)(2,1)}, bf16[640,1280]{1,0:T(8,128)(2,1)}, u32[]{:S(2)}, u32[]{:S(2)}) collective-permute-start(bf16[640,1280]{1,0:T(8,128)(2,1)} %collective-permute-done.21.refs_8_), channel_id=1, source_target_pairs={{0,8},{1,5},{2,6},{3,11},{4,0},{5,13},{6,14},{7,3},{8,16},{9,1},{1... | collective-permute-start | bytes 4915208 | tf_op jit(solution)/shard_map/ppermute | solution.py:348
  168.2 62.9 %collective-permute-start.26 = (bf16[640,1280]{1,0:T(8,128)(2,1)}, bf16[640,1280]{1,0:T(8,128)(2,1)}, u32[]{:S(2)}, u32[]{:S(2)}) collective-permute-start(bf16[640,1280]{1,0:T(8,128)(2,1)} %collective-permute-done.21.refs_8_), channel_id=1, source_target_pairs={{0,1},{1,0},{2,3},{3,2},{4,5},{5,4},{6,7},{7,6},{8,9},{9,8},{10,11... | collective-permute-start | bytes 4915208 | tf_op jit(solution)/shard_map/ppermute | solution.py:348
  208.6 22.5 %collective-permute-start.25 = (bf16[640,1280]{1,0:T(8,128)(2,1)}, bf16[640,1280]{1,0:T(8,128)(2,1)S(1)}, u32[]{:S(2)}, u32[]{:S(2)}) collective-permute-start(bf16[640,1280]{1,0:T(8,128)(2,1)} %collective-permute-done.24.refs_6_), channel_id=1, source_target_pairs={{0,4},{1,9},{2,10},{3,7},{4,12},{5,1},{6,2},{7,15},{8,0},{9,17},{1... | collective-permute-start | bytes 4915208 | tf_op jit(solution)/shard_map/ppermute | solution.py:348
  272.9 21.4 %collective-permute-start.27 = (bf16[1024,1280]{1,0:T(8,128)(2,1)}, bf16[1024,1280]{1,0:T(8,128)(2,1)S(1)}, u32[]{:S(2)}, u32[]{:S(2)}) collective-permute-start(bf16[1024,1280]{1,0:T(8,128)(2,1)} %get-tuple-element.348), channel_id=1, source_target_pairs={{0,2},{1,3},{2,0},{3,1},{4,6},{5,7},{6,4},{7,5},{8,10},{9,11},{10,... | collective-permute-start | bytes 7864328 | tf_op jit(solution)/shard_map/ppermute | solution.py:348
  273.0 21.3 %collective-permute-start.28 = (bf16[1024,1280]{1,0:T(8,128)(2,1)}, bf16[1024,1280]{1,0:T(8,128)(2,1)}, u32[]{:S(2)}, u32[]{:S(2)}) collective-permute-start(bf16[1024,1280]{1,0:T(8,128)(2,1)} %get-tuple-element.349), channel_id=1, source_target_pairs={{0,2},{1,3},{2,0},{3,1},{4,6},{5,7},{6,4},{7,5},{8,10},{9,11},{10,... | collective-permute-start | bytes 7864328 | tf_op jit(solution)/shard_map/ppermute | solution.py:348
  294.3 56.9 %collective-permute-start.29 = (bf16[640,1280]{1,0:T(8,128)(2,1)}, bf16[640,1280]{1,0:T(8,128)(2,1)}, u32[]{:S(2)}, u32[]{:S(2)}) collective-permute-start(bf16[640,1280]{1,0:T(8,128)(2,1)} %get-tuple-element.364), channel_id=1, source_target_pairs={{0,4},{1,9},{2,10},{3,7},{4,12},{5,1},{6,2},{7,15},{8,0},{9,17},{1... | collective-permute-start | bytes 4915208 | tf_op jit(solution)/shard_map/ppermute | solution.py:348
  295.8 55.3 %collective-permute-start.30 = (bf16[640,1280]{1,0:T(8,128)(2,1)}, bf16[640,1280]{1,0:T(8,128)(2,1)}, u32[]{:S(2)}, u32[]{:S(2)}) collective-permute-start(bf16[640,1280]{1,0:T(8,128)(2,1)} %get-tuple-element.365), channel_id=1, source_target_pairs={{0,1},{1,0},{2,3},{3,2},{4,5},{5,4},{6,7},{7,6},{8,9},{9,8},{10,11... | collective-permute-start | bytes 4915208 | tf_op jit(solution)/shard_map/ppermute | solution.py:348
  298.0 79.0 %collective-permute-start.32 = (bf16[640,1280]{1,0:T(8,128)(2,1)}, bf16[640,1280]{1,0:T(8,128)(2,1)}, u32[]{:S(2)}, u32[]{:S(2)}) collective-permute-start(bf16[640,1280]{1,0:T(8,128)(2,1)} %get-tuple-element.385), channel_id=1, source_target_pairs={{0,8},{1,5},{2,6},{3,11},{4,0},{5,13},{6,14},{7,3},{8,16},{9,1},{1... | collective-permute-start | bytes 4915208 | tf_op jit(solution)/shard_map/ppermute | solution.py:348
  298.4 78.6 %collective-permute-start.33 = (bf16[640,1280]{1,0:T(8,128)(2,1)}, bf16[640,1280]{1,0:T(8,128)(2,1)}, u32[]{:S(2)}, u32[]{:S(2)}) collective-permute-start(bf16[640,1280]{1,0:T(8,128)(2,1)} %get-tuple-element.386), channel_id=1, source_target_pairs={{0,1},{1,0},{2,3},{3,2},{4,5},{5,4},{6,7},{7,6},{8,9},{9,8},{10,11... | collective-permute-start | bytes 4915208 | tf_op jit(solution)/shard_map/ppermute | solution.py:348
  355.6 21.7 %collective-permute-start.31 = (bf16[640,1280]{1,0:T(8,128)(2,1)}, bf16[640,1280]{1,0:T(8,128)(2,1)S(1)}, u32[]{:S(2)}, u32[]{:S(2)}) collective-permute-start(bf16[640,1280]{1,0:T(8,128)(2,1)} %add_convert_fusion.3), channel_id=1, source_target_pairs={{0,4},{1,9},{2,10},{3,7},{4,12},{5,1},{6,2},{7,15},{8,0},{9,17},{1... | collective-permute-start | bytes 4915208 | tf_op jit(solution)/shard_map/ppermute | solution.py:348
  380.7 33.6 %collective-permute-start.37 = (bf16[640,1280]{1,0:T(8,128)(2,1)}, bf16[640,1280]{1,0:T(8,128)(2,1)S(1)}, u32[]{:S(2)}, u32[]{:S(2)}) collective-permute-start(bf16[640,1280]{1,0:T(8,128)(2,1)} %add_convert_fusion.2), channel_id=1, source_target_pairs={{0,4},{1,9},{2,10},{3,7},{4,12},{5,1},{6,2},{7,15},{8,0},{9,17},{1... | collective-permute-start | bytes 4915208 | tf_op jit(solution)/shard_map/ppermute | solution.py:348
  382.3 32.0 %collective-permute-start.38 = (bf16[256,1280]{1,0:T(8,128)(2,1)}, bf16[256,1280]{1,0:T(8,128)(2,1)S(1)}, u32[]{:S(2)}, u32[]{:S(2)}) collective-permute-start(bf16[256,1280]{1,0:T(8,128)(2,1)} %get-tuple-element.430), channel_id=1, source_target_pairs={{0,1},{1,0},{2,3},{3,2},{4,5},{5,4},{6,7},{7,6},{8,9},{9,8},{10,11... | collective-permute-start | bytes 1966088 | tf_op jit(solution)/shard_map/ppermute | solution.py:348
  416.1 27.6 %collective-permute-start.41 = (bf16[640,1280]{1,0:T(8,128)(2,1)}, bf16[640,1280]{1,0:T(8,128)(2,1)S(1)}, u32[]{:S(2)}, u32[]{:S(2)}) collective-permute-start(bf16[640,1280]{1,0:T(8,128)(2,1)} %add_convert_fusion.1), channel_id=1, source_target_pairs={{0,4},{1,9},{2,10},{3,7},{4,12},{5,1},{6,2},{7,15},{8,0},{9,17},{1... | collective-permute-start | bytes 4915208 | tf_op jit(solution)/shard_map/ppermute | solution.py:348
  417.4 26.3 %collective-permute-start.40 = (bf16[256,1280]{1,0:T(8,128)(2,1)}, bf16[256,1280]{1,0:T(8,128)(2,1)S(1)}, u32[]{:S(2)}, u32[]{:S(2)}) collective-permute-start(bf16[256,1280]{1,0:T(8,128)(2,1)} %get-tuple-element.452), channel_id=1, source_target_pairs={{0,1},{1,0},{2,3},{3,2},{4,5},{5,4},{6,7},{7,6},{8,9},{9,8},{10,11... | collective-permute-start | bytes 1966088 | tf_op jit(solution)/shard_map/ppermute | solution.py:348
  421.1 22.6 %collective-permute-start.39 = (bf16[80,3584]{1,0:T(8,128)(2,1)}, bf16[80,3584]{1,0:T(8,128)(2,1)}, u32[]{:S(2)}, u32[]{:S(2)}) collective-permute-start(bf16[80,3584]{1,0:T(8,128)(2,1)} %fusion.5), channel_id=1, source_target_pairs={{0,4},{1,9},{2,10},{3,7},{4,12},{5,1},{6,2},{7,15},{8,0},{9,17},{1... | collective-permute-start | bytes 1720328 | tf_op jit(solution)/shard_map/ppermute | solution.py:348
  468.7 63.5 %collective-permute-start.52 = (bf16[512,1280]{1,0:T(8,128)(2,1)}, bf16[512,1280]{1,0:T(8,128)(2,1)}, u32[]{:S(2)}, u32[]{:S(2)}) collective-permute-start(bf16[512,1280]{1,0:T(8,128)(2,1)} %get-tuple-element.508), channel_id=1, source_target_pairs={{0,1},{1,0},{2,3},{3,2},{4,5},{5,4},{6,7},{7,6},{8,9},{9,8},{10,11... | collective-permute-start | bytes 3932168 | tf_op jit(solution)/shard_map/ppermute | solution.py:348
  473.2 23.5 %collective-permute-start.45 = (bf16[80,3584]{1,0:T(8,128)(2,1)}, bf16[80,3584]{1,0:T(8,128)(2,1)}, u32[]{:S(2)}, u32[]{:S(2)}) collective-permute-start(bf16[80,3584]{1,0:T(8,128)(2,1)} %get-tuple-element.550), channel_id=1, source_target_pairs={{0,4},{1,9},{2,10},{3,7},{4,12},{5,1},{6,2},{7,15},{8,0},{9,17},{1... | collective-permute-start | bytes 1720328 | tf_op jit(solution)/shard_map/ppermute | solution.py:348
  474.4 22.3 %collective-permute-start.46 = (bf16[80,3584]{1,0:T(8,128)(2,1)S(1)}, bf16[80,3584]{1,0:T(8,128)(2,1)}, u32[]{:S(2)}, u32[]{:S(2)}) collective-permute-start(bf16[80,3584]{1,0:T(8,128)(2,1)S(1)} %get-tuple-element.549), channel_id=1, source_target_pairs={{0,8},{1,5},{2,6},{3,11},{4,0},{5,13},{6,14},{7,3},{8,16},{9,1},{1... | collective-permute-start | bytes 1720328 | tf_op jit(solution)/shard_map/ppermute | solution.py:348
  501.1 31.1 %collective-permute-start.50 = (bf16[320,1280]{1,0:T(8,128)(2,1)S(1)}, bf16[320,1280]{1,0:T(8,128)(2,1)S(1)}, u32[]{:S(2)}, u32[]{:S(2)}) collective-permute-start(bf16[320,1280]{1,0:T(8,128)(2,1)S(1)} %get-tuple-element.537), channel_id=1, source_target_pairs={{0,1},{1,0},{2,3},{3,2},{4,5},{5,4},{6,7},{7,6},{8,9},{9,8},{10,11... | collective-permute-start | bytes 2457608 | tf_op jit(solution)/shard_map/ppermute | solution.py:348
  511.2 23.3 %collective-permute-start.51 = (bf16[80,3584]{1,0:T(8,128)(2,1)S(1)}, bf16[80,3584]{1,0:T(8,128)(2,1)S(1)}, u32[]{:S(2)}, u32[]{:S(2)}) collective-permute-start(bf16[80,3584]{1,0:T(8,128)(2,1)S(1)} %fusion), channel_id=1, source_target_pairs={{0,1},{1,0},{2,3},{3,2},{4,5},{5,4},{6,7},{7,6},{8,9},{9,8},{10,11... | collective-permute-start | bytes 1720328 | tf_op jit(solution)/shard_map/ppermute | solution.py:348
  (107 other events, 1177.3 us)
